TPU v7x, 32 devices: a whole 2x2x4 slice. The times are simulated.
32 devices in a mesh: row: 2 (over y), chan: 4 (over z), dp: 4 (over x, core).
Axes of the slice: x: 2, y: 2, z: 4, core: 2. Of those that a mesh axis runs over, the one named last changes fastest.
Arguments:
- features_in: bfloat16 [4, 36, 64, 2048], P('dp', 'row', None, 'chan'), may hold values from -6 to 6
- depth_weights: bfloat16 [3, 3, 3, 2048], P(None, None, None, 'chan'), may hold values from -2 to 2
- point_weights: bfloat16 [4, 2048, 256], P(None, 'chan'), may hold values from -0.125 to 0.125
- proj_weights: bfloat16 [4, 256, 256], replicated, may hold values from -0.1875 to 0.1875
- cotangent: bfloat16 [4, 36, 64, 256], P('dp', 'row', 'chan'), may hold values from -18 to 18
Outputs:
- output: bfloat16 [4, 36, 64, 256], P('dp', 'row', 'chan')
- grad_input: bfloat16 [4, 36, 64, 2048], P('dp', 'row', None, 'chan')
- grad_depth: float32 [3, 3, 3, 2048], P(None, None, None, 'chan')
- grad_point: float32 [4, 2048, 256], P(None, 'chan')
- grad_proj: float32 [4, 256, 256], replicated
All inputs are finite; a program needn't handle non-finite values.
Results may differ from a plain program's by a relative error of at most 0.0059.
Values may be sent and summed in bfloat16 or wider, within the bound.
No kernel may reach another device: no remote copies, remote signals or barrier semaphores. Data moves between devices by JAX's collectives and lax.ppermute only.
A program may use at most 64 MiB of HBM per device.

v0:
```python
import math

import jax
import jax.numpy as jnp
from jax import lax
from jax.sharding import PartitionSpec as P

BASE_DILATION = 12


def shifted(value, axis, steps):
    count = lax.axis_size(axis)
    first, last = (max(0, -steps), min(count, count - steps))
    return lax.ppermute(value, axis, [(source, source + steps) for source in range(first, last)])


def window(source, top, left, band_rows, band_cols):
    upper = lax.slice_in_dim(source, top, top + band_rows, axis=1)
    return lax.slice_in_dim(upper, left, left + band_cols, axis=2)


def on_device(features_in, depth_weights, point_weights, proj_weights, cotangent):
    samples, band_rows, band_cols, channels = features_in.shape
    weight_scale = 1.0 / math.sqrt(
        samples * lax.axis_size("dp") * band_rows * lax.axis_size("row") * band_cols
    )
    largest_reach = 3 * BASE_DILATION
    offsets = (2, 1, -1, -2)
    arrivals = []
    for offset in offsets:
        arrivals.append(shifted(features_in, "row", offset))
    tall_rows = jnp.concatenate(
        [arrivals[0], arrivals[1], features_in, arrivals[2], arrivals[3]], axis=1
    )
    padded = jnp.pad(tall_rows, ((0, 0), (0, 0), (largest_reach, largest_reach), (0, 0)))
    branch_maps = [features_in]
    for branch_level in range(3):
        tap_spacing = (branch_level + 1) * BASE_DILATION
        summed = jnp.zeros(features_in.shape, jnp.float32)
        for row_tap in range(3):
            for col_tap in range(3):
                input_kernel_tap = window(
                    padded,
                    largest_reach + (row_tap - 1) * tap_spacing,
                    largest_reach + (col_tap - 1) * tap_spacing,
                    band_rows,
                    band_cols,
                )
                summed = summed + input_kernel_tap.astype(jnp.float32) * depth_weights[
                    branch_level, row_tap, col_tap
                ].astype(jnp.float32)
        branch_maps.append(summed.astype(jnp.bfloat16))
    spread = jnp.stack(branch_maps)
    full_point = lax.all_gather(point_weights, "chan", axis=1, tiled=True)
    preact = jnp.einsum(
        "bsrwc,bcf->bsrwf",
        lax.all_to_all(spread, "chan", split_axis=3, concat_axis=4, tiled=True),
        full_point,
        preferred_element_type=jnp.float32,
    )
    activation = jax.nn.silu(preact).astype(jnp.bfloat16)
    output = jnp.einsum(
        "bsrwf,bfg->srwg", activation, proj_weights, preferred_element_type=jnp.float32
    ).astype(jnp.bfloat16)
    silu_gradient = jnp.einsum(
        "srwg,bfg->bsrwf", cotangent, proj_weights, preferred_element_type=jnp.float32
    )
    logistic = jax.nn.sigmoid(preact)
    pre_grad = (silu_gradient * logistic * (1.0 + preact * (1.0 - logistic))).astype(jnp.bfloat16)
    proj_term = jnp.einsum(
        "bsrwf,srwg->bfg", activation, cotangent, preferred_element_type=jnp.float32
    )
    grad_proj = lax.psum(proj_term, ("row", "chan", "dp")) * weight_scale
    incoming = lax.all_gather(pre_grad, "chan", axis=3, tiled=True)
    local_grad = jnp.einsum(
        "bsrwf,bcf->bsrwc", incoming, point_weights, preferred_element_type=jnp.float32
    ).astype(jnp.bfloat16)
    spread_grad = local_grad
    point_sum = jnp.einsum("bsrwc,bsrwf->bcf", spread, incoming, preferred_element_type=jnp.float32)
    spread_grad, point_term = (spread_grad, point_sum)
    depth_rows = []
    for branch_level in range(3):
        tap_spacing = (branch_level + 1) * BASE_DILATION
        branch_grad = spread_grad[branch_level + 1].astype(jnp.float32)
        gathered = []
        for row_tap in range(3):
            for col_tap in range(3):
                input_kernel_tap = window(
                    padded,
                    largest_reach + (row_tap - 1) * tap_spacing,
                    largest_reach + (col_tap - 1) * tap_spacing,
                    band_rows,
                    band_cols,
                )
                gathered.append(
                    jnp.sum(input_kernel_tap.astype(jnp.float32) * branch_grad, axis=(0, 1, 2))
                )
        depth_rows.append(jnp.stack(gathered).reshape(3, 3, channels))
    depth_term = jnp.stack(depth_rows)
    point_summed, depth_summed = lax.psum((point_term, depth_term), ("row", "dp"))
    grad_point = point_summed * weight_scale
    grad_depth = depth_summed * weight_scale
    neighbour_sets = []
    for branch_level in range(3):
        neighbour_sets.append(
            [shifted(spread_grad[branch_level + 1], "row", offset) for offset in offsets]
        )
    grad_in = spread_grad[0].astype(jnp.float32)
    for branch_level in range(3):
        tap_spacing = (branch_level + 1) * BASE_DILATION
        received = neighbour_sets[branch_level]
        grad_tall = jnp.concatenate(
            [received[0], received[1], spread_grad[branch_level + 1], received[2], received[3]],
            axis=1,
        )
        grad_padded = jnp.pad(grad_tall, ((0, 0), (0, 0), (largest_reach, largest_reach), (0, 0)))
        for row_tap in range(3):
            for col_tap in range(3):
                grad_tap = window(
                    grad_padded,
                    largest_reach - (row_tap - 1) * tap_spacing,
                    largest_reach - (col_tap - 1) * tap_spacing,
                    band_rows,
                    band_cols,
                )
                grad_in = grad_in + grad_tap.astype(jnp.float32) * depth_weights[
                    branch_level, row_tap, col_tap
                ].astype(jnp.float32)
    return (output, grad_in.astype(jnp.bfloat16), grad_depth, grad_point, grad_proj)


def solution(mesh):
    in_specs = (
        P("dp", "row", None, "chan"),
        P(None, None, None, "chan"),
        P(None, "chan", None),
        P(),
        P("dp", "row", "chan", None),
    )
    out_specs = (
        P("dp", "row", "chan", None),
        P("dp", "row", None, "chan"),
        P(None, None, None, "chan"),
        P(None, "chan", None),
        P(),
    )
    return jax.shard_map(
        on_device, mesh=mesh, in_specs=in_specs, out_specs=out_specs, check_vma=False
    )
```

profile of v0, /device:TPU:0, one launch (start us, length us, event | category | flops | bytes accessed | tf_op | source)
XLA Modules:
  0.0 646.2 jit_solution(15700242984806619548)
XLA Ops:
  7.2 0.9 collective-permute-start
  8.1 4.9 collective-permute-start.1
  13.0 1.3 collective-permute-start.2
  14.3 0.8 slice_convert_fusion.25
  15.1 0.9 slice_convert_fusion.26
  16.2 22.2 %collective-permute-done.1 = bf16[1,18,64,512]{3,2,1,0:T(8,128)(2,1)S(1)} collective-permute-done((bf16[1,18,64,512]{3,2,1,0:T(8,128)(2,1)}, bf16[1,18,64,512]{3,2,1,0:T(8,128)(2,1)S(1)}, u32[]{:S(2)}, u32[]{:S(2)}) %collective-permute-start.1) | collective-permute-done | bytes 1179680 | tf_op jit(solution)/shard_map/ppermute | solution.py:14
  38.7 3.9 collective-permute-done.2
  42.5 0.1 constant_dynamic-update-slice_fusion.1
  42.7 2.0 fusion.92
  44.8 2.6 fusion.91
  47.4 3.9 fusion.93
  51.3 1.0 copy-done.12
  52.3 0.6 pad_maximum_fusion
  52.9 5.7 copy.23
  58.7 5.0 all-to-all-start
  63.7 0.7 all-gather.3.cloned.1.call-update
  64.3 0.2 all-reduce.9.cloned.1.call-start
  64.6 170.0 %all-to-all-done = bf16[4,1,18,64,512]{4,0,2,1,3:T(4,128)(2,1)} async-done(((bf16[4,1,18,64,512]{4,0,2,1,3:T(4,128)(2,1)}), bf16[4,1,18,64,512]{4,0,2,1,3:T(4,128)(2,1)}, u32[]{:S(2)}, u32[]{:S(2)}) %all-to-all-start) | async-done | bytes 4718624 | tf_op jit(solution)/shard_map/all_to_all | solution.py:57
  234.6 8.1 %copy.36 = bf16[4,1,18,4,16,512]{5,3,4,2,0,1:T(4,128)(2,1)} copy(bf16[4,1,18,4,16,512]{5,0,2,4,3,1:T(4,128)(2,1)} %bitcast.31) | data formatting | bytes 9437184 | tf_op jit(solution)/shard_map/all_to_all | solution.py:57
  242.6 8.7 %reshape.148 = bf16[4,18,16,2048]{3,2,1,0:T(8,128)(2,1)} reshape(bf16[4,1,18,16,4,512]{5,4,3,2,0,1:T(4,128)(2,1)} %bitcast.142) | data formatting | bytes 9437184 | tf_op jit(solution)/shard_map/reshape.32
  251.4 6.1 multiply_convert_fusion
  257.5 1.4 convolution_bitcast_fusion.1
  259.0 2.7 fusion.90
  261.8 1.0 fusion.95
  262.8 124.2 %all-reduce.9.cloned.1.call-done = f32[4,256,256]{2,1,0:T(8,128)} async-done(((f32[4,256,256]{2,1,0:T(8,128)}), f32[4,256,256]{2,1,0:T(8,128)}) %all-reduce.9.cloned.1.call-update) | async-done | bytes 1048592 | tf_op jit(solution)/shard_map/psum | solution.py:73
  387.0 2.3 broadcast_multiply_fusion.1
  389.3 48.8 %all-gather.5.cloned.1.call-done = bf16[4,1,18,64,256]{4,3,2,0,1:T(8,128)(2,1)} async-done(((bf16[4,1,18,16,256]{4,3,2,0,1:T(8,128)(2,1)}), bf16[4,1,18,64,256]{4,3,2,0,1:T(8,128)(2,1)}) %all-gather.5.cloned.1.call-update) | async-done | bytes 2359312 | tf_op jit(solution)/shard_map/all_gather | solution.py:74
  438.1 3.4 convolution_convert_fusion
  441.5 7.5 %fusion.71 = (f32[512]{0:T(512)S(1)}, f32[512]{0:T(512)S(1)}, f32[512]{0:T(512)S(1)}, f32[512]{0:T(512)S(1)}, f32[512]{0:T(512)S(1)}, /*index=5*/f32[512]{0:T(51...) fusion(bf16[1,90,64,512]{3,2,1,0:T(8,128)(2,1)} %copy-done.2, bf16[4,18,64,512]{3,2,1,0:T(8,128)(2,1)S(1)} %convolution_convert_fusion), kind=kLoop, calls=%fused_computation.168 | loop fusion | flops 17690112 | bytes 9455616 | tf_op jit(solution)/shard_map/reduce_sum | solution.py:96
  449.1 2.0 fusion.101
  451.1 1.8 collective-permute-start.6
  452.9 4.4 collective-permute-start.7
  457.3 1.7 collective-permute-start.3
  459.0 2.4 collective-permute-start.4
  461.4 3.3 fusion.83
  464.7 1.8 collective-permute-start.9
  466.6 5.8 fusion.80
  472.4 2.2 fusion.70
  474.9 23.8 %psum.21 = f32[3,3,3,512]{3,2,1,0:T(4,128)S(1)} all-reduce(f32[3,3,3,512]{3,2,1,0:T(4,128)S(1)} %pad_maximum_fusion.9), channel_id=1, replica_groups=mesh['row'=2,'chan'=4,'dp'=4] {'row','dp'}, use_global_device_ids=true, to_apply=%region_26.27 | all-reduce | flops 13824 | bytes 110592 | tf_op jit(solution)/shard_map/psum | solution.py:100
  498.7 4.9 collective-permute-start.10
  503.6 0.7 broadcast_multiply_fusion.2
  504.2 37.1 %all-reduce.7.cloned.1.call-done = f32[4,512,256]{2,1,0:T(8,128)} async-done(((f32[4,512,256]{2,1,0:T(8,128)}), f32[4,512,256]{2,1,0:T(8,128)}) %all-reduce.7.cloned.1.call-update) | async-done | bytes 2097168 | tf_op jit(solution)/shard_map/psum | solution.py:100
  541.4 3.3 broadcast_multiply_fusion
  544.7 1.3 collective-permute-start.11
  546.0 1.4 constant_dynamic-update-slice_fusion.14
  547.3 1.4 constant_dynamic-update-slice_fusion.9
  548.7 1.4 collective-permute-start.8
  550.1 1.4 constant_dynamic-update-slice_fusion.19
  551.5 1.3 collective-permute-start.5
  552.8 1.4 constant_dynamic-update-slice_fusion.13
  554.2 1.4 constant_dynamic-update-slice_fusion.8
  555.6 0.3 collective-permute-done.10
  555.9 1.4 constant_dynamic-update-slice_fusion.18
  557.3 0.4 constant_dynamic-update-slice_fusion.17
  557.7 18.1 %collective-permute-done.11 = bf16[1,18,64,512]{3,2,1,0:T(8,128)(2,1)S(1)} collective-permute-done((bf16[1,18,64,512]{3,2,1,0:T(8,128)(2,1)}, bf16[1,18,64,512]{3,2,1,0:T(8,128)(2,1)S(1)}, u32[]{:S(2)}, u32[]{:S(2)}) %collective-permute-start.11) | collective-permute-done | bytes 1179680 | tf_op jit(solution)/shard_map/ppermute | solution.py:14
  575.7 0.1 constant_dynamic-update-slice_fusion.16
  575.9 1.4 constant_dynamic-update-slice_fusion.15
  577.2 23.8 %collective-permute-done.8 = bf16[1,18,64,512]{3,2,1,0:T(8,128)(2,1)S(1)} collective-permute-done((bf16[1,18,64,512]{3,2,1,0:T(8,128)(2,1)}, bf16[1,18,64,512]{3,2,1,0:T(8,128)(2,1)S(1)}, u32[]{:S(2)}, u32[]{:S(2)}) %collective-permute-start.8) | collective-permute-done | bytes 1179680 | tf_op jit(solution)/shard_map/ppermute | solution.py:14
  601.0 0.1 constant_dynamic-update-slice_fusion.11
  601.1 1.4 constant_dynamic-update-slice_fusion.10
  602.5 23.2 %collective-permute-done.5 = bf16[1,18,64,512]{3,2,1,0:T(8,128)(2,1)S(1)} collective-permute-done((bf16[1,18,64,512]{3,2,1,0:T(8,128)(2,1)}, bf16[1,18,64,512]{3,2,1,0:T(8,128)(2,1)S(1)}, u32[]{:S(2)}, u32[]{:S(2)}) %collective-permute-start.5) | collective-permute-done | bytes 1179680 | tf_op jit(solution)/shard_map/ppermute | solution.py:14
  625.8 0.1 constant_dynamic-update-slice_fusion.6
  625.9 1.4 constant_dynamic-update-slice_fusion.5
  627.3 12.4 %fusion.39 = bf16[1,18,64,512]{3,2,1,0:T(8,128)(2,1)} fusion(bf16[1,18,64,512]{3,2,1,0:T(8,128)(2,1)} %collective-permute-done.9, bf16[1,18,64,512]{3,2,1,0:T(8,128)(2,1)} %get-tuple-element.36, bf16[1,90,64,512]{3,2,1,0:T(8,128)(2,1)S(1)} %constant_dynamic-update-slice_fusion.5, bf16[1,90,64,512]{3,2,1,0:T(8,128)(2,1)S(1)} %constant_dynamic-update-slice_fusion.10, ...), kind=kLoop, calls=%fused_computation.136 | loop fusion | flops 55443456 | bytes 30726144 | tf_op jit(solution)/shard_map/convert_element_type | solution.py:129
  (95 shorter events, 0.9 us)
Async XLA Ops:
  7.2 251.8 %copy-start = (bf16[4,256,256]{2,1,0:T(8,128)(2,1)S(1)}, bf16[4,256,256]{2,1,0:T(8,128)(2,1)}, u32[]{:S(2)}) copy-start(bf16[4,256,256]{2,1,0:T(8,128)(2,1)} %param.8) | copy-start | bytes 1572868
  7.2 8.9 %collective-permute-start = (bf16[1,18,64,512]{3,2,1,0:T(8,128)(2,1)}, bf16[1,18,64,512]{3,2,1,0:T(8,128)(2,1)S(1)}, u32[]{:S(2)}, u32[]{:S(2)}) collective-permute-start(bf16[1,18,64,512]{3,2,1,0:T(8,128)(2,1)} %param.5), channel_id=1, source_target_pairs={} | collective-permute-start | bytes 3538952 | tf_op jit(solution)/shard_map/ppermute | solution.py:14
  8.1 30.4 %collective-permute-start.1 = (bf16[1,18,64,512]{3,2,1,0:T(8,128)(2,1)}, bf16[1,18,64,512]{3,2,1,0:T(8,128)(2,1)S(1)}, u32[]{:S(2)}, u32[]{:S(2)}) collective-permute-start(bf16[1,18,64,512]{3,2,1,0:T(8,128)(2,1)} %param.5), channel_id=1, source_target_pairs={{0,16},{1,17},{2,18},{3,19},{4,20},{5,21},{6,22},{7,23},{8,24},{9,... | collective-permute-start | bytes 3538952 | tf_op jit(solution)/shard_map/ppermute | solution.py:14
  13.0 29.5 %collective-permute-start.2 = (bf16[1,18,64,512]{3,2,1,0:T(8,128)(2,1)}, bf16[1,18,64,512]{3,2,1,0:T(8,128)(2,1)S(1)}, u32[]{:S(2)}, u32[]{:S(2)}) collective-permute-start(bf16[1,18,64,512]{3,2,1,0:T(8,128)(2,1)} %param.5), channel_id=1, source_target_pairs={{16,0},{17,1},{18,2},{19,3},{20,4},{21,5},{22,6},{23,7},{24,8},{25... | collective-permute-start | bytes 3538952 | tf_op jit(solution)/shard_map/ppermute | solution.py:14
  16.0 28.7 %copy-start.16 = (f32[1,1,1,512]{3,2,1,0:T(1,128)}, f32[1,1,1,512]{3,2,1,0:T(1,128)S(1)}, u32[]{:S(2)}) copy-start(f32[1,1,1,512]{3,2,1,0:T(1,128)S(1)} %get-tuple-element.38) | copy-start | bytes 6148
  16.0 28.7 %copy-start.18 = (f32[1,1,1,512]{3,2,1,0:T(1,128)}, f32[1,1,1,512]{3,2,1,0:T(1,128)S(1)}, u32[]{:S(2)}) copy-start(f32[1,1,1,512]{3,2,1,0:T(1,128)S(1)} %get-tuple-element.39) | copy-start | bytes 6148
  16.1 28.7 %copy-start.20 = (f32[1,1,1,512]{3,2,1,0:T(1,128)}, f32[1,1,1,512]{3,2,1,0:T(1,128)S(1)}, u32[]{:S(2)}) copy-start(f32[1,1,1,512]{3,2,1,0:T(1,128)S(1)} %get-tuple-element.40) | copy-start | bytes 6148
  16.1 28.7 %copy-start.22 = (f32[1,1,1,512]{3,2,1,0:T(1,128)}, f32[1,1,1,512]{3,2,1,0:T(1,128)S(1)}, u32[]{:S(2)}) copy-start(f32[1,1,1,512]{3,2,1,0:T(1,128)S(1)} %get-tuple-element.41) | copy-start | bytes 6148
  16.1 28.7 %copy-start.24 = (f32[1,1,1,512]{3,2,1,0:T(1,128)}, f32[1,1,1,512]{3,2,1,0:T(1,128)S(1)}, u32[]{:S(2)}) copy-start(f32[1,1,1,512]{3,2,1,0:T(1,128)S(1)} %get-tuple-element.42) | copy-start | bytes 6148
  16.1 28.7 %copy-start.26 = (f32[1,1,1,512]{3,2,1,0:T(1,128)}, f32[1,1,1,512]{3,2,1,0:T(1,128)S(1)}, u32[]{:S(2)}) copy-start(f32[1,1,1,512]{3,2,1,0:T(1,128)S(1)} %get-tuple-element.43) | copy-start | bytes 6148
  16.1 28.7 %copy-start.28 = (f32[1,1,1,512]{3,2,1,0:T(1,128)}, f32[1,1,1,512]{3,2,1,0:T(1,128)S(1)}, u32[]{:S(2)}) copy-start(f32[1,1,1,512]{3,2,1,0:T(1,128)S(1)} %get-tuple-element.44) | copy-start | bytes 6148
  16.1 22.5 %copy-start.4 = (bf16[1,18,64,512]{3,2,1,0:T(8,128)(2,1)S(1)}, bf16[1,18,64,512]{3,2,1,0:T(8,128)(2,1)}, u32[]{:S(2)}) copy-start(bf16[1,18,64,512]{3,2,1,0:T(8,128)(2,1)} %param.5) | copy-start | bytes 3538948
  38.5 8.9 %copy-start.5 = (bf16[1,18,64,512]{3,2,1,0:T(8,128)(2,1)}, bf16[1,18,64,512]{3,2,1,0:T(8,128)(2,1)S(1)}, u32[]{:S(2)}) copy-start(bf16[1,18,64,512]{3,2,1,0:T(8,128)(2,1)S(1)} %collective-permute-done.1) | copy-start | bytes 3538948
  42.5 4.9 copy-start.7
  42.7 4.7 copy-start.2
  44.7 6.6 %copy-start.10 = (bf16[1,1,18,64,512]{4,3,2,1,0:T(8,128)(2,1)}, bf16[1,1,18,64,512]{4,3,2,1,0:T(8,128)(2,1)S(1)}, u32[]{:S(2)}) copy-start(bf16[1,1,18,64,512]{4,3,2,1,0:T(8,128)(2,1)S(1)} %fusion.92) | copy-start | bytes 3538948
  47.4 3.9 copy-start.14
  51.3 1.0 copy-start.12
  58.7 175.9 %all-to-all-start = ((bf16[4,1,18,64,512]{4,0,2,1,3:T(4,128)(2,1)}), bf16[4,1,18,64,512]{4,0,2,1,3:T(4,128)(2,1)}, u32[]{:S(2)}, u32[]{:S(2)}) async-start(bf16[4,1,18,64,512]{4,0,2,1,3:T(4,128)(2,1)} %copy.23), calls=%async_computation | async-start | bytes 9437184 | tf_op jit(solution)/shard_map/all_to_all | solution.py:57
  63.6 187.8 %all-gather.3.cloned.1.call-start = ((), (), s32[]{:S(2)}) async-start(), calls=%async_computation.1 | async-start | bytes 5242880 | tf_op jit(solution)/shard_map/all_gather | solution.py:54
  64.3 322.7 %all-reduce.9.cloned.1.call-start = ((), (), s32[]{:S(2)}) async-start(), calls=%async_computation.4 | async-start | bytes 2097152 | tf_op jit(solution)/shard_map/psum | solution.py:73
  251.4 6.1 copy-start.30
  258.9 179.2 %all-gather.5.cloned.1.call-start = ((), (), s32[]{:S(2)}) async-start(), calls=%async_computation.2 | async-start | bytes 2949120 | tf_op jit(solution)/shard_map/all_gather | solution.py:74
  261.8 279.6 %all-reduce.7.cloned.1.call-start = ((), (), s32[]{:S(2)}) async-start(), calls=%async_computation.3 | async-start | bytes 4194304 | tf_op jit(solution)/shard_map/psum | solution.py:100
  441.5 7.6 %copy-start.3 = (bf16[4,18,64,512]{3,2,1,0:T(8,128)(2,1)}, bf16[4,18,64,512]{3,2,1,0:T(8,128)(2,1)S(1)}, u32[]{:S(2)}) copy-start(bf16[4,18,64,512]{3,2,1,0:T(8,128)(2,1)S(1)} %convolution_convert_fusion) | copy-start | bytes 14155780
  449.1 12.3 %copy-start.9 = (bf16[4,1,18,64,256]{4,3,2,0,1:T(8,128)(2,1)S(1)}, bf16[4,1,18,64,256]{4,3,2,0,1:T(8,128)(2,1)}, u32[]{:S(2)}) copy-start(bf16[4,1,18,64,256]{4,3,2,0,1:T(8,128)(2,1)} %all-gather.5.cloned.1.call-done) | copy-start | bytes 7077892
  449.1 12.3 %copy-start.11 = (bf16[1,1,18,64,512]{4,3,2,1,0:T(8,128)(2,1)S(1)}, bf16[1,1,18,64,512]{4,3,2,1,0:T(8,128)(2,1)}, u32[]{:S(2)}) copy-start(bf16[1,1,18,64,512]{4,3,2,1,0:T(8,128)(2,1)} %copy-done.10) | copy-start | bytes 3538948
  449.1 12.3 %copy-start.13 = (bf16[1,1,18,64,512]{4,3,2,1,0:T(8,128)(2,1)S(1)}, bf16[1,1,18,64,512]{4,3,2,1,0:T(8,128)(2,1)}, u32[]{:S(2)}) copy-start(bf16[1,1,18,64,512]{4,3,2,1,0:T(8,128)(2,1)} %copy-done.12) | copy-start | bytes 3538948
  449.1 12.3 %copy-start.15 = (bf16[1,1,18,64,512]{4,3,2,1,0:T(8,128)(2,1)S(1)}, bf16[1,1,18,64,512]{4,3,2,1,0:T(8,128)(2,1)}, u32[]{:S(2)}) copy-start(bf16[1,1,18,64,512]{4,3,2,1,0:T(8,128)(2,1)} %copy-done.14) | copy-start | bytes 3538948
  451.1 47.6 %collective-permute-start.6 = (bf16[1,18,64,512]{3,2,1,0:T(8,128)(2,1)}, bf16[1,18,64,512]{3,2,1,0:T(8,128)(2,1)}, u32[]{:S(2)}, u32[]{:S(2)}) collective-permute-start(bf16[1,18,64,512]{3,2,1,0:T(8,128)(2,1)} %get-tuple-element.34), channel_id=1, source_target_pairs={} | collective-permute-start | bytes 3538952 | tf_op jit(solution)/shard_map/ppermute | solution.py:14
  452.9 98.6 %collective-permute-start.7 = (bf16[1,18,64,512]{3,2,1,0:T(8,128)(2,1)}, bf16[1,18,64,512]{3,2,1,0:T(8,128)(2,1)}, u32[]{:S(2)}, u32[]{:S(2)}) collective-permute-start(bf16[1,18,64,512]{3,2,1,0:T(8,128)(2,1)} %get-tuple-element.34), channel_id=1, source_target_pairs={{0,16},{1,17},{2,18},{3,19},{4,20},{5,21},{6,22},{7,23},{8,24},{9,... | collective-permute-start | bytes 3538952 | tf_op jit(solution)/shard_map/ppermute | solution.py:14
  457.3 87.3 %collective-permute-start.3 = (bf16[1,18,64,512]{3,2,1,0:T(8,128)(2,1)}, bf16[1,18,64,512]{3,2,1,0:T(8,128)(2,1)}, u32[]{:S(2)}, u32[]{:S(2)}) collective-permute-start(bf16[1,18,64,512]{3,2,1,0:T(8,128)(2,1)} %get-tuple-element.36), channel_id=1, source_target_pairs={} | collective-permute-start | bytes 3538952 | tf_op jit(solution)/shard_map/ppermute | solution.py:14
  459.0 95.2 %collective-permute-start.4 = (bf16[1,18,64,512]{3,2,1,0:T(8,128)(2,1)}, bf16[1,18,64,512]{3,2,1,0:T(8,128)(2,1)}, u32[]{:S(2)}, u32[]{:S(2)}) collective-permute-start(bf16[1,18,64,512]{3,2,1,0:T(8,128)(2,1)} %get-tuple-element.36), channel_id=1, source_target_pairs={{0,16},{1,17},{2,18},{3,19},{4,20},{5,21},{6,22},{7,23},{8,24},{9,... | collective-permute-start | bytes 3538952 | tf_op jit(solution)/shard_map/ppermute | solution.py:14
  464.7 7.7 %slice-start = ((s8[4718592]{0:T(1024)(128)(4,1)}), s8[524288]{0:T(1024)(128)(4,1)S(1)}, s32[]{:S(2)}) async-start(s8[4718592]{0:T(1024)(128)(4,1)} %bitcast.136), calls=%async_computation.5 | async-start | bytes 1048576
  464.7 7.7 %slice-start.1 = ((s8[4718592]{0:T(1024)(128)(4,1)}), s8[4194304]{0:T(1024)(128)(4,1)S(1)}, s32[]{:S(2)}) async-start(s8[4718592]{0:T(1024)(128)(4,1)} %bitcast.136), calls=%async_computation.6 | async-start | bytes 8388608
  464.7 7.7 %copy-start.6 = (bf16[1,18,64,512]{3,2,1,0:T(8,128)(2,1)S(1)}, bf16[1,18,64,512]{3,2,1,0:T(8,128)(2,1)}, u32[]{:S(2)}) copy-start(bf16[1,18,64,512]{3,2,1,0:T(8,128)(2,1)} %copy-done.5) | copy-start | bytes 3538948
  464.7 7.7 %copy-start.8 = (bf16[1,18,64,512]{3,2,1,0:T(8,128)(2,1)S(1)}, bf16[1,18,64,512]{3,2,1,0:T(8,128)(2,1)}, u32[]{:S(2)}) copy-start(bf16[1,18,64,512]{3,2,1,0:T(8,128)(2,1)} %copy-done.7) | copy-start | bytes 3538948
  464.7 84.0 %collective-permute-start.9 = (bf16[1,18,64,512]{3,2,1,0:T(8,128)(2,1)}, bf16[1,18,64,512]{3,2,1,0:T(8,128)(2,1)}, u32[]{:S(2)}, u32[]{:S(2)}) collective-permute-start(bf16[1,18,64,512]{3,2,1,0:T(8,128)(2,1)} %get-tuple-element.35), channel_id=1, source_target_pairs={} | collective-permute-start | bytes 3538952 | tf_op jit(solution)/shard_map/ppermute | solution.py:14
  498.7 57.2 %collective-permute-start.10 = (bf16[1,18,64,512]{3,2,1,0:T(8,128)(2,1)}, bf16[1,18,64,512]{3,2,1,0:T(8,128)(2,1)}, u32[]{:S(2)}, u32[]{:S(2)}) collective-permute-start(bf16[1,18,64,512]{3,2,1,0:T(8,128)(2,1)} %get-tuple-element.35), channel_id=1, source_target_pairs={{0,16},{1,17},{2,18},{3,19},{4,20},{5,21},{6,22},{7,23},{8,24},{9,... | collective-permute-start | bytes 3538952 | tf_op jit(solution)/shard_map/ppermute | solution.py:14
  541.4 15.9 %slice-start.2 = ((s8[4718592]{0:T(1024)(128)(4,1)}), s8[4194304]{0:T(1024)(128)(4,1)S(1)}, s32[]{:S(2)}) async-start(s8[4718592]{0:T(1024)(128)(4,1)} %bitcast.138), calls=%async_computation.7 | async-start | bytes 8388608
  544.7 31.1 %collective-permute-start.11 = (bf16[1,18,64,512]{3,2,1,0:T(8,128)(2,1)}, bf16[1,18,64,512]{3,2,1,0:T(8,128)(2,1)S(1)}, u32[]{:S(2)}, u32[]{:S(2)}) collective-permute-start(bf16[1,18,64,512]{3,2,1,0:T(8,128)(2,1)} %get-tuple-element.35), channel_id=1, source_target_pairs={{16,0},{17,1},{18,2},{19,3},{20,4},{21,5},{22,6},{23,7},{24,8},{25... | collective-permute-start | bytes 3538952 | tf_op jit(solution)/shard_map/ppermute | solution.py:14
  548.7 8.5 %slice-start.3 = ((s8[4718592]{0:T(1024)(128)(4,1)}), s8[524288]{0:T(1024)(128)(4,1)S(1)}, s32[]{:S(2)}) async-start(s8[4718592]{0:T(1024)(128)(4,1)} %bitcast.138), calls=%async_computation.8 | async-start | bytes 1048576
  548.7 52.3 %collective-permute-start.8 = (bf16[1,18,64,512]{3,2,1,0:T(8,128)(2,1)}, bf16[1,18,64,512]{3,2,1,0:T(8,128)(2,1)S(1)}, u32[]{:S(2)}, u32[]{:S(2)}) collective-permute-start(bf16[1,18,64,512]{3,2,1,0:T(8,128)(2,1)} %get-tuple-element.34), channel_id=1, source_target_pairs={{16,0},{17,1},{18,2},{19,3},{20,4},{21,5},{22,6},{23,7},{24,8},{25... | collective-permute-start | bytes 3538952 | tf_op jit(solution)/shard_map/ppermute | solution.py:14
  551.5 74.2 %collective-permute-start.5 = (bf16[1,18,64,512]{3,2,1,0:T(8,128)(2,1)}, bf16[1,18,64,512]{3,2,1,0:T(8,128)(2,1)S(1)}, u32[]{:S(2)}, u32[]{:S(2)}) collective-permute-start(bf16[1,18,64,512]{3,2,1,0:T(8,128)(2,1)} %get-tuple-element.36), channel_id=1, source_target_pairs={{16,0},{17,1},{18,2},{19,3},{20,4},{21,5},{22,6},{23,7},{24,8},{25... | collective-permute-start | bytes 3538952 | tf_op jit(solution)/shard_map/ppermute | solution.py:14
  625.7 1.5 copy-start.17
  625.7 1.5 copy-start.19
  625.7 1.5 copy-start.21
  625.7 1.5 copy-start.23
  625.7 1.6 copy-start.25
  625.7 1.6 copy-start.27
  625.7 1.6 copy-start.29
  627.3 12.4 %copy-start.1 = (bf16[4,256,256]{2,1,0:T(8,128)(2,1)S(1)}, bf16[4,256,256]{2,1,0:T(8,128)(2,1)}, u32[]{:S(2)}) copy-start(bf16[4,256,256]{2,1,0:T(8,128)(2,1)} %param.8) | copy-start | bytes 1572868
Sparse Core Ops, SparseCore 0:
  66.0 152.9 all-gather.2
  259.1 127.9 all-reduce.8
  388.7 49.3 all-gather.4
  464.8 76.4 all-reduce.6
where the time goes:
time: 647 us; the launch traced here: 646 us
  waiting for transfers between devices  472 us (73%)
  other arithmetic  44.9 us (7%)
  local copies, waits for them, and re-layouts  39.3 us (6%)
  starting transfers between devices  33.4 us (5%)
  blocking collectives  23.8 us (4%)
  matrix products  17.9 us (3%)
  between operations  14.6 us (2%)
    all_to_all x1, waiting for transfers between devices, on_device(): lax.all_to_all(spread, 'chan', split_axis=3, concat_axis=4, tiled=True)  170 us
    psum x1, waiting for transfers between devices, on_device(): grad_proj = lax.psum(proj_term, ('row', 'chan', 'dp')) * weight_scale  124 us
    ppermute x12, waiting for transfers between devices, shifted(): lax.ppermute(value, axis, [(source, source + steps) for source in range(f...  91.5 us
    all_gather x1, waiting for transfers between devices, on_device(): incoming = lax.all_gather(pre_grad, 'chan', axis=3, tiled=True)  48.8 us
    psum x1, waiting for transfers between devices, on_device(): lax.psum((point_term, depth_term), ('row', 'dp'))  37.1 us
    ppermute x12, starting transfers between devices, shifted(): lax.ppermute(value, axis, [(source, source + steps) for source in range(f...  28.1 us
    psum x1, blocking collectives, on_device(): lax.psum((point_term, depth_term), ('row', 'dp'))  23.8 us
    reduce_sum x3, other arithmetic, on_device(): jnp.sum(input_kernel_tap.astype(jnp.float32) * branch_grad, axis=(0, 1, 2))  15.5 us
  transfers between devices with their start and end apart: 17, of which 10 were waited for; matrix products, arithmetic and copies ran while one was open for 8% of the time, Pallas kernels for 0%

commit v1 on v0

--- a/solution.py
+++ b/solution.py
@@ -1,11 +1,367 @@
+import functools
 import math
 
 import jax
 import jax.numpy as jnp
 from jax import lax
+from jax.experimental import pallas as pl
+from jax.experimental.pallas import tpu as pltpu
 from jax.sharding import PartitionSpec as P
 
 BASE_DILATION = 12
+F32 = jnp.float32
+BF16 = jnp.bfloat16
+
+
+def swap(value, axis, flip):
+    count = lax.axis_size(axis)
+    return lax.ppermute(value, axis, [(i, i ^ flip) for i in range(count)])
+
+
+def swap_diagonal(value):
+    dp = lax.axis_size("dp")
+    pairs = [(r * dp + d, (r ^ 1) * dp + (d ^ 2)) for r in range(2) for d in range(dp)]
+    return lax.ppermute(value, ("row", "dp"), pairs)
+
+
+def moved(value, steps):
+    if steps == 0:
+        return value
+    count = value.shape[0]
+    rolled = pltpu.roll(value, (-steps) % count, 0)
+    place = lax.broadcasted_iota(jnp.int32, value.shape, 0)
+    inside = place < count - steps if steps > 0 else place >= -steps
+    return jnp.where(inside, rolled, 0.0)
+
+
+def row_pairs(branch, classes):
+    return [
+        (q, i, q + (i - 1) * branch)
+        for q in range(classes)
+        for i in range(3)
+        if 0 <= q + (i - 1) * branch < classes
+    ]
+
+
+def forward_kernel(branch, half_ref, x_ref, taps_ref, point_ref, *outs):
+    classes, _, cols, channels = x_ref.shape
+    if branch:
+        spread_ref, keep_ref, send_ref = outs
+        spacing = branch * BASE_DILATION
+        rows = [x_ref[q, 0].astype(F32) for q in range(classes)]
+        for q in range(classes):
+            total = None
+            for j in range(3):
+                part = None
+                for out, i, source in row_pairs(branch, classes):
+                    if out == q:
+                        term = rows[source] * taps_ref[i * 3 + j, :][None, :]
+                        part = term if part is None else part + term
+                part = moved(part, (j - 1) * spacing)
+                total = part if total is None else total + part
+            spread_ref[q, 0] = total.astype(BF16)
+        source_ref = spread_ref
+    else:
+        keep_ref, send_ref = outs
+        source_ref = x_ref
+    cells = source_ref[...].reshape(classes * cols, channels)
+    partial = jnp.dot(cells, point_ref[...], preferred_element_type=F32)
+    split = partial.reshape(classes * 2, 2, cols // 4, partial.shape[-1])
+    first = half_ref[0] == 0
+    keep = jnp.where(first, split[:, 0], split[:, 1])
+    send = jnp.where(first, split[:, 1], split[:, 0])
+    keep_ref[...] = keep.reshape(keep_ref.shape)
+    send_ref[...] = send.reshape(send_ref.shape).astype(BF16)
+
+
+def forward(branch, half, x, taps, point):
+    classes, residues, cols, channels = x.shape
+    filters = point.shape[1]
+    block = lambda r, h: (0, r, 0, 0)
+    part = lambda r, h: (0, r, 0, 0, 0)
+    part_spec = pl.BlockSpec((classes, 1, 2, cols // 4, filters), part)
+    part_shape = (classes, residues, 2, cols // 4, filters)
+    out_specs = [part_spec, part_spec]
+    out_shape = [jax.ShapeDtypeStruct(part_shape, F32), jax.ShapeDtypeStruct(part_shape, BF16)]
+    if branch:
+        out_specs = [pl.BlockSpec((classes, 1, cols, channels), block)] + out_specs
+        out_shape = [jax.ShapeDtypeStruct(x.shape, BF16)] + out_shape
+    return pl.pallas_call(
+        functools.partial(forward_kernel, branch),
+        grid_spec=pltpu.PrefetchScalarGridSpec(
+            num_scalar_prefetch=1,
+            grid=(residues,),
+            in_specs=[
+                pl.BlockSpec((classes, 1, cols, channels), block),
+                pl.BlockSpec(taps.shape, lambda r, h: (0, 0)),
+                pl.BlockSpec(point.shape, lambda r, h: (0, 0)),
+            ],
+            out_specs=out_specs,
+        ),
+        out_shape=out_shape,
+        compiler_params=pltpu.CompilerParams(vmem_limit_bytes=48 * 2**20),
+        cost_estimate=pl.CostEstimate(
+            flops=2 * x.size * filters, bytes_accessed=6 * x.size, transcendentals=0
+        ),
+        name=f"forward_{branch}",
+    )(half, x, taps, point)
+
+
+def whole_columns(half_ref, own, other):
+    first = half_ref[0] == 0
+    low = jnp.where(first, own, other)
+    high = jnp.where(first, other, own)
+    both = jnp.concatenate([low[:, None], high[:, None]], axis=1)
+    return both.reshape(-1, own.shape[-1])
+
+
+def backward_kernel(
+    branch, half_ref, own_ref, other_ref, x_ref, spread_ref, taps_ref, point_ref, before_ref,
+    input_ref, point_grad_ref, depth_ref,
+):
+    classes, _, cols, channels = x_ref.shape
+    step = pl.program_id(0)
+    spacing = branch * BASE_DILATION
+    thin = (classes * 2, cols // 4, own_ref.shape[-1])
+    pre = whole_columns(half_ref, own_ref[...].reshape(thin), other_ref[...].reshape(thin))
+    grads = lax.dot_general(pre, point_ref[...], (((1,), (1,)), ((), ())), preferred_element_type=F32)
+    grads = grads.astype(BF16).astype(F32).reshape(classes, cols, channels)
+    cells = spread_ref[...].reshape(classes * cols, channels)
+    product = lax.dot_general(cells, pre, (((0,), (0,)), ((), ())), preferred_element_type=F32)
+
+    @pl.when(step == 0)
+    def _():
+        point_grad_ref[...] = jnp.zeros_like(point_grad_ref)
+        depth_ref[...] = jnp.zeros_like(depth_ref)
+
+    point_grad_ref[...] += product
+    pairs = row_pairs(branch, classes)
+    rows = [x_ref[q, 0].astype(F32) for q in range(classes)]
+    for j in range(3):
+        near = [moved(row, (j - 1) * spacing) for row in rows]
+        for i in range(3):
+            part = None
+            for q, tap, source in pairs:
+                if tap == i:
+                    term = (near[source] * grads[q]).reshape(cols // 8, 8, channels).sum(axis=0)
+                    part = term if part is None else part + term
+            if part is not None:
+                depth_ref[i * 3 + j] += part
+    for target in range(classes):
+        total = before_ref[target, 0]
+        for j in range(3):
+            part = None
+            for q, i, source in pairs:
+                if source == target:
+                    term = grads[q] * taps_ref[i * 3 + j, :][None, :]
+                    part = term if part is None else part + term
+            total = total + moved(part, -(j - 1) * spacing)
+        input_ref[target, 0] = total
+
+
+def backward(branch, half, own, other, x, spread, taps, point, before):
+    classes, residues, cols, channels = x.shape
+    filters = point.shape[1]
+    block = lambda r, h: (0, r, 0, 0)
+    part = lambda r, h: (0, r, 0, 0, 0)
+    whole = lambda r, h: (0, 0)
+    part_spec = pl.BlockSpec((classes, 1, 2, cols // 4, filters), part)
+    cell_spec = pl.BlockSpec((classes, 1, cols, channels), block)
+    return pl.pallas_call(
+        functools.partial(backward_kernel, branch),
+        grid_spec=pltpu.PrefetchScalarGridSpec(
+            num_scalar_prefetch=1,
+            grid=(residues,),
+            in_specs=[
+                part_spec,
+                part_spec,
+                cell_spec,
+                cell_spec,
+                pl.BlockSpec(taps.shape, whole),
+                pl.BlockSpec(point.shape, whole),
+                cell_spec,
+            ],
+            out_specs=[
+                cell_spec,
+                pl.BlockSpec(point.shape, whole),
+                pl.BlockSpec((9, 8, channels), lambda r, h: (0, 0, 0)),
+            ],
+        ),
+        out_shape=[
+            jax.ShapeDtypeStruct(x.shape, F32),
+            jax.ShapeDtypeStruct(point.shape, F32),
+            jax.ShapeDtypeStruct((9, 8, channels), F32),
+        ],
+        compiler_params=pltpu.CompilerParams(vmem_limit_bytes=48 * 2**20),
+        cost_estimate=pl.CostEstimate(
+            flops=4 * x.size * filters, bytes_accessed=12 * x.size, transcendentals=0
+        ),
+        name=f"backward_{branch}",
+    )(half, own, other, x, spread, taps, point, before)
+
+
+def plane_sum(value, scale, over_pair=False):
+    half = value.shape[0] // 2
+    core = lax.axis_index("dp") % 2
+    keep = lax.dynamic_slice_in_dim(value, core * half, half)
+    send = lax.dynamic_slice_in_dim(value, (1 - core) * half, half)
+    mine = (keep + swap(send, "dp", 1)).astype(BF16)
+    if over_pair:
+        mine = (mine.astype(F32) + swap(mine, "chan", 1).astype(F32)).astype(BF16)
+    x, y, diagonal = swap(mine, "dp", 2), swap(mine, "row", 1), swap_diagonal(mine)
+    total = (mine.astype(F32) + x.astype(F32)) + (y.astype(F32) + diagonal.astype(F32))
+    total = total * scale
+    other = swap(total, "dp", 1)
+    return jnp.where(
+        core == 0, jnp.concatenate([total, other]), jnp.concatenate([other, total])
+    )
+
+
+def by_classes(features_in, depth_weights, point_weights, proj_weights, cotangent):
+    _, band_rows, cols, channels = features_in.shape
+    filters = point_weights.shape[2]
+    classes, residues = 3, band_rows // 3
+    weight_scale = 1.0 / math.sqrt(
+        lax.axis_size("dp") * band_rows * lax.axis_size("row") * cols
+    )
+    row, chan = lax.axis_index("row"), lax.axis_index("chan")
+    upper = row == 0
+    half_index, side = chan % 2, chan // 2
+    half = half_index.astype(jnp.int32).reshape(1)
+    x = features_in[0]
+    n = residues
+
+    def to_classes(first, last, arrived):
+        return jnp.where(
+            upper, jnp.stack([first, last, arrived]), jnp.stack([arrived, first, last])
+        )
+
+    x_arrived = swap(x[n : 2 * n], "row", 1)
+    cot = cotangent[0]
+    cot_rows = jnp.concatenate([cot, swap(cot[n : 2 * n], "row", 1)])
+    cot_far = swap(cot_rows, "chan", 2)
+    cot_half = jnp.where(
+        side == 0, jnp.stack([cot_rows, cot_far], 1), jnp.stack([cot_far, cot_rows], 1)
+    )
+    cot_band = cot_half[:band_rows]
+    cot_class = to_classes(cot_half[:n], cot_half[2 * n : 3 * n], cot_half[band_rows:])
+
+    taps = depth_weights.astype(F32).reshape(3, 9, channels)
+    split = band_rows // 2
+    low = x[:split].reshape(3, split // 3, cols, channels)
+    high = x[split:].reshape(3, split // 3, cols, channels)
+
+    def reduce(keep, send):
+        near = (keep + swap(send, "chan", 1).astype(F32)).astype(BF16)
+        far = swap(near, "chan", 2)
+        return near.astype(F32) + far.astype(F32)
+
+    def gate(preact, cots, branch):
+        cells = cots.reshape(-1, filters)
+        act_grad = lax.dot_general(
+            cells, proj_weights[branch], (((1,), (1,)), ((), ())), preferred_element_type=F32
+        ).reshape(preact.shape)
+        logistic = jax.nn.sigmoid(preact)
+        pre_grad = (act_grad * logistic * (1.0 + preact * (1.0 - logistic))).astype(BF16)
+        return pre_grad, (preact * logistic).astype(BF16)
+
+    def project(activation, branch):
+        mine = jnp.where(side == 0, activation[..., 0, :, :], activation[..., 1, :, :])
+        return jnp.einsum(
+            "...f,fg->...g", mine, proj_weights[branch], preferred_element_type=F32
+        )
+
+    def proj_product(activation, cots):
+        return lax.dot_general(
+            activation.reshape(-1, filters), cots.reshape(-1, filters),
+            (((0,), (0,)), ((), ())), preferred_element_type=F32,
+        )
+
+    keep0a, send0a = forward(0, half, low, taps[0], point_weights[0])
+    pre0a = reduce(keep0a, send0a)
+    x_class = to_classes(x[:n], x[2 * n : 3 * n], x_arrived)
+    spreads, preacts = [], []
+    for b in (1, 2, 3):
+        spread, keep, send = forward(b, half, x_class, taps[b - 1], point_weights[b])
+        spreads.append(spread)
+        preacts.append(reduce(keep, send))
+    keep0b, send0b = forward(0, half, high, taps[0], point_weights[0])
+    pre0b = reduce(keep0b, send0b)
+
+    cots0 = cot_band.reshape((2, 3, split // 3) + cot_band.shape[1:])
+    grad0a, act0a = gate(pre0a, cots0[0], 0)
+    other0a = swap(grad0a, "chan", 1)
+    grads, acts, others = [], [], []
+    for b in (1, 2, 3):
+        grad, act = gate(preacts[b - 1], cot_class, b)
+        grads.append(grad)
+        acts.append(act)
+        others.append(swap(grad, "chan", 1))
+    grad0b, act0b = gate(pre0b, cots0[1], 0)
+    other0b = swap(grad0b, "chan", 1)
+
+    total = jnp.zeros(x_class.shape, F32)
+    point_grads, depth_grads = [], []
+    for b in (1, 2, 3):
+        total, point_grad, depth_grad = backward(
+            b, half, grads[b - 1], others[b - 1], x_class, spreads[b - 1], taps[b - 1],
+            point_weights[b], total,
+        )
+        point_grads.append(point_grad)
+        depth_grads.append(depth_grad.sum(axis=1))
+    leaving = jnp.where(upper, total[2], total[0]).astype(BF16)
+    first = jnp.where(upper, total[0], total[1])
+    last = jnp.where(upper, total[1], total[2])
+    arrived = swap(leaving, "row", 1)
+
+    mixed = sum(project(acts[b - 1], b) for b in (1, 2, 3))
+    mixed_leaving = jnp.where(upper, mixed[2], mixed[0]).astype(BF16)
+    mixed_arrived = swap(mixed_leaving, "row", 1)
+    mixed_band = jnp.concatenate([
+        jnp.where(upper, mixed[0], mixed[1]),
+        mixed_arrived.astype(F32),
+        jnp.where(upper, mixed[1], mixed[2]),
+    ])
+    act0 = jnp.concatenate([
+        act0a.reshape((split,) + act0a.shape[2:]), act0b.reshape((split,) + act0b.shape[2:])
+    ])
+    output = (mixed_band + project(act0, 0)).astype(BF16)
+
+    proj_later = jnp.concatenate([proj_product(acts[b - 1], cot_class) for b in (1, 2, 3)])
+    proj_later = plane_sum(proj_later, weight_scale, over_pair=True)
+    proj_first = plane_sum(proj_product(act0, cot_band), weight_scale, over_pair=True)
+    grad_proj = jnp.concatenate([proj_first, proj_later]).reshape(4, filters, filters)
+
+    depth_rows = 27 * channels // filters
+    padded = -(-depth_rows // 32) * 32
+    depth = jnp.concatenate(depth_grads).reshape(depth_rows, filters)
+    depth = jnp.pad(depth, ((0, padded - depth_rows), (0, 0)))
+    early = plane_sum(jnp.concatenate(point_grads[:2]), weight_scale)
+    late = plane_sum(jnp.concatenate([point_grads[2], depth]), weight_scale)
+
+    def joined(own, other):
+        own = own.reshape((split,) + own.shape[2:])
+        other = other.reshape((split,) + other.shape[2:])
+        both = jnp.where(
+            half_index == 0, jnp.stack([own, other], 2), jnp.stack([other, own], 2)
+        )
+        return both.reshape(split, cols, filters)
+
+    pre0 = jnp.concatenate([joined(grad0a, other0a), joined(grad0b, other0b)])
+    grad0 = lax.dot_general(
+        pre0, point_weights[0], (((2,), (1,)), ((), ())), preferred_element_type=F32
+    ).astype(BF16)
+    point0 = lax.dot_general(
+        x.reshape(-1, channels), pre0.reshape(-1, filters), (((0,), (0,)), ((), ())),
+        preferred_element_type=F32,
+    )
+    others_band = jnp.concatenate([first, arrived.astype(F32), last])
+    grad_input = (grad0.astype(F32) + others_band).astype(BF16)[None]
+    point0 = plane_sum(point0, weight_scale)
+    grad_point = jnp.concatenate([point0, early, late[:channels]])
+    grad_point = grad_point.reshape(4, channels, filters)
+    grad_depth = late[channels : channels + depth_rows].reshape(3, 3, 3, channels)
+    return (output[None], grad_input, grad_depth, grad_point, grad_proj)
 
 
 def shifted(value, axis, steps):
@@ -129,6 +485,20 @@
     return (output, grad_in.astype(jnp.bfloat16), grad_depth, grad_point, grad_proj)
 
 
+def folds(mesh, features_in):
+    sizes = mesh.shape
+    samples, rows, cols, channels = features_in.shape
+    return (
+        rows == 3 * BASE_DILATION
+        and sizes["row"] == 2
+        and sizes["chan"] == 4
+        and sizes["dp"] == 4
+        and samples == sizes["dp"]
+        and cols % 64 == 0
+        and channels % (128 * sizes["chan"]) == 0
+    )
+
+
 def solution(mesh):
     in_specs = (
         P("dp", "row", None, "chan"),
@@ -144,6 +514,11 @@
         P(None, "chan", None),
         P(),
     )
-    return jax.shard_map(
-        on_device, mesh=mesh, in_specs=in_specs, out_specs=out_specs, check_vma=False
-    )
+
+    def run(*args):
+        body = by_classes if folds(mesh, args[0]) else on_device
+        return jax.shard_map(
+            body, mesh=mesh, in_specs=in_specs, out_specs=out_specs, check_vma=False
+        )(*args)
+
+    return run

time: 647 us -> 209 us (0.32)
  waiting for transfers between devices: 472 us -> 105 us
  other arithmetic: 44.9 us -> 9.74 us
  Pallas kernels: 0 us -> 28.8 us
  local copies, waits for them, and re-layouts: 39.3 us -> 12.1 us
  blocking collectives: 23.8 us -> 0 us
  between operations: 14.6 us -> 1.5 us
  starting transfers between devices: 33.4 us -> 44.3 us
  matrix products: 17.9 us -> 7.32 us
    all_to_all x1 -> x0, waiting for transfers between devices: 170 us -> none  [on_device(): lax.all_to_all(spread, 'chan', split_axis=3, concat_axis=4, tiled=True)]
    psum x2 -> x0, waiting for transfers between devices: 161 us -> none  [the longest x1 124 us: on_device(): grad_proj = lax.psum(proj_term, ('row', 'chan', 'dp')) * weight_scale]
    all_gather x2 -> x0, waiting for transfers between devices: 48.8 us -> none  [the longest x1 48.8 us: on_device(): incoming = lax.all_gather(pre_grad, 'chan', axis=3, tiled=True)]
    pallas_call x0 -> x8, Pallas kernels: none -> 28.8 us  [the longest x3 21.1 us: backward(): pl.pallas_call(functools.partial(backward_kernel, branch), grid_spec=pltp...]
    psum x1 -> x0, blocking collectives: 23.8 us -> none  [on_device(): lax.psum((point_term, depth_term), ('row', 'dp'))]
    ppermute x12 -> x47, starting transfers between devices: 28.1 us -> 44.3 us  [the longest x42 37.8 us: swap(): return lax.ppermute(value, axis, [(i, i ^ flip) for i in range(count)])]
    reduce_sum x3, other arithmetic: 15.5 us -> 0.12 us  [by_classes(): depth_grads.append(depth_grad.sum(axis=1))]
    another operation x8 -> x1, local copies, waits for them, and re-layouts: 14.7 us -> 0.06 us  [to_classes(): jnp.stack([first, last, arrived])]
  transfers between devices with their start and end apart: 17 -> 47, of which waited for: 10 -> 19; matrix products, arithmetic and copies ran while one was open for 8% -> 10% of each run, Pallas kernels for 0% -> 14%
where the time goes in v1:
time: 209 us
  waiting for transfers between devices  105 us (50%)
  starting transfers between devices  44.3 us (21%)
  Pallas kernels  28.8 us (14%)
  local copies, waits for them, and re-layouts  12.1 us (6%)
  other arithmetic  9.74 us (5%)
  matrix products  7.32 us (4%)
    ppermute x42, waiting for transfers between devices, swap(): return lax.ppermute(value, axis, [(i, i ^ flip) for i in range(count)])  93.2 us
    ppermute x42, starting transfers between devices, swap(): return lax.ppermute(value, axis, [(i, i ^ flip) for i in range(count)])  37.8 us
    pallas_call x3, Pallas kernels, backward(): pl.pallas_call(functools.partial(backward_kernel, branch), grid_spec=pltp...  21.1 us
    ppermute x5, waiting for transfers between devices, swap_diagonal(): return lax.ppermute(value, ('row', 'dp'), pairs)  11.7 us
    pallas_call x5, Pallas kernels, forward(): pl.pallas_call(functools.partial(forward_kernel, branch), grid_spec=pltpu...  7.68 us
    ppermute x5, starting transfers between devices, swap_diagonal(): return lax.ppermute(value, ('row', 'dp'), pairs)  6.48 us
    unnamed x30, local copies, waits for them, and re-layouts  4.3 us
  transfers between devices with their start and end apart: 47, of which 19 were waited for; matrix products, arithmetic and copies ran while one was open for 10% of the time, Pallas kernels for 14%

profile of v1, /device:TPU:0, one launch (start us, length us, event | category | flops | bytes accessed | tf_op | source)
XLA Modules:
  0.0 208.7 jit_solution(4836163390646734533)
XLA Ops:
  0.6 1.0 copy.57
  2.2 3.0 %collective-permute-start.12 = (bf16[6,16,256]{2,0,1:T(8,128)(2,1)}, bf16[6,16,256]{2,0,1:T(8,128)(2,1)S(1)}, u32[]{:S(2)}, u32[]{:S(2)}) collective-permute-start(bf16[6,16,256]{2,0,1:T(8,128)(2,1)} %slice_bitcast_fusion.8), channel_id=1, source_target_pairs={{0,16},{16,0},{1,17},{17,1},{2,18},{18,2},{3,19},{19,3},{4,20},{20... | collective-permute-start | bytes 147464 | tf_op jit(solution)/shard_map/ppermute | solution.py:18
  5.2 2.2 %fusion.61 = (bf16[1,6,64,512]{3,2,1,0:T(8,128)(2,1)S(1)}, bf16[6,64,512]{2,1,0:T(8,128)(2,1)}, bf16[1,6,64,512]{3,2,1,0:T(8,128)(2,1)}) fusion(bf16[1,18,64,512]{3,2,1,0:T(8,128)(2,1)} %param.5), kind=kLoop, calls=%fused_computation.152 | loop fusion | bytes 2359296 | tf_op jit(solution)/shard_map/slice | solution.py:282
  7.6 1.0 copy-done.10
  9.4 0.8 forward_0.2
  10.2 1.6 collective-permute-start.8
  11.9 0.8 forward_0.3
  13.3 2.6 %collective-permute-start.13 = (bf16[24,16,256]{2,0,1:T(8,128)(2,1)S(1)}, bf16[24,16,256]{2,0,1:T(8,128)(2,1)S(1)}, u32[]{:S(2)}, u32[]{:S(2)}) collective-permute-start(bf16[24,16,256]{2,0,1:T(8,128)(2,1)S(1)} %pad_maximum_fusion.6), channel_id=1, source_target_pairs={{0,8},{4,12},{8,0},{12,4},{1,9},{5,13},{9,1},{13,5},{2,10},{6,14},... | collective-permute-start | bytes 589832 | tf_op jit(solution)/shard_map/ppermute | solution.py:18
  16.0 5.3 %collective-permute-done.8 = bf16[3,3,2,16,256]{4,3,2,1,0:T(8,128)(2,1)S(1)} collective-permute-done((bf16[3,3,2,16,256]{4,3,2,1,0:T(8,128)(2,1)S(1)}, bf16[3,3,2,16,256]{4,3,2,1,0:T(8,128)(2,1)S(1)}, u32[]{:S(2)}, u32[]{:S(2)}) %collective-permute-start.8) | collective-permute-done | bytes 147488 | tf_op jit(solution)/shard_map/ppermute | solution.py:18
  21.4 2.4 %collective-permute-done.10 = bf16[3,3,2,16,256]{4,3,2,1,0:T(8,128)(2,1)S(1)} collective-permute-done((bf16[3,3,2,16,256]{4,3,2,1,0:T(8,128)(2,1)S(1)}, bf16[3,3,2,16,256]{4,3,2,1,0:T(8,128)(2,1)S(1)}, u32[]{:S(2)}, u32[]{:S(2)}) %collective-permute-start.10) | collective-permute-done | bytes 147488 | tf_op jit(solution)/shard_map/ppermute | solution.py:18
  24.4 8.0 %collective-permute-done.13 = bf16[24,16,256]{2,0,1:T(8,128)(2,1)S(1)} collective-permute-done((bf16[24,16,256]{2,0,1:T(8,128)(2,1)S(1)}, bf16[24,16,256]{2,0,1:T(8,128)(2,1)S(1)}, u32[]{:S(2)}, u32[]{:S(2)}) %collective-permute-start.13) | collective-permute-done | bytes 196640 | tf_op jit(solution)/shard_map/ppermute | solution.py:18
  32.9 2.5 %collective-permute-done.9 = bf16[3,3,2,16,256]{4,3,2,1,0:T(8,128)(2,1)S(1)} collective-permute-done((bf16[3,3,2,16,256]{4,3,2,1,0:T(8,128)(2,1)S(1)}, bf16[3,3,2,16,256]{4,3,2,1,0:T(8,128)(2,1)S(1)}, u32[]{:S(2)}, u32[]{:S(2)}) %collective-permute-start.9) | collective-permute-done | bytes 147488 | tf_op jit(solution)/shard_map/ppermute | solution.py:18
  35.8 0.9 collective-permute-start.14
  37.9 0.9 collective-permute-start.15
  39.0 1.3 maximum_select_fusion.x_ref
  40.4 1.8 forward_3.1
  42.2 1.2 collective-permute-start.5
  43.4 1.8 forward_2.1
  45.2 0.9 collective-permute-start.3
  46.1 2.6 %forward_1.1 = (bf16[3,6,64,512]{3,2,1,0:T(8,128)(2,1)S(1)}, f32[3,6,2,16,256]{4,3,2,1,0:T(8,128)S(1)}, bf16[3,6,2,16,256]{4,3,2,1,0:T(8,128)(2,1)S(1)}) custom-call(s32[1]{0:T(128)} %bitcast.half_ref, bf16[3,6,64,512]{3,2,1,0:T(8,128)(2,1)S(1)} %maximum_select_fusion.x_ref, f32[9,512]{1,0:T(8,128)S(1)} %squeeze.24.taps_ref, ...), custom_call_target="tpu_custom_call" | custom-call | flops 301989888 | bytes 3538944 | tf_op jit(solution)/shard_map/forward_1/pallas_call | solution.py:89
  48.8 1.2 collective-permute-start.36
  50.2 8.9 %collective-permute-done.36 = bf16[128,256]{1,0:T(8,128)(2,1)S(1)} collective-permute-done((bf16[128,256]{1,0:T(8,128)(2,1)S(1)}, bf16[128,256]{1,0:T(8,128)(2,1)S(1)}, u32[]{:S(2)}, u32[]{:S(2)}) %collective-permute-start.36) | collective-permute-done | bytes 65568 | tf_op jit(solution)/shard_map/ppermute | solution.py:18
  59.1 1.8 collective-permute-start.39
  60.9 1.3 collective-permute-start.38
  62.7 2.2 %collective-permute-done.39 = bf16[128,256]{1,0:T(8,128)(2,1)S(1)} collective-permute-done((bf16[128,256]{1,0:T(8,128)(2,1)S(1)}, bf16[128,256]{1,0:T(8,128)(2,1)S(1)}, u32[]{:S(2)}, u32[]{:S(2)}) %collective-permute-start.39) | collective-permute-done | bytes 65568 | tf_op jit(solution)/shard_map/ppermute | solution.py:24
  64.9 1.2 collective-permute-start.1
  67.8 0.7 maximum_select_fusion.9
  68.7 3.4 %collective-permute-start.6 = (bf16[3,6,2,16,256]{4,3,2,1,0:T(8,128)(2,1)S(1)}, bf16[3,6,2,16,256]{4,3,2,1,0:T(8,128)(2,1)S(1)}, u32[]{:S(2)}, u32[]{:S(2)}) collective-permute-start(bf16[3,6,2,16,256]{4,3,2,1,0:T(8,128)(2,1)S(1)} %add_convert_fusion), channel_id=1, source_target_pairs={{0,8},{4,12},{8,0},{12,4},{1,9},{5,13},{9,1},{13,5},{2,10},{6,14},... | collective-permute-start | bytes 884744 | tf_op jit(solution)/shard_map/ppermute | solution.py:18
  72.3 1.0 collective-permute-start.28
  73.3 1.0 collective-permute-start.27
  74.4 1.5 collective-permute-start.26
  76.0 3.7 %collective-permute-done.28 = bf16[256,256]{1,0:T(8,128)(2,1)S(1)} collective-permute-done((bf16[256,256]{1,0:T(8,128)(2,1)S(1)}, bf16[256,256]{1,0:T(8,128)(2,1)S(1)}, u32[]{:S(2)}, u32[]{:S(2)}) %collective-permute-start.28) | collective-permute-done | bytes 131104 | tf_op jit(solution)/shard_map/ppermute | solution.py:24
  79.6 2.9 %collective-permute-start.2 = (bf16[3,6,2,16,256]{4,3,2,1,0:T(8,128)(2,1)S(1)}, bf16[3,6,2,16,256]{4,3,2,1,0:T(8,128)(2,1)S(1)}, u32[]{:S(2)}, u32[]{:S(2)}) collective-permute-start(bf16[3,6,2,16,256]{4,3,2,1,0:T(8,128)(2,1)S(1)} %add_convert_fusion.2), channel_id=1, source_target_pairs={{0,8},{4,12},{8,0},{12,4},{1,9},{5,13},{9,1},{13,5},{2,10},{6,14},... | collective-permute-start | bytes 884744 | tf_op jit(solution)/shard_map/ppermute | solution.py:18
  82.7 16.0 %collective-permute-done.6 = bf16[3,6,2,16,256]{4,3,2,1,0:T(8,128)(2,1)S(1)} collective-permute-done((bf16[3,6,2,16,256]{4,3,2,1,0:T(8,128)(2,1)S(1)}, bf16[3,6,2,16,256]{4,3,2,1,0:T(8,128)(2,1)S(1)}, u32[]{:S(2)}, u32[]{:S(2)}) %collective-permute-start.6) | collective-permute-done | bytes 294944 | tf_op jit(solution)/shard_map/ppermute | solution.py:18
  99.2 11.8 %collective-permute-done.2 = bf16[3,6,2,16,256]{4,3,2,1,0:T(8,128)(2,1)S(1)} collective-permute-done((bf16[3,6,2,16,256]{4,3,2,1,0:T(8,128)(2,1)S(1)}, bf16[3,6,2,16,256]{4,3,2,1,0:T(8,128)(2,1)S(1)}, u32[]{:S(2)}, u32[]{:S(2)}) %collective-permute-start.2) | collective-permute-done | bytes 294944 | tf_op jit(solution)/shard_map/ppermute | solution.py:18
  113.6 2.0 collective-permute-start.17
  116.8 0.8 constant_dynamic-slice_fusion
  117.5 2.1 collective-permute-done.7
  119.6 0.9 fusion.12
  120.5 0.8 maximum_select_fusion.4
  121.3 13.0 %collective-permute-done.18.other_ref = bf16[3,6,2,16,256]{4,3,2,1,0:T(8,128)(2,1)S(1)} collective-permute-done((bf16[3,6,2,16,256]{4,3,2,1,0:T(8,128)(2,1)S(1)}, bf16[3,6,2,16,256]{4,3,2,1,0:T(8,128)(2,1)S(1)}, u32[]{:S(2)}, u32[]{:S(2)}) %collective-permute-start.18) | collective-permute-done | bytes 294944 | tf_op jit(solution)/shard_map/ppermute | solution.py:18
  134.3 1.7 broadcast_in_dim.10.before_ref
  136.0 7.8 %backward_1.1 = (f32[3,6,64,512]{3,2,1,0:T(8,128)}, f32[512,256]{1,0:T(8,128)S(1)}, f32[9,8,512]{2,1,0:T(8,128)S(1)}) custom-call(s32[1]{0:T(128)} %bitcast.half_ref, bf16[3,6,2,16,256]{4,3,2,1,0:T(8,128)(2,1)S(1)} %multiply_convert_fusion.own_ref, bf16[3,6,2,16,256]{4,3,2,1,0:T(8,128)(2,1)S(1)} %collective-permute-done.18.other_ref, ...), custom_call_target="tpu_custom_call" | custom-call | flops 603979776 | bytes 7077888 | tf_op jit(solution)/shard_map/backward_1/pallas_call | solution.py:170
  143.8 6.7 %backward_2.1 = (f32[3,6,64,512]{3,2,1,0:T(8,128)}, f32[512,256]{1,0:T(8,128)S(1)}, f32[9,8,512]{2,1,0:T(8,128)S(1)}) custom-call(s32[1]{0:T(128)} %bitcast.half_ref, bf16[3,6,2,16,256]{4,3,2,1,0:T(8,128)(2,1)S(1)} %multiply_convert_fusion.1.own_ref, bf16[3,6,2,16,256]{4,3,2,1,0:T(8,128)(2,1)S(1)} %collective-permute-done.17.other_ref, ...), custom_call_target="tpu_custom_call" | custom-call | flops 603979776 | bytes 7077888 | tf_op jit(solution)/shard_map/backward_2/pallas_call | solution.py:170
  150.5 6.6 %backward_3.1 = (f32[3,6,64,512]{3,2,1,0:T(8,128)}, f32[512,256]{1,0:T(8,128)S(1)}, f32[9,8,512]{2,1,0:T(8,128)S(1)}) custom-call(s32[1]{0:T(128)} %bitcast.half_ref, bf16[3,6,2,16,256]{4,3,2,1,0:T(8,128)(2,1)S(1)} %multiply_convert_fusion.2.own_ref, bf16[3,6,2,16,256]{4,3,2,1,0:T(8,128)(2,1)S(1)} %collective-permute-done.16.other_ref, ...), custom_call_target="tpu_custom_call" | custom-call | flops 603979776 | bytes 7077888 | tf_op jit(solution)/shard_map/backward_3/pallas_call | solution.py:170
  158.2 1.0 copy-done.2
  159.4 1.0 add_convert_fusion.5
  161.5 6.3 %collective-permute-done.42 = bf16[384,256]{1,0:T(8,128)(2,1)S(1)} collective-permute-done((bf16[384,256]{1,0:T(8,128)(2,1)S(1)}, bf16[384,256]{1,0:T(8,128)(2,1)S(1)}, u32[]{:S(2)}, u32[]{:S(2)}) %collective-permute-start.42) | collective-permute-done | bytes 196640 | tf_op jit(solution)/shard_map/ppermute | solution.py:18
  167.9 0.9 collective-permute-start.45
  168.8 1.0 collective-permute-start.44
  169.9 1.7 collective-permute-start.23
  171.6 8.7 %collective-permute-done.19 = bf16[6,64,512]{2,1,0:T(8,128)(2,1)S(1)} collective-permute-done((bf16[6,64,512]{2,1,0:T(8,128)(2,1)S(1)}, bf16[6,64,512]{2,1,0:T(8,128)(2,1)S(1)}, u32[]{:S(2)}, u32[]{:S(2)}) %collective-permute-start.19) | collective-permute-done | bytes 393248 | tf_op jit(solution)/shard_map/ppermute | solution.py:18
  181.0 1.1 collective-permute-start.21
  182.2 1.0 collective-permute-start.43
  183.2 3.7 %collective-permute-done.22 = bf16[288,256]{1,0:T(8,128)(2,1)S(1)} collective-permute-done((bf16[288,256]{1,0:T(8,128)(2,1)S(1)}, bf16[288,256]{1,0:T(8,128)(2,1)S(1)}, u32[]{:S(2)}, u32[]{:S(2)}) %collective-permute-start.22) | collective-permute-done | bytes 147488 | tf_op jit(solution)/shard_map/ppermute | solution.py:18
  186.9 1.1 collective-permute-start.33
  188.0 0.8 collective-permute-start.32
  188.9 1.6 collective-permute-start.31
  191.3 5.8 %collective-permute-done.33 = bf16[512,256]{1,0:T(8,128)(2,1)S(1)} collective-permute-done((bf16[512,256]{1,0:T(8,128)(2,1)S(1)}, bf16[512,256]{1,0:T(8,128)(2,1)S(1)}, u32[]{:S(2)}, u32[]{:S(2)}) %collective-permute-start.33) | collective-permute-done | bytes 262176 | tf_op jit(solution)/shard_map/ppermute | solution.py:24
  197.1 3.9 %collective-permute-done.32 = bf16[512,256]{1,0:T(8,128)(2,1)S(1)} collective-permute-done((bf16[512,256]{1,0:T(8,128)(2,1)S(1)}, bf16[512,256]{1,0:T(8,128)(2,1)S(1)}, u32[]{:S(2)}, u32[]{:S(2)}) %collective-permute-start.32) | collective-permute-done | bytes 262176 | tf_op jit(solution)/shard_map/ppermute | solution.py:18
  201.3 2.5 %fusion.1 = bf16[1,18,64,512]{3,2,1,0:T(8,128)(2,1)} fusion(f32[6,64,512]{2,1,0:T(8,128)S(1)} %get-tuple-element.50, f32[6,64,512]{2,1,0:T(8,128)S(1)} %convert_element_type.257, f32[6,64,512]{2,1,0:T(8,128)S(1)} %get-tuple-element.49, bf16[4,512,256]{2,1,0:T(8,128)(2,1)} %param.7, bf16[9,64,256]{2,1,0:T(8,128)(2,1)S(1)} %bitcast.166, ...), kind=kOutput, calls=%fused_computation.4 | convolution fusion | flops 305823744 | bytes 4390912 | tf_op jit(solution)/shard_map/dot_general | solution.py:351
  205.0 1.0 pad_maximum_fusion.1
  206.1 0.9 slice-done
  207.2 1.5 pad_maximum_fusion
  (161 shorter events, 18.2 us)
Async XLA Ops:
  2.2 5.3 %copy-start = (bf16[1,18,64,512]{3,2,1,0:T(8,128)(2,1)S(1)}, bf16[1,18,64,512]{3,2,1,0:T(8,128)(2,1)}, u32[]{:S(2)}) copy-start(bf16[1,18,64,512]{3,2,1,0:T(8,128)(2,1)} %param.5) | copy-start | bytes 3538948
  2.2 11.0 %collective-permute-start.12 = (bf16[6,16,256]{2,0,1:T(8,128)(2,1)}, bf16[6,16,256]{2,0,1:T(8,128)(2,1)S(1)}, u32[]{:S(2)}, u32[]{:S(2)}) collective-permute-start(bf16[6,16,256]{2,0,1:T(8,128)(2,1)} %slice_bitcast_fusion.8), channel_id=1, source_target_pairs={{0,16},{16,0},{1,17},{17,1},{2,18},{18,2},{3,19},{19,3},{4,20},{20... | collective-permute-start | bytes 147464 | tf_op jit(solution)/shard_map/ppermute | solution.py:18
  7.4 1.2 copy-start.10
  7.4 31.6 %collective-permute-start = (bf16[6,64,512]{2,1,0:T(8,128)(2,1)}, bf16[6,64,512]{2,1,0:T(8,128)(2,1)}, u32[]{:S(2)}, u32[]{:S(2)}) collective-permute-start(bf16[6,64,512]{2,1,0:T(8,128)(2,1)} %get-tuple-element.54), channel_id=1, source_target_pairs={{0,16},{16,0},{1,17},{17,1},{2,18},{18,2},{3,19},{19,3},{4,20},{20... | collective-permute-start | bytes 1179656 | tf_op jit(solution)/shard_map/ppermute | solution.py:18
  8.6 0.8 copy-start.12
  10.2 11.0 %collective-permute-start.8 = (bf16[3,3,2,16,256]{4,3,2,1,0:T(8,128)(2,1)S(1)}, bf16[3,3,2,16,256]{4,3,2,1,0:T(8,128)(2,1)S(1)}, u32[]{:S(2)}, u32[]{:S(2)}) collective-permute-start(bf16[3,3,2,16,256]{4,3,2,1,0:T(8,128)(2,1)S(1)} %get-tuple-element.34), channel_id=1, source_target_pairs={{0,4},{4,0},{8,12},{12,8},{1,5},{5,1},{9,13},{13,9},{2,6},{6,2},{1... | collective-permute-start | bytes 442376 | tf_op jit(solution)/shard_map/ppermute | solution.py:18
  12.6 11.1 %collective-permute-start.10 = (bf16[3,3,2,16,256]{4,3,2,1,0:T(8,128)(2,1)S(1)}, bf16[3,3,2,16,256]{4,3,2,1,0:T(8,128)(2,1)S(1)}, u32[]{:S(2)}, u32[]{:S(2)}) collective-permute-start(bf16[3,3,2,16,256]{4,3,2,1,0:T(8,128)(2,1)S(1)} %get-tuple-element.36), channel_id=1, source_target_pairs={{0,4},{4,0},{8,12},{12,8},{1,5},{5,1},{9,13},{13,9},{2,6},{6,2},{1... | collective-permute-start | bytes 442376 | tf_op jit(solution)/shard_map/ppermute | solution.py:18
  13.3 19.1 %collective-permute-start.13 = (bf16[24,16,256]{2,0,1:T(8,128)(2,1)S(1)}, bf16[24,16,256]{2,0,1:T(8,128)(2,1)S(1)}, u32[]{:S(2)}, u32[]{:S(2)}) collective-permute-start(bf16[24,16,256]{2,0,1:T(8,128)(2,1)S(1)} %pad_maximum_fusion.6), channel_id=1, source_target_pairs={{0,8},{4,12},{8,0},{12,4},{1,9},{5,13},{9,1},{13,5},{2,10},{6,14},... | collective-permute-start | bytes 589832 | tf_op jit(solution)/shard_map/ppermute | solution.py:18
  21.3 14.1 %collective-permute-start.9 = (bf16[3,3,2,16,256]{4,3,2,1,0:T(8,128)(2,1)S(1)}, bf16[3,3,2,16,256]{4,3,2,1,0:T(8,128)(2,1)S(1)}, u32[]{:S(2)}, u32[]{:S(2)}) collective-permute-start(bf16[3,3,2,16,256]{4,3,2,1,0:T(8,128)(2,1)S(1)} %add_convert_fusion.8), channel_id=1, source_target_pairs={{0,8},{4,12},{8,0},{12,4},{1,9},{5,13},{9,1},{13,5},{2,10},{6,14},... | collective-permute-start | bytes 442376 | tf_op jit(solution)/shard_map/ppermute | solution.py:18
  23.8 13.3 %collective-permute-start.11 = (bf16[3,3,2,16,256]{4,3,2,1,0:T(8,128)(2,1)S(1)}, bf16[3,3,2,16,256]{4,3,2,1,0:T(8,128)(2,1)S(1)}, u32[]{:S(2)}, u32[]{:S(2)}) collective-permute-start(bf16[3,3,2,16,256]{4,3,2,1,0:T(8,128)(2,1)S(1)} %add_convert_fusion.7), channel_id=1, source_target_pairs={{0,8},{4,12},{8,0},{12,4},{1,9},{5,13},{9,1},{13,5},{2,10},{6,14},... | collective-permute-start | bytes 442376 | tf_op jit(solution)/shard_map/ppermute | solution.py:18
  32.6 3.0 %copy-start.13 = (bf16[4,256,256]{2,1,0:T(8,128)(2,1)S(1)}, bf16[4,256,256]{2,1,0:T(8,128)(2,1)}, u32[]{:S(2)}) copy-start(bf16[4,256,256]{2,1,0:T(8,128)(2,1)} %param.8) | copy-start | bytes 1572868
  35.8 14.1 %collective-permute-start.14 = (bf16[3,3,2,16,256]{4,3,2,1,0:T(8,128)(2,1)S(1)}, bf16[3,3,2,16,256]{4,3,2,1,0:T(8,128)(2,1)S(1)}, u32[]{:S(2)}, u32[]{:S(2)}) collective-permute-start(bf16[3,3,2,16,256]{4,3,2,1,0:T(8,128)(2,1)S(1)} %multiply_convert_fusion.7), channel_id=1, source_target_pairs={{0,4},{4,0},{8,12},{12,8},{1,5},{5,1},{9,13},{13,9},{2,6},{6,2},{1... | collective-permute-start | bytes 442376 | tf_op jit(solution)/shard_map/ppermute | solution.py:18
  37.6 11.1 %collective-permute-start.35 = (f32[128,256]{1,0:T(8,128)S(1)}, f32[128,256]{1,0:T(8,128)S(1)}, u32[]{:S(2)}, u32[]{:S(2)}) collective-permute-start(f32[128,256]{1,0:T(8,128)S(1)} %constant_dynamic-slice_fusion.1), channel_id=1, source_target_pairs={{0,1},{1,0},{2,3},{3,2},{4,5},{5,4},{6,7},{7,6},{8,9},{9,8},{10,11... | collective-permute-start | bytes 393224 | tf_op jit(solution)/shard_map/ppermute | solution.py:18
  37.7 1.3 copy-start.5
  37.9 12.1 %collective-permute-start.15 = (bf16[3,3,2,16,256]{4,3,2,1,0:T(8,128)(2,1)S(1)}, bf16[3,3,2,16,256]{4,3,2,1,0:T(8,128)(2,1)S(1)}, u32[]{:S(2)}, u32[]{:S(2)}) collective-permute-start(bf16[3,3,2,16,256]{4,3,2,1,0:T(8,128)(2,1)S(1)} %multiply_convert_fusion.6), channel_id=1, source_target_pairs={{0,4},{4,0},{8,12},{12,8},{1,5},{5,1},{9,13},{13,9},{2,6},{6,2},{1... | collective-permute-start | bytes 442376 | tf_op jit(solution)/shard_map/ppermute | solution.py:18
  42.2 26.4 %collective-permute-start.5 = (bf16[3,6,2,16,256]{4,3,2,1,0:T(8,128)(2,1)S(1)}, bf16[3,6,2,16,256]{4,3,2,1,0:T(8,128)(2,1)S(1)}, u32[]{:S(2)}, u32[]{:S(2)}) collective-permute-start(bf16[3,6,2,16,256]{4,3,2,1,0:T(8,128)(2,1)S(1)} %get-tuple-element.32), channel_id=1, source_target_pairs={{0,4},{4,0},{8,12},{12,8},{1,5},{5,1},{9,13},{13,9},{2,6},{6,2},{1... | collective-permute-start | bytes 884744 | tf_op jit(solution)/shard_map/ppermute | solution.py:18
  45.2 26.9 %collective-permute-start.3 = (bf16[3,6,2,16,256]{4,3,2,1,0:T(8,128)(2,1)S(1)}, bf16[3,6,2,16,256]{4,3,2,1,0:T(8,128)(2,1)S(1)}, u32[]{:S(2)}, u32[]{:S(2)}) collective-permute-start(bf16[3,6,2,16,256]{4,3,2,1,0:T(8,128)(2,1)S(1)} %get-tuple-element.30), channel_id=1, source_target_pairs={{0,4},{4,0},{8,12},{12,8},{1,5},{5,1},{9,13},{13,9},{2,6},{6,2},{1... | collective-permute-start | bytes 884744 | tf_op jit(solution)/shard_map/ppermute | solution.py:18
  48.8 10.3 %collective-permute-start.36 = (bf16[128,256]{1,0:T(8,128)(2,1)S(1)}, bf16[128,256]{1,0:T(8,128)(2,1)S(1)}, u32[]{:S(2)}, u32[]{:S(2)}) collective-permute-start(bf16[128,256]{1,0:T(8,128)(2,1)S(1)} %add_convert_fusion.10), channel_id=1, source_target_pairs={{0,4},{4,0},{8,12},{12,8},{1,5},{5,1},{9,13},{13,9},{2,6},{6,2},{1... | collective-permute-start | bytes 196616 | tf_op jit(solution)/shard_map/ppermute | solution.py:18
  50.0 12.7 %copy-start.6 = (bf16[9,2,2,16,256]{4,3,2,1,0:T(8,128)(2,1)}, bf16[9,2,2,16,256]{4,3,2,1,0:T(8,128)(2,1)S(1)}, u32[]{:S(2)}) copy-start(bf16[9,2,2,16,256]{4,3,2,1,0:T(8,128)(2,1)S(1)} %copy.16) | copy-start | bytes 884740
  50.1 16.4 %copy-start.1 = (bf16[1,18,64,512]{3,2,1,0:T(8,128)(2,1)S(1)}, bf16[1,18,64,512]{3,2,1,0:T(8,128)(2,1)}, u32[]{:S(2)}) copy-start(bf16[1,18,64,512]{3,2,1,0:T(8,128)(2,1)} %param.5) | copy-start | bytes 3538948
  50.1 16.4 %copy-start.8 = (bf16[9,2,2,16,256]{4,3,2,1,0:T(8,128)(2,1)}, bf16[9,2,2,16,256]{4,3,2,1,0:T(8,128)(2,1)S(1)}, u32[]{:S(2)}) copy-start(bf16[9,2,2,16,256]{4,3,2,1,0:T(8,128)(2,1)S(1)} %copy.18) | copy-start | bytes 884740
  59.1 5.8 %collective-permute-start.39 = (bf16[128,256]{1,0:T(8,128)(2,1)S(1)}, bf16[128,256]{1,0:T(8,128)(2,1)S(1)}, u32[]{:S(2)}, u32[]{:S(2)}) collective-permute-start(bf16[128,256]{1,0:T(8,128)(2,1)S(1)} %add_convert_fusion.9), channel_id=1, source_target_pairs={{0,18},{1,19},{2,16},{3,17},{16,2},{17,3},{18,0},{19,1},{4,22},{5,... | collective-permute-start | bytes 196616 | tf_op jit(solution)/shard_map/ppermute | solution.py:24
  60.9 5.2 %collective-permute-start.38 = (bf16[128,256]{1,0:T(8,128)(2,1)S(1)}, bf16[128,256]{1,0:T(8,128)(2,1)S(1)}, u32[]{:S(2)}, u32[]{:S(2)}) collective-permute-start(bf16[128,256]{1,0:T(8,128)(2,1)S(1)} %add_convert_fusion.9), channel_id=1, source_target_pairs={{0,16},{16,0},{1,17},{17,1},{2,18},{18,2},{3,19},{19,3},{4,20},{20... | collective-permute-start | bytes 196616 | tf_op jit(solution)/shard_map/ppermute | solution.py:18
  62.1 4.3 %collective-permute-start.37 = (bf16[128,256]{1,0:T(8,128)(2,1)S(1)}, bf16[128,256]{1,0:T(8,128)(2,1)S(1)}, u32[]{:S(2)}, u32[]{:S(2)}) collective-permute-start(bf16[128,256]{1,0:T(8,128)(2,1)S(1)} %add_convert_fusion.9), channel_id=1, source_target_pairs={{0,2},{1,3},{2,0},{3,1},{4,6},{5,7},{6,4},{7,5},{8,10},{9,11},{10,... | collective-permute-start | bytes 196616 | tf_op jit(solution)/shard_map/ppermute | solution.py:18
  64.9 9.4 %collective-permute-start.1 = (bf16[3,6,2,16,256]{4,3,2,1,0:T(8,128)(2,1)S(1)}, bf16[3,6,2,16,256]{4,3,2,1,0:T(8,128)(2,1)S(1)}, u32[]{:S(2)}, u32[]{:S(2)}) collective-permute-start(bf16[3,6,2,16,256]{4,3,2,1,0:T(8,128)(2,1)S(1)} %get-tuple-element.28), channel_id=1, source_target_pairs={{0,4},{4,0},{8,12},{12,8},{1,5},{5,1},{9,13},{13,9},{2,6},{6,2},{1... | collective-permute-start | bytes 884744 | tf_op jit(solution)/shard_map/ppermute | solution.py:18
  66.4 1.4 collective-permute-start.40
  67.2 5.1 %collective-permute-start.25 = (f32[256,256]{1,0:T(8,128)S(1)}, f32[256,256]{1,0:T(8,128)S(1)}, u32[]{:S(2)}, u32[]{:S(2)}) collective-permute-start(f32[256,256]{1,0:T(8,128)S(1)} %dynamic-slice_bitcast_fusion), channel_id=1, source_target_pairs={{0,1},{1,0},{2,3},{3,2},{4,5},{5,4},{6,7},{7,6},{8,9},{9,8},{10,11... | collective-permute-start | bytes 786440 | tf_op jit(solution)/shard_map/ppermute | solution.py:18
  68.7 30.0 %collective-permute-start.6 = (bf16[3,6,2,16,256]{4,3,2,1,0:T(8,128)(2,1)S(1)}, bf16[3,6,2,16,256]{4,3,2,1,0:T(8,128)(2,1)S(1)}, u32[]{:S(2)}, u32[]{:S(2)}) collective-permute-start(bf16[3,6,2,16,256]{4,3,2,1,0:T(8,128)(2,1)S(1)} %add_convert_fusion), channel_id=1, source_target_pairs={{0,8},{4,12},{8,0},{12,4},{1,9},{5,13},{9,1},{13,5},{2,10},{6,14},... | collective-permute-start | bytes 884744 | tf_op jit(solution)/shard_map/ppermute | solution.py:18
  72.2 39.5 %collective-permute-start.4 = (bf16[3,6,2,16,256]{4,3,2,1,0:T(8,128)(2,1)S(1)}, bf16[3,6,2,16,256]{4,3,2,1,0:T(8,128)(2,1)S(1)}, u32[]{:S(2)}, u32[]{:S(2)}) collective-permute-start(bf16[3,6,2,16,256]{4,3,2,1,0:T(8,128)(2,1)S(1)} %add_convert_fusion.1), channel_id=1, source_target_pairs={{0,8},{4,12},{8,0},{12,4},{1,9},{5,13},{9,1},{13,5},{2,10},{6,14},... | collective-permute-start | bytes 884744 | tf_op jit(solution)/shard_map/ppermute | solution.py:18
  72.3 7.3 %collective-permute-start.28 = (bf16[256,256]{1,0:T(8,128)(2,1)S(1)}, bf16[256,256]{1,0:T(8,128)(2,1)S(1)}, u32[]{:S(2)}, u32[]{:S(2)}) collective-permute-start(bf16[256,256]{1,0:T(8,128)(2,1)S(1)} %fusion.5), channel_id=1, source_target_pairs={{0,18},{1,19},{2,16},{3,17},{16,2},{17,3},{18,0},{19,1},{4,22},{5,... | collective-permute-start | bytes 393224 | tf_op jit(solution)/shard_map/ppermute | solution.py:24
  73.3 9.2 %collective-permute-start.27 = (bf16[256,256]{1,0:T(8,128)(2,1)S(1)}, bf16[256,256]{1,0:T(8,128)(2,1)S(1)}, u32[]{:S(2)}, u32[]{:S(2)}) collective-permute-start(bf16[256,256]{1,0:T(8,128)(2,1)S(1)} %fusion.5), channel_id=1, source_target_pairs={{0,16},{16,0},{1,17},{17,1},{2,18},{18,2},{3,19},{19,3},{4,20},{20... | collective-permute-start | bytes 393224 | tf_op jit(solution)/shard_map/ppermute | solution.py:18
  74.4 8.2 %collective-permute-start.26 = (bf16[256,256]{1,0:T(8,128)(2,1)S(1)}, bf16[256,256]{1,0:T(8,128)(2,1)S(1)}, u32[]{:S(2)}, u32[]{:S(2)}) collective-permute-start(bf16[256,256]{1,0:T(8,128)(2,1)S(1)} %fusion.5), channel_id=1, source_target_pairs={{0,2},{1,3},{2,0},{3,1},{4,6},{5,7},{6,4},{7,5},{8,10},{9,11},{10,... | collective-permute-start | bytes 393224 | tf_op jit(solution)/shard_map/ppermute | solution.py:18
  79.6 31.3 %collective-permute-start.2 = (bf16[3,6,2,16,256]{4,3,2,1,0:T(8,128)(2,1)S(1)}, bf16[3,6,2,16,256]{4,3,2,1,0:T(8,128)(2,1)S(1)}, u32[]{:S(2)}, u32[]{:S(2)}) collective-permute-start(bf16[3,6,2,16,256]{4,3,2,1,0:T(8,128)(2,1)S(1)} %add_convert_fusion.2), channel_id=1, source_target_pairs={{0,8},{4,12},{8,0},{12,4},{1,9},{5,13},{9,1},{13,5},{2,10},{6,14},... | collective-permute-start | bytes 884744 | tf_op jit(solution)/shard_map/ppermute | solution.py:18
  82.7 37.8 %collective-permute-start.29 = (f32[256,256]{1,0:T(8,128)S(1)}, f32[256,256]{1,0:T(8,128)S(1)}, u32[]{:S(2)}, u32[]{:S(2)}) collective-permute-start(f32[256,256]{1,0:T(8,128)S(1)} %add_multiply_fusion.3), channel_id=1, source_target_pairs={{0,1},{1,0},{2,3},{3,2},{4,5},{5,4},{6,7},{7,6},{8,9},{9,8},{10,11... | collective-permute-start | bytes 786440 | tf_op jit(solution)/shard_map/ppermute | solution.py:18
  113.0 37.5 %collective-permute-start.16 = (bf16[3,6,2,16,256]{4,3,2,1,0:T(8,128)(2,1)S(1)}, bf16[3,6,2,16,256]{4,3,2,1,0:T(8,128)(2,1)S(1)}, u32[]{:S(2)}, u32[]{:S(2)}) collective-permute-start(bf16[3,6,2,16,256]{4,3,2,1,0:T(8,128)(2,1)S(1)} %multiply_convert_fusion.2.own_ref), channel_id=1, source_target_pairs={{0,4},{4,0},{8,12},{12,8},{1,5},{5,1},{9,13},{13,9},{2,6},{6,2},{1... | collective-permute-start | bytes 884744 | tf_op jit(solution)/shard_map/ppermute | solution.py:18
  113.6 30.2 %collective-permute-start.17 = (bf16[3,6,2,16,256]{4,3,2,1,0:T(8,128)(2,1)S(1)}, bf16[3,6,2,16,256]{4,3,2,1,0:T(8,128)(2,1)S(1)}, u32[]{:S(2)}, u32[]{:S(2)}) collective-permute-start(bf16[3,6,2,16,256]{4,3,2,1,0:T(8,128)(2,1)S(1)} %multiply_convert_fusion.1.own_ref), channel_id=1, source_target_pairs={{0,4},{4,0},{8,12},{12,8},{1,5},{5,1},{9,13},{13,9},{2,6},{6,2},{1... | collective-permute-start | bytes 884744 | tf_op jit(solution)/shard_map/ppermute | solution.py:18
  115.5 4.1 %collective-permute-start.7 = (bf16[6,16,256]{2,1,0:T(8,128)(2,1)S(1)}, bf16[6,16,256]{2,1,0:T(8,128)(2,1)S(1)}, u32[]{:S(2)}, u32[]{:S(2)}) collective-permute-start(bf16[6,16,256]{2,1,0:T(8,128)(2,1)S(1)} %fusion.52), channel_id=1, source_target_pairs={{0,16},{16,0},{1,17},{17,1},{2,18},{18,2},{3,19},{19,3},{4,20},{20... | collective-permute-start | bytes 147464 | tf_op jit(solution)/shard_map/ppermute | solution.py:18
  116.5 17.8 %collective-permute-start.18 = (bf16[3,6,2,16,256]{4,3,2,1,0:T(8,128)(2,1)S(1)}, bf16[3,6,2,16,256]{4,3,2,1,0:T(8,128)(2,1)S(1)}, u32[]{:S(2)}, u32[]{:S(2)}) collective-permute-start(bf16[3,6,2,16,256]{4,3,2,1,0:T(8,128)(2,1)S(1)} %multiply_convert_fusion.own_ref), channel_id=1, source_target_pairs={{0,4},{4,0},{8,12},{12,8},{1,5},{5,1},{9,13},{13,9},{2,6},{6,2},{1... | collective-permute-start | bytes 884744 | tf_op jit(solution)/shard_map/ppermute | solution.py:18
  119.6 39.8 %collective-permute-start.41 = (f32[384,256]{1,0:T(8,128)}, f32[384,256]{1,0:T(8,128)}, u32[]{:S(2)}, u32[]{:S(2)}) collective-permute-start(f32[384,256]{1,0:T(8,128)} %constant_dynamic-slice_fusion), channel_id=1, source_target_pairs={{0,1},{1,0},{2,3},{3,2},{4,5},{5,4},{6,7},{7,6},{8,9},{9,8},{10,11... | collective-permute-start | bytes 1179656 | tf_op jit(solution)/shard_map/ppermute | solution.py:18
  157.4 12.5 %collective-permute-start.20 = (f32[288,256]{1,0:T(8,128)S(1)}, f32[288,256]{1,0:T(8,128)S(1)}, u32[]{:S(2)}, u32[]{:S(2)}) collective-permute-start(f32[288,256]{1,0:T(8,128)S(1)} %constant_dynamic-slice_fusion.3), channel_id=1, source_target_pairs={{0,1},{1,0},{2,3},{3,2},{4,5},{5,4},{6,7},{7,6},{8,9},{9,8},{10,11... | collective-permute-start | bytes 884744 | tf_op jit(solution)/shard_map/ppermute | solution.py:18
  157.5 1.7 copy-start.2
  157.6 23.3 %collective-permute-start.30 = (f32[512,256]{1,0:T(8,128)S(1)}, f32[512,256]{1,0:T(8,128)S(1)}, u32[]{:S(2)}, u32[]{:S(2)}) collective-permute-start(f32[512,256]{1,0:T(8,128)S(1)} %constant_dynamic-slice_fusion.2), channel_id=1, source_target_pairs={{0,1},{1,0},{2,3},{3,2},{4,5},{5,4},{6,7},{7,6},{8,9},{9,8},{10,11... | collective-permute-start | bytes 1572872 | tf_op jit(solution)/shard_map/ppermute | solution.py:18
  160.5 7.4 %collective-permute-start.42 = (bf16[384,256]{1,0:T(8,128)(2,1)S(1)}, bf16[384,256]{1,0:T(8,128)(2,1)S(1)}, u32[]{:S(2)}, u32[]{:S(2)}) collective-permute-start(bf16[384,256]{1,0:T(8,128)(2,1)S(1)} %add_convert_fusion.5), channel_id=1, source_target_pairs={{0,4},{4,0},{8,12},{12,8},{1,5},{5,1},{9,13},{13,9},{2,6},{6,2},{1... | collective-permute-start | bytes 589832 | tf_op jit(solution)/shard_map/ppermute | solution.py:18
  160.9 19.4 %collective-permute-start.19 = (bf16[6,64,512]{2,1,0:T(8,128)(2,1)S(1)}, bf16[6,64,512]{2,1,0:T(8,128)(2,1)S(1)}, u32[]{:S(2)}, u32[]{:S(2)}) collective-permute-start(bf16[6,64,512]{2,1,0:T(8,128)(2,1)S(1)} %fusion.2), channel_id=1, source_target_pairs={{0,16},{16,0},{1,17},{17,1},{2,18},{18,2},{3,19},{19,3},{4,20},{20... | collective-permute-start | bytes 1179656 | tf_op jit(solution)/shard_map/ppermute | solution.py:18
  167.9 21.0 %collective-permute-start.45 = (bf16[384,256]{1,0:T(8,128)(2,1)S(1)}, bf16[384,256]{1,0:T(8,128)(2,1)S(1)}, u32[]{:S(2)}, u32[]{:S(2)}) collective-permute-start(bf16[384,256]{1,0:T(8,128)(2,1)S(1)} %add_convert_fusion.4), channel_id=1, source_target_pairs={{0,18},{1,19},{2,16},{3,17},{16,2},{17,3},{18,0},{19,1},{4,22},{5,... | collective-permute-start | bytes 589832 | tf_op jit(solution)/shard_map/ppermute | solution.py:24
  168.8 21.7 %collective-permute-start.44 = (bf16[384,256]{1,0:T(8,128)(2,1)S(1)}, bf16[384,256]{1,0:T(8,128)(2,1)S(1)}, u32[]{:S(2)}, u32[]{:S(2)}) collective-permute-start(bf16[384,256]{1,0:T(8,128)(2,1)S(1)} %add_convert_fusion.4), channel_id=1, source_target_pairs={{0,16},{16,0},{1,17},{17,1},{2,18},{18,2},{3,19},{19,3},{4,20},{20... | collective-permute-start | bytes 589832 | tf_op jit(solution)/shard_map/ppermute | solution.py:18
  169.9 12.3 %collective-permute-start.23 = (bf16[288,256]{1,0:T(8,128)(2,1)S(1)}, bf16[288,256]{1,0:T(8,128)(2,1)S(1)}, u32[]{:S(2)}, u32[]{:S(2)}) collective-permute-start(bf16[288,256]{1,0:T(8,128)(2,1)S(1)} %add_convert_fusion.6), channel_id=1, source_target_pairs={{0,18},{1,19},{2,16},{3,17},{16,2},{17,3},{18,0},{19,1},{4,22},{5,... | collective-permute-start | bytes 442376 | tf_op jit(solution)/shard_map/ppermute | solution.py:24
  180.3 6.7 %collective-permute-start.22 = (bf16[288,256]{1,0:T(8,128)(2,1)S(1)}, bf16[288,256]{1,0:T(8,128)(2,1)S(1)}, u32[]{:S(2)}, u32[]{:S(2)}) collective-permute-start(bf16[288,256]{1,0:T(8,128)(2,1)S(1)} %add_convert_fusion.6), channel_id=1, source_target_pairs={{0,16},{16,0},{1,17},{17,1},{2,18},{18,2},{3,19},{19,3},{4,20},{20... | collective-permute-start | bytes 442376 | tf_op jit(solution)/shard_map/ppermute | solution.py:18
  181.0 7.1 %collective-permute-start.21 = (bf16[288,256]{1,0:T(8,128)(2,1)S(1)}, bf16[288,256]{1,0:T(8,128)(2,1)S(1)}, u32[]{:S(2)}, u32[]{:S(2)}) collective-permute-start(bf16[288,256]{1,0:T(8,128)(2,1)S(1)} %add_convert_fusion.6), channel_id=1, source_target_pairs={{0,2},{1,3},{2,0},{3,1},{4,6},{5,7},{6,4},{7,5},{8,10},{9,11},{10,... | collective-permute-start | bytes 442376 | tf_op jit(solution)/shard_map/ppermute | solution.py:18
  182.2 8.4 %collective-permute-start.43 = (bf16[384,256]{1,0:T(8,128)(2,1)S(1)}, bf16[384,256]{1,0:T(8,128)(2,1)S(1)}, u32[]{:S(2)}, u32[]{:S(2)}) collective-permute-start(bf16[384,256]{1,0:T(8,128)(2,1)S(1)} %add_convert_fusion.4), channel_id=1, source_target_pairs={{0,2},{1,3},{2,0},{3,1},{4,6},{5,7},{6,4},{7,5},{8,10},{9,11},{10,... | collective-permute-start | bytes 589832 | tf_op jit(solution)/shard_map/ppermute | solution.py:18
  186.9 10.2 %collective-permute-start.33 = (bf16[512,256]{1,0:T(8,128)(2,1)S(1)}, bf16[512,256]{1,0:T(8,128)(2,1)S(1)}, u32[]{:S(2)}, u32[]{:S(2)}) collective-permute-start(bf16[512,256]{1,0:T(8,128)(2,1)S(1)} %add_convert_fusion.3), channel_id=1, source_target_pairs={{0,18},{1,19},{2,16},{3,17},{16,2},{17,3},{18,0},{19,1},{4,22},{5,... | collective-permute-start | bytes 786440 | tf_op jit(solution)/shard_map/ppermute | solution.py:24
  188.0 12.9 %collective-permute-start.32 = (bf16[512,256]{1,0:T(8,128)(2,1)S(1)}, bf16[512,256]{1,0:T(8,128)(2,1)S(1)}, u32[]{:S(2)}, u32[]{:S(2)}) collective-permute-start(bf16[512,256]{1,0:T(8,128)(2,1)S(1)} %add_convert_fusion.3), channel_id=1, source_target_pairs={{0,16},{16,0},{1,17},{17,1},{2,18},{18,2},{3,19},{19,3},{4,20},{20... | collective-permute-start | bytes 786440 | tf_op jit(solution)/shard_map/ppermute | solution.py:18
  188.9 12.1 %collective-permute-start.31 = (bf16[512,256]{1,0:T(8,128)(2,1)S(1)}, bf16[512,256]{1,0:T(8,128)(2,1)S(1)}, u32[]{:S(2)}, u32[]{:S(2)}) collective-permute-start(bf16[512,256]{1,0:T(8,128)(2,1)S(1)} %add_convert_fusion.3), channel_id=1, source_target_pairs={{0,2},{1,3},{2,0},{3,1},{4,6},{5,7},{6,4},{7,5},{8,10},{9,11},{10,... | collective-permute-start | bytes 786440 | tf_op jit(solution)/shard_map/ppermute | solution.py:18
  190.5 10.7 %copy-start.7 = (bf16[9,2,2,16,256]{4,3,2,1,0:T(8,128)(2,1)S(1)}, bf16[9,2,2,16,256]{4,3,2,1,0:T(8,128)(2,1)}, u32[]{:S(2)}) copy-start(bf16[9,2,2,16,256]{4,3,2,1,0:T(8,128)(2,1)} %copy-done.6) | copy-start | bytes 884740
  190.5 10.7 %copy-start.9 = (bf16[9,2,2,16,256]{4,3,2,1,0:T(8,128)(2,1)S(1)}, bf16[9,2,2,16,256]{4,3,2,1,0:T(8,128)(2,1)}, u32[]{:S(2)}) copy-start(bf16[9,2,2,16,256]{4,3,2,1,0:T(8,128)(2,1)} %copy-done.8) | copy-start | bytes 884740
  190.6 13.2 %collective-permute-start.24 = (f32[288,256]{1,0:T(8,128)S(1)}, f32[288,256]{1,0:T(8,128)S(1)}, u32[]{:S(2)}, u32[]{:S(2)}) collective-permute-start(f32[288,256]{1,0:T(8,128)S(1)} %add_multiply_fusion.2), channel_id=1, source_target_pairs={{0,1},{1,0},{2,3},{3,2},{4,5},{5,4},{6,7},{7,6},{8,9},{9,8},{10,11... | collective-permute-start | bytes 884744 | tf_op jit(solution)/shard_map/ppermute | solution.py:18
  190.8 13.7 %collective-permute-start.46 = (f32[384,256]{1,0:T(8,128)S(1)}, f32[384,256]{1,0:T(8,128)S(1)}, u32[]{:S(2)}, u32[]{:S(2)}) collective-permute-start(f32[384,256]{1,0:T(8,128)S(1)} %add_multiply_fusion.1), channel_id=1, source_target_pairs={{0,1},{1,0},{2,3},{3,2},{4,5},{5,4},{6,7},{7,6},{8,9},{9,8},{10,11... | collective-permute-start | bytes 1179656 | tf_op jit(solution)/shard_map/ppermute | solution.py:18
  201.2 4.9 %collective-permute-start.34 = (f32[512,256]{1,0:T(8,128)S(1)}, f32[512,256]{1,0:T(8,128)S(1)}, u32[]{:S(2)}, u32[]{:S(2)}) collective-permute-start(f32[512,256]{1,0:T(8,128)S(1)} %add_multiply_fusion), channel_id=1, source_target_pairs={{0,1},{1,0},{2,3},{3,2},{4,5},{5,4},{6,7},{7,6},{8,9},{9,8},{10,11... | collective-permute-start | bytes 1572872 | tf_op jit(solution)/shard_map/ppermute | solution.py:18
  203.8 0.8 copy-start.3
  203.8 1.2 copy-start.11
  206.0 1.0 slice-start
  206.0 1.2 copy-start.4

commit v2 on v0

--- a/solution.py
+++ b/solution.py
@@ -1,11 +1,608 @@
+import functools
 import math
 
 import jax
 import jax.numpy as jnp
 from jax import lax
+from jax.experimental import pallas as pl
+from jax.experimental.pallas import tpu as pltpu
 from jax.sharding import PartitionSpec as P
 
 BASE_DILATION = 12
+F32 = jnp.float32
+BF16 = jnp.bfloat16
+VMEM_BYTES = 16 * 2**20
+
+
+def swap(value, axis, flip):
+    count = lax.axis_size(axis)
+    return lax.ppermute(value, axis, [(i, i ^ flip) for i in range(count)])
+
+
+def moved(value, steps):
+    if steps == 0:
+        return value
+    count = value.shape[0]
+    rolled = pltpu.roll(value, (-steps) % count, 0)
+    place = lax.broadcasted_iota(jnp.int32, value.shape, 0)
+    inside = place < count - steps if steps > 0 else place >= -steps
+    return jnp.where(inside, rolled, 0.0)
+
+
+def row_pairs(branch, classes):
+    return [
+        (q, i, q + (i - 1) * branch)
+        for q in range(classes)
+        for i in range(3)
+        if 0 <= q + (i - 1) * branch < classes
+    ]
+
+
+def class_rows(upper, first, last, arrived):
+    return (
+        jnp.where(upper, first, arrived),
+        jnp.where(upper, last, first),
+        jnp.where(upper, arrived, last),
+    )
+
+
+def shape_of(shape, dtype):
+    return jax.ShapeDtypeStruct(shape, dtype)
+
+
+def in_hbm(value):
+    return pltpu.with_memory_space_constraint(value, pltpu.HBM)
+
+
+def result_of(shape, dtype):
+    return jax.ShapeDtypeStruct(shape, dtype)
+
+
+TOKEN = (8, 128)
+STEPS = 2
+
+
+def call(body, place, grid, after, ins, outs, name, scratch=()):
+    def spec(block, split):
+        dims = len(block)
+        if isinstance(split, tuple):
+            return pl.BlockSpec(block, lambda r, p: tuple(r if k is None else k for k in split))
+        return pl.BlockSpec(block, lambda r, p: tuple(r if k == split else 0 for k in range(dims)))
+
+    def kernel(place_ref, after_ref, *refs):
+        last = len(ins) + len(outs) - 2
+        body(place_ref, *refs[:last], *refs[last + 1 :])
+        refs[last][...] = after_ref[...]
+
+    ins = [(after, TOKEN, None)] + list(ins)
+    outs = list(outs) + [(shape_of(TOKEN, F32), TOKEN, None)]
+    return pl.pallas_call(
+        kernel,
+        grid_spec=pltpu.PrefetchScalarGridSpec(
+            num_scalar_prefetch=1,
+            grid=(grid,),
+            in_specs=[spec(block, split) for _, block, split in ins],
+            out_specs=[spec(block, split) for _, block, split in outs],
+            scratch_shapes=list(scratch),
+        ),
+        out_shape=[s for s, _, _ in outs],
+        compiler_params=pltpu.CompilerParams(vmem_limit_bytes=VMEM_BYTES),
+        cost_estimate=pl.CostEstimate(flops=1, bytes_accessed=1, transcendentals=0),
+        name=name,
+    )(place, *[a for a, _, _ in ins])
+
+
+def forward_kernel(branches, folded, place, x_ref, arrived_ref, taps_ref, *refs):
+    classes, group, cols, channels = x_ref.shape
+    count = len(branches)
+    points, refs = refs[:count], refs[count:]
+    keeps, sends, refs = refs[:count], refs[count : 2 * count], refs[2 * count :]
+    spreads = dict(zip([b for b in branches if b], refs))
+    if not folded:
+        refs[-1][...] = x_ref[1]
+
+    def residue(r, carry):
+        rows = [x_ref[q, r].astype(F32) for q in range(classes)]
+        if folded:
+            rows = class_rows(place[1] == 0, rows[0], rows[2], arrived_ref[r].astype(F32))
+        for branch, spread_ref in spreads.items():
+            for q in range(classes):
+                total = None
+                for j in range(3):
+                    part = None
+                    for out, i, source in row_pairs(branch, classes):
+                        if out == q:
+                            tap = taps_ref[branch - 1, i, j].astype(F32)
+                            term = rows[source] * tap[None, :]
+                            part = term if part is None else part + term
+                    part = moved(part, (j - 1) * branch * BASE_DILATION)
+                    total = part if total is None else total + part
+                spread_ref[q, r] = total.astype(BF16)
+        return carry
+
+    lax.fori_loop(0, group, residue, 0)
+    for k, branch in enumerate(branches):
+        cells = spreads[branch][...] if branch else x_ref[...]
+        cells = cells.reshape(classes * group * cols, channels)
+        partial = jnp.dot(cells, points[k][0], preferred_element_type=F32)
+        split = partial.reshape(classes * group * 2, 2, cols // 4, partial.shape[-1])
+        first = place[0] % 2 == 0
+        keep = jnp.where(first, split[:, 0], split[:, 1])
+        send = jnp.where(first, split[:, 1], split[:, 0])
+        keeps[k][0] = keep.reshape(keeps[k].shape[1:])
+        sends[k][0] = send.reshape(sends[k].shape[1:]).astype(BF16)
+
+
+def forward(branches, folded, place, after, x, arrived, taps, point):
+    classes, residues, cols, channels = x.shape
+    filters = point.shape[2]
+    group = residues // STEPS
+    cell = (classes, group, cols, channels)
+    part = (1, classes, group, 2, cols // 4, filters)
+    part_shape = (1, classes, residues, 2, cols // 4, filters)
+    outs = [(shape_of(part_shape, F32), part, 2) for _ in branches]
+    outs += [(shape_of(part_shape, BF16), part, 2) for _ in branches]
+    outs += [(pltpu.HBM(x.shape, BF16), cell, 1) for b in branches if b]
+    if not folded:
+        outs += [(shape_of(x.shape[1:], BF16), (group, cols, channels), 0)]
+    return call(
+        functools.partial(forward_kernel, branches, folded), place, STEPS, after,
+        [
+            (x, cell, 1),
+            (arrived, (group, cols, channels) if folded else (1, 1, 8, 128), 0 if folded else None),
+            (taps, taps.shape, None),
+        ]
+        + [(point, (1, channels, filters), (b, 0, 0)) for b in branches],
+        outs, "forward_" + "_".join(map(str, branches)),
+    )
+
+
+def near_kernel(place, keep_ref, arrived_ref, *near_refs):
+    for k, near_ref in enumerate(near_refs):
+        near_ref[0] = (keep_ref[k] + arrived_ref[k].astype(F32)).astype(BF16)
+
+
+def near_sum(name, place, after, keep, arrived):
+    block = keep.shape[:2] + (keep.shape[2] // STEPS,) + keep.shape[3:]
+    out = (1,) + block[1:]
+    return call(
+        near_kernel, place, STEPS, after, [(keep, block, 2), (arrived, block, 2)],
+        [(shape_of((1,) + keep.shape[1:], BF16), out, 2)] * keep.shape[0], f"near_{name}",
+    )
+
+
+def first_near_kernel(place, keep_ref, arrived_ref, cot_ref, far_ref, near_ref, cots_ref, leaving_ref):
+    near_ref[...] = (keep_ref[...] + arrived_ref[...].astype(F32)).astype(BF16)
+    low_side = place[0] // 2 == 0
+    cots_ref[:, 0] = jnp.where(low_side, cot_ref[...], far_ref[...])
+    cots_ref[:, 1] = jnp.where(low_side, far_ref[...], cot_ref[...])
+    n = leaving_ref.shape[0]
+    leaving_ref[...] = cots_ref[n : 2 * n]
+
+
+def first_near_sum(place, after, keep, arrived, cot, far):
+    rows, width, filters = cot.shape
+    cots = (rows, 2, width, filters)
+    leaving = (rows // 3, 2, width, filters)
+    return call(
+        first_near_kernel, place, 1, after,
+        [(a, a.shape, None) for a in (keep, arrived, cot, far)],
+        [(shape_of(s, BF16), s, None) for s in (keep.shape, cots, leaving)], "near_first",
+    )
+
+
+def gate_kernel(branches, folded, place, *refs):
+    count = len(branches)
+    nears, fars, cot_ref, refs = refs[:count], refs[count : 2 * count], refs[2 * count], refs[2 * count + 1 :]
+    _, classes, residues, sides, width, filters = nears[0].shape
+    if folded:
+        arrived_ref, refs = refs[0], refs[1:]
+    projs, (mixed_ref, grad_ref, out_ref, proj_grad_ref, *leaving) = refs[:count], refs[count:]
+    n = residues
+    cots = cot_ref[...]
+    if folded:
+        cots = jnp.concatenate(
+            class_rows(place[1] == 0, cots[:n], cots[2 * n : 3 * n], arrived_ref[...])
+        )
+    cells = cots.reshape(-1, filters)
+    shape = (classes * residues, sides, width, filters)
+    mixed = mixed_ref[...]
+    for k in range(count):
+        proj = projs[k][0]
+        act_grad = lax.dot_general(cells, proj, (((1,), (1,)), ((), ())), preferred_element_type=F32)
+        preact = (nears[k][0].astype(F32) + fars[k][0].astype(F32)).reshape(shape)
+        logistic = 1.0 / (1.0 + jnp.exp(-preact))
+        grad = act_grad.reshape(shape) * logistic * (1.0 + preact * (1.0 - logistic))
+        grad_ref[k] = grad.astype(BF16).reshape(grad_ref.shape[1:])
+        active = (preact * logistic).astype(BF16)
+        mine = jnp.where(place[0] // 2 == 0, active[:, 0], active[:, 1]).reshape(-1, filters)
+        mixed = mixed + jnp.dot(mine, proj, preferred_element_type=F32).reshape(mixed.shape)
+        proj_grad_ref[k] = lax.dot_general(
+            active.reshape(-1, filters), cells, (((0,), (0,)), ((), ())), preferred_element_type=F32
+        )
+    out_ref[...] = mixed
+    if leaving:
+        upper = place[1] == 0
+        leaving[0][...] = jnp.where(upper, mixed[2 * n :], mixed[:n]).astype(BF16)
+
+
+def gate(branches, folded, place, after, nears, fars, cots, arrived, proj, mixed, leaves=False):
+    filters = proj.shape[-1]
+    count = len(branches)
+    arrays = [*nears, *fars, cots] + ([arrived] if folded else [])
+    shapes = [
+        ((count,) + nears[0].shape[1:], BF16), (mixed.shape, F32), ((count, filters, filters), F32)
+    ]
+    if leaves:
+        shapes.append(((mixed.shape[0] // 3,) + mixed.shape[1:], BF16))
+    return call(
+        functools.partial(gate_kernel, branches, folded), place, 1, after,
+        [(a, a.shape, None) for a in arrays]
+        + [(proj, (1, filters, filters), (b, 0, 0)) for b in branches]
+        + [(mixed, mixed.shape, None)],
+        [(shape_of(shape, kind), shape, None) for shape, kind in shapes],
+        "gate_" + "_".join(map(str, branches)),
+    )
+
+
+def whole_columns(place, own, other):
+    thin = (-1,) + own.shape[-2:]
+    own, other = own.reshape(thin), other.reshape(thin)
+    first = place[0] % 2 == 0
+    low = jnp.where(first, own, other)
+    high = jnp.where(first, other, own)
+    both = jnp.concatenate([low[:, None], high[:, None]], axis=1)
+    return both.reshape(-1, own.shape[-1])
+
+
+def backward_kernel(
+    branch, folded, chained, place, own_ref, other_ref, x_ref, arrived_ref, spread_ref, taps_ref, point_ref,
+    before_ref, *refs
+):
+    classes, group, cols, channels = x_ref.shape
+    point_grad_ref, depth_ref, grads_ref = refs[-3:]
+    upper = place[1] == 0
+    pre = whole_columns(place, own_ref[0], other_ref[0])
+    grads = lax.dot_general(pre, point_ref[0], (((1,), (1,)), ((), ())), preferred_element_type=F32)
+    grads_ref[...] = grads.astype(BF16).reshape(grads_ref.shape)
+    cells = spread_ref[...].reshape(classes * group * cols, channels)
+    product = lax.dot_general(cells, pre, (((0,), (0,)), ((), ())), preferred_element_type=F32)
+
+    @pl.when(pl.program_id(0) == 0)
+    def _():
+        point_grad_ref[...] = product
+        depth_ref[...] = jnp.zeros_like(depth_ref)
+
+    @pl.when(pl.program_id(0) > 0)
+    def _():
+        point_grad_ref[...] += product
+
+    pairs = row_pairs(branch, classes)
+
+    def residue(r, carry):
+        rows = [x_ref[q, r].astype(F32) for q in range(classes)]
+        if folded:
+            rows = class_rows(upper, rows[0], rows[2], arrived_ref[r].astype(F32))
+        grads = [grads_ref[q, r].astype(F32) for q in range(classes)]
+        for j in range(3):
+            near = [moved(row, (j - 1) * branch * BASE_DILATION) for row in rows]
+            for i in range(3):
+                part = None
+                for q, tap, source in pairs:
+                    if tap == i:
+                        term = (near[source] * grads[q]).reshape(cols // 8, 8, channels).sum(axis=0)
+                        part = term if part is None else part + term
+                if part is not None:
+                    depth_ref[i * 3 + j] += part
+        totals = []
+        for target in range(classes):
+            total = before_ref[target, r] if chained else None
+            for j in range(3):
+                part = None
+                for q, i, source in pairs:
+                    if source == target:
+                        term = grads[q] * taps_ref[branch - 1, i, j].astype(F32)[None, :]
+                        part = term if part is None else part + term
+                part = moved(part, -(j - 1) * branch * BASE_DILATION)
+                total = part if total is None else total + part
+            totals.append(total)
+        if chained:
+            leaving_ref, stay_ref = refs[:2]
+            leaving_ref[r] = jnp.where(upper, totals[2], totals[0]).astype(BF16)
+            stay_ref[0, r] = jnp.where(upper, totals[0], totals[1])
+            stay_ref[1, r] = jnp.where(upper, totals[1], totals[2])
+        else:
+            for q in range(classes):
+                refs[0][q, r] = totals[q]
+        return carry
+
+    lax.fori_loop(0, group, residue, 0)
+
+
+def backward(branch, folded, place, after, own, other, index, x, arrived, spread, taps, point, before=None):
+    classes, residues, cols, channels = x.shape
+    filters = point.shape[2]
+    group = residues // STEPS
+    part = (1, classes, group, 2, cols // 4, filters)
+    cell = (classes, group, cols, channels)
+    thin = (group, cols, channels)
+    chained = before is not None
+    if chained:
+        outs = [
+            (shape_of(x.shape[1:], BF16), thin, 0),
+            (pltpu.HBM((2,) + x.shape[1:], F32), (2,) + thin, 1),
+        ]
+    else:
+        outs = [(pltpu.HBM(x.shape, F32), cell, 1)]
+    outs += [
+        (shape_of((channels, filters), F32), (channels, filters), None),
+        (shape_of((9, 8, channels), F32), (9, 8, channels), None),
+    ]
+    small = (1, 1, 8, 128)
+    return call(
+        functools.partial(backward_kernel, branch, folded, chained), place, STEPS, after,
+        [
+            (own, part, (index, 0, None, 0, 0, 0)),
+            (other, part, (index, 0, None, 0, 0, 0)),
+            (x, cell, 1),
+            (arrived, thin, 0) if folded else (x, small, None),
+            (spread, cell, 1),
+            (taps, taps.shape, None),
+            (point, (1, channels, filters), (branch, 0, 0)),
+            (before, cell, 1) if chained else (x, small, None),
+        ],
+        outs, f"backward_{branch}", scratch=[pltpu.VMEM(cell, BF16)],
+    )
+
+
+def join_kernel(place, own_ref, other_ref, x_ref, pre_ref, point_grad_ref):
+    pre = whole_columns(place, own_ref[0], other_ref[0])
+    pre_ref[...] = pre.reshape(pre_ref.shape)
+    cells = x_ref[...].reshape(-1, x_ref.shape[-1])
+    product = lax.dot_general(cells, pre, (((0,), (0,)), ((), ())), preferred_element_type=F32)
+
+    @pl.when(pl.program_id(0) == 0)
+    def _():
+        point_grad_ref[...] = product
+
+    @pl.when(pl.program_id(0) > 0)
+    def _():
+        point_grad_ref[...] += product
+
+
+def join(place, after, own, other, index, x):
+    classes, residues, cols, channels = x.shape
+    filters = own.shape[-1]
+    group = residues // STEPS
+    part = (1, classes, group, 2, cols // 4, filters)
+    return call(
+        join_kernel, place, STEPS, after,
+        [
+            (own, part, (index, 0, None, 0, 0, 0)),
+            (other, part, (index, 0, None, 0, 0, 0)),
+            (x, (classes, group, cols, channels), 1),
+        ],
+        [
+            (shape_of((classes, residues, cols, filters), BF16), (classes, group, cols, filters), 1),
+            (shape_of((channels, filters), F32), (channels, filters), None),
+        ],
+        "join",
+    )
+
+
+def last_kernel(
+    place, pre_ref, point_ref, band_ref, stay_ref, arrived_ref, mixed_ref, folded_ref, mixed_arrived_ref,
+    input_ref, output_ref
+):
+    classes, group, cols, channels = band_ref.shape
+    pre = pre_ref[...].reshape(classes * group * cols, -1)
+    grads = lax.dot_general(pre, point_ref[0], (((1,), (1,)), ((), ())), preferred_element_type=F32)
+    grads = grads.astype(BF16).astype(F32).reshape(band_ref.shape)
+    others = (stay_ref[0], arrived_ref[...].astype(F32), stay_ref[1])
+    for q in range(classes):
+        input_ref[q] = (grads[q] + band_ref[q] + others[q]).astype(BF16)
+    upper = place[1] == 0
+    mixed = (
+        jnp.where(upper, folded_ref[0], folded_ref[1]),
+        mixed_arrived_ref[...].astype(F32),
+        jnp.where(upper, folded_ref[1], folded_ref[2]),
+    )
+    for q in range(classes):
+        output_ref[q] = (mixed_ref[q] + mixed[q]).astype(BF16)
+
+
+def last(place, after, pre, point, band, stay, arrived, mixed, folded, mixed_arrived):
+    classes, residues, cols, channels = band.shape
+    filters = point.shape[2]
+    group = residues // STEPS
+    cell = (classes, group, cols, channels)
+    thin = (classes, group) + mixed.shape[2:]
+    return call(
+        last_kernel, place, STEPS, after,
+        [
+            (pre, (classes, group, cols, filters), 1),
+            (point, (1, channels, filters), (0, 0, 0)),
+            (band, cell, 1),
+            (stay, (2, group, cols, channels), 1),
+            (arrived, (group, cols, channels), 0),
+            (mixed, thin, 1),
+            (folded, thin, 1),
+            (mixed_arrived, thin[1:], 0),
+        ],
+        [(result_of(band.shape, BF16), cell, 1), (result_of(mixed.shape, BF16), thin, 1)], "last",
+    )
+
+
+def add_kernel(scale, place, *refs):
+    *pairs, out_ref = refs
+    at = 0
+    for own_ref, other_ref in zip(pairs[::2], pairs[1::2]):
+        rows = other_ref.shape[0]
+        if len(own_ref.shape) == 3:
+            own = jnp.where(place[2] == 0, own_ref[0], own_ref[1])
+        else:
+            own = own_ref[...]
+        total = own.astype(F32) + other_ref[...].astype(F32)
+        if scale != 1.0:
+            total = total * scale
+        out_ref[at : at + rows] = total.astype(out_ref.dtype)
+        at += rows
+
+
+def add(name, place, after, pairs, kind, scale=1.0):
+    rows = sum(other.shape[0] for _, other in pairs)
+    shape = (rows, pairs[0][1].shape[1])
+    return call(
+        functools.partial(add_kernel, scale), place, 1, after,
+        [(a, a.shape, None) for pair in pairs for a in pair],
+        [(shape_of(shape, kind), shape, None)], name,
+    )
+
+
+def finish_kernel(place, own30, far30, own1, far1, own2, far2, proj_ref, depth_ref, point_ref):
+    core = place[2] == 0
+
+    def halves(own, far, first, count):
+        own, far = own[first : first + count], far[first : first + count]
+        return jnp.where(core, own, far), jnp.where(core, far, own)
+
+    channels = point_ref.shape[1]
+    filters = proj_ref.shape[1]
+    point_ref[3], point_ref[0] = halves(own30, far30, 0, channels)
+    proj_ref[3], proj_ref[0] = halves(own30, far30, channels, filters)
+    point_ref[1, : channels // 2], point_ref[1, channels // 2 :] = halves(own1, far1, 0, channels // 2)
+    rows = own2.shape[0] - filters
+    low, high = halves(own2, far2, 0, rows)
+    point_ref[2, :rows] = low
+    point_ref[2, rows:] = high[: channels - rows]
+    depth_ref[...] = high[channels - rows :]
+    proj_ref[1], proj_ref[2] = halves(own2, far2, rows, filters)
+
+
+def finish(place, after, early, middle, late, channels, filters):
+    arrays = [*early, *middle, *late]
+    rows = 2 * (late[0].shape[0] - filters) - channels
+    shapes = [(4, filters, filters), (rows, filters), (4, channels, filters)]
+    return call(
+        finish_kernel, place, 1, after, [(a, a.shape, None) for a in arrays],
+        [(result_of(s, F32), s, None) for s in shapes], "finish",
+    )
+
+
+def cores(value):
+    if len(value.shape) == 2:
+        value = value.reshape((2, -1) + value.shape[1:])
+    far = lax.dynamic_index_in_dim(value, 1 - lax.axis_index("dp") % 2, 0, keepdims=False)
+    return value, swap(far, "dp", 1)
+
+
+def by_classes(features_in, depth_weights, point_weights, proj_weights, cotangent):
+    _, band_rows, cols, channels = features_in.shape
+    filters = point_weights.shape[2]
+    classes, n = 3, band_rows // 3
+    scale = 1.0 / math.sqrt(lax.axis_size("dp") * band_rows * lax.axis_size("row") * cols)
+    chan, row = lax.axis_index("chan"), lax.axis_index("row")
+    core = lax.axis_index("dp") % 2
+    place = jnp.stack([chan, row, core]).astype(jnp.int32)
+    x = features_in[0].reshape(classes, n, cols, channels)
+
+    weights = (depth_weights, point_weights)
+    cot = cotangent[0]
+    cot_far = swap(cot, "chan", 2)
+
+    token = jnp.zeros(TOKEN, F32)
+    keep3, keep0, send3, send0, spread3, x_leaving, token = forward(
+        (3, 0), False, place, token, in_hbm(x), x, depth_weights, in_hbm(point_weights)
+    )
+    sent3, sent0 = swap(send3, "chan", 1), swap(send0, "chan", 1)
+    arrived = swap(x_leaving, "row", 1)
+    near3, cots, cots_leaving, token = first_near_sum(place, token, keep3, sent3, cot, cot_far)
+    far3 = swap(near3, "chan", 2)
+    near0, token = near_sum("0", place, token, keep0, sent0)
+    far0 = swap(near0, "chan", 2)
+    cots_arrived = swap(cots_leaving, "row", 1)
+    keep1, keep2, send1, send2, spread1, spread2, token = forward(
+        (1, 2), True, place, token, x, arrived, *weights
+    )
+    sent1, sent2 = swap(send1, "chan", 1), swap(send2, "chan", 1)
+    near1, token = near_sum("1", place, token, keep1, sent1)
+    far1 = swap(near1, "chan", 2)
+    mixed = jnp.zeros(cot.shape, F32)
+    grad30, band_mixed, proj30, token = gate(
+        (3, 0), False, place, token, [near3, near0], [far3, far0], cots, None, proj_weights, mixed
+    )
+    other30 = swap(grad30, "chan", 1)
+    proj30_own, proj30_near = cores(proj30)
+    near2, token = near_sum("2", place, token, keep2, sent2)
+    far2 = swap(near2, "chan", 2)
+    grad1, class_mixed, proj1, token = gate(
+        (1,), True, place, token, [near1], [far1], cots, cots_arrived, proj_weights, mixed
+    )
+    other1 = swap(grad1, "chan", 1)
+    proj30_sum, token = add("proj_3_0", place, token, [(proj30_own, proj30_near)], BF16)
+    proj30_pair = swap(proj30_sum, "chan", 1)
+    band, point3, depth3, token = backward(
+        3, False, place, token, grad30, other30, 0, x, x, spread3, *weights
+    )
+    grad2, class_mixed, proj2, mixed_leaving, token = gate(
+        (2,), True, place, token, [near2], [far2], cots, cots_arrived, proj_weights, class_mixed, True
+    )
+    other2 = swap(grad2, "chan", 1)
+    mixed_arrived = swap(mixed_leaving, "row", 1)
+    proj12_own, proj12_near = cores(jnp.concatenate([proj1, proj2]))
+    pre0, point0, token = join(place, token, grad30, other30, 1, x)
+    point30_own, point30_near = cores(jnp.stack([point3, point0]))
+    total1, point1, depth1, token = backward(
+        1, True, place, token, grad1, other1, 0, x, arrived, spread1, *weights
+    )
+    point1_own, point1_near = cores(point1)
+    early, token = add(
+        "early_y", place, token, [(point30_own, point30_near), (proj30_sum, proj30_pair)], BF16
+    )
+    early_y = swap(early, "row", 1)
+    proj12_sum, token = add("proj_1_2", place, token, [(proj12_own, proj12_near)], BF16)
+    proj12_pair = swap(proj12_sum, "chan", 1)
+    middle, token = add("middle_y", place, token, [(point1_own, point1_near)], BF16)
+    middle_y = swap(middle, "row", 1)
+    leaving, stay, point2, depth2, token = backward(
+        2, True, place, token, grad2, other2, 0, x, arrived, spread2, *weights, before=total1
+    )
+    input_arrived = swap(leaving, "row", 1)
+    early, token = add("early_x", place, token, [(early, early_y)], BF16)
+    early_x = swap(early, "dp", 2)
+    depth_rows = 27 * channels // filters
+    padded = -(-depth_rows // 32) * 32
+    depth = jnp.concatenate([depth1, depth2, depth3]).sum(axis=1).reshape(depth_rows, filters)
+    depth = jnp.pad(depth, ((0, padded - depth_rows), (0, 0)))
+    late_own, late_near = cores(jnp.concatenate([point2, depth]))
+    late, token = add(
+        "late_x", place, token, [(late_own, late_near), (proj12_sum, proj12_pair)], BF16
+    )
+    late_x = swap(late, "dp", 2)
+    middle, token = add("middle_x", place, token, [(middle, middle_y)], BF16)
+    middle_x = swap(middle, "dp", 2)
+    bands = band_mixed.reshape((classes, n) + band_mixed.shape[1:])
+    folds = class_mixed.reshape(bands.shape)
+    grad_input, output, token = last(
+        place, token, pre0, point_weights, in_hbm(band), in_hbm(stay), input_arrived, bands, folds,
+        mixed_arrived,
+    )
+    late, token = add("late_y", place, token, [(late, late_x)], BF16)
+    late_y = swap(late, "row", 1)
+    early, token = add("early", place, token, [(early, early_x)], F32, scale)
+    early_far = swap(early, "dp", 1)
+    middle, token = add("middle", place, token, [(middle, middle_x)], F32, scale)
+    middle_far = swap(middle, "dp", 1)
+    late, token = add("late", place, token, [(late, late_y)], F32, scale)
+    late_far = swap(late, "dp", 1)
+    grad_proj, depth, grad_point, token = finish(
+        place, token, (early, early_far), (middle, middle_far), (late, late_far), channels, filters
+    )
+    grad_depth = depth[:depth_rows].reshape(3, 3, 3, channels)
+    return (
+        output.reshape(cotangent.shape), grad_input.reshape(features_in.shape), grad_depth, grad_point,
+        grad_proj,
+    )
 
 
 def shifted(value, axis, steps):
@@ -129,6 +726,20 @@
     return (output, grad_in.astype(jnp.bfloat16), grad_depth, grad_point, grad_proj)
 
 
+def folds(mesh, features_in):
+    sizes = mesh.shape
+    samples, rows, cols, channels = features_in.shape
+    return (
+        rows == 3 * BASE_DILATION
+        and sizes["row"] == 2
+        and sizes["chan"] == 4
+        and sizes["dp"] == 4
+        and samples == sizes["dp"]
+        and cols % 64 == 0
+        and channels % (128 * sizes["chan"]) == 0
+    )
+
+
 def solution(mesh):
     in_specs = (
         P("dp", "row", None, "chan"),
@@ -144,6 +755,11 @@
         P(None, "chan", None),
         P(),
     )
-    return jax.shard_map(
-        on_device, mesh=mesh, in_specs=in_specs, out_specs=out_specs, check_vma=False
-    )
+
+    def run(*args):
+        body = by_classes if folds(mesh, args[0]) else on_device
+        return jax.shard_map(
+            body, mesh=mesh, in_specs=in_specs, out_specs=out_specs, check_vma=False
+        )(*args)
+
+    return run

time: 647 us -> 162 us (0.25)
  waiting for transfers between devices: 472 us -> 66 us
  Pallas kernels: 0 us -> 52.9 us
  other arithmetic: 44.9 us -> 0.4 us
  local copies, waits for them, and re-layouts: 39.3 us -> 8.22 us
  blocking collectives: 23.8 us -> 0 us
  matrix products: 17.9 us -> 0 us
  between operations: 14.6 us -> 1.12 us
    all_to_all x1 -> x0, waiting for transfers between devices: 170 us -> none  [on_device(): lax.all_to_all(spread, 'chan', split_axis=3, concat_axis=4, tiled=True)]
    psum x2 -> x0, waiting for transfers between devices: 161 us -> none  [the longest x1 124 us: on_device(): grad_proj = lax.psum(proj_term, ('row', 'chan', 'dp')) * weight_scale]
    pallas_call x0 -> x26, Pallas kernels: none -> 52.9 us  [call(): pl.pallas_call(kernel, grid_spec=pltpu.PrefetchScalarGridSpec(num_scalar_...]
    all_gather x2 -> x0, waiting for transfers between devices: 48.8 us -> none  [the longest x1 48.8 us: on_device(): incoming = lax.all_gather(pre_grad, 'chan', axis=3, tiled=True)]
    ppermute x12 -> x32, waiting for transfers between devices: 91.5 us -> 66 us  [swap(): return lax.ppermute(value, axis, [(i, i ^ flip) for i in range(count)])]
    psum x1 -> x0, blocking collectives: 23.8 us -> none  [on_device(): lax.psum((point_term, depth_term), ('row', 'dp'))]
    dot_general x6 -> x0, matrix products: 17.9 us -> none  [the longest x1 6.08 us: on_device(): jnp.einsum('bsrwc,bcf->bsrwf', lax.all_to_all(spread, 'chan', split_axis=...]
    reduce_sum x3 -> x1, other arithmetic: 15.5 us -> 0.11 us  [by_classes(): jnp.concatenate([depth1, depth2, depth3]).sum(axis=1)]
  transfers between devices with their start and end apart: 17 -> 32, of which waited for: 10 -> 13; matrix products, arithmetic and copies ran while one was open for 8% -> 1% of each run, Pallas kernels for 0% -> 25%
where the time goes in v2:
time: 162 us
  waiting for transfers between devices  66 us (41%)
  Pallas kernels  52.9 us (33%)
  starting transfers between devices  33.3 us (21%)
  local copies, waits for them, and re-layouts  8.22 us (5%)
    ppermute x32, waiting for transfers between devices, swap(): return lax.ppermute(value, axis, [(i, i ^ flip) for i in range(count)])  66 us
    pallas_call x26, Pallas kernels, call(): pl.pallas_call(kernel, grid_spec=pltpu.PrefetchScalarGridSpec(num_scalar_...  52.9 us
    ppermute x32, starting transfers between devices, swap(): return lax.ppermute(value, axis, [(i, i ^ flip) for i in range(count)])  33.3 us
    unnamed x53, local copies, waits for them, and re-layouts  6.46 us
  transfers between devices with their start and end apart: 32, of which 13 were waited for; matrix products, arithmetic and copies ran while one was open for 1% of the time, Pallas kernels for 25%

profile of v2, /device:TPU:0, one launch (start us, length us, event | category | flops | bytes accessed | tf_op | source)
XLA Modules:
  0.0 161.9 jit_solution(15341784031762270325)
XLA Ops:
  0.7 0.8 copy-done.11
  1.5 4.4 %forward_3_0.1 = (f32[1,3,6,2,16,256]{5,4,3,2,1,0:T(8,128)S(1)}, f32[1,3,6,2,16,256]{5,4,3,2,1,0:T(8,128)S(1)}, bf16[1,3,6,2,16,256]{5,4,3,2,1,0:T(8,128)(2,1)S(...) custom-call(s32[3]{0:T(128)S(1)} %pad_add_fusion.place_ref, ...), custom_call_target="tpu_custom_call" | custom-call | flops 1 | bytes 1 | tf_op jit(solution)/shard_map/forward_3_0/pallas_call | solution.py:79
  5.9 3.0 %collective-permute-start.3 = (bf16[6,64,512]{2,1,0:T(8,128)(2,1)S(1)}, bf16[6,64,512]{2,1,0:T(8,128)(2,1)S(1)}, u32[]{:S(2)}, u32[]{:S(2)}) collective-permute-start(bf16[6,64,512]{2,1,0:T(8,128)(2,1)S(1)} %get-tuple-element.93), channel_id=1, source_target_pairs={{0,16},{16,0},{1,17},{17,1},{2,18},{18,2},{3,19},{19,3},{4,20},{20... | collective-permute-start | bytes 1179656 | tf_op jit(solution)/shard_map/ppermute | solution.py:19
  8.9 1.6 collective-permute-start
  10.9 2.6 %collective-permute-start.1 = (bf16[18,16,256]{2,1,0:T(8,128)(2,1)S(1)}, bf16[18,16,256]{2,1,0:T(8,128)(2,1)S(1)}, u32[]{:S(2)}, u32[]{:S(2)}) collective-permute-start(bf16[18,16,256]{2,1,0:T(8,128)(2,1)S(1)} %bitcast.43), channel_id=1, source_target_pairs={{0,8},{4,12},{8,0},{12,4},{1,9},{5,13},{9,1},{13,5},{2,10},{6,14},... | collective-permute-start | bytes 442376 | tf_op jit(solution)/shard_map/ppermute | solution.py:19
  13.5 12.4 %collective-permute-done.1.refs_3_ = bf16[18,16,256]{2,1,0:T(8,128)(2,1)S(1)} collective-permute-done((bf16[18,16,256]{2,1,0:T(8,128)(2,1)S(1)}, bf16[18,16,256]{2,1,0:T(8,128)(2,1)S(1)}, u32[]{:S(2)}, u32[]{:S(2)}) %collective-permute-start.1) | collective-permute-done | bytes 147488 | tf_op jit(solution)/shard_map/ppermute | solution.py:19
  25.9 0.7 near_first.1
  26.8 0.7 near_0.1
  27.6 5.3 %forward_1_2.1 = (f32[1,3,6,2,16,256]{5,4,3,2,1,0:T(8,128)S(1)}, f32[1,3,6,2,16,256]{5,4,3,2,1,0:T(8,128)S(1)}, bf16[1,3,6,2,16,256]{5,4,3,2,1,0:T(8,128)(2,1)S(...) custom-call(s32[3]{0:T(128)S(1)} %pad_add_fusion.place_ref, ...), custom_call_target="tpu_custom_call" | custom-call | flops 1 | bytes 1 | tf_op jit(solution)/shard_map/forward_1_2/pallas_call | solution.py:79
  32.9 0.8 copy-done.15
  33.8 3.3 %collective-permute-start.4 = (bf16[1,3,6,2,16,256]{5,4,3,2,1,0:T(8,128)(2,1)S(1)}, bf16[1,3,6,2,16,256]{5,4,3,2,1,0:T(8,128)(2,1)S(1)}, u32[]{:S(2)}, u32[]{:S(2)}) collective-permute-start(bf16[1,3,6,2,16,256]{5,4,3,2,1,0:T(8,128)(2,1)S(1)} %get-tuple-element.96), channel_id=1, source_target_pairs={{0,4},{4,0},{8,12},{12,8},{1,5},{5,1},{9,13},{13,9},{2,6},{6,2},{1... | collective-permute-start | bytes 884744 | tf_op jit(solution)/shard_map/ppermute | solution.py:19
  37.1 0.9 collective-permute-start.5
  37.9 2.1 %collective-permute-start.6 = (bf16[1,3,6,2,16,256]{5,4,3,2,1,0:T(8,128)(2,1)S(1)}, bf16[1,3,6,2,16,256]{5,4,3,2,1,0:T(8,128)(2,1)S(1)}, u32[]{:S(2)}, u32[]{:S(2)}) collective-permute-start(bf16[1,3,6,2,16,256]{5,4,3,2,1,0:T(8,128)(2,1)S(1)} %get-tuple-element.99.refs_1_), channel_id=1, source_target_pairs={{0,8},{4,12},{8,0},{12,4},{1,9},{5,13},{9,1},{13,5},{2,10},{6,14},... | collective-permute-start | bytes 884744 | tf_op jit(solution)/shard_map/ppermute | solution.py:19
  40.0 10.1 %collective-permute-done.4.refs_1_ = bf16[1,3,6,2,16,256]{5,4,3,2,1,0:T(8,128)(2,1)S(1)} collective-permute-done((bf16[1,3,6,2,16,256]{5,4,3,2,1,0:T(8,128)(2,1)S(1)}, bf16[1,3,6,2,16,256]{5,4,3,2,1,0:T(8,128)(2,1)S(1)}, u32[]{:S(2)}, u32[]{:S(2)}) %collective-permute-start.4) | collective-permute-done | bytes 294944 | tf_op jit(solution)/shard_map/ppermute | solution.py:19
  50.1 0.7 near_1.1
  50.8 9.7 %collective-permute-done.5.refs_2_ = bf16[1,3,6,2,16,256]{5,4,3,2,1,0:T(8,128)(2,1)S(1)} collective-permute-done((bf16[1,3,6,2,16,256]{5,4,3,2,1,0:T(8,128)(2,1)S(1)}, bf16[1,3,6,2,16,256]{5,4,3,2,1,0:T(8,128)(2,1)S(1)}, u32[]{:S(2)}, u32[]{:S(2)}) %collective-permute-start.5) | collective-permute-done | bytes 294944 | tf_op jit(solution)/shard_map/ppermute | solution.py:19
  60.5 3.7 %collective-permute-done.6.refs_3_ = bf16[1,3,6,2,16,256]{5,4,3,2,1,0:T(8,128)(2,1)S(1)} collective-permute-done((bf16[1,3,6,2,16,256]{5,4,3,2,1,0:T(8,128)(2,1)S(1)}, bf16[1,3,6,2,16,256]{5,4,3,2,1,0:T(8,128)(2,1)S(1)}, u32[]{:S(2)}, u32[]{:S(2)}) %collective-permute-start.6) | collective-permute-done | bytes 294944 | tf_op jit(solution)/shard_map/ppermute | solution.py:19
  64.3 2.1 %gate_3_0.1 = (bf16[2,3,6,2,16,256]{5,4,3,2,1,0:T(8,128)(2,1)}, f32[18,16,256]{2,1,0:T(8,128)S(1)}, f32[2,256,256]{2,1,0:T(8,128)S(1)}, f32[8,128]{1,0:T(8,128)S(1)}) custom-call(s32[3]{0:T(128)S(1)} %pad_add_fusion.place_ref, f32[8,128]{1,0:T(8,128)S(1)} %get-tuple-element.97.after_ref, bf16[1,3,6,2,16,256]{5,4,3,2,1,0:T(8,128)(2,1)S(1)} %get-tuple-element.98.refs_0_, ...), custom_call_target="tpu_custom_call" | custom-call | flops 1 | bytes 1 | tf_op jit(solution)/shard_map/gate_3_0/pallas_call | solution.py:79
  66.4 0.8 copy-done.6
  67.2 0.7 copy-done.17
  67.9 1.9 %collective-permute-start.8 = (bf16[1,3,6,2,16,256]{5,4,3,2,1,0:T(8,128)(2,1)}, bf16[1,3,6,2,16,256]{5,4,3,2,1,0:T(8,128)(2,1)S(1)}, u32[]{:S(2)}, u32[]{:S(2)}) collective-permute-start(bf16[1,3,6,2,16,256]{5,4,3,2,1,0:T(8,128)(2,1)} %copy-done.19), channel_id=1, source_target_pairs={{0,8},{4,12},{8,0},{12,4},{1,9},{5,13},{9,1},{13,5},{2,10},{6,14},... | collective-permute-start | bytes 884744 | tf_op jit(solution)/shard_map/ppermute | solution.py:19
  69.8 1.0 dynamic-slice_bitcast_fusion.3
  70.9 1.1 copy-done.16
  72.0 1.6 near_2.1
  73.6 1.1 collective-permute-start.12
  75.2 4.4 %collective-permute-done.9.refs_3_ = bf16[6,2,16,256]{3,2,1,0:T(8,128)(2,1)S(1)} collective-permute-done((bf16[6,2,16,256]{3,2,1,0:T(8,128)(2,1)S(1)}, bf16[6,2,16,256]{3,2,1,0:T(8,128)(2,1)S(1)}, u32[]{:S(2)}, u32[]{:S(2)}) %collective-permute-start.9) | collective-permute-done | bytes 98336 | tf_op jit(solution)/shard_map/ppermute | solution.py:19
  79.6 8.8 %collective-permute-done.8.refs_1_ = bf16[1,3,6,2,16,256]{5,4,3,2,1,0:T(8,128)(2,1)S(1)} collective-permute-done((bf16[1,3,6,2,16,256]{5,4,3,2,1,0:T(8,128)(2,1)}, bf16[1,3,6,2,16,256]{5,4,3,2,1,0:T(8,128)(2,1)S(1)}, u32[]{:S(2)}, u32[]{:S(2)}) %collective-permute-start.8) | collective-permute-done | bytes 294944 | tf_op jit(solution)/shard_map/ppermute | solution.py:19
  88.4 1.0 copy-done.20
  89.3 1.0 gate_1.1
  90.4 2.3 %collective-permute-start.13 = (bf16[1,3,6,2,16,256]{5,4,3,2,1,0:T(8,128)(2,1)S(1)}, bf16[1,3,6,2,16,256]{5,4,3,2,1,0:T(8,128)(2,1)S(1)}, u32[]{:S(2)}, u32[]{:S(2)}) collective-permute-start(bf16[1,3,6,2,16,256]{5,4,3,2,1,0:T(8,128)(2,1)S(1)} %get-tuple-element.117.refs_0_), channel_id=1, source_target_pairs={{0,4},{4,0},{8,12},{12,8},{1,5},{5,1},{9,13},{13,9},{2,6},{6,2},{1... | collective-permute-start | bytes 884744 | tf_op jit(solution)/shard_map/ppermute | solution.py:19
  92.7 0.6 proj_3_0.1
  93.4 5.0 %backward_3.1 = (f32[3,6,64,512]{3,2,1,0:T(8,128)}, f32[512,256]{1,0:T(8,128)S(1)}, f32[9,8,512]{2,1,0:T(8,128)S(1)}, f32[8,128]{1,0:T(8,128)S(1)}) custom-call(s32[3]{0:T(128)S(1)} %pad_add_fusion.place_ref, f32[8,128]{1,0:T(8,128)S(1)} %get-tuple-element.109.after_ref, bf16[2,3,6,2,16,256]{5,4,3,2,1,0:T(8,128)(2,1)} %get-tuple-element.110.refs_0_, ...), custom_call_target="tpu_custom_call" | custom-call | flops 1 | bytes 1 | tf_op jit(solution)/shard_map/backward_3/pallas_call | solution.py:79
  98.4 1.0 gate_2.1
  99.4 2.5 %join.1 = (bf16[3,6,64,256]{3,2,1,0:T(8,128)(2,1)S(1)}, f32[512,256]{1,0:T(8,128)S(1)}, f32[8,128]{1,0:T(8,128)S(1)}) custom-call(s32[3]{0:T(128)S(1)} %pad_add_fusion.place_ref, f32[8,128]{1,0:T(8,128)S(1)} %get-tuple-element.115.after_ref, bf16[2,3,6,2,16,256]{5,4,3,2,1,0:T(8,128)(2,1)} %get-tuple-element.110.refs_0_, ...), custom_call_target="tpu_custom_call" | custom-call | flops 1 | bytes 1 | tf_op jit(solution)/shard_map/join/pallas_call | solution.py:79
  102.0 0.8 copy-done.13
  103.0 0.6 collective-permute-start.16
  104.1 6.3 %backward_1.1 = (f32[3,6,64,512]{3,2,1,0:T(8,128)}, f32[512,256]{1,0:T(8,128)S(1)}, f32[9,8,512]{2,1,0:T(8,128)S(1)}, f32[8,128]{1,0:T(8,128)S(1)}) custom-call(s32[3]{0:T(128)S(1)} %pad_add_fusion.place_ref, f32[8,128]{1,0:T(8,128)S(1)} %get-tuple-element.116.after_ref, bf16[1,3,6,2,16,256]{5,4,3,2,1,0:T(8,128)(2,1)S(1)} %get-tuple-element.117.refs_0_, ...), custom_call_target="tpu_custom_call" | custom-call | flops 1 | bytes 1 | tf_op jit(solution)/shard_map/backward_1/pallas_call | solution.py:79
  110.5 1.6 %collective-permute-start.15 = (bf16[256,256]{1,0:T(8,128)(2,1)S(1)}, bf16[256,256]{1,0:T(8,128)(2,1)S(1)}, u32[]{:S(2)}, u32[]{:S(2)}) collective-permute-start(bf16[256,256]{1,0:T(8,128)(2,1)S(1)} %get-tuple-element.122.refs_2_), channel_id=1, source_target_pairs={{0,4},{4,0},{8,12},{12,8},{1,5},{5,1},{9,13},{13,9},{2,6},{6,2},{1... | collective-permute-start | bytes 393224 | tf_op jit(solution)/shard_map/ppermute | solution.py:19
  112.2 4.2 %collective-permute-done.15.refs_3_ = bf16[256,256]{1,0:T(8,128)(2,1)S(1)} collective-permute-done((bf16[256,256]{1,0:T(8,128)(2,1)S(1)}, bf16[256,256]{1,0:T(8,128)(2,1)S(1)}, u32[]{:S(2)}, u32[]{:S(2)}) %collective-permute-start.15) | collective-permute-done | bytes 131104 | tf_op jit(solution)/shard_map/ppermute | solution.py:19
  116.4 1.4 early_y.1
  118.3 1.2 proj_1_2.1
  119.5 0.6 middle_y.1
  120.2 5.0 %backward_2.1 = (bf16[6,64,512]{2,1,0:T(8,128)(2,1)}, f32[2,6,64,512]{3,2,1,0:T(8,128)}, f32[512,256]{1,0:T(8,128)S(1)}, f32[9,8,512]{2,1,0:T(8,128)S(1)}, f32[8,128]{1,0:T(8,128)S(1)}) custom-call(s32[3]{0:T(128)S(1)} %pad_add_fusion.place_ref, f32[8,128]{1,0:T(8,128)S(1)} %get-tuple-element.128.after_ref, ...), custom_call_target="tpu_custom_call" | custom-call | flops 1 | bytes 1 | tf_op jit(solution)/shard_map/backward_2/pallas_call | solution.py:79
  125.5 1.6 %collective-permute-start.21 = (bf16[256,256]{1,0:T(8,128)(2,1)}, bf16[256,256]{1,0:T(8,128)(2,1)S(1)}, u32[]{:S(2)}, u32[]{:S(2)}) collective-permute-start(bf16[256,256]{1,0:T(8,128)(2,1)} %get-tuple-element.139.refs_2_), channel_id=1, source_target_pairs={{0,4},{4,0},{8,12},{12,8},{1,5},{5,1},{9,13},{13,9},{2,6},{6,2},{1... | collective-permute-start | bytes 393224 | tf_op jit(solution)/shard_map/ppermute | solution.py:19
  127.1 1.5 collective-permute-start.23
  128.8 1.7 %early_x.1 = (bf16[768,256]{1,0:T(8,128)(2,1)S(1)}, f32[8,128]{1,0:T(8,128)S(1)}) custom-call(s32[3]{0:T(128)S(1)} %pad_add_fusion.place_ref, f32[8,128]{1,0:T(8,128)S(1)} %get-tuple-element.132.after_ref, bf16[768,256]{1,0:T(8,128)(2,1)} %get-tuple-element.133.refs_0_, bf16[768,256]{1,0:T(8,128)(2,1)} %collective-permute-done.19.refs_1_), custom_call_target="tpu_custom_call" | custom-call | flops 1 | bytes 1 | tf_op jit(solution)/shard_map/early_x/pallas_call | solution.py:79
  130.5 1.5 collective-permute-start.26
  132.1 1.5 late_x.1
  133.6 1.1 collective-permute-start.25
  134.7 1.5 collective-permute-start.22
  136.7 5.1 %collective-permute-done.22.refs_1_ = bf16[256,256]{1,0:T(8,128)(2,1)S(1)} collective-permute-done((bf16[256,256]{1,0:T(8,128)(2,1)S(1)}, bf16[256,256]{1,0:T(8,128)(2,1)S(1)}, u32[]{:S(2)}, u32[]{:S(2)}) %collective-permute-start.22) | collective-permute-done | bytes 131104 | tf_op jit(solution)/shard_map/ppermute | solution.py:19
  141.9 0.6 middle_x.1
  142.5 3.9 %last.1 = (bf16[3,6,64,512]{3,2,1,0:T(8,128)(2,1)}, bf16[3,6,16,256]{3,2,1,0:T(8,128)(2,1)}, f32[8,128]{1,0:T(8,128)S(1)}) custom-call(s32[3]{0:T(128)S(1)} %pad_add_fusion.place_ref, f32[8,128]{1,0:T(8,128)S(1)} %get-tuple-element.142.after_ref, bf16[3,6,64,256]{3,2,1,0:T(8,128)(2,1)S(1)} %copy-done.14, bf16[4,512,256]{2,1,0:T(8,128)(2,1)S(1)} %copy-done.1, ...), custom_call_target="tpu_custom_call" | custom-call | flops 1 | bytes 1 | tf_op jit(solution)/shard_map/last/pallas_call | solution.py:79
  146.4 1.0 collective-permute-done.25.refs_1_
  147.3 0.6 late_y.1
  148.0 0.6 collective-permute-start.28
  148.6 0.6 early.1
  149.3 1.5 collective-permute-start.27
  150.9 4.4 %collective-permute-done.27.refs_1_ = bf16[256,256]{1,0:T(8,128)(2,1)S(1)} collective-permute-done((bf16[256,256]{1,0:T(8,128)(2,1)S(1)}, bf16[256,256]{1,0:T(8,128)(2,1)S(1)}, u32[]{:S(2)}, u32[]{:S(2)}) %collective-permute-start.27) | collective-permute-done | bytes 131104 | tf_op jit(solution)/shard_map/ppermute | solution.py:19
  155.2 0.6 middle.1
  155.8 0.6 late.1
  157.0 1.8 %collective-permute-done.30.refs_3_ = f32[256,256]{1,0:T(8,128)S(1)} collective-permute-done((f32[256,256]{1,0:T(8,128)S(1)}, f32[256,256]{1,0:T(8,128)S(1)}, u32[]{:S(2)}, u32[]{:S(2)}) %collective-permute-start.30) | collective-permute-done | bytes 262176 | tf_op jit(solution)/shard_map/ppermute | solution.py:19
  158.9 2.4 %finish.1 = (f32[4,256,256]{2,1,0:T(8,128)}, f32[64,256]{1,0:T(8,128)S(1)}, f32[4,512,256]{2,1,0:T(8,128)}, f32[8,128]{1,0:T(8,128)}) custom-call(s32[3]{0:T(128)S(1)} %pad_add_fusion.place_ref, f32[8,128]{1,0:T(8,128)S(1)} %get-tuple-element.160.after_ref, f32[768,256]{1,0:T(8,128)S(1)} %get-tuple-element.161.refs_0_, ...), custom_call_target="tpu_custom_call" | custom-call | flops 1 | bytes 1 | tf_op jit(solution)/shard_map/finish/pallas_call | solution.py:79
  161.3 0.7 reshape.41
  (94 shorter events, 4.4 us)
Async XLA Ops:
  0.7 0.8 copy-start.11
  1.5 9.4 %copy-start.21 = (bf16[1,18,16,256]{3,2,1,0:T(8,128)(2,1)S(1)}, bf16[1,18,16,256]{3,2,1,0:T(8,128)(2,1)}, u32[]{:S(2)}) copy-start(bf16[1,18,16,256]{3,2,1,0:T(8,128)(2,1)} %param.9) | copy-start | bytes 442372
  1.5 26.1 %copy-start.1 = (bf16[4,512,256]{2,1,0:T(8,128)(2,1)S(1)}, bf16[4,512,256]{2,1,0:T(8,128)(2,1)}, u32[]{:S(2)}) copy-start(bf16[4,512,256]{2,1,0:T(8,128)(2,1)} %refs_1_.1) | copy-start | bytes 3145732
  5.9 21.7 %copy-start = (bf16[1,18,64,512]{3,2,1,0:T(8,128)(2,1)S(1)}, bf16[1,18,64,512]{3,2,1,0:T(8,128)(2,1)}, u32[]{:S(2)}) copy-start(bf16[1,18,64,512]{3,2,1,0:T(8,128)(2,1)} %param.5) | copy-start | bytes 3538948
  5.9 21.7 %copy-start.12 = (bf16[3,3,3,512]{3,2,1,0:T(4,128)(2,1)S(1)}, bf16[3,3,3,512]{3,2,1,0:T(4,128)(2,1)}, u32[]{:S(2)}) copy-start(bf16[3,3,3,512]{3,2,1,0:T(4,128)(2,1)} %refs_5_.7) | copy-start | bytes 82948
  5.9 21.7 %collective-permute-start.3 = (bf16[6,64,512]{2,1,0:T(8,128)(2,1)S(1)}, bf16[6,64,512]{2,1,0:T(8,128)(2,1)S(1)}, u32[]{:S(2)}, u32[]{:S(2)}) collective-permute-start(bf16[6,64,512]{2,1,0:T(8,128)(2,1)S(1)} %get-tuple-element.93), channel_id=1, source_target_pairs={{0,16},{16,0},{1,17},{17,1},{2,18},{18,2},{3,19},{19,3},{4,20},{20... | collective-permute-start | bytes 1179656 | tf_op jit(solution)/shard_map/ppermute | solution.py:19
  8.9 17.0 %collective-permute-start = (bf16[1,3,6,2,16,256]{5,4,3,2,1,0:T(8,128)(2,1)S(1)}, bf16[1,3,6,2,16,256]{5,4,3,2,1,0:T(8,128)(2,1)S(1)}, u32[]{:S(2)}, u32[]{:S(2)}) collective-permute-start(bf16[1,3,6,2,16,256]{5,4,3,2,1,0:T(8,128)(2,1)S(1)} %get-tuple-element.88), channel_id=1, source_target_pairs={{0,4},{4,0},{8,12},{12,8},{1,5},{5,1},{9,13},{13,9},{2,6},{6,2},{1... | collective-permute-start | bytes 884744 | tf_op jit(solution)/shard_map/ppermute | solution.py:19
  10.5 16.4 %collective-permute-start.2 = (bf16[1,3,6,2,16,256]{5,4,3,2,1,0:T(8,128)(2,1)S(1)}, bf16[1,3,6,2,16,256]{5,4,3,2,1,0:T(8,128)(2,1)S(1)}, u32[]{:S(2)}, u32[]{:S(2)}) collective-permute-start(bf16[1,3,6,2,16,256]{5,4,3,2,1,0:T(8,128)(2,1)S(1)} %get-tuple-element.91), channel_id=1, source_target_pairs={{0,4},{4,0},{8,12},{12,8},{1,5},{5,1},{9,13},{13,9},{2,6},{6,2},{1... | collective-permute-start | bytes 884744 | tf_op jit(solution)/shard_map/ppermute | solution.py:19
  10.9 15.0 %collective-permute-start.1 = (bf16[18,16,256]{2,1,0:T(8,128)(2,1)S(1)}, bf16[18,16,256]{2,1,0:T(8,128)(2,1)S(1)}, u32[]{:S(2)}, u32[]{:S(2)}) collective-permute-start(bf16[18,16,256]{2,1,0:T(8,128)(2,1)S(1)} %bitcast.43), channel_id=1, source_target_pairs={{0,8},{4,12},{8,0},{12,4},{1,9},{5,13},{9,1},{13,5},{2,10},{6,14},... | collective-permute-start | bytes 442376 | tf_op jit(solution)/shard_map/ppermute | solution.py:19
  26.6 1.0 copy-start.24
  26.6 37.7 %copy-start.3 = (bf16[18,2,16,256]{3,2,1,0:T(8,128)(2,1)}, bf16[18,2,16,256]{3,2,1,0:T(8,128)(2,1)S(1)}, u32[]{:S(2)}) copy-start(bf16[18,2,16,256]{3,2,1,0:T(8,128)(2,1)S(1)} %get-tuple-element.100.refs_4_.refs_2_) | copy-start | bytes 884740
  32.9 0.8 copy-start.15
  33.8 30.5 %copy-start.2 = (bf16[4,256,256]{2,1,0:T(8,128)(2,1)S(1)}, bf16[4,256,256]{2,1,0:T(8,128)(2,1)}, u32[]{:S(2)}) copy-start(bf16[4,256,256]{2,1,0:T(8,128)(2,1)} %refs_4_.7) | copy-start | bytes 1572868
  33.8 16.3 %collective-permute-start.4 = (bf16[1,3,6,2,16,256]{5,4,3,2,1,0:T(8,128)(2,1)S(1)}, bf16[1,3,6,2,16,256]{5,4,3,2,1,0:T(8,128)(2,1)S(1)}, u32[]{:S(2)}, u32[]{:S(2)}) collective-permute-start(bf16[1,3,6,2,16,256]{5,4,3,2,1,0:T(8,128)(2,1)S(1)} %get-tuple-element.96), channel_id=1, source_target_pairs={{0,4},{4,0},{8,12},{12,8},{1,5},{5,1},{9,13},{13,9},{2,6},{6,2},{1... | collective-permute-start | bytes 884744 | tf_op jit(solution)/shard_map/ppermute | solution.py:19
  37.1 23.5 %collective-permute-start.5 = (bf16[1,3,6,2,16,256]{5,4,3,2,1,0:T(8,128)(2,1)S(1)}, bf16[1,3,6,2,16,256]{5,4,3,2,1,0:T(8,128)(2,1)S(1)}, u32[]{:S(2)}, u32[]{:S(2)}) collective-permute-start(bf16[1,3,6,2,16,256]{5,4,3,2,1,0:T(8,128)(2,1)S(1)} %get-tuple-element.98.refs_0_), channel_id=1, source_target_pairs={{0,8},{4,12},{8,0},{12,4},{1,9},{5,13},{9,1},{13,5},{2,10},{6,14},... | collective-permute-start | bytes 884744 | tf_op jit(solution)/shard_map/ppermute | solution.py:19
  37.9 26.3 %collective-permute-start.6 = (bf16[1,3,6,2,16,256]{5,4,3,2,1,0:T(8,128)(2,1)S(1)}, bf16[1,3,6,2,16,256]{5,4,3,2,1,0:T(8,128)(2,1)S(1)}, u32[]{:S(2)}, u32[]{:S(2)}) collective-permute-start(bf16[1,3,6,2,16,256]{5,4,3,2,1,0:T(8,128)(2,1)S(1)} %get-tuple-element.99.refs_1_), channel_id=1, source_target_pairs={{0,8},{4,12},{8,0},{12,4},{1,9},{5,13},{9,1},{13,5},{2,10},{6,14},... | collective-permute-start | bytes 884744 | tf_op jit(solution)/shard_map/ppermute | solution.py:19
  40.0 30.9 %collective-permute-start.7 = (bf16[1,3,6,2,16,256]{5,4,3,2,1,0:T(8,128)(2,1)}, bf16[1,3,6,2,16,256]{5,4,3,2,1,0:T(8,128)(2,1)}, u32[]{:S(2)}, u32[]{:S(2)}) collective-permute-start(bf16[1,3,6,2,16,256]{5,4,3,2,1,0:T(8,128)(2,1)} %get-tuple-element.103), channel_id=1, source_target_pairs={{0,4},{4,0},{8,12},{12,8},{1,5},{5,1},{9,13},{13,9},{2,6},{6,2},{1... | collective-permute-start | bytes 884744 | tf_op jit(solution)/shard_map/ppermute | solution.py:19
  50.8 13.4 %copy-start.19 = (bf16[1,3,6,2,16,256]{5,4,3,2,1,0:T(8,128)(2,1)}, bf16[1,3,6,2,16,256]{5,4,3,2,1,0:T(8,128)(2,1)S(1)}, u32[]{:S(2)}) copy-start(bf16[1,3,6,2,16,256]{5,4,3,2,1,0:T(8,128)(2,1)S(1)} %get-tuple-element.105.refs_0_) | copy-start | bytes 884740
  66.4 0.8 copy-start.6
  67.2 0.7 copy-start.17
  67.9 25.4 %collective-permute-start.11 = (bf16[2,3,6,2,16,256]{5,4,3,2,1,0:T(8,128)(2,1)}, bf16[2,3,6,2,16,256]{5,4,3,2,1,0:T(8,128)(2,1)}, u32[]{:S(2)}, u32[]{:S(2)}) collective-permute-start(bf16[2,3,6,2,16,256]{5,4,3,2,1,0:T(8,128)(2,1)} %get-tuple-element.110.refs_0_), channel_id=1, source_target_pairs={{0,4},{4,0},{8,12},{12,8},{1,5},{5,1},{9,13},{13,9},{2,6},{6,2},{1... | collective-permute-start | bytes 1769480 | tf_op jit(solution)/shard_map/ppermute | solution.py:19
  67.9 6.8 %copy-start.25 = (bf16[6,2,16,256]{3,2,1,0:T(8,128)(2,1)S(1)}, bf16[6,2,16,256]{3,2,1,0:T(8,128)(2,1)}, u32[]{:S(2)}) copy-start(bf16[6,2,16,256]{3,2,1,0:T(8,128)(2,1)} %copy-done.24) | copy-start | bytes 294916
  67.9 20.5 %copy-start.4 = (bf16[18,2,16,256]{3,2,1,0:T(8,128)(2,1)S(1)}, bf16[18,2,16,256]{3,2,1,0:T(8,128)(2,1)}, u32[]{:S(2)}) copy-start(bf16[18,2,16,256]{3,2,1,0:T(8,128)(2,1)} %copy-done.3) | copy-start | bytes 884740
  67.9 20.5 %collective-permute-start.8 = (bf16[1,3,6,2,16,256]{5,4,3,2,1,0:T(8,128)(2,1)}, bf16[1,3,6,2,16,256]{5,4,3,2,1,0:T(8,128)(2,1)S(1)}, u32[]{:S(2)}, u32[]{:S(2)}) collective-permute-start(bf16[1,3,6,2,16,256]{5,4,3,2,1,0:T(8,128)(2,1)} %copy-done.19), channel_id=1, source_target_pairs={{0,8},{4,12},{8,0},{12,4},{1,9},{5,13},{9,1},{13,5},{2,10},{6,14},... | collective-permute-start | bytes 884744 | tf_op jit(solution)/shard_map/ppermute | solution.py:19
  70.8 21.9 %collective-permute-start.10 = (f32[256,256]{1,0:T(8,128)S(1)}, f32[256,256]{1,0:T(8,128)S(1)}, u32[]{:S(2)}, u32[]{:S(2)}) collective-permute-start(f32[256,256]{1,0:T(8,128)S(1)} %dynamic-slice_bitcast_fusion.3), channel_id=1, source_target_pairs={{0,1},{1,0},{2,3},{3,2},{4,5},{5,4},{6,7},{7,6},{8,9},{9,8},{10,11... | collective-permute-start | bytes 786440 | tf_op jit(solution)/shard_map/ppermute | solution.py:19
  70.9 1.1 copy-start.16
  72.0 20.8 %copy-start.7 = (f32[2,256,256]{2,1,0:T(8,128)S(1)}, f32[2,256,256]{2,1,0:T(8,128)}, u32[]{:S(2)}) copy-start(f32[2,256,256]{2,1,0:T(8,128)} %copy-done.6) | copy-start | bytes 1572868
  73.6 24.8 %collective-permute-start.12 = (bf16[1,3,6,2,16,256]{5,4,3,2,1,0:T(8,128)(2,1)S(1)}, bf16[1,3,6,2,16,256]{5,4,3,2,1,0:T(8,128)(2,1)S(1)}, u32[]{:S(2)}, u32[]{:S(2)}) collective-permute-start(bf16[1,3,6,2,16,256]{5,4,3,2,1,0:T(8,128)(2,1)S(1)} %get-tuple-element.113.refs_0_), channel_id=1, source_target_pairs={{0,8},{4,12},{8,0},{12,4},{1,9},{5,13},{9,1},{13,5},{2,10},{6,14},... | collective-permute-start | bytes 884744 | tf_op jit(solution)/shard_map/ppermute | solution.py:19
  74.7 4.9 %collective-permute-start.9 = (bf16[6,2,16,256]{3,2,1,0:T(8,128)(2,1)S(1)}, bf16[6,2,16,256]{3,2,1,0:T(8,128)(2,1)S(1)}, u32[]{:S(2)}, u32[]{:S(2)}) collective-permute-start(bf16[6,2,16,256]{3,2,1,0:T(8,128)(2,1)S(1)} %copy-done.25), channel_id=1, source_target_pairs={{0,16},{16,0},{1,17},{17,1},{2,18},{18,2},{3,19},{19,3},{4,20},{20... | collective-permute-start | bytes 294920 | tf_op jit(solution)/shard_map/ppermute | solution.py:19
  88.4 1.0 copy-start.20
  89.3 4.0 %copy-start.9 = (bf16[3,6,64,512]{3,2,1,0:T(8,128)(2,1)S(1)}, bf16[3,6,64,512]{3,2,1,0:T(8,128)(2,1)}, u32[]{:S(2)}) copy-start(bf16[3,6,64,512]{3,2,1,0:T(8,128)(2,1)} %get-tuple-element.111.refs_4_) | copy-start | bytes 3538948
  90.4 13.2 %collective-permute-start.13 = (bf16[1,3,6,2,16,256]{5,4,3,2,1,0:T(8,128)(2,1)S(1)}, bf16[1,3,6,2,16,256]{5,4,3,2,1,0:T(8,128)(2,1)S(1)}, u32[]{:S(2)}, u32[]{:S(2)}) collective-permute-start(bf16[1,3,6,2,16,256]{5,4,3,2,1,0:T(8,128)(2,1)S(1)} %get-tuple-element.117.refs_0_), channel_id=1, source_target_pairs={{0,4},{4,0},{8,12},{12,8},{1,5},{5,1},{9,13},{13,9},{2,6},{6,2},{1... | collective-permute-start | bytes 884744 | tf_op jit(solution)/shard_map/ppermute | solution.py:19
  102.0 0.8 copy-start.13
  102.8 1.3 copy-start.10
  102.9 13.5 %collective-permute-start.14 = (f32[512,256]{1,0:T(8,128)S(1)}, f32[512,256]{1,0:T(8,128)S(1)}, u32[]{:S(2)}, u32[]{:S(2)}) collective-permute-start(f32[512,256]{1,0:T(8,128)S(1)} %fusion.1), channel_id=1, source_target_pairs={{0,1},{1,0},{2,3},{3,2},{4,5},{5,4},{6,7},{7,6},{8,9},{9,8},{10,11... | collective-permute-start | bytes 1572872 | tf_op jit(solution)/shard_map/ppermute | solution.py:19
  103.0 15.3 %collective-permute-start.16 = (f32[256,256]{1,0:T(8,128)S(1)}, f32[256,256]{1,0:T(8,128)S(1)}, u32[]{:S(2)}, u32[]{:S(2)}) collective-permute-start(f32[256,256]{1,0:T(8,128)S(1)} %dynamic-slice_bitcast_fusion.2), channel_id=1, source_target_pairs={{0,1},{1,0},{2,3},{3,2},{4,5},{5,4},{6,7},{7,6},{8,9},{9,8},{10,11... | collective-permute-start | bytes 786440 | tf_op jit(solution)/shard_map/ppermute | solution.py:19
  103.6 16.5 %collective-permute-start.18 = (bf16[1,3,6,2,16,256]{5,4,3,2,1,0:T(8,128)(2,1)S(1)}, bf16[1,3,6,2,16,256]{5,4,3,2,1,0:T(8,128)(2,1)S(1)}, u32[]{:S(2)}, u32[]{:S(2)}) collective-permute-start(bf16[1,3,6,2,16,256]{5,4,3,2,1,0:T(8,128)(2,1)S(1)} %get-tuple-element.129.refs_0_), channel_id=1, source_target_pairs={{0,4},{4,0},{8,12},{12,8},{1,5},{5,1},{9,13},{13,9},{2,6},{6,2},{1... | collective-permute-start | bytes 884744 | tf_op jit(solution)/shard_map/ppermute | solution.py:19
  110.4 9.2 %collective-permute-start.17 = (f32[256,256]{1,0:T(8,128)S(1)}, f32[256,256]{1,0:T(8,128)S(1)}, u32[]{:S(2)}, u32[]{:S(2)}) collective-permute-start(f32[256,256]{1,0:T(8,128)S(1)} %dynamic-slice_bitcast_fusion.1), channel_id=1, source_target_pairs={{0,1},{1,0},{2,3},{3,2},{4,5},{5,4},{6,7},{7,6},{8,9},{9,8},{10,11... | collective-permute-start | bytes 786440 | tf_op jit(solution)/shard_map/ppermute | solution.py:19
  110.5 5.9 %collective-permute-start.15 = (bf16[256,256]{1,0:T(8,128)(2,1)S(1)}, bf16[256,256]{1,0:T(8,128)(2,1)S(1)}, u32[]{:S(2)}, u32[]{:S(2)}) collective-permute-start(bf16[256,256]{1,0:T(8,128)(2,1)S(1)} %get-tuple-element.122.refs_2_), channel_id=1, source_target_pairs={{0,4},{4,0},{8,12},{12,8},{1,5},{5,1},{9,13},{13,9},{2,6},{6,2},{1... | collective-permute-start | bytes 393224 | tf_op jit(solution)/shard_map/ppermute | solution.py:19
  112.1 8.1 %copy-start.8 = (bf16[3,6,64,512]{3,2,1,0:T(8,128)(2,1)S(1)}, bf16[3,6,64,512]{3,2,1,0:T(8,128)(2,1)}, u32[]{:S(2)}) copy-start(bf16[3,6,64,512]{3,2,1,0:T(8,128)(2,1)} %get-tuple-element.130.refs_4_) | copy-start | bytes 3538948
  116.4 3.8 %copy-start.5 = (f32[3,6,64,512]{3,2,1,0:T(8,128)S(1)}, f32[3,6,64,512]{3,2,1,0:T(8,128)}, u32[]{:S(2)}) copy-start(f32[3,6,64,512]{3,2,1,0:T(8,128)} %get-tuple-element.131.refs_7_) | copy-start | bytes 7077892
  117.8 11.0 %collective-permute-start.19 = (bf16[768,256]{1,0:T(8,128)(2,1)}, bf16[768,256]{1,0:T(8,128)(2,1)}, u32[]{:S(2)}, u32[]{:S(2)}) collective-permute-start(bf16[768,256]{1,0:T(8,128)(2,1)} %get-tuple-element.133.refs_0_), channel_id=1, source_target_pairs={{0,16},{16,0},{1,17},{17,1},{2,18},{18,2},{3,19},{19,3},{4,20},{20... | collective-permute-start | bytes 1179656 | tf_op jit(solution)/shard_map/ppermute | solution.py:19
  120.1 5.0 %copy-start.22 = (bf16[256,256]{1,0:T(8,128)(2,1)}, bf16[256,256]{1,0:T(8,128)(2,1)S(1)}, u32[]{:S(2)}) copy-start(bf16[256,256]{1,0:T(8,128)(2,1)S(1)} %get-tuple-element.141.refs_0_) | copy-start | bytes 393220
  125.3 9.4 %copy-start.23 = (bf16[256,256]{1,0:T(8,128)(2,1)S(1)}, bf16[256,256]{1,0:T(8,128)(2,1)}, u32[]{:S(2)}) copy-start(bf16[256,256]{1,0:T(8,128)(2,1)} %copy-done.22) | copy-start | bytes 393220
  125.4 17.1 %copy-start.14 = (bf16[3,6,64,256]{3,2,1,0:T(8,128)(2,1)S(1)}, bf16[3,6,64,256]{3,2,1,0:T(8,128)(2,1)}, u32[]{:S(2)}) copy-start(bf16[3,6,64,256]{3,2,1,0:T(8,128)(2,1)} %copy-done.13) | copy-start | bytes 1769476
  125.4 17.1 %copy-start.18 = (f32[18,16,256]{2,1,0:T(8,128)S(1)}, f32[18,16,256]{2,1,0:T(8,128)}, u32[]{:S(2)}) copy-start(f32[18,16,256]{2,1,0:T(8,128)} %copy-done.17) | copy-start | bytes 884740
  125.4 6.7 %collective-permute-start.20 = (f32[288,256]{1,0:T(8,128)S(1)}, f32[288,256]{1,0:T(8,128)S(1)}, u32[]{:S(2)}, u32[]{:S(2)}) collective-permute-start(f32[288,256]{1,0:T(8,128)S(1)} %dynamic-slice_bitcast_fusion), channel_id=1, source_target_pairs={{0,1},{1,0},{2,3},{3,2},{4,5},{5,4},{6,7},{7,6},{8,9},{9,8},{10,11... | collective-permute-start | bytes 884744 | tf_op jit(solution)/shard_map/ppermute | solution.py:19
  125.5 6.6 %collective-permute-start.21 = (bf16[256,256]{1,0:T(8,128)(2,1)}, bf16[256,256]{1,0:T(8,128)(2,1)S(1)}, u32[]{:S(2)}, u32[]{:S(2)}) collective-permute-start(bf16[256,256]{1,0:T(8,128)(2,1)} %get-tuple-element.139.refs_2_), channel_id=1, source_target_pairs={{0,4},{4,0},{8,12},{12,8},{1,5},{5,1},{9,13},{13,9},{2,6},{6,2},{1... | collective-permute-start | bytes 393224 | tf_op jit(solution)/shard_map/ppermute | solution.py:19
  127.1 15.3 %collective-permute-start.23 = (bf16[6,64,512]{2,1,0:T(8,128)(2,1)}, bf16[6,64,512]{2,1,0:T(8,128)(2,1)S(1)}, u32[]{:S(2)}, u32[]{:S(2)}) collective-permute-start(bf16[6,64,512]{2,1,0:T(8,128)(2,1)} %get-tuple-element.146), channel_id=1, source_target_pairs={{0,16},{16,0},{1,17},{17,1},{2,18},{18,2},{3,19},{19,3},{4,20},{20... | collective-permute-start | bytes 1179656 | tf_op jit(solution)/shard_map/ppermute | solution.py:19
  130.5 18.0 %collective-permute-start.26 = (bf16[768,256]{1,0:T(8,128)(2,1)S(1)}, bf16[768,256]{1,0:T(8,128)(2,1)S(1)}, u32[]{:S(2)}, u32[]{:S(2)}) collective-permute-start(bf16[768,256]{1,0:T(8,128)(2,1)S(1)} %get-tuple-element.155.refs_0_), channel_id=1, source_target_pairs={{0,2},{1,3},{2,0},{3,1},{4,6},{5,7},{6,4},{7,5},{8,10},{9,11},{10,... | collective-permute-start | bytes 1179656 | tf_op jit(solution)/shard_map/ppermute | solution.py:19
  133.6 13.7 %collective-permute-start.25 = (bf16[544,256]{1,0:T(8,128)(2,1)S(1)}, bf16[544,256]{1,0:T(8,128)(2,1)S(1)}, u32[]{:S(2)}, u32[]{:S(2)}) collective-permute-start(bf16[544,256]{1,0:T(8,128)(2,1)S(1)} %get-tuple-element.153.refs_0_), channel_id=1, source_target_pairs={{0,2},{1,3},{2,0},{3,1},{4,6},{5,7},{6,4},{7,5},{8,10},{9,11},{10,... | collective-permute-start | bytes 835592 | tf_op jit(solution)/shard_map/ppermute | solution.py:19
  134.7 7.1 %collective-permute-start.22 = (bf16[256,256]{1,0:T(8,128)(2,1)S(1)}, bf16[256,256]{1,0:T(8,128)(2,1)S(1)}, u32[]{:S(2)}, u32[]{:S(2)}) collective-permute-start(bf16[256,256]{1,0:T(8,128)(2,1)S(1)} %copy-done.23), channel_id=1, source_target_pairs={{0,16},{16,0},{1,17},{17,1},{2,18},{18,2},{3,19},{19,3},{4,20},{20... | collective-permute-start | bytes 393224 | tf_op jit(solution)/shard_map/ppermute | solution.py:19
  136.2 6.2 %collective-permute-start.24 = (bf16[6,16,256]{2,1,0:T(8,128)(2,1)S(1)}, bf16[6,16,256]{2,1,0:T(8,128)(2,1)S(1)}, u32[]{:S(2)}, u32[]{:S(2)}) collective-permute-start(bf16[6,16,256]{2,1,0:T(8,128)(2,1)S(1)} %get-tuple-element.149), channel_id=1, source_target_pairs={{0,16},{16,0},{1,17},{17,1},{2,18},{18,2},{3,19},{19,3},{4,20},{20... | collective-permute-start | bytes 147464 | tf_op jit(solution)/shard_map/ppermute | solution.py:19
  148.0 7.9 %collective-permute-start.28 = (bf16[544,256]{1,0:T(8,128)(2,1)S(1)}, bf16[544,256]{1,0:T(8,128)(2,1)S(1)}, u32[]{:S(2)}, u32[]{:S(2)}) collective-permute-start(bf16[544,256]{1,0:T(8,128)(2,1)S(1)} %get-tuple-element.159.refs_0_), channel_id=1, source_target_pairs={{0,16},{16,0},{1,17},{17,1},{2,18},{18,2},{3,19},{19,3},{4,20},{20... | collective-permute-start | bytes 835592 | tf_op jit(solution)/shard_map/ppermute | solution.py:19
  149.2 9.6 %collective-permute-start.29 = (f32[768,256]{1,0:T(8,128)S(1)}, f32[768,256]{1,0:T(8,128)S(1)}, u32[]{:S(2)}, u32[]{:S(2)}) collective-permute-start(f32[768,256]{1,0:T(8,128)S(1)} %get-tuple-element.161.refs_0_), channel_id=1, source_target_pairs={{0,1},{1,0},{2,3},{3,2},{4,5},{5,4},{6,7},{7,6},{8,9},{9,8},{10,11... | collective-permute-start | bytes 2359304 | tf_op jit(solution)/shard_map/ppermute | solution.py:19
  149.3 5.9 %collective-permute-start.27 = (bf16[256,256]{1,0:T(8,128)(2,1)S(1)}, bf16[256,256]{1,0:T(8,128)(2,1)S(1)}, u32[]{:S(2)}, u32[]{:S(2)}) collective-permute-start(bf16[256,256]{1,0:T(8,128)(2,1)S(1)} %get-tuple-element.157.refs_0_), channel_id=1, source_target_pairs={{0,2},{1,3},{2,0},{3,1},{4,6},{5,7},{6,4},{7,5},{8,10},{9,11},{10,... | collective-permute-start | bytes 393224 | tf_op jit(solution)/shard_map/ppermute | solution.py:19
  156.4 2.4 %collective-permute-start.31 = (f32[544,256]{1,0:T(8,128)S(1)}, f32[544,256]{1,0:T(8,128)S(1)}, u32[]{:S(2)}, u32[]{:S(2)}) collective-permute-start(f32[544,256]{1,0:T(8,128)S(1)} %get-tuple-element.163.refs_4_), channel_id=1, source_target_pairs={{0,1},{1,0},{2,3},{3,2},{4,5},{5,4},{6,7},{7,6},{8,9},{9,8},{10,11... | collective-permute-start | bytes 1671176 | tf_op jit(solution)/shard_map/ppermute | solution.py:19
  156.5 2.3 %collective-permute-start.30 = (f32[256,256]{1,0:T(8,128)S(1)}, f32[256,256]{1,0:T(8,128)S(1)}, u32[]{:S(2)}, u32[]{:S(2)}) collective-permute-start(f32[256,256]{1,0:T(8,128)S(1)} %get-tuple-element.162.refs_2_), channel_id=1, source_target_pairs={{0,1},{1,0},{2,3},{3,2},{4,5},{5,4},{6,7},{7,6},{8,9},{9,8},{10,11... | collective-permute-start | bytes 786440 | tf_op jit(solution)/shard_map/ppermute | solution.py:19

commit v3 on v2

--- a/solution.py
+++ b/solution.py
@@ -157,22 +157,19 @@
     )
 
 
-def near_kernel(place, keep_ref, arrived_ref, *near_refs):
-    for k, near_ref in enumerate(near_refs):
-        near_ref[0] = (keep_ref[k] + arrived_ref[k].astype(F32)).astype(BF16)
+def near_kernel(place, keep_ref, arrived_ref, near_ref):
+    near_ref[...] = (keep_ref[...] + arrived_ref[...].astype(F32)).astype(BF16)
 
 
 def near_sum(name, place, after, keep, arrived):
-    block = keep.shape[:2] + (keep.shape[2] // STEPS,) + keep.shape[3:]
-    out = (1,) + block[1:]
     return call(
-        near_kernel, place, STEPS, after, [(keep, block, 2), (arrived, block, 2)],
-        [(shape_of((1,) + keep.shape[1:], BF16), out, 2)] * keep.shape[0], f"near_{name}",
-    )
-
-
-def first_near_kernel(place, keep_ref, arrived_ref, cot_ref, far_ref, near_ref, cots_ref, leaving_ref):
-    near_ref[...] = (keep_ref[...] + arrived_ref[...].astype(F32)).astype(BF16)
+        near_kernel, place, 1, after, [(keep, keep.shape, None), (arrived, keep.shape, None)],
+        [(shape_of(keep.shape, BF16), keep.shape, None)], f"near_{name}",
+    )
+
+
+def near_cots_kernel(place, keep_ref, arrived_ref, cot_ref, far_ref, near_ref, cots_ref, leaving_ref):
+    near_kernel(place, keep_ref, arrived_ref, near_ref)
     low_side = place[0] // 2 == 0
     cots_ref[:, 0] = jnp.where(low_side, cot_ref[...], far_ref[...])
     cots_ref[:, 1] = jnp.where(low_side, far_ref[...], cot_ref[...])
@@ -180,24 +177,30 @@
     leaving_ref[...] = cots_ref[n : 2 * n]
 
 
-def first_near_sum(place, after, keep, arrived, cot, far):
+def near_sum_cots(name, place, after, keep, arrived, cot, far):
     rows, width, filters = cot.shape
     cots = (rows, 2, width, filters)
     leaving = (rows // 3, 2, width, filters)
     return call(
-        first_near_kernel, place, 1, after,
+        near_cots_kernel, place, 1, after,
         [(a, a.shape, None) for a in (keep, arrived, cot, far)],
-        [(shape_of(s, BF16), s, None) for s in (keep.shape, cots, leaving)], "near_first",
-    )
-
-
-def gate_kernel(branches, folded, place, *refs):
-    count = len(branches)
-    nears, fars, cot_ref, refs = refs[:count], refs[count : 2 * count], refs[2 * count], refs[2 * count + 1 :]
-    _, classes, residues, sides, width, filters = nears[0].shape
+        [(shape_of(s, BF16), s, None) for s in (keep.shape, cots, leaving)], f"near_{name}",
+    )
+
+
+def gate_kernel(branch, folded, stacked, place, near_ref, far_ref, cot_ref, *refs):
+    _, classes, residues, sides, width, filters = near_ref.shape
     if folded:
         arrived_ref, refs = refs[0], refs[1:]
-    projs, (mixed_ref, grad_ref, out_ref, proj_grad_ref, *leaving) = refs[:count], refs[count:]
+    paired = len(refs) > 5
+    if paired:
+        proj_ref, mixed_ref, earlier_ref, *refs = refs
+        above = []
+        if stacked:
+            above, refs = refs[:2], refs[2:]
+        grad_ref, out_ref, keep_ref, send_ref, *leaving = refs
+    else:
+        proj_ref, mixed_ref, grad_ref, out_ref, proj_grad_ref = refs
     n = residues
     cots = cot_ref[...]
     if folded:
@@ -206,42 +209,47 @@
         )
     cells = cots.reshape(-1, filters)
     shape = (classes * residues, sides, width, filters)
-    mixed = mixed_ref[...]
-    for k in range(count):
-        proj = projs[k][0]
-        act_grad = lax.dot_general(cells, proj, (((1,), (1,)), ((), ())), preferred_element_type=F32)
-        preact = (nears[k][0].astype(F32) + fars[k][0].astype(F32)).reshape(shape)
-        logistic = 1.0 / (1.0 + jnp.exp(-preact))
-        grad = act_grad.reshape(shape) * logistic * (1.0 + preact * (1.0 - logistic))
-        grad_ref[k] = grad.astype(BF16).reshape(grad_ref.shape[1:])
-        active = (preact * logistic).astype(BF16)
-        mine = jnp.where(place[0] // 2 == 0, active[:, 0], active[:, 1]).reshape(-1, filters)
-        mixed = mixed + jnp.dot(mine, proj, preferred_element_type=F32).reshape(mixed.shape)
-        proj_grad_ref[k] = lax.dot_general(
-            active.reshape(-1, filters), cells, (((0,), (0,)), ((), ())), preferred_element_type=F32
-        )
+    proj = proj_ref[0]
+    act_grad = lax.dot_general(cells, proj, (((1,), (1,)), ((), ())), preferred_element_type=F32)
+    preact = (near_ref[0].astype(F32) + far_ref[0].astype(F32)).reshape(shape)
+    logistic = 1.0 / (1.0 + jnp.exp(-preact))
+    grad = act_grad.reshape(shape) * logistic * (1.0 + preact * (1.0 - logistic))
+    grad_ref[0] = grad.astype(BF16).reshape(grad_ref.shape[1:])
+    active = (preact * logistic).astype(BF16)
+    mine = jnp.where(place[0] // 2 == 0, active[:, 0], active[:, 1]).reshape(-1, filters)
+    mixed = mixed_ref[...] + jnp.dot(mine, proj, preferred_element_type=F32).reshape(out_ref.shape)
     out_ref[...] = mixed
+    proj_grad = lax.dot_general(
+        active.reshape(-1, filters), cells, (((0,), (0,)), ((), ())), preferred_element_type=F32
+    )
+    if not paired:
+        proj_grad_ref[...] = proj_grad
+        return
+    first = place[2] == 0
+    at = keep_ref.shape[0] - filters
+    keep_ref[at:] = jnp.where(first, earlier_ref[...], proj_grad)
+    send_ref[at:] = jnp.where(first, proj_grad, earlier_ref[...]).astype(BF16)
+    if above:
+        keep_ref[:at] = above[0][...]
+        send_ref[:at] = above[1][...]
     if leaving:
-        upper = place[1] == 0
-        leaving[0][...] = jnp.where(upper, mixed[2 * n :], mixed[:n]).astype(BF16)
-
-
-def gate(branches, folded, place, after, nears, fars, cots, arrived, proj, mixed, leaves=False):
+        leaving[0][...] = jnp.where(place[1] == 0, mixed[2 * n :], mixed[:n]).astype(BF16)
+
+
+def gate(branch, folded, place, after, near, far, cots, arrived, proj, mixed, earlier=None, above=()):
     filters = proj.shape[-1]
-    count = len(branches)
-    arrays = [*nears, *fars, cots] + ([arrived] if folded else [])
-    shapes = [
-        ((count,) + nears[0].shape[1:], BF16), (mixed.shape, F32), ((count, filters, filters), F32)
-    ]
-    if leaves:
+    arrays = [near, far, cots] + ([arrived] if folded else [])
+    ins = [(a, a.shape, None) for a in arrays] + [(proj, (1, filters, filters), (branch, 0, 0))]
+    ins += [(a, a.shape, None) for a in ([mixed] if earlier is None else [mixed, earlier, *above])]
+    part = (2 * filters if above else filters, filters)
+    shapes = [(near.shape, BF16), (mixed.shape, F32), (part, F32)]
+    if earlier is not None:
+        shapes.append((part, BF16))
+    if above:
         shapes.append(((mixed.shape[0] // 3,) + mixed.shape[1:], BF16))
     return call(
-        functools.partial(gate_kernel, branches, folded), place, 1, after,
-        [(a, a.shape, None) for a in arrays]
-        + [(proj, (1, filters, filters), (b, 0, 0)) for b in branches]
-        + [(mixed, mixed.shape, None)],
-        [(shape_of(shape, kind), shape, None) for shape, kind in shapes],
-        "gate_" + "_".join(map(str, branches)),
+        functools.partial(gate_kernel, branch, folded, bool(above)), place, 1, after, ins,
+        [(shape_of(shape, kind), shape, None) for shape, kind in shapes], f"gate_{branch}",
     )
 
 
@@ -255,12 +263,20 @@
     return both.reshape(-1, own.shape[-1])
 
 
+def split_by_core(place, low, high, keep_ref, send_ref):
+    first = place[2] == 0
+    rows = low.shape[0]
+    keep_ref[:rows] = jnp.where(first, low, high)
+    send_ref[:rows] = jnp.where(first, high, low).astype(send_ref.dtype)
+
+
 def backward_kernel(
-    branch, folded, chained, place, own_ref, other_ref, x_ref, arrived_ref, spread_ref, taps_ref, point_ref,
-    before_ref, *refs
+    branch, folded, final, chained, place, own_ref, other_ref, x_ref, arrived_ref, spread_ref, taps_ref,
+    point_ref, before_ref, *refs
 ):
     classes, group, cols, channels = x_ref.shape
     point_grad_ref, depth_ref, grads_ref = refs[-3:]
+    refs = refs[:-3]
     upper = place[1] == 0
     pre = whole_columns(place, own_ref[0], other_ref[0])
     grads = lax.dot_general(pre, point_ref[0], (((1,), (1,)), ((), ())), preferred_element_type=F32)
@@ -277,6 +293,7 @@
     def _():
         point_grad_ref[...] += product
 
+    outs = refs[2:] if chained else refs
     pairs = row_pairs(branch, classes)
 
     def residue(r, carry):
@@ -307,19 +324,43 @@
                 total = part if total is None else total + part
             totals.append(total)
         if chained:
-            leaving_ref, stay_ref = refs[:2]
+            leaving_ref, stay_ref = outs[:2]
             leaving_ref[r] = jnp.where(upper, totals[2], totals[0]).astype(BF16)
             stay_ref[0, r] = jnp.where(upper, totals[0], totals[1])
             stay_ref[1, r] = jnp.where(upper, totals[1], totals[2])
         else:
             for q in range(classes):
-                refs[0][q, r] = totals[q]
+                outs[0][q, r] = totals[q]
         return carry
 
     lax.fori_loop(0, group, residue, 0)
 
-
-def backward(branch, folded, place, after, own, other, index, x, arrived, spread, taps, point, before=None):
+    @pl.when(pl.program_id(0) == STEPS - 1)
+    def _():
+        depth = depth_ref[...].sum(axis=1)
+        if final:
+            keep_ref, send_ref = outs[-2:]
+            half, filters = channels // 2, point_grad_ref.shape[1]
+            split_by_core(place, point_grad_ref[:half], point_grad_ref[half:], keep_ref, send_ref)
+            if chained:
+                depths = jnp.concatenate([refs[0][...], depth, refs[1][...]])
+                low, high = depths[:, :filters], depths[:, filters:]
+                first = place[2] == 0
+                keep_ref[half : half + 27] = jnp.where(first, low, high)
+                send_ref[half : half + 27] = jnp.where(first, high, low).astype(BF16)
+                blank = jnp.zeros((keep_ref.shape[0] - half - 27, filters), F32)
+                keep_ref[half + 27 :] = blank
+                send_ref[half + 27 :] = blank.astype(BF16)
+            else:
+                outs[-3][...] = depth
+        else:
+            outs[-2][...] = point_grad_ref[...]
+            outs[-1][...] = depth
+
+
+def backward(
+    branch, folded, final, place, after, own, other, x, arrived, spread, taps, point, before=None, depths=()
+):
     classes, residues, cols, channels = x.shape
     filters = point.shape[2]
     group = residues // STEPS
@@ -334,28 +375,37 @@
         ]
     else:
         outs = [(pltpu.HBM(x.shape, F32), cell, 1)]
-    outs += [
-        (shape_of((channels, filters), F32), (channels, filters), None),
-        (shape_of((9, 8, channels), F32), (9, 8, channels), None),
-    ]
+    halves = (channels // 2 + (32 if chained else 0), filters)
+    shapes = [(channels, filters), (9, channels)]
+    if final:
+        shapes = [halves, halves] if chained else [(9, channels), halves, halves]
+    outs += [(shape_of(shape, F32), shape, None) for shape in shapes]
+    if final:
+        outs[-1] = (shape_of(halves, BF16), halves, None)
     small = (1, 1, 8, 128)
     return call(
-        functools.partial(backward_kernel, branch, folded, chained), place, STEPS, after,
+        functools.partial(backward_kernel, branch, folded, final, chained), place, STEPS, after,
         [
-            (own, part, (index, 0, None, 0, 0, 0)),
-            (other, part, (index, 0, None, 0, 0, 0)),
+            (own, part, 2),
+            (other, part, 2),
             (x, cell, 1),
             (arrived, thin, 0) if folded else (x, small, None),
             (spread, cell, 1),
             (taps, taps.shape, None),
             (point, (1, channels, filters), (branch, 0, 0)),
             (before, cell, 1) if chained else (x, small, None),
+        ]
+        + [(d, d.shape, None) for d in depths],
+        outs, f"backward_{branch}",
+        scratch=[
+            pltpu.VMEM((channels, filters), F32),
+            pltpu.VMEM((9, 8, channels), F32),
+            pltpu.VMEM(cell, BF16),
         ],
-        outs, f"backward_{branch}", scratch=[pltpu.VMEM(cell, BF16)],
-    )
-
-
-def join_kernel(place, own_ref, other_ref, x_ref, pre_ref, point_grad_ref):
+    )
+
+
+def join_kernel(place, own_ref, other_ref, x_ref, earlier_ref, pre_ref, keep_ref, send_ref, total_ref):
     pre = whole_columns(place, own_ref[0], other_ref[0])
     pre_ref[...] = pre.reshape(pre_ref.shape)
     cells = x_ref[...].reshape(-1, x_ref.shape[-1])
@@ -363,14 +413,18 @@
 
     @pl.when(pl.program_id(0) == 0)
     def _():
-        point_grad_ref[...] = product
+        total_ref[...] = product
 
     @pl.when(pl.program_id(0) > 0)
     def _():
-        point_grad_ref[...] += product
-
-
-def join(place, after, own, other, index, x):
+        total_ref[...] += product
+
+    @pl.when(pl.program_id(0) == STEPS - 1)
+    def _():
+        split_by_core(place, earlier_ref[...], total_ref[...], keep_ref, send_ref)
+
+
+def join(place, after, own, other, x, earlier):
     classes, residues, cols, channels = x.shape
     filters = own.shape[-1]
     group = residues // STEPS
@@ -378,15 +432,17 @@
     return call(
         join_kernel, place, STEPS, after,
         [
-            (own, part, (index, 0, None, 0, 0, 0)),
-            (other, part, (index, 0, None, 0, 0, 0)),
+            (own, part, 2),
+            (other, part, 2),
             (x, (classes, group, cols, channels), 1),
+            (earlier, earlier.shape, None),
         ],
         [
             (shape_of((classes, residues, cols, filters), BF16), (classes, group, cols, filters), 1),
-            (shape_of((channels, filters), F32), (channels, filters), None),
+            (shape_of(earlier.shape, F32), earlier.shape, None),
+            (shape_of(earlier.shape, BF16), earlier.shape, None),
         ],
-        "join",
+        "join", scratch=[pltpu.VMEM(earlier.shape, F32)],
     )
 
 
@@ -433,28 +489,26 @@
     )
 
 
-def add_kernel(scale, place, *refs):
-    *pairs, out_ref = refs
+def add_kernel(scale, counts, place, *refs):
+    *terms, out_ref = refs
     at = 0
-    for own_ref, other_ref in zip(pairs[::2], pairs[1::2]):
-        rows = other_ref.shape[0]
-        if len(own_ref.shape) == 3:
-            own = jnp.where(place[2] == 0, own_ref[0], own_ref[1])
-        else:
-            own = own_ref[...]
-        total = own.astype(F32) + other_ref[...].astype(F32)
+    for count in counts:
+        group, terms = terms[:count], terms[count:]
+        values = [ref[...].astype(F32) for ref in group]
+        total = values[0] + values[1]
         if scale != 1.0:
             total = total * scale
+        rows = group[0].shape[0]
         out_ref[at : at + rows] = total.astype(out_ref.dtype)
         at += rows
 
 
-def add(name, place, after, pairs, kind, scale=1.0):
-    rows = sum(other.shape[0] for _, other in pairs)
-    shape = (rows, pairs[0][1].shape[1])
+def add(name, place, after, groups, kind, scale=1.0):
+    shape = (sum(group[0].shape[0] for group in groups), groups[0][0].shape[1])
+    counts = [len(group) for group in groups]
     return call(
-        functools.partial(add_kernel, scale), place, 1, after,
-        [(a, a.shape, None) for pair in pairs for a in pair],
+        functools.partial(add_kernel, scale, counts), place, 1, after,
+        [(a, a.shape, None) for group in groups for a in group],
         [(shape_of(shape, kind), shape, None)], name,
     )
 
@@ -468,32 +522,26 @@
 
     channels = point_ref.shape[1]
     filters = proj_ref.shape[1]
+    half = channels // 2
     point_ref[3], point_ref[0] = halves(own30, far30, 0, channels)
-    proj_ref[3], proj_ref[0] = halves(own30, far30, channels, filters)
-    point_ref[1, : channels // 2], point_ref[1, channels // 2 :] = halves(own1, far1, 0, channels // 2)
-    rows = own2.shape[0] - filters
-    low, high = halves(own2, far2, 0, rows)
-    point_ref[2, :rows] = low
-    point_ref[2, rows:] = high[: channels - rows]
-    depth_ref[...] = high[channels - rows :]
-    proj_ref[1], proj_ref[2] = halves(own2, far2, rows, filters)
+    point_ref[1, :half], point_ref[1, half:] = halves(own1, far1, 0, half)
+    proj_ref[3], proj_ref[0] = halves(own1, far1, half, filters)
+    proj_ref[1], proj_ref[2] = halves(own1, far1, half + filters, filters)
+    point_ref[2, :half], point_ref[2, half:] = halves(own2, far2, 0, half)
+    low, high = halves(own2, far2, half, 27)
+    for k in range(9):
+        rows = slice(3 * k, 3 * k + 3)
+        depth_ref[k // 3, k % 3, :, :filters] = low[rows]
+        depth_ref[k // 3, k % 3, :, filters:] = high[rows]
 
 
 def finish(place, after, early, middle, late, channels, filters):
     arrays = [*early, *middle, *late]
-    rows = 2 * (late[0].shape[0] - filters) - channels
-    shapes = [(4, filters, filters), (rows, filters), (4, channels, filters)]
+    shapes = [(4, filters, filters), (3, 3, 3, channels), (4, channels, filters)]
     return call(
         finish_kernel, place, 1, after, [(a, a.shape, None) for a in arrays],
         [(result_of(s, F32), s, None) for s in shapes], "finish",
     )
-
-
-def cores(value):
-    if len(value.shape) == 2:
-        value = value.reshape((2, -1) + value.shape[1:])
-    far = lax.dynamic_index_in_dim(value, 1 - lax.axis_index("dp") % 2, 0, keepdims=False)
-    return value, swap(far, "dp", 1)
 
 
 def by_classes(features_in, depth_weights, point_weights, proj_weights, cotangent):
@@ -510,95 +558,88 @@
     cot = cotangent[0]
     cot_far = swap(cot, "chan", 2)
 
-    token = jnp.zeros(TOKEN, F32)
+    token, blank = jnp.zeros(TOKEN, F32), jnp.zeros(cot.shape, F32)
     keep3, keep0, send3, send0, spread3, x_leaving, token = forward(
-        (3, 0), False, place, token, in_hbm(x), x, depth_weights, in_hbm(point_weights)
+        (3, 0), False, place, token, in_hbm(x), x, in_hbm(depth_weights), in_hbm(point_weights)
     )
     sent3, sent0 = swap(send3, "chan", 1), swap(send0, "chan", 1)
     arrived = swap(x_leaving, "row", 1)
-    near3, cots, cots_leaving, token = first_near_sum(place, token, keep3, sent3, cot, cot_far)
+    near3, token = near_sum("3", place, token, keep3, sent3)
     far3 = swap(near3, "chan", 2)
-    near0, token = near_sum("0", place, token, keep0, sent0)
+    keep1, keep2, send1, send2, spread1, spread2, token = forward(
+        (1, 2), True, place, token, x, arrived, *weights
+    )
+    sent1, sent2 = swap(send1, "chan", 1), swap(send2, "chan", 1)
+    near0, cots, cots_leaving, token = near_sum_cots("0", place, token, keep0, sent0, cot, cot_far)
     far0 = swap(near0, "chan", 2)
     cots_arrived = swap(cots_leaving, "row", 1)
-    keep1, keep2, send1, send2, spread1, spread2, token = forward(
-        (1, 2), True, place, token, x, arrived, *weights
-    )
-    sent1, sent2 = swap(send1, "chan", 1), swap(send2, "chan", 1)
+    grad3, band_mixed, proj3, token = gate(
+        3, False, place, token, near3, far3, cots, None, proj_weights, blank
+    )
+    other3 = swap(grad3, "chan", 1)
     near1, token = near_sum("1", place, token, keep1, sent1)
     far1 = swap(near1, "chan", 2)
-    mixed = jnp.zeros(cot.shape, F32)
-    grad30, band_mixed, proj30, token = gate(
-        (3, 0), False, place, token, [near3, near0], [far3, far0], cots, None, proj_weights, mixed
-    )
-    other30 = swap(grad30, "chan", 1)
-    proj30_own, proj30_near = cores(proj30)
+    grad0, band_mixed, proj_keep, proj_send, token = gate(
+        0, False, place, token, near0, far0, cots, None, proj_weights, band_mixed, proj3
+    )
+    other0 = swap(grad0, "chan", 1)
     near2, token = near_sum("2", place, token, keep2, sent2)
     far2 = swap(near2, "chan", 2)
     grad1, class_mixed, proj1, token = gate(
-        (1,), True, place, token, [near1], [far1], cots, cots_arrived, proj_weights, mixed
+        1, True, place, token, near1, far1, cots, cots_arrived, proj_weights, blank
     )
     other1 = swap(grad1, "chan", 1)
-    proj30_sum, token = add("proj_3_0", place, token, [(proj30_own, proj30_near)], BF16)
-    proj30_pair = swap(proj30_sum, "chan", 1)
     band, point3, depth3, token = backward(
-        3, False, place, token, grad30, other30, 0, x, x, spread3, *weights
-    )
-    grad2, class_mixed, proj2, mixed_leaving, token = gate(
-        (2,), True, place, token, [near2], [far2], cots, cots_arrived, proj_weights, class_mixed, True
+        3, False, False, place, token, grad3, other3, x, x, spread3, *weights
+    )
+    pre0, point_keep, point_send, token = join(place, token, grad0, other0, x, point3)
+    point30 = (point_keep, swap(point_send, "dp", 1))
+    grad2, class_mixed, proj_keep, proj_send, mixed_leaving, token = gate(
+        2, True, place, token, near2, far2, cots, cots_arrived, proj_weights, class_mixed, proj1,
+        (proj_keep, proj_send),
     )
     other2 = swap(grad2, "chan", 1)
     mixed_arrived = swap(mixed_leaving, "row", 1)
-    proj12_own, proj12_near = cores(jnp.concatenate([proj1, proj2]))
-    pre0, point0, token = join(place, token, grad30, other30, 1, x)
-    point30_own, point30_near = cores(jnp.stack([point3, point0]))
-    total1, point1, depth1, token = backward(
-        1, True, place, token, grad1, other1, 0, x, arrived, spread1, *weights
-    )
-    point1_own, point1_near = cores(point1)
-    early, token = add(
-        "early_y", place, token, [(point30_own, point30_near), (proj30_sum, proj30_pair)], BF16
-    )
-    early_y = swap(early, "row", 1)
-    proj12_sum, token = add("proj_1_2", place, token, [(proj12_own, proj12_near)], BF16)
-    proj12_pair = swap(proj12_sum, "chan", 1)
-    middle, token = add("middle_y", place, token, [(point1_own, point1_near)], BF16)
-    middle_y = swap(middle, "row", 1)
-    leaving, stay, point2, depth2, token = backward(
-        2, True, place, token, grad2, other2, 0, x, arrived, spread2, *weights, before=total1
+    proj = (proj_keep, swap(proj_send, "dp", 1))
+    total1, depth1, point_keep, point_send, token = backward(
+        1, True, True, place, token, grad1, other1, x, arrived, spread1, *weights
+    )
+    point1 = (point_keep, swap(point_send, "dp", 1))
+    early, token = add("early_y", place, token, [point30], BF16)
+    early = (early, swap(early, "row", 1))
+    leaving, stay, late_keep, late_send, token = backward(
+        2, True, True, place, token, grad2, other2, x, arrived, spread2, *weights, before=total1,
+        depths=(depth1, depth3),
     )
     input_arrived = swap(leaving, "row", 1)
-    early, token = add("early_x", place, token, [(early, early_y)], BF16)
-    early_x = swap(early, "dp", 2)
-    depth_rows = 27 * channels // filters
-    padded = -(-depth_rows // 32) * 32
-    depth = jnp.concatenate([depth1, depth2, depth3]).sum(axis=1).reshape(depth_rows, filters)
-    depth = jnp.pad(depth, ((0, padded - depth_rows), (0, 0)))
-    late_own, late_near = cores(jnp.concatenate([point2, depth]))
-    late, token = add(
-        "late_x", place, token, [(late_own, late_near), (proj12_sum, proj12_pair)], BF16
-    )
-    late_x = swap(late, "dp", 2)
-    middle, token = add("middle_x", place, token, [(middle, middle_y)], BF16)
-    middle_x = swap(middle, "dp", 2)
+    late = (late_keep, swap(late_send, "dp", 1))
+    proj, token = add("proj", place, token, [proj], BF16)
+    proj = (proj, swap(proj, "chan", 1))
+    early, token = add("early_x", place, token, [early], BF16)
+    early = (early, swap(early, "dp", 2))
+    late, token = add("late_x", place, token, [late], BF16)
+    late = (late, swap(late, "dp", 2))
+    middle, token = add("middle_y", place, token, [point1, proj], BF16)
+    middle = (middle, swap(middle, "row", 1))
+    late, token = add("late_y", place, token, [late], BF16)
+    late = (late, swap(late, "row", 1))
+    early, token = add("early", place, token, [early], F32, scale)
+    early = (early, swap(early, "dp", 1))
+    middle, token = add("middle_x", place, token, [middle], BF16)
+    middle = (middle, swap(middle, "dp", 2))
+    late, token = add("late", place, token, [late], F32, scale)
+    late = (late, swap(late, "dp", 1))
     bands = band_mixed.reshape((classes, n) + band_mixed.shape[1:])
     folds = class_mixed.reshape(bands.shape)
     grad_input, output, token = last(
         place, token, pre0, point_weights, in_hbm(band), in_hbm(stay), input_arrived, bands, folds,
         mixed_arrived,
     )
-    late, token = add("late_y", place, token, [(late, late_x)], BF16)
-    late_y = swap(late, "row", 1)
-    early, token = add("early", place, token, [(early, early_x)], F32, scale)
-    early_far = swap(early, "dp", 1)
-    middle, token = add("middle", place, token, [(middle, middle_x)], F32, scale)
-    middle_far = swap(middle, "dp", 1)
-    late, token = add("late", place, token, [(late, late_y)], F32, scale)
-    late_far = swap(late, "dp", 1)
-    grad_proj, depth, grad_point, token = finish(
-        place, token, (early, early_far), (middle, middle_far), (late, late_far), channels, filters
-    )
-    grad_depth = depth[:depth_rows].reshape(3, 3, 3, channels)
+    middle, token = add("middle", place, token, [middle], F32, scale)
+    middle = (middle, swap(middle, "dp", 1))
+    grad_proj, grad_depth, grad_point, token = finish(
+        place, token, early, middle, late, channels, filters
+    )
     return (
         output.reshape(cotangent.shape), grad_input.reshape(features_in.shape), grad_depth, grad_point,
         grad_proj,

time: 162 us -> 141 us (0.87)
  local copies, waits for them, and re-layouts: 8.22 us -> 1.72 us
  Pallas kernels: 52.9 us -> 46.4 us
  starting transfers between devices: 33.3 us -> 29.1 us
  waiting for transfers between devices: 66 us -> 62 us
    pallas_call x26, Pallas kernels: 52.9 us -> 46.4 us  [call(): pl.pallas_call(kernel, grid_spec=pltpu.PrefetchScalarGridSpec(num_scalar_...]
    unnamed x53 -> x18, local copies, waits for them, and re-layouts: 6.46 us -> 1.7 us
    ppermute x32 -> x31, starting transfers between devices: 33.3 us -> 29.1 us  [swap(): return lax.ppermute(value, axis, [(i, i ^ flip) for i in range(count)])]
    ppermute x32 -> x31, waiting for transfers between devices: 66 us -> 62 us  [swap(): return lax.ppermute(value, axis, [(i, i ^ flip) for i in range(count)])]
  transfers between devices with their start and end apart: 32 -> 31, of which waited for: 13 -> 15; matrix products, arithmetic and copies ran while one was open for 1% -> 0% of each run, Pallas kernels for 25% -> 27%
where the time goes in v3:
time: 141 us; the launch traced here: 140 us
  waiting for transfers between devices  62 us (44%)
  Pallas kernels  46.4 us (33%)
  starting transfers between devices  29.1 us (21%)
  local copies, waits for them, and re-layouts  1.72 us (1%)
    ppermute x31, waiting for transfers between devices, swap(): return lax.ppermute(value, axis, [(i, i ^ flip) for i in range(count)])  62 us
    pallas_call x26, Pallas kernels, call(): pl.pallas_call(kernel, grid_spec=pltpu.PrefetchScalarGridSpec(num_scalar_...  46.4 us
    ppermute x31, starting transfers between devices, swap(): return lax.ppermute(value, axis, [(i, i ^ flip) for i in range(count)])  29.1 us
  transfers between devices with their start and end apart: 31, of which 15 were waited for; matrix products, arithmetic and copies ran while one was open for 0% of the time, Pallas kernels for 27%

profile of v3, /device:TPU:0, one launch (start us, length us, event | category | flops | bytes accessed | tf_op | source)
XLA Modules:
  0.0 140.2 jit_solution(10234840659896940056)
XLA Ops:
  0.7 4.6 %forward_3_0.1 = (f32[1,3,6,2,16,256]{5,4,3,2,1,0:T(8,128)S(1)}, f32[1,3,6,2,16,256]{5,4,3,2,1,0:T(8,128)S(1)}, bf16[1,3,6,2,16,256]{5,4,3,2,1,0:T(8,128)(2,1)S(...) custom-call(s32[3]{0:T(128)S(1)} %pad_add_fusion.place_ref, ...), custom_call_target="tpu_custom_call" | custom-call | flops 1 | bytes 1 | tf_op jit(solution)/shard_map/forward_3_0/pallas_call | solution.py:79
  5.3 3.0 %collective-permute-start.1 = (bf16[6,64,512]{2,1,0:T(8,128)(2,1)S(1)}, bf16[6,64,512]{2,1,0:T(8,128)(2,1)S(1)}, u32[]{:S(2)}, u32[]{:S(2)}) collective-permute-start(bf16[6,64,512]{2,1,0:T(8,128)(2,1)S(1)} %get-tuple-element.96), channel_id=1, source_target_pairs={{0,16},{16,0},{1,17},{17,1},{2,18},{18,2},{3,19},{19,3},{4,20},{20... | collective-permute-start | bytes 1179656 | tf_op jit(solution)/shard_map/ppermute | solution.py:19
  8.3 1.6 %collective-permute-start = (bf16[1,3,6,2,16,256]{5,4,3,2,1,0:T(8,128)(2,1)S(1)}, bf16[1,3,6,2,16,256]{5,4,3,2,1,0:T(8,128)(2,1)S(1)}, u32[]{:S(2)}, u32[]{:S(2)}) collective-permute-start(bf16[1,3,6,2,16,256]{5,4,3,2,1,0:T(8,128)(2,1)S(1)} %get-tuple-element.94), channel_id=1, source_target_pairs={{0,4},{4,0},{8,12},{12,8},{1,5},{5,1},{9,13},{13,9},{2,6},{6,2},{1... | collective-permute-start | bytes 884744 | tf_op jit(solution)/shard_map/ppermute | solution.py:19
  9.9 0.5 collective-permute-start.2
  10.3 2.6 %collective-permute-start.3 = (bf16[18,16,256]{2,1,0:T(8,128)(2,1)S(1)}, bf16[18,16,256]{2,1,0:T(8,128)(2,1)S(1)}, u32[]{:S(2)}, u32[]{:S(2)}) collective-permute-start(bf16[18,16,256]{2,1,0:T(8,128)(2,1)S(1)} %bitcast.21), channel_id=1, source_target_pairs={{0,8},{4,12},{8,0},{12,4},{1,9},{5,13},{9,1},{13,5},{2,10},{6,14},... | collective-permute-start | bytes 442376 | tf_op jit(solution)/shard_map/ppermute | solution.py:19
  12.9 8.5 %collective-permute-done.refs_1_ = bf16[1,3,6,2,16,256]{5,4,3,2,1,0:T(8,128)(2,1)S(1)} collective-permute-done((bf16[1,3,6,2,16,256]{5,4,3,2,1,0:T(8,128)(2,1)S(1)}, bf16[1,3,6,2,16,256]{5,4,3,2,1,0:T(8,128)(2,1)S(1)}, u32[]{:S(2)}, u32[]{:S(2)}) %collective-permute-start) | collective-permute-done | bytes 294944 | tf_op jit(solution)/shard_map/ppermute | solution.py:19
  21.4 0.6 near_3.1
  22.0 1.7 %collective-permute-start.4 = (bf16[1,3,6,2,16,256]{5,4,3,2,1,0:T(8,128)(2,1)S(1)}, bf16[1,3,6,2,16,256]{5,4,3,2,1,0:T(8,128)(2,1)S(1)}, u32[]{:S(2)}, u32[]{:S(2)}) collective-permute-start(bf16[1,3,6,2,16,256]{5,4,3,2,1,0:T(8,128)(2,1)S(1)} %get-tuple-element.101.refs_0_), channel_id=1, source_target_pairs={{0,8},{4,12},{8,0},{12,4},{1,9},{5,13},{9,1},{13,5},{2,10},{6,14},... | collective-permute-start | bytes 884744 | tf_op jit(solution)/shard_map/ppermute | solution.py:19
  23.8 5.3 %forward_1_2.1 = (f32[1,3,6,2,16,256]{5,4,3,2,1,0:T(8,128)S(1)}, f32[1,3,6,2,16,256]{5,4,3,2,1,0:T(8,128)S(1)}, bf16[1,3,6,2,16,256]{5,4,3,2,1,0:T(8,128)(2,1)S(...) custom-call(s32[3]{0:T(128)S(1)} %pad_add_fusion.place_ref, ...), custom_call_target="tpu_custom_call" | custom-call | flops 1 | bytes 1 | tf_op jit(solution)/shard_map/forward_1_2/pallas_call | solution.py:79
  29.1 2.5 %collective-permute-start.5 = (bf16[1,3,6,2,16,256]{5,4,3,2,1,0:T(8,128)(2,1)S(1)}, bf16[1,3,6,2,16,256]{5,4,3,2,1,0:T(8,128)(2,1)S(1)}, u32[]{:S(2)}, u32[]{:S(2)}) collective-permute-start(bf16[1,3,6,2,16,256]{5,4,3,2,1,0:T(8,128)(2,1)S(1)} %get-tuple-element.105), channel_id=1, source_target_pairs={{0,4},{4,0},{8,12},{12,8},{1,5},{5,1},{9,13},{13,9},{2,6},{6,2},{1... | collective-permute-start | bytes 884744 | tf_op jit(solution)/shard_map/ppermute | solution.py:19
  31.5 0.7 near_0.1
  32.2 0.1 collective-permute-start.6
  32.3 0.8 collective-permute-start.7
  33.1 9.4 %collective-permute-done.4.refs_1_ = bf16[1,3,6,2,16,256]{5,4,3,2,1,0:T(8,128)(2,1)S(1)} collective-permute-done((bf16[1,3,6,2,16,256]{5,4,3,2,1,0:T(8,128)(2,1)S(1)}, bf16[1,3,6,2,16,256]{5,4,3,2,1,0:T(8,128)(2,1)S(1)}, u32[]{:S(2)}, u32[]{:S(2)}) %collective-permute-start.4) | collective-permute-done | bytes 294944 | tf_op jit(solution)/shard_map/ppermute | solution.py:19
  42.5 1.0 gate_3.1
  43.6 2.1 %collective-permute-done.5.refs_1_ = bf16[1,3,6,2,16,256]{5,4,3,2,1,0:T(8,128)(2,1)S(1)} collective-permute-done((bf16[1,3,6,2,16,256]{5,4,3,2,1,0:T(8,128)(2,1)S(1)}, bf16[1,3,6,2,16,256]{5,4,3,2,1,0:T(8,128)(2,1)S(1)}, u32[]{:S(2)}, u32[]{:S(2)}) %collective-permute-start.5) | collective-permute-done | bytes 294944 | tf_op jit(solution)/shard_map/ppermute | solution.py:19
  45.8 0.6 near_1.1
  46.4 3.4 %collective-permute-start.8 = (bf16[1,3,6,2,16,256]{5,4,3,2,1,0:T(8,128)(2,1)S(1)}, bf16[1,3,6,2,16,256]{5,4,3,2,1,0:T(8,128)(2,1)S(1)}, u32[]{:S(2)}, u32[]{:S(2)}) collective-permute-start(bf16[1,3,6,2,16,256]{5,4,3,2,1,0:T(8,128)(2,1)S(1)} %get-tuple-element.114.refs_0_), channel_id=1, source_target_pairs={{0,8},{4,12},{8,0},{12,4},{1,9},{5,13},{9,1},{13,5},{2,10},{6,14},... | collective-permute-start | bytes 884744 | tf_op jit(solution)/shard_map/ppermute | solution.py:19
  49.8 3.9 %collective-permute-done.6.refs_1_ = bf16[1,3,6,2,16,256]{5,4,3,2,1,0:T(8,128)(2,1)S(1)} collective-permute-done((bf16[1,3,6,2,16,256]{5,4,3,2,1,0:T(8,128)(2,1)S(1)}, bf16[1,3,6,2,16,256]{5,4,3,2,1,0:T(8,128)(2,1)S(1)}, u32[]{:S(2)}, u32[]{:S(2)}) %collective-permute-start.6) | collective-permute-done | bytes 294944 | tf_op jit(solution)/shard_map/ppermute | solution.py:19
  53.7 1.0 gate_0.1
  54.9 9.9 %collective-permute-done.7.refs_1_ = bf16[1,3,6,2,16,256]{5,4,3,2,1,0:T(8,128)(2,1)S(1)} collective-permute-done((bf16[1,3,6,2,16,256]{5,4,3,2,1,0:T(8,128)(2,1)S(1)}, bf16[1,3,6,2,16,256]{5,4,3,2,1,0:T(8,128)(2,1)S(1)}, u32[]{:S(2)}, u32[]{:S(2)}) %collective-permute-start.7) | collective-permute-done | bytes 294944 | tf_op jit(solution)/shard_map/ppermute | solution.py:19
  64.7 0.6 near_2.1
  65.4 0.6 collective-permute-start.9
  66.0 4.1 %collective-permute-done.9.refs_3_ = bf16[6,2,16,256]{3,2,1,0:T(8,128)(2,1)S(1)} collective-permute-done((bf16[6,2,16,256]{3,2,1,0:T(8,128)(2,1)S(1)}, bf16[6,2,16,256]{3,2,1,0:T(8,128)(2,1)S(1)}, u32[]{:S(2)}, u32[]{:S(2)}) %collective-permute-start.9) | collective-permute-done | bytes 98336 | tf_op jit(solution)/shard_map/ppermute | solution.py:19
  70.1 1.1 gate_1.1
  71.2 2.0 %collective-permute-start.13 = (bf16[1,3,6,2,16,256]{5,4,3,2,1,0:T(8,128)(2,1)S(1)}, bf16[1,3,6,2,16,256]{5,4,3,2,1,0:T(8,128)(2,1)S(1)}, u32[]{:S(2)}, u32[]{:S(2)}) collective-permute-start(bf16[1,3,6,2,16,256]{5,4,3,2,1,0:T(8,128)(2,1)S(1)} %get-tuple-element.129.refs_0_), channel_id=1, source_target_pairs={{0,4},{4,0},{8,12},{12,8},{1,5},{5,1},{9,13},{13,9},{2,6},{6,2},{1... | collective-permute-start | bytes 884744 | tf_op jit(solution)/shard_map/ppermute | solution.py:19
  73.2 1.3 collective-permute-done.10.refs_1_
  74.6 4.4 %backward_3.1 = (f32[3,6,64,512]{3,2,1,0:T(8,128)}, f32[512,256]{1,0:T(8,128)S(1)}, f32[9,512]{1,0:T(8,128)S(1)}, f32[8,128]{1,0:T(8,128)S(1)}) custom-call(s32[3]{0:T(128)S(1)} %pad_add_fusion.place_ref, f32[8,128]{1,0:T(8,128)S(1)} %get-tuple-element.116.after_ref, bf16[1,3,6,2,16,256]{5,4,3,2,1,0:T(8,128)(2,1)S(1)} %get-tuple-element.117.refs_0_, ...), custom_call_target="tpu_custom_call" | custom-call | flops 1 | bytes 1 | tf_op jit(solution)/shard_map/backward_3/pallas_call | solution.py:79
  78.9 1.9 %collective-permute-done.11.refs_1_ = bf16[1,3,6,2,16,256]{5,4,3,2,1,0:T(8,128)(2,1)S(1)} collective-permute-done((bf16[1,3,6,2,16,256]{5,4,3,2,1,0:T(8,128)(2,1)S(1)}, bf16[1,3,6,2,16,256]{5,4,3,2,1,0:T(8,128)(2,1)S(1)}, u32[]{:S(2)}, u32[]{:S(2)}) %collective-permute-start.11) | collective-permute-done | bytes 294944 | tf_op jit(solution)/shard_map/ppermute | solution.py:19
  80.8 1.7 %join.1 = (bf16[3,6,64,256]{3,2,1,0:T(8,128)(2,1)S(1)}, f32[512,256]{1,0:T(8,128)S(1)}, bf16[512,256]{1,0:T(8,128)(2,1)S(1)}, f32[8,128]{1,0:T(8,128)S(1)}) custom-call(s32[3]{0:T(128)S(1)} %pad_add_fusion.place_ref, f32[8,128]{1,0:T(8,128)S(1)} %get-tuple-element.119.after_ref, bf16[1,3,6,2,16,256]{5,4,3,2,1,0:T(8,128)(2,1)S(1)} %get-tuple-element.120.refs_0_, ...), custom_call_target="tpu_custom_call" | custom-call | flops 1 | bytes 1 | tf_op jit(solution)/shard_map/join/pallas_call | solution.py:79
  82.6 1.1 gate_2.1
  83.8 0.5 collective-permute-start.16
  84.3 2.6 %collective-permute-done.13.refs_1_ = bf16[1,3,6,2,16,256]{5,4,3,2,1,0:T(8,128)(2,1)S(1)} collective-permute-done((bf16[1,3,6,2,16,256]{5,4,3,2,1,0:T(8,128)(2,1)S(1)}, bf16[1,3,6,2,16,256]{5,4,3,2,1,0:T(8,128)(2,1)S(1)}, u32[]{:S(2)}, u32[]{:S(2)}) %collective-permute-start.13) | collective-permute-done | bytes 294944 | tf_op jit(solution)/shard_map/ppermute | solution.py:19
  86.9 6.3 %backward_1.1 = (f32[3,6,64,512]{3,2,1,0:T(8,128)}, f32[9,512]{1,0:T(8,128)S(1)}, f32[256,256]{1,0:T(8,128)S(1)}, bf16[256,256]{1,0:T(8,128)(2,1)S(1)}, f32[8,128]{1,0:T(8,128)S(1)}) custom-call(s32[3]{0:T(128)S(1)} %pad_add_fusion.place_ref, f32[8,128]{1,0:T(8,128)S(1)} %get-tuple-element.128.after_ref, ...), custom_call_target="tpu_custom_call" | custom-call | flops 1 | bytes 1 | tf_op jit(solution)/shard_map/backward_1/pallas_call | solution.py:79
  93.2 0.6 early_y.1
  93.8 0.7 collective-permute-start.17
  94.5 1.7 %copy-done.3 = f32[3,6,64,512]{3,2,1,0:T(8,128)S(1)} copy-done((f32[3,6,64,512]{3,2,1,0:T(8,128)S(1)}, f32[3,6,64,512]{3,2,1,0:T(8,128)}, u32[]{:S(2)}) %copy-start.3) | copy-done | bytes 2359320
  96.2 5.0 %backward_2.1 = (bf16[6,64,512]{2,1,0:T(8,128)(2,1)S(1)}, f32[2,6,64,512]{3,2,1,0:T(8,128)}, f32[288,256]{1,0:T(8,128)S(1)}, bf16[288,256]{1,0:T(8,128)(2,1)S(1)}, f32[8,128]{1,0:T(8,128)S(1)}) custom-call(s32[3]{0:T(128)S(1)} %pad_add_fusion.place_ref, f32[8,128]{1,0:T(8,128)S(1)} %get-tuple-element.134.after_ref, ...), custom_call_target="tpu_custom_call" | custom-call | flops 1 | bytes 1 | tf_op jit(solution)/shard_map/backward_2/pallas_call | solution.py:79
  101.2 0.6 proj.1
  101.9 0.5 collective-permute-start.19
  102.4 0.6 early_x.1
  103.0 0.2 collective-permute-done.18.refs_1_
  103.3 0.6 late_x.1
  103.9 4.3 %collective-permute-done.20.refs_3_ = bf16[512,256]{1,0:T(8,128)(2,1)S(1)} collective-permute-done((bf16[512,256]{1,0:T(8,128)(2,1)S(1)}, bf16[512,256]{1,0:T(8,128)(2,1)S(1)}, u32[]{:S(2)}, u32[]{:S(2)}) %collective-permute-start.20) | collective-permute-done | bytes 262176 | tf_op jit(solution)/shard_map/ppermute | solution.py:19
  108.2 0.6 middle_y.1
  108.8 1.4 %collective-permute-start.23 = (bf16[768,256]{1,0:T(8,128)(2,1)S(1)}, bf16[768,256]{1,0:T(8,128)(2,1)S(1)}, u32[]{:S(2)}, u32[]{:S(2)}) collective-permute-start(bf16[768,256]{1,0:T(8,128)(2,1)S(1)} %get-tuple-element.157.refs_0_), channel_id=1, source_target_pairs={{0,16},{16,0},{1,17},{17,1},{2,18},{18,2},{3,19},{19,3},{4,20},{20... | collective-permute-start | bytes 1179656 | tf_op jit(solution)/shard_map/ppermute | solution.py:19
  110.3 1.5 %collective-permute-start.22 = (bf16[512,256]{1,0:T(8,128)(2,1)S(1)}, bf16[512,256]{1,0:T(8,128)(2,1)S(1)}, u32[]{:S(2)}, u32[]{:S(2)}) collective-permute-start(bf16[512,256]{1,0:T(8,128)(2,1)S(1)} %get-tuple-element.155.refs_0_), channel_id=1, source_target_pairs={{0,2},{1,3},{2,0},{3,1},{4,6},{5,7},{6,4},{7,5},{8,10},{9,11},{10,... | collective-permute-start | bytes 786440 | tf_op jit(solution)/shard_map/ppermute | solution.py:19
  111.8 0.5 collective-permute-start.21
  112.3 0.7 collective-permute-start.25
  113.0 5.3 %collective-permute-done.21.refs_1_ = bf16[288,256]{1,0:T(8,128)(2,1)S(1)} collective-permute-done((bf16[288,256]{1,0:T(8,128)(2,1)S(1)}, bf16[288,256]{1,0:T(8,128)(2,1)S(1)}, u32[]{:S(2)}, u32[]{:S(2)}) %collective-permute-start.21) | collective-permute-done | bytes 147488 | tf_op jit(solution)/shard_map/ppermute | solution.py:19
  118.2 0.6 late_y.1
  118.8 0.6 early.1
  119.4 1.5 %collective-permute-done.23.refs_1_ = bf16[768,256]{1,0:T(8,128)(2,1)S(1)} collective-permute-done((bf16[768,256]{1,0:T(8,128)(2,1)S(1)}, bf16[768,256]{1,0:T(8,128)(2,1)S(1)}, u32[]{:S(2)}, u32[]{:S(2)}) %collective-permute-start.23) | collective-permute-done | bytes 393248 | tf_op jit(solution)/shard_map/ppermute | solution.py:19
  121.0 0.6 middle_x.1
  121.6 1.4 %collective-permute-start.27 = (bf16[768,256]{1,0:T(8,128)(2,1)S(1)}, bf16[768,256]{1,0:T(8,128)(2,1)S(1)}, u32[]{:S(2)}, u32[]{:S(2)}) collective-permute-start(bf16[768,256]{1,0:T(8,128)(2,1)S(1)} %get-tuple-element.171.refs_0_), channel_id=1, source_target_pairs={{0,2},{1,3},{2,0},{3,1},{4,6},{5,7},{6,4},{7,5},{8,10},{9,11},{10,... | collective-permute-start | bytes 1179656 | tf_op jit(solution)/shard_map/ppermute | solution.py:19
  123.0 1.5 %collective-permute-start.24 = (bf16[288,256]{1,0:T(8,128)(2,1)S(1)}, bf16[288,256]{1,0:T(8,128)(2,1)S(1)}, u32[]{:S(2)}, u32[]{:S(2)}) collective-permute-start(bf16[288,256]{1,0:T(8,128)(2,1)S(1)} %get-tuple-element.159.refs_0_), channel_id=1, source_target_pairs={{0,16},{16,0},{1,17},{17,1},{2,18},{18,2},{3,19},{19,3},{4,20},{20... | collective-permute-start | bytes 442376 | tf_op jit(solution)/shard_map/ppermute | solution.py:19
  124.5 0.5 collective-permute-start.26
  125.0 4.0 %collective-permute-done.24.refs_1_ = bf16[288,256]{1,0:T(8,128)(2,1)S(1)} collective-permute-done((bf16[288,256]{1,0:T(8,128)(2,1)S(1)}, bf16[288,256]{1,0:T(8,128)(2,1)S(1)}, u32[]{:S(2)}, u32[]{:S(2)}) %collective-permute-start.24) | collective-permute-done | bytes 147488 | tf_op jit(solution)/shard_map/ppermute | solution.py:19
  129.0 0.6 late.1
  129.6 3.9 %last.1 = (bf16[3,6,64,512]{3,2,1,0:T(8,128)(2,1)}, bf16[3,6,16,256]{3,2,1,0:T(8,128)(2,1)}, f32[8,128]{1,0:T(8,128)S(1)}) custom-call(s32[3]{0:T(128)S(1)} %pad_add_fusion.place_ref, f32[8,128]{1,0:T(8,128)S(1)} %get-tuple-element.160.after_ref, bf16[3,6,64,256]{3,2,1,0:T(8,128)(2,1)S(1)} %get-tuple-element.161.refs_0_, bf16[4,512,256]{2,1,0:T(8,128)(2,1)S(1)} %copy-done.1, ...), custom_call_target="tpu_custom_call" | custom-call | flops 1 | bytes 1 | tf_op jit(solution)/shard_map/last/pallas_call | solution.py:79
  133.5 0.6 middle.1
  134.3 0.5 collective-permute-start.28
  134.8 2.9 %collective-permute-done.30.refs_5_ = f32[288,256]{1,0:T(8,128)S(1)} collective-permute-done((f32[288,256]{1,0:T(8,128)S(1)}, f32[288,256]{1,0:T(8,128)S(1)}, u32[]{:S(2)}, u32[]{:S(2)}) %collective-permute-start.30) | collective-permute-done | bytes 294944 | tf_op jit(solution)/shard_map/ppermute | solution.py:19
  137.7 2.5 %finish.1 = (f32[4,256,256]{2,1,0:T(8,128)}, f32[3,3,3,512]{3,2,1,0:T(4,128)}, f32[4,512,256]{2,1,0:T(8,128)}, f32[8,128]{1,0:T(8,128)}) custom-call(s32[3]{0:T(128)S(1)} %pad_add_fusion.place_ref, f32[8,128]{1,0:T(8,128)S(1)} %get-tuple-element.172.after_ref, f32[512,256]{1,0:T(8,128)S(1)} %get-tuple-element.173.refs_0_, ...), custom_call_target="tpu_custom_call" | custom-call | flops 1 | bytes 1 | tf_op jit(solution)/shard_map/finish/pallas_call | solution.py:79
  (45 shorter events, 0.8 us)
Async XLA Ops:
  0.7 9.6 %copy-start.8 = (bf16[1,18,16,256]{3,2,1,0:T(8,128)(2,1)S(1)}, bf16[1,18,16,256]{3,2,1,0:T(8,128)(2,1)}, u32[]{:S(2)}) copy-start(bf16[1,18,16,256]{3,2,1,0:T(8,128)(2,1)} %param.9) | copy-start | bytes 442372
  0.7 23.0 %copy-start = (bf16[1,18,64,512]{3,2,1,0:T(8,128)(2,1)S(1)}, bf16[1,18,64,512]{3,2,1,0:T(8,128)(2,1)}, u32[]{:S(2)}) copy-start(bf16[1,18,64,512]{3,2,1,0:T(8,128)(2,1)} %param.5) | copy-start | bytes 3538948
  0.7 23.0 %copy-start.1 = (bf16[4,512,256]{2,1,0:T(8,128)(2,1)S(1)}, bf16[4,512,256]{2,1,0:T(8,128)(2,1)}, u32[]{:S(2)}) copy-start(bf16[4,512,256]{2,1,0:T(8,128)(2,1)} %refs_1_.1) | copy-start | bytes 3145732
  0.7 23.0 %copy-start.7 = (bf16[3,3,3,512]{3,2,1,0:T(4,128)(2,1)S(1)}, bf16[3,3,3,512]{3,2,1,0:T(4,128)(2,1)}, u32[]{:S(2)}) copy-start(bf16[3,3,3,512]{3,2,1,0:T(4,128)(2,1)} %refs_5_.5) | copy-start | bytes 82948
  5.3 18.4 %collective-permute-start.1 = (bf16[6,64,512]{2,1,0:T(8,128)(2,1)S(1)}, bf16[6,64,512]{2,1,0:T(8,128)(2,1)S(1)}, u32[]{:S(2)}, u32[]{:S(2)}) collective-permute-start(bf16[6,64,512]{2,1,0:T(8,128)(2,1)S(1)} %get-tuple-element.96), channel_id=1, source_target_pairs={{0,16},{16,0},{1,17},{17,1},{2,18},{18,2},{3,19},{19,3},{4,20},{20... | collective-permute-start | bytes 1179656 | tf_op jit(solution)/shard_map/ppermute | solution.py:19
  8.3 13.1 %collective-permute-start = (bf16[1,3,6,2,16,256]{5,4,3,2,1,0:T(8,128)(2,1)S(1)}, bf16[1,3,6,2,16,256]{5,4,3,2,1,0:T(8,128)(2,1)S(1)}, u32[]{:S(2)}, u32[]{:S(2)}) collective-permute-start(bf16[1,3,6,2,16,256]{5,4,3,2,1,0:T(8,128)(2,1)S(1)} %get-tuple-element.94), channel_id=1, source_target_pairs={{0,4},{4,0},{8,12},{12,8},{1,5},{5,1},{9,13},{13,9},{2,6},{6,2},{1... | collective-permute-start | bytes 884744 | tf_op jit(solution)/shard_map/ppermute | solution.py:19
  9.9 21.7 %collective-permute-start.2 = (bf16[1,3,6,2,16,256]{5,4,3,2,1,0:T(8,128)(2,1)S(1)}, bf16[1,3,6,2,16,256]{5,4,3,2,1,0:T(8,128)(2,1)S(1)}, u32[]{:S(2)}, u32[]{:S(2)}) collective-permute-start(bf16[1,3,6,2,16,256]{5,4,3,2,1,0:T(8,128)(2,1)S(1)} %get-tuple-element.99), channel_id=1, source_target_pairs={{0,4},{4,0},{8,12},{12,8},{1,5},{5,1},{9,13},{13,9},{2,6},{6,2},{1... | collective-permute-start | bytes 884744 | tf_op jit(solution)/shard_map/ppermute | solution.py:19
  10.3 21.2 %collective-permute-start.3 = (bf16[18,16,256]{2,1,0:T(8,128)(2,1)S(1)}, bf16[18,16,256]{2,1,0:T(8,128)(2,1)S(1)}, u32[]{:S(2)}, u32[]{:S(2)}) collective-permute-start(bf16[18,16,256]{2,1,0:T(8,128)(2,1)S(1)} %bitcast.21), channel_id=1, source_target_pairs={{0,8},{4,12},{8,0},{12,4},{1,9},{5,13},{9,1},{13,5},{2,10},{6,14},... | collective-permute-start | bytes 442376 | tf_op jit(solution)/shard_map/ppermute | solution.py:19
  22.0 20.5 %collective-permute-start.4 = (bf16[1,3,6,2,16,256]{5,4,3,2,1,0:T(8,128)(2,1)S(1)}, bf16[1,3,6,2,16,256]{5,4,3,2,1,0:T(8,128)(2,1)S(1)}, u32[]{:S(2)}, u32[]{:S(2)}) collective-permute-start(bf16[1,3,6,2,16,256]{5,4,3,2,1,0:T(8,128)(2,1)S(1)} %get-tuple-element.101.refs_0_), channel_id=1, source_target_pairs={{0,8},{4,12},{8,0},{12,4},{1,9},{5,13},{9,1},{13,5},{2,10},{6,14},... | collective-permute-start | bytes 884744 | tf_op jit(solution)/shard_map/ppermute | solution.py:19
  29.1 13.4 %copy-start.2 = (bf16[4,256,256]{2,1,0:T(8,128)(2,1)S(1)}, bf16[4,256,256]{2,1,0:T(8,128)(2,1)}, u32[]{:S(2)}) copy-start(bf16[4,256,256]{2,1,0:T(8,128)(2,1)} %refs_4_.7) | copy-start | bytes 1572868
  29.1 16.7 %collective-permute-start.5 = (bf16[1,3,6,2,16,256]{5,4,3,2,1,0:T(8,128)(2,1)S(1)}, bf16[1,3,6,2,16,256]{5,4,3,2,1,0:T(8,128)(2,1)S(1)}, u32[]{:S(2)}, u32[]{:S(2)}) collective-permute-start(bf16[1,3,6,2,16,256]{5,4,3,2,1,0:T(8,128)(2,1)S(1)} %get-tuple-element.105), channel_id=1, source_target_pairs={{0,4},{4,0},{8,12},{12,8},{1,5},{5,1},{9,13},{13,9},{2,6},{6,2},{1... | collective-permute-start | bytes 884744 | tf_op jit(solution)/shard_map/ppermute | solution.py:19
  32.2 21.5 %collective-permute-start.6 = (bf16[1,3,6,2,16,256]{5,4,3,2,1,0:T(8,128)(2,1)S(1)}, bf16[1,3,6,2,16,256]{5,4,3,2,1,0:T(8,128)(2,1)S(1)}, u32[]{:S(2)}, u32[]{:S(2)}) collective-permute-start(bf16[1,3,6,2,16,256]{5,4,3,2,1,0:T(8,128)(2,1)S(1)} %get-tuple-element.107.refs_0_), channel_id=1, source_target_pairs={{0,8},{4,12},{8,0},{12,4},{1,9},{5,13},{9,1},{13,5},{2,10},{6,14},... | collective-permute-start | bytes 884744 | tf_op jit(solution)/shard_map/ppermute | solution.py:19
  32.3 32.4 %collective-permute-start.7 = (bf16[1,3,6,2,16,256]{5,4,3,2,1,0:T(8,128)(2,1)S(1)}, bf16[1,3,6,2,16,256]{5,4,3,2,1,0:T(8,128)(2,1)S(1)}, u32[]{:S(2)}, u32[]{:S(2)}) collective-permute-start(bf16[1,3,6,2,16,256]{5,4,3,2,1,0:T(8,128)(2,1)S(1)} %get-tuple-element.112), channel_id=1, source_target_pairs={{0,4},{4,0},{8,12},{12,8},{1,5},{5,1},{9,13},{13,9},{2,6},{6,2},{1... | collective-permute-start | bytes 884744 | tf_op jit(solution)/shard_map/ppermute | solution.py:19
  43.6 31.0 %collective-permute-start.10 = (bf16[1,3,6,2,16,256]{5,4,3,2,1,0:T(8,128)(2,1)S(1)}, bf16[1,3,6,2,16,256]{5,4,3,2,1,0:T(8,128)(2,1)S(1)}, u32[]{:S(2)}, u32[]{:S(2)}) collective-permute-start(bf16[1,3,6,2,16,256]{5,4,3,2,1,0:T(8,128)(2,1)S(1)} %get-tuple-element.117.refs_0_), channel_id=1, source_target_pairs={{0,4},{4,0},{8,12},{12,8},{1,5},{5,1},{9,13},{13,9},{2,6},{6,2},{1... | collective-permute-start | bytes 884744 | tf_op jit(solution)/shard_map/ppermute | solution.py:19
  46.4 23.7 %collective-permute-start.8 = (bf16[1,3,6,2,16,256]{5,4,3,2,1,0:T(8,128)(2,1)S(1)}, bf16[1,3,6,2,16,256]{5,4,3,2,1,0:T(8,128)(2,1)S(1)}, u32[]{:S(2)}, u32[]{:S(2)}) collective-permute-start(bf16[1,3,6,2,16,256]{5,4,3,2,1,0:T(8,128)(2,1)S(1)} %get-tuple-element.114.refs_0_), channel_id=1, source_target_pairs={{0,8},{4,12},{8,0},{12,4},{1,9},{5,13},{9,1},{13,5},{2,10},{6,14},... | collective-permute-start | bytes 884744 | tf_op jit(solution)/shard_map/ppermute | solution.py:19
  54.8 26.0 %collective-permute-start.11 = (bf16[1,3,6,2,16,256]{5,4,3,2,1,0:T(8,128)(2,1)S(1)}, bf16[1,3,6,2,16,256]{5,4,3,2,1,0:T(8,128)(2,1)S(1)}, u32[]{:S(2)}, u32[]{:S(2)}) collective-permute-start(bf16[1,3,6,2,16,256]{5,4,3,2,1,0:T(8,128)(2,1)S(1)} %get-tuple-element.120.refs_0_), channel_id=1, source_target_pairs={{0,4},{4,0},{8,12},{12,8},{1,5},{5,1},{9,13},{13,9},{2,6},{6,2},{1... | collective-permute-start | bytes 884744 | tf_op jit(solution)/shard_map/ppermute | solution.py:19
  64.7 9.8 %copy-start.4 = (bf16[3,6,64,512]{3,2,1,0:T(8,128)(2,1)S(1)}, bf16[3,6,64,512]{3,2,1,0:T(8,128)(2,1)}, u32[]{:S(2)}) copy-start(bf16[3,6,64,512]{3,2,1,0:T(8,128)(2,1)} %get-tuple-element.118.refs_4_) | copy-start | bytes 3538948
  65.4 17.2 %collective-permute-start.12 = (bf16[1,3,6,2,16,256]{5,4,3,2,1,0:T(8,128)(2,1)S(1)}, bf16[1,3,6,2,16,256]{5,4,3,2,1,0:T(8,128)(2,1)S(1)}, u32[]{:S(2)}, u32[]{:S(2)}) collective-permute-start(bf16[1,3,6,2,16,256]{5,4,3,2,1,0:T(8,128)(2,1)S(1)} %get-tuple-element.123.refs_0_), channel_id=1, source_target_pairs={{0,8},{4,12},{8,0},{12,4},{1,9},{5,13},{9,1},{13,5},{2,10},{6,14},... | collective-permute-start | bytes 884744 | tf_op jit(solution)/shard_map/ppermute | solution.py:19
  65.4 4.7 %collective-permute-start.9 = (bf16[6,2,16,256]{3,2,1,0:T(8,128)(2,1)S(1)}, bf16[6,2,16,256]{3,2,1,0:T(8,128)(2,1)S(1)}, u32[]{:S(2)}, u32[]{:S(2)}) collective-permute-start(bf16[6,2,16,256]{3,2,1,0:T(8,128)(2,1)S(1)} %get-tuple-element.115), channel_id=1, source_target_pairs={{0,16},{16,0},{1,17},{17,1},{2,18},{18,2},{3,19},{19,3},{4,20},{20... | collective-permute-start | bytes 294920 | tf_op jit(solution)/shard_map/ppermute | solution.py:19
  71.2 15.7 %collective-permute-start.13 = (bf16[1,3,6,2,16,256]{5,4,3,2,1,0:T(8,128)(2,1)S(1)}, bf16[1,3,6,2,16,256]{5,4,3,2,1,0:T(8,128)(2,1)S(1)}, u32[]{:S(2)}, u32[]{:S(2)}) collective-permute-start(bf16[1,3,6,2,16,256]{5,4,3,2,1,0:T(8,128)(2,1)S(1)} %get-tuple-element.129.refs_0_), channel_id=1, source_target_pairs={{0,4},{4,0},{8,12},{12,8},{1,5},{5,1},{9,13},{13,9},{2,6},{6,2},{1... | collective-permute-start | bytes 884744 | tf_op jit(solution)/shard_map/ppermute | solution.py:19
  82.6 4.3 %copy-start.6 = (bf16[3,6,64,512]{3,2,1,0:T(8,128)(2,1)S(1)}, bf16[3,6,64,512]{3,2,1,0:T(8,128)(2,1)}, u32[]{:S(2)}) copy-start(bf16[3,6,64,512]{3,2,1,0:T(8,128)(2,1)} %get-tuple-element.130.refs_4_) | copy-start | bytes 3538948
  83.6 10.9 %collective-permute-start.15 = (bf16[1,3,6,2,16,256]{5,4,3,2,1,0:T(8,128)(2,1)S(1)}, bf16[1,3,6,2,16,256]{5,4,3,2,1,0:T(8,128)(2,1)S(1)}, u32[]{:S(2)}, u32[]{:S(2)}) collective-permute-start(bf16[1,3,6,2,16,256]{5,4,3,2,1,0:T(8,128)(2,1)S(1)} %get-tuple-element.135.refs_0_), channel_id=1, source_target_pairs={{0,4},{4,0},{8,12},{12,8},{1,5},{5,1},{9,13},{13,9},{2,6},{6,2},{1... | collective-permute-start | bytes 884744 | tf_op jit(solution)/shard_map/ppermute | solution.py:19
  83.7 9.4 %collective-permute-start.14 = (bf16[512,256]{1,0:T(8,128)(2,1)S(1)}, bf16[512,256]{1,0:T(8,128)(2,1)S(1)}, u32[]{:S(2)}, u32[]{:S(2)}) collective-permute-start(bf16[512,256]{1,0:T(8,128)(2,1)S(1)} %get-tuple-element.133), channel_id=1, source_target_pairs={{0,1},{1,0},{2,3},{3,2},{4,5},{5,4},{6,7},{7,6},{8,9},{9,8},{10,11... | collective-permute-start | bytes 786440 | tf_op jit(solution)/shard_map/ppermute | solution.py:19
  83.8 17.4 %collective-permute-start.16 = (bf16[512,256]{1,0:T(8,128)(2,1)S(1)}, bf16[512,256]{1,0:T(8,128)(2,1)S(1)}, u32[]{:S(2)}, u32[]{:S(2)}) collective-permute-start(bf16[512,256]{1,0:T(8,128)(2,1)S(1)} %get-tuple-element.142), channel_id=1, source_target_pairs={{0,1},{1,0},{2,3},{3,2},{4,5},{5,4},{6,7},{7,6},{8,9},{9,8},{10,11... | collective-permute-start | bytes 786440 | tf_op jit(solution)/shard_map/ppermute | solution.py:19
  86.9 7.6 %copy-start.5 = (bf16[3,6,64,512]{3,2,1,0:T(8,128)(2,1)S(1)}, bf16[3,6,64,512]{3,2,1,0:T(8,128)(2,1)}, u32[]{:S(2)}) copy-start(bf16[3,6,64,512]{3,2,1,0:T(8,128)(2,1)} %get-tuple-element.136.refs_4_) | copy-start | bytes 3538948
  93.8 8.7 %collective-permute-start.17 = (bf16[512,256]{1,0:T(8,128)(2,1)S(1)}, bf16[512,256]{1,0:T(8,128)(2,1)S(1)}, u32[]{:S(2)}, u32[]{:S(2)}) collective-permute-start(bf16[512,256]{1,0:T(8,128)(2,1)S(1)} %get-tuple-element.144.refs_0_), channel_id=1, source_target_pairs={{0,16},{16,0},{1,17},{17,1},{2,18},{18,2},{3,19},{19,3},{4,20},{20... | collective-permute-start | bytes 786440 | tf_op jit(solution)/shard_map/ppermute | solution.py:19
  94.5 1.7 %copy-start.3 = (f32[3,6,64,512]{3,2,1,0:T(8,128)S(1)}, f32[3,6,64,512]{3,2,1,0:T(8,128)}, u32[]{:S(2)}) copy-start(f32[3,6,64,512]{3,2,1,0:T(8,128)} %get-tuple-element.137.refs_7_) | copy-start | bytes 7077892
  101.8 6.4 %collective-permute-start.20 = (bf16[512,256]{1,0:T(8,128)(2,1)S(1)}, bf16[512,256]{1,0:T(8,128)(2,1)S(1)}, u32[]{:S(2)}, u32[]{:S(2)}) collective-permute-start(bf16[512,256]{1,0:T(8,128)(2,1)S(1)} %get-tuple-element.151.refs_2_), channel_id=1, source_target_pairs={{0,4},{4,0},{8,12},{12,8},{1,5},{5,1},{9,13},{13,9},{2,6},{6,2},{1... | collective-permute-start | bytes 786440 | tf_op jit(solution)/shard_map/ppermute | solution.py:19
  101.8 1.4 %collective-permute-start.18 = (bf16[288,256]{1,0:T(8,128)(2,1)S(1)}, bf16[288,256]{1,0:T(8,128)(2,1)S(1)}, u32[]{:S(2)}, u32[]{:S(2)}) collective-permute-start(bf16[288,256]{1,0:T(8,128)(2,1)S(1)} %get-tuple-element.147), channel_id=1, source_target_pairs={{0,1},{1,0},{2,3},{3,2},{4,5},{5,4},{6,7},{7,6},{8,9},{9,8},{10,11... | collective-permute-start | bytes 442376 | tf_op jit(solution)/shard_map/ppermute | solution.py:19
  101.9 1.9 %collective-permute-start.19 = (bf16[256,256]{1,0:T(8,128)(2,1)S(1)}, bf16[256,256]{1,0:T(8,128)(2,1)S(1)}, u32[]{:S(2)}, u32[]{:S(2)}) collective-permute-start(bf16[256,256]{1,0:T(8,128)(2,1)S(1)} %get-tuple-element.150), channel_id=1, source_target_pairs={{0,1},{1,0},{2,3},{3,2},{4,5},{5,4},{6,7},{7,6},{8,9},{9,8},{10,11... | collective-permute-start | bytes 393224 | tf_op jit(solution)/shard_map/ppermute | solution.py:19
  108.8 12.1 %collective-permute-start.23 = (bf16[768,256]{1,0:T(8,128)(2,1)S(1)}, bf16[768,256]{1,0:T(8,128)(2,1)S(1)}, u32[]{:S(2)}, u32[]{:S(2)}) collective-permute-start(bf16[768,256]{1,0:T(8,128)(2,1)S(1)} %get-tuple-element.157.refs_0_), channel_id=1, source_target_pairs={{0,16},{16,0},{1,17},{17,1},{2,18},{18,2},{3,19},{19,3},{4,20},{20... | collective-permute-start | bytes 1179656 | tf_op jit(solution)/shard_map/ppermute | solution.py:19
  110.3 8.5 %collective-permute-start.22 = (bf16[512,256]{1,0:T(8,128)(2,1)S(1)}, bf16[512,256]{1,0:T(8,128)(2,1)S(1)}, u32[]{:S(2)}, u32[]{:S(2)}) collective-permute-start(bf16[512,256]{1,0:T(8,128)(2,1)S(1)} %get-tuple-element.155.refs_0_), channel_id=1, source_target_pairs={{0,2},{1,3},{2,0},{3,1},{4,6},{5,7},{6,4},{7,5},{8,10},{9,11},{10,... | collective-permute-start | bytes 786440 | tf_op jit(solution)/shard_map/ppermute | solution.py:19
  111.8 6.5 %collective-permute-start.21 = (bf16[288,256]{1,0:T(8,128)(2,1)S(1)}, bf16[288,256]{1,0:T(8,128)(2,1)S(1)}, u32[]{:S(2)}, u32[]{:S(2)}) collective-permute-start(bf16[288,256]{1,0:T(8,128)(2,1)S(1)} %get-tuple-element.153.refs_0_), channel_id=1, source_target_pairs={{0,2},{1,3},{2,0},{3,1},{4,6},{5,7},{6,4},{7,5},{8,10},{9,11},{10,... | collective-permute-start | bytes 442376 | tf_op jit(solution)/shard_map/ppermute | solution.py:19
  112.3 17.3 %collective-permute-start.25 = (bf16[6,64,512]{2,1,0:T(8,128)(2,1)S(1)}, bf16[6,64,512]{2,1,0:T(8,128)(2,1)S(1)}, u32[]{:S(2)}, u32[]{:S(2)}) collective-permute-start(bf16[6,64,512]{2,1,0:T(8,128)(2,1)S(1)} %get-tuple-element.164), channel_id=1, source_target_pairs={{0,16},{16,0},{1,17},{17,1},{2,18},{18,2},{3,19},{19,3},{4,20},{20... | collective-permute-start | bytes 1179656 | tf_op jit(solution)/shard_map/ppermute | solution.py:19
  121.6 11.9 %collective-permute-start.27 = (bf16[768,256]{1,0:T(8,128)(2,1)S(1)}, bf16[768,256]{1,0:T(8,128)(2,1)S(1)}, u32[]{:S(2)}, u32[]{:S(2)}) collective-permute-start(bf16[768,256]{1,0:T(8,128)(2,1)S(1)} %get-tuple-element.171.refs_0_), channel_id=1, source_target_pairs={{0,2},{1,3},{2,0},{3,1},{4,6},{5,7},{6,4},{7,5},{8,10},{9,11},{10,... | collective-permute-start | bytes 1179656 | tf_op jit(solution)/shard_map/ppermute | solution.py:19
  123.0 6.0 %collective-permute-start.24 = (bf16[288,256]{1,0:T(8,128)(2,1)S(1)}, bf16[288,256]{1,0:T(8,128)(2,1)S(1)}, u32[]{:S(2)}, u32[]{:S(2)}) collective-permute-start(bf16[288,256]{1,0:T(8,128)(2,1)S(1)} %get-tuple-element.159.refs_0_), channel_id=1, source_target_pairs={{0,16},{16,0},{1,17},{17,1},{2,18},{18,2},{3,19},{19,3},{4,20},{20... | collective-permute-start | bytes 442376 | tf_op jit(solution)/shard_map/ppermute | solution.py:19
  124.5 5.1 %collective-permute-start.26 = (bf16[6,16,256]{2,1,0:T(8,128)(2,1)S(1)}, bf16[6,16,256]{2,1,0:T(8,128)(2,1)S(1)}, u32[]{:S(2)}, u32[]{:S(2)}) collective-permute-start(bf16[6,16,256]{2,1,0:T(8,128)(2,1)S(1)} %get-tuple-element.167), channel_id=1, source_target_pairs={{0,16},{16,0},{1,17},{17,1},{2,18},{18,2},{3,19},{19,3},{4,20},{20... | collective-permute-start | bytes 147464 | tf_op jit(solution)/shard_map/ppermute | solution.py:19
  134.2 3.5 %collective-permute-start.29 = (f32[768,256]{1,0:T(8,128)S(1)}, f32[768,256]{1,0:T(8,128)S(1)}, u32[]{:S(2)}, u32[]{:S(2)}) collective-permute-start(f32[768,256]{1,0:T(8,128)S(1)} %get-tuple-element.174.refs_2_), channel_id=1, source_target_pairs={{0,1},{1,0},{2,3},{3,2},{4,5},{5,4},{6,7},{7,6},{8,9},{9,8},{10,11... | collective-permute-start | bytes 2359304 | tf_op jit(solution)/shard_map/ppermute | solution.py:19
  134.3 3.4 %collective-permute-start.28 = (f32[512,256]{1,0:T(8,128)S(1)}, f32[512,256]{1,0:T(8,128)S(1)}, u32[]{:S(2)}, u32[]{:S(2)}) collective-permute-start(f32[512,256]{1,0:T(8,128)S(1)} %get-tuple-element.173.refs_0_), channel_id=1, source_target_pairs={{0,1},{1,0},{2,3},{3,2},{4,5},{5,4},{6,7},{7,6},{8,9},{9,8},{10,11... | collective-permute-start | bytes 1572872 | tf_op jit(solution)/shard_map/ppermute | solution.py:19
  134.7 2.9 %collective-permute-start.30 = (f32[288,256]{1,0:T(8,128)S(1)}, f32[288,256]{1,0:T(8,128)S(1)}, u32[]{:S(2)}, u32[]{:S(2)}) collective-permute-start(f32[288,256]{1,0:T(8,128)S(1)} %get-tuple-element.175.refs_4_), channel_id=1, source_target_pairs={{0,1},{1,0},{2,3},{3,2},{4,5},{5,4},{6,7},{7,6},{8,9},{9,8},{10,11... | collective-permute-start | bytes 884744 | tf_op jit(solution)/shard_map/ppermute | solution.py:19

commit v4 on v3

--- a/solution.py
+++ b/solution.py
@@ -98,7 +98,7 @@
     points, refs = refs[:count], refs[count:]
     keeps, sends, refs = refs[:count], refs[count : 2 * count], refs[2 * count :]
     spreads = dict(zip([b for b in branches if b], refs))
-    if not folded:
+    if not branches[0]:
         refs[-1][...] = x_ref[1]
 
     def residue(r, carry):
@@ -143,7 +143,7 @@
     outs = [(shape_of(part_shape, F32), part, 2) for _ in branches]
     outs += [(shape_of(part_shape, BF16), part, 2) for _ in branches]
     outs += [(pltpu.HBM(x.shape, BF16), cell, 1) for b in branches if b]
-    if not folded:
+    if not branches[0]:
         outs += [(shape_of(x.shape[1:], BF16), (group, cols, channels), 0)]
     return call(
         functools.partial(forward_kernel, branches, folded), place, STEPS, after,
@@ -168,40 +168,42 @@
     )
 
 
-def near_cots_kernel(place, keep_ref, arrived_ref, cot_ref, far_ref, near_ref, cots_ref, leaving_ref):
-    near_kernel(place, keep_ref, arrived_ref, near_ref)
-    low_side = place[0] // 2 == 0
-    cots_ref[:, 0] = jnp.where(low_side, cot_ref[...], far_ref[...])
-    cots_ref[:, 1] = jnp.where(low_side, far_ref[...], cot_ref[...])
-    n = leaving_ref.shape[0]
-    leaving_ref[...] = cots_ref[n : 2 * n]
-
-
-def near_sum_cots(name, place, after, keep, arrived, cot, far):
-    rows, width, filters = cot.shape
-    cots = (rows, 2, width, filters)
-    leaving = (rows // 3, 2, width, filters)
+def near_cot_kernel(place, keep_ref, arrived_ref, cot_ref, near_ref):
+    near_ref[:, :, :, :2] = (keep_ref[...] + arrived_ref[...].astype(F32)).astype(BF16)
+    near_ref[0, :, :, 2] = cot_ref[...].reshape(near_ref.shape[1:3] + near_ref.shape[4:])
+
+
+def near_sum_cot(name, place, after, keep, arrived, cot):
+    shape = keep.shape[:3] + (3,) + keep.shape[4:]
     return call(
-        near_cots_kernel, place, 1, after,
-        [(a, a.shape, None) for a in (keep, arrived, cot, far)],
-        [(shape_of(s, BF16), s, None) for s in (keep.shape, cots, leaving)], f"near_{name}",
-    )
-
-
-def gate_kernel(branch, folded, stacked, place, near_ref, far_ref, cot_ref, *refs):
+        near_cot_kernel, place, 1, after,
+        [(keep, keep.shape, None), (arrived, keep.shape, None), (cot, cot.shape, None)],
+        [(shape_of(shape, BF16), shape, None)], f"near_{name}",
+    )
+
+
+def gate_kernel(branch, folded, first_gate, place, near_ref, far_ref, *refs):
+    cot_ref = None
+    if not first_gate:
+        cot_ref, refs = refs[0], refs[1:]
     _, classes, residues, sides, width, filters = near_ref.shape
     if folded:
         arrived_ref, refs = refs[0], refs[1:]
+    n, sides = residues, 2
+    low_side = place[0] // 2 == 0
+    if cot_ref is None:
+        cots_ref, cots_leaving_ref, *refs = refs[-2:] + refs[:-2]
+        own = near_ref[0, :, :, 2].reshape(classes * n, width, filters)
+        far = far_ref[0, :, :, 2].reshape(classes * n, width, filters)
+        cots_ref[:, 0] = jnp.where(low_side, own, far)
+        cots_ref[:, 1] = jnp.where(low_side, far, own)
+        cots_leaving_ref[...] = cots_ref[n : 2 * n]
+        cot_ref = cots_ref
     paired = len(refs) > 5
     if paired:
-        proj_ref, mixed_ref, earlier_ref, *refs = refs
-        above = []
-        if stacked:
-            above, refs = refs[:2], refs[2:]
-        grad_ref, out_ref, keep_ref, send_ref, *leaving = refs
+        proj_ref, mixed_ref, earlier_ref, grad_ref, out_ref, keep_ref, send_ref, *leaving = refs
     else:
         proj_ref, mixed_ref, grad_ref, out_ref, proj_grad_ref = refs
-    n = residues
     cots = cot_ref[...]
     if folded:
         cots = jnp.concatenate(
@@ -211,12 +213,12 @@
     shape = (classes * residues, sides, width, filters)
     proj = proj_ref[0]
     act_grad = lax.dot_general(cells, proj, (((1,), (1,)), ((), ())), preferred_element_type=F32)
-    preact = (near_ref[0].astype(F32) + far_ref[0].astype(F32)).reshape(shape)
+    preact = (near_ref[0, :, :, :2].astype(F32) + far_ref[0, :, :, :2].astype(F32)).reshape(shape)
     logistic = 1.0 / (1.0 + jnp.exp(-preact))
     grad = act_grad.reshape(shape) * logistic * (1.0 + preact * (1.0 - logistic))
     grad_ref[0] = grad.astype(BF16).reshape(grad_ref.shape[1:])
     active = (preact * logistic).astype(BF16)
-    mine = jnp.where(place[0] // 2 == 0, active[:, 0], active[:, 1]).reshape(-1, filters)
+    mine = jnp.where(low_side, active[:, 0], active[:, 1]).reshape(-1, filters)
     mixed = mixed_ref[...] + jnp.dot(mine, proj, preferred_element_type=F32).reshape(out_ref.shape)
     out_ref[...] = mixed
     proj_grad = lax.dot_general(
@@ -226,29 +228,29 @@
         proj_grad_ref[...] = proj_grad
         return
     first = place[2] == 0
-    at = keep_ref.shape[0] - filters
-    keep_ref[at:] = jnp.where(first, earlier_ref[...], proj_grad)
-    send_ref[at:] = jnp.where(first, proj_grad, earlier_ref[...]).astype(BF16)
-    if above:
-        keep_ref[:at] = above[0][...]
-        send_ref[:at] = above[1][...]
+    keep_ref[...] = jnp.where(first, earlier_ref[...], proj_grad)
+    send_ref[...] = jnp.where(first, proj_grad, earlier_ref[...]).astype(BF16)
     if leaving:
         leaving[0][...] = jnp.where(place[1] == 0, mixed[2 * n :], mixed[:n]).astype(BF16)
 
 
-def gate(branch, folded, place, after, near, far, cots, arrived, proj, mixed, earlier=None, above=()):
+def gate(branch, folded, place, after, near, far, cots, arrived, proj, mixed, earlier=None, leaves=False):
     filters = proj.shape[-1]
-    arrays = [near, far, cots] + ([arrived] if folded else [])
+    first_gate = cots is None
+    arrays = [near, far] + ([] if first_gate else [cots]) + ([arrived] if folded else [])
     ins = [(a, a.shape, None) for a in arrays] + [(proj, (1, filters, filters), (branch, 0, 0))]
-    ins += [(a, a.shape, None) for a in ([mixed] if earlier is None else [mixed, earlier, *above])]
-    part = (2 * filters if above else filters, filters)
-    shapes = [(near.shape, BF16), (mixed.shape, F32), (part, F32)]
+    ins += [(a, a.shape, None) for a in ([mixed] if earlier is None else [mixed, earlier])]
+    part = (filters, filters)
+    shapes = [(near.shape[:3] + (2,) + near.shape[4:], BF16), (mixed.shape, F32), (part, F32)]
     if earlier is not None:
         shapes.append((part, BF16))
-    if above:
+    if first_gate:
+        shapes.append(((mixed.shape[0], 2) + mixed.shape[1:], BF16))
+        shapes.append(((mixed.shape[0] // 3, 2) + mixed.shape[1:], BF16))
+    if leaves:
         shapes.append(((mixed.shape[0] // 3,) + mixed.shape[1:], BF16))
     return call(
-        functools.partial(gate_kernel, branch, folded, bool(above)), place, 1, after, ins,
+        functools.partial(gate_kernel, branch, folded, first_gate), place, 1, after, ins,
         [(shape_of(shape, kind), shape, None) for shape, kind in shapes], f"gate_{branch}",
     )
 
@@ -277,6 +279,8 @@
     classes, group, cols, channels = x_ref.shape
     point_grad_ref, depth_ref, grads_ref = refs[-3:]
     refs = refs[:-3]
+    if chained:
+        mixed_ref, refs = refs[0], refs[1:]
     upper = place[1] == 0
     pre = whole_columns(place, own_ref[0], other_ref[0])
     grads = lax.dot_general(pre, point_ref[0], (((1,), (1,)), ((), ())), preferred_element_type=F32)
@@ -325,7 +329,8 @@
             totals.append(total)
         if chained:
             leaving_ref, stay_ref = outs[:2]
-            leaving_ref[r] = jnp.where(upper, totals[2], totals[0]).astype(BF16)
+            leaving_ref[r, :cols] = jnp.where(upper, totals[2], totals[0]).astype(BF16)
+            leaving_ref[r, cols:, : mixed_ref.shape[2]] = mixed_ref[r]
             stay_ref[0, r] = jnp.where(upper, totals[0], totals[1])
             stay_ref[1, r] = jnp.where(upper, totals[1], totals[2])
         else:
@@ -359,7 +364,8 @@
 
 
 def backward(
-    branch, folded, final, place, after, own, other, x, arrived, spread, taps, point, before=None, depths=()
+    branch, folded, final, place, after, own, other, x, arrived, spread, taps, point, before=None, depths=(),
+    mixed=None
 ):
     classes, residues, cols, channels = x.shape
     filters = point.shape[2]
@@ -370,7 +376,7 @@
     chained = before is not None
     if chained:
         outs = [
-            (shape_of(x.shape[1:], BF16), thin, 0),
+            (shape_of((residues, cols + cols // 4, channels), BF16), (group, cols + cols // 4, channels), 0),
             (pltpu.HBM((2,) + x.shape[1:], F32), (2,) + thin, 1),
         ]
     else:
@@ -395,6 +401,7 @@
             (point, (1, channels, filters), (branch, 0, 0)),
             (before, cell, 1) if chained else (x, small, None),
         ]
+        + ([(mixed, (group,) + mixed.shape[1:], 0)] if chained else [])
         + [(d, d.shape, None) for d in depths],
         outs, f"backward_{branch}",
         scratch=[
@@ -447,27 +454,26 @@
 
 
 def last_kernel(
-    place, pre_ref, point_ref, band_ref, stay_ref, arrived_ref, mixed_ref, folded_ref, mixed_arrived_ref,
-    input_ref, output_ref
+    place, pre_ref, point_ref, band_ref, stay_ref, arrived_ref, mixed_ref, folded_ref, input_ref, output_ref
 ):
     classes, group, cols, channels = band_ref.shape
     pre = pre_ref[...].reshape(classes * group * cols, -1)
     grads = lax.dot_general(pre, point_ref[0], (((1,), (1,)), ((), ())), preferred_element_type=F32)
     grads = grads.astype(BF16).astype(F32).reshape(band_ref.shape)
-    others = (stay_ref[0], arrived_ref[...].astype(F32), stay_ref[1])
+    others = (stay_ref[0], arrived_ref[:, :cols].astype(F32), stay_ref[1])
     for q in range(classes):
         input_ref[q] = (grads[q] + band_ref[q] + others[q]).astype(BF16)
     upper = place[1] == 0
     mixed = (
         jnp.where(upper, folded_ref[0], folded_ref[1]),
-        mixed_arrived_ref[...].astype(F32),
+        arrived_ref[:, cols:, : mixed_ref.shape[-1]].astype(F32),
         jnp.where(upper, folded_ref[1], folded_ref[2]),
     )
     for q in range(classes):
         output_ref[q] = (mixed_ref[q] + mixed[q]).astype(BF16)
 
 
-def last(place, after, pre, point, band, stay, arrived, mixed, folded, mixed_arrived):
+def last(place, after, pre, point, band, stay, arrived, mixed, folded):
     classes, residues, cols, channels = band.shape
     filters = point.shape[2]
     group = residues // STEPS
@@ -480,22 +486,21 @@
             (point, (1, channels, filters), (0, 0, 0)),
             (band, cell, 1),
             (stay, (2, group, cols, channels), 1),
-            (arrived, (group, cols, channels), 0),
+            (arrived, (group,) + arrived.shape[1:], 0),
             (mixed, thin, 1),
             (folded, thin, 1),
-            (mixed_arrived, thin[1:], 0),
         ],
         [(result_of(band.shape, BF16), cell, 1), (result_of(mixed.shape, BF16), thin, 1)], "last",
     )
 
 
 def add_kernel(scale, counts, place, *refs):
-    *terms, out_ref = refs
+    terms, out_ref = refs[: sum(counts)], refs[-1]
     at = 0
     for count in counts:
         group, terms = terms[:count], terms[count:]
         values = [ref[...].astype(F32) for ref in group]
-        total = values[0] + values[1]
+        total = sum(values[1:], values[0])
         if scale != 1.0:
             total = total * scale
         rows = group[0].shape[0]
@@ -503,17 +508,18 @@
         at += rows
 
 
-def add(name, place, after, groups, kind, scale=1.0):
+def add(name, place, after, groups, kind, scale=1.0, arrived=()):
     shape = (sum(group[0].shape[0] for group in groups), groups[0][0].shape[1])
     counts = [len(group) for group in groups]
     return call(
         functools.partial(add_kernel, scale, counts), place, 1, after,
-        [(a, a.shape, None) for group in groups for a in group],
+        [(a, a.shape, None) for group in groups for a in group]
+        + [(a, (1,) * (len(a.shape) - 2) + a.shape[-2:], None) for a in arrived],
         [(shape_of(shape, kind), shape, None)], name,
     )
 
 
-def finish_kernel(place, own30, far30, own1, far1, own2, far2, proj_ref, depth_ref, point_ref):
+def finish_kernel(place, own30, far30, own_proj, far_proj, own21, far21, proj_ref, depth_ref, point_ref):
     core = place[2] == 0
 
     def halves(own, far, first, count):
@@ -524,19 +530,20 @@
     filters = proj_ref.shape[1]
     half = channels // 2
     point_ref[3], point_ref[0] = halves(own30, far30, 0, channels)
-    point_ref[1, :half], point_ref[1, half:] = halves(own1, far1, 0, half)
-    proj_ref[3], proj_ref[0] = halves(own1, far1, half, filters)
-    proj_ref[1], proj_ref[2] = halves(own1, far1, half + filters, filters)
-    point_ref[2, :half], point_ref[2, half:] = halves(own2, far2, 0, half)
-    low, high = halves(own2, far2, half, 27)
+    proj_ref[3], proj_ref[0] = halves(own_proj, far_proj, 0, filters)
+    proj_ref[1], proj_ref[2] = halves(own_proj, far_proj, filters, filters)
+    point_ref[2, :half], point_ref[2, half:] = halves(own21, far21, 0, half)
+    low, high = halves(own21, far21, half, 27)
     for k in range(9):
         rows = slice(3 * k, 3 * k + 3)
         depth_ref[k // 3, k % 3, :, :filters] = low[rows]
         depth_ref[k // 3, k % 3, :, filters:] = high[rows]
-
-
-def finish(place, after, early, middle, late, channels, filters):
-    arrays = [*early, *middle, *late]
+    first = own21.shape[0] - half
+    point_ref[1, :half], point_ref[1, half:] = halves(own21, far21, first, half)
+
+
+def finish(place, after, early, proj, late, channels, filters):
+    arrays = [*early, *proj, *late]
     shapes = [(4, filters, filters), (3, 3, 3, channels), (4, channels, filters)]
     return call(
         finish_kernel, place, 1, after, [(a, a.shape, None) for a in arrays],
@@ -556,33 +563,37 @@
 
     weights = (depth_weights, point_weights)
     cot = cotangent[0]
-    cot_far = swap(cot, "chan", 2)
 
     token, blank = jnp.zeros(TOKEN, F32), jnp.zeros(cot.shape, F32)
-    keep3, keep0, send3, send0, spread3, x_leaving, token = forward(
-        (3, 0), False, place, token, in_hbm(x), x, in_hbm(depth_weights), in_hbm(point_weights)
-    )
-    sent3, sent0 = swap(send3, "chan", 1), swap(send0, "chan", 1)
+    keep3, send3, spread3, token = forward(
+        (3,), False, place, token, in_hbm(x), x, in_hbm(depth_weights), in_hbm(point_weights)
+    )
+    sent3 = swap(send3, "chan", 1)
+    keep0, send0, x_leaving, token = forward(
+        (0,), False, place, token, x, x, in_hbm(depth_weights), in_hbm(point_weights)
+    )
+    sent0 = swap(send0, "chan", 1)
     arrived = swap(x_leaving, "row", 1)
-    near3, token = near_sum("3", place, token, keep3, sent3)
+    near3, token = near_sum_cot("3", place, token, keep3, sent3, cot)
     far3 = swap(near3, "chan", 2)
     keep1, keep2, send1, send2, spread1, spread2, token = forward(
         (1, 2), True, place, token, x, arrived, *weights
     )
     sent1, sent2 = swap(send1, "chan", 1), swap(send2, "chan", 1)
-    near0, cots, cots_leaving, token = near_sum_cots("0", place, token, keep0, sent0, cot, cot_far)
+    near0, token = near_sum("0", place, token, keep0, sent0)
     far0 = swap(near0, "chan", 2)
+    grad3, band_mixed, proj3, cots, cots_leaving, token = gate(
+        3, False, place, token, near3, far3, None, None, proj_weights, blank
+    )
+    other3 = swap(grad3, "chan", 1)
     cots_arrived = swap(cots_leaving, "row", 1)
-    grad3, band_mixed, proj3, token = gate(
-        3, False, place, token, near3, far3, cots, None, proj_weights, blank
-    )
-    other3 = swap(grad3, "chan", 1)
     near1, token = near_sum("1", place, token, keep1, sent1)
     far1 = swap(near1, "chan", 2)
     grad0, band_mixed, proj_keep, proj_send, token = gate(
         0, False, place, token, near0, far0, cots, None, proj_weights, band_mixed, proj3
     )
     other0 = swap(grad0, "chan", 1)
+    proj30 = (proj_keep, swap(proj_send, "dp", 1))
     near2, token = near_sum("2", place, token, keep2, sent2)
     far2 = swap(near2, "chan", 2)
     grad1, class_mixed, proj1, token = gate(
@@ -596,49 +607,47 @@
     point30 = (point_keep, swap(point_send, "dp", 1))
     grad2, class_mixed, proj_keep, proj_send, mixed_leaving, token = gate(
         2, True, place, token, near2, far2, cots, cots_arrived, proj_weights, class_mixed, proj1,
-        (proj_keep, proj_send),
+        leaves=True,
     )
     other2 = swap(grad2, "chan", 1)
-    mixed_arrived = swap(mixed_leaving, "row", 1)
-    proj = (proj_keep, swap(proj_send, "dp", 1))
+    proj12 = (proj_keep, swap(proj_send, "dp", 1))
     total1, depth1, point_keep, point_send, token = backward(
         1, True, True, place, token, grad1, other1, x, arrived, spread1, *weights
     )
     point1 = (point_keep, swap(point_send, "dp", 1))
-    early, token = add("early_y", place, token, [point30], BF16)
+    proj, token = add("proj", place, token, [proj30, proj12], BF16)
+    proj = (proj, swap(proj, "chan", 1))
+    early, token = add("early_1", place, token, [point30], BF16)
     early = (early, swap(early, "row", 1))
     leaving, stay, late_keep, late_send, token = backward(
-        2, True, True, place, token, grad2, other2, x, arrived, spread2, *weights, before=total1,
-        depths=(depth1, depth3),
+        2, True, True, place, token, grad2, other2, x, arrived, spread2, *weights, before=in_hbm(total1),
+        depths=(depth1, depth3), mixed=mixed_leaving,
     )
     input_arrived = swap(leaving, "row", 1)
     late = (late_keep, swap(late_send, "dp", 1))
-    proj, token = add("proj", place, token, [proj], BF16)
-    proj = (proj, swap(proj, "chan", 1))
-    early, token = add("early_x", place, token, [early], BF16)
+    proj, token = add("proj_1", place, token, [proj], BF16)
+    proj = (proj, swap(proj, "row", 1))
+    early, token = add("early_2", place, token, [early], BF16)
     early = (early, swap(early, "dp", 2))
-    late, token = add("late_x", place, token, [late], BF16)
+    late, token = add("late_1", place, token, [late, point1], BF16)
     late = (late, swap(late, "dp", 2))
-    middle, token = add("middle_y", place, token, [point1, proj], BF16)
-    middle = (middle, swap(middle, "row", 1))
-    late, token = add("late_y", place, token, [late], BF16)
-    late = (late, swap(late, "row", 1))
     early, token = add("early", place, token, [early], F32, scale)
     early = (early, swap(early, "dp", 1))
-    middle, token = add("middle_x", place, token, [middle], BF16)
-    middle = (middle, swap(middle, "dp", 2))
-    late, token = add("late", place, token, [late], F32, scale)
-    late = (late, swap(late, "dp", 1))
+    late, token = add("late_2", place, token, [late], BF16)
+    late = (late, swap(late, "row", 1))
+    proj, token = add("proj_2", place, token, [proj], BF16)
+    proj = (proj, swap(proj, "dp", 2))
     bands = band_mixed.reshape((classes, n) + band_mixed.shape[1:])
     folds = class_mixed.reshape(bands.shape)
     grad_input, output, token = last(
-        place, token, pre0, point_weights, in_hbm(band), in_hbm(stay), input_arrived, bands, folds,
-        mixed_arrived,
-    )
-    middle, token = add("middle", place, token, [middle], F32, scale)
-    middle = (middle, swap(middle, "dp", 1))
+        place, token, pre0, point_weights, in_hbm(band), in_hbm(stay), input_arrived, bands, folds
+    )
+    proj, token = add("proj_sum", place, token, [proj], F32, scale)
+    proj = (proj, swap(proj, "dp", 1))
+    late, token = add("late", place, token, [late], F32, scale)
+    late = (late, swap(late, "dp", 1))
     grad_proj, grad_depth, grad_point, token = finish(
-        place, token, early, middle, late, channels, filters
+        place, token, early, proj, late, channels, filters
     )
     return (
         output.reshape(cotangent.shape), grad_input.reshape(features_in.shape), grad_depth, grad_point,

time: 141 us -> 134 us (0.950)
  waiting for transfers between devices: 62 us -> 49.5 us
  starting transfers between devices: 29.1 us -> 34.6 us
  Pallas kernels: 46.4 us -> 48.9 us
  local copies, waits for them, and re-layouts: 1.72 us -> 0.06 us
    ppermute x31 -> x30, waiting for transfers between devices: 62 us -> 49.5 us  [swap(): return lax.ppermute(value, axis, [(i, i ^ flip) for i in range(count)])]
    ppermute x31 -> x30, starting transfers between devices: 29.1 us -> 34.6 us  [swap(): return lax.ppermute(value, axis, [(i, i ^ flip) for i in range(count)])]
    pallas_call x26 -> x27, Pallas kernels: 46.4 us -> 48.9 us  [call(): pl.pallas_call(kernel, grid_spec=pltpu.PrefetchScalarGridSpec(num_scalar_...]
    unnamed x18 -> x16, local copies, waits for them, and re-layouts: 1.7 us -> 0.03 us
  transfers between devices with their start and end apart: 31 -> 30, of which waited for: 15 -> 12; matrix products, arithmetic and copies ran while one was open for 0% -> 0% of each run, Pallas kernels for 27% -> 31%
where the time goes in v4:
time: 134 us
  waiting for transfers between devices  49.5 us (37%)
  Pallas kernels  48.9 us (36%)
  starting transfers between devices  34.6 us (26%)
    ppermute x30, waiting for transfers between devices, swap(): return lax.ppermute(value, axis, [(i, i ^ flip) for i in range(count)])  49.5 us
    pallas_call x27, Pallas kernels, call(): pl.pallas_call(kernel, grid_spec=pltpu.PrefetchScalarGridSpec(num_scalar_...  48.9 us
    ppermute x30, starting transfers between devices, swap(): return lax.ppermute(value, axis, [(i, i ^ flip) for i in range(count)])  34.6 us
  transfers between devices with their start and end apart: 30, of which 12 were waited for; matrix products, arithmetic and copies ran while one was open for 0% of the time, Pallas kernels for 31%

profile of v4, /device:TPU:0, one launch (start us, length us, event | category | flops | bytes accessed | tf_op | source)
XLA Modules:
  0.0 134.1 jit_solution(7662203468199364198)
XLA Ops:
  0.7 3.9 %forward_3.1 = (f32[1,3,6,2,16,256]{5,4,3,2,1,0:T(8,128)S(1)}, bf16[1,3,6,2,16,256]{5,4,3,2,1,0:T(8,128)(2,1)S(1)}, bf16[3,6,64,512]{3,2,1,0:T(8,128)(2,1)}, f32[8,128]{1,0:T(8,128)S(1)}) custom-call(s32[3]{0:T(128)S(1)} %pad_add_fusion.place_ref, f32[8,128]{1,0:T(8,128)S(1)} %broadcast_in_dim.6.after_ref, bf16[3,6,64,512]{3,2,1,0:T(8,128)(2,1)} %bitcast.9, ...), custom_call_target="tpu_custom_call" | custom-call | flops 1 | bytes 1 | tf_op jit(solution)/shard_map/forward_3/pallas_call | solution.py:79
  4.6 3.0 %collective-permute-start = (bf16[1,3,6,2,16,256]{5,4,3,2,1,0:T(8,128)(2,1)S(1)}, bf16[1,3,6,2,16,256]{5,4,3,2,1,0:T(8,128)(2,1)S(1)}, u32[]{:S(2)}, u32[]{:S(2)}) collective-permute-start(bf16[1,3,6,2,16,256]{5,4,3,2,1,0:T(8,128)(2,1)S(1)} %get-tuple-element.96), channel_id=1, source_target_pairs={{0,4},{4,0},{8,12},{12,8},{1,5},{5,1},{9,13},{13,9},{2,6},{6,2},{1... | collective-permute-start | bytes 884744 | tf_op jit(solution)/shard_map/ppermute | solution.py:19
  7.6 2.3 %forward_0.1 = (f32[1,3,6,2,16,256]{5,4,3,2,1,0:T(8,128)S(1)}, bf16[1,3,6,2,16,256]{5,4,3,2,1,0:T(8,128)(2,1)S(1)}, bf16[6,64,512]{2,1,0:T(8,128)(2,1)S(1)}, f32[8,128]{1,0:T(8,128)S(1)}) custom-call(s32[3]{0:T(128)S(1)} %pad_add_fusion.place_ref, f32[8,128]{1,0:T(8,128)S(1)} %get-tuple-element.93.after_ref, bf16[3,6,64,512]{3,2,1,0:T(8,128)(2,1)S(1)} %bitcast.11, ...), custom_call_target="tpu_custom_call" | custom-call | flops 1 | bytes 1 | tf_op jit(solution)/shard_map/forward_0/pallas_call | solution.py:79
  10.0 1.6 %collective-permute-start.1 = (bf16[6,64,512]{2,1,0:T(8,128)(2,1)S(1)}, bf16[6,64,512]{2,1,0:T(8,128)(2,1)S(1)}, u32[]{:S(2)}, u32[]{:S(2)}) collective-permute-start(bf16[6,64,512]{2,1,0:T(8,128)(2,1)S(1)} %get-tuple-element.98), channel_id=1, source_target_pairs={{0,16},{16,0},{1,17},{17,1},{2,18},{18,2},{3,19},{19,3},{4,20},{20... | collective-permute-start | bytes 1179656 | tf_op jit(solution)/shard_map/ppermute | solution.py:19
  11.6 0.5 collective-permute-start.2
  12.0 3.5 %collective-permute-done.refs_1_ = bf16[1,3,6,2,16,256]{5,4,3,2,1,0:T(8,128)(2,1)S(1)} collective-permute-done((bf16[1,3,6,2,16,256]{5,4,3,2,1,0:T(8,128)(2,1)S(1)}, bf16[1,3,6,2,16,256]{5,4,3,2,1,0:T(8,128)(2,1)S(1)}, u32[]{:S(2)}, u32[]{:S(2)}) %collective-permute-start) | collective-permute-done | bytes 294944 | tf_op jit(solution)/shard_map/ppermute | solution.py:19
  15.5 0.6 near_3.1
  16.1 3.1 %collective-permute-start.3 = (bf16[1,3,6,3,16,256]{5,4,3,2,1,0:T(8,128)(2,1)S(1)}, bf16[1,3,6,3,16,256]{5,4,3,2,1,0:T(8,128)(2,1)S(1)}, u32[]{:S(2)}, u32[]{:S(2)}) collective-permute-start(bf16[1,3,6,3,16,256]{5,4,3,2,1,0:T(8,128)(2,1)S(1)} %get-tuple-element.103.refs_0_), channel_id=1, source_target_pairs={{0,8},{4,12},{8,0},{12,4},{1,9},{5,13},{9,1},{13,5},{2,10},{6,14},... | collective-permute-start | bytes 1327112 | tf_op jit(solution)/shard_map/ppermute | solution.py:19
  19.2 1.4 %collective-permute-done.1.refs_1_.refs_3_ = bf16[6,64,512]{2,1,0:T(8,128)(2,1)S(1)} collective-permute-done((bf16[6,64,512]{2,1,0:T(8,128)(2,1)S(1)}, bf16[6,64,512]{2,1,0:T(8,128)(2,1)S(1)}, u32[]{:S(2)}, u32[]{:S(2)}) %collective-permute-start.1) | collective-permute-done | bytes 393248 | tf_op jit(solution)/shard_map/ppermute | solution.py:19
  20.6 5.3 %forward_1_2.1 = (f32[1,3,6,2,16,256]{5,4,3,2,1,0:T(8,128)S(1)}, f32[1,3,6,2,16,256]{5,4,3,2,1,0:T(8,128)S(1)}, bf16[1,3,6,2,16,256]{5,4,3,2,1,0:T(8,128)(2,1)S(...) custom-call(s32[3]{0:T(128)S(1)} %pad_add_fusion.place_ref, ...), custom_call_target="tpu_custom_call" | custom-call | flops 1 | bytes 1 | tf_op jit(solution)/shard_map/forward_1_2/pallas_call | solution.py:79
  25.9 0.3 collective-permute-start.4
  26.2 0.6 near_0.1
  26.8 2.8 %collective-permute-start.5 = (bf16[1,3,6,2,16,256]{5,4,3,2,1,0:T(8,128)(2,1)S(1)}, bf16[1,3,6,2,16,256]{5,4,3,2,1,0:T(8,128)(2,1)S(1)}, u32[]{:S(2)}, u32[]{:S(2)}) collective-permute-start(bf16[1,3,6,2,16,256]{5,4,3,2,1,0:T(8,128)(2,1)S(1)} %get-tuple-element.108.refs_0_), channel_id=1, source_target_pairs={{0,8},{4,12},{8,0},{12,4},{1,9},{5,13},{9,1},{13,5},{2,10},{6,14},... | collective-permute-start | bytes 884744 | tf_op jit(solution)/shard_map/ppermute | solution.py:19
  29.6 1.6 %collective-permute-start.6 = (bf16[1,3,6,2,16,256]{5,4,3,2,1,0:T(8,128)(2,1)S(1)}, bf16[1,3,6,2,16,256]{5,4,3,2,1,0:T(8,128)(2,1)S(1)}, u32[]{:S(2)}, u32[]{:S(2)}) collective-permute-start(bf16[1,3,6,2,16,256]{5,4,3,2,1,0:T(8,128)(2,1)S(1)} %get-tuple-element.114), channel_id=1, source_target_pairs={{0,4},{4,0},{8,12},{12,8},{1,5},{5,1},{9,13},{13,9},{2,6},{6,2},{1... | collective-permute-start | bytes 884744 | tf_op jit(solution)/shard_map/ppermute | solution.py:19
  31.2 14.6 %collective-permute-done.3.refs_1_ = bf16[1,3,6,3,16,256]{5,4,3,2,1,0:T(8,128)(2,1)S(1)} collective-permute-done((bf16[1,3,6,3,16,256]{5,4,3,2,1,0:T(8,128)(2,1)S(1)}, bf16[1,3,6,3,16,256]{5,4,3,2,1,0:T(8,128)(2,1)S(1)}, u32[]{:S(2)}, u32[]{:S(2)}) %collective-permute-start.3) | collective-permute-done | bytes 442400 | tf_op jit(solution)/shard_map/ppermute | solution.py:19
  45.8 1.1 gate_3.1
  46.9 0.6 near_1.1
  47.6 4.3 %collective-permute-start.9 = (bf16[1,3,6,2,16,256]{5,4,3,2,1,0:T(8,128)(2,1)S(1)}, bf16[1,3,6,2,16,256]{5,4,3,2,1,0:T(8,128)(2,1)S(1)}, u32[]{:S(2)}, u32[]{:S(2)}) collective-permute-start(bf16[1,3,6,2,16,256]{5,4,3,2,1,0:T(8,128)(2,1)S(1)} %get-tuple-element.119.refs_0_), channel_id=1, source_target_pairs={{0,4},{4,0},{8,12},{12,8},{1,5},{5,1},{9,13},{13,9},{2,6},{6,2},{1... | collective-permute-start | bytes 884744 | tf_op jit(solution)/shard_map/ppermute | solution.py:19
  51.9 6.5 %collective-permute-done.5.refs_1_ = bf16[1,3,6,2,16,256]{5,4,3,2,1,0:T(8,128)(2,1)S(1)} collective-permute-done((bf16[1,3,6,2,16,256]{5,4,3,2,1,0:T(8,128)(2,1)S(1)}, bf16[1,3,6,2,16,256]{5,4,3,2,1,0:T(8,128)(2,1)S(1)}, u32[]{:S(2)}, u32[]{:S(2)}) %collective-permute-start.5) | collective-permute-done | bytes 294944 | tf_op jit(solution)/shard_map/ppermute | solution.py:19
  58.4 1.1 gate_0.1
  59.5 1.0 collective-permute-start.10
  60.5 0.6 near_2.1
  61.1 3.5 %collective-permute-start.11 = (bf16[1,3,6,2,16,256]{5,4,3,2,1,0:T(8,128)(2,1)S(1)}, bf16[1,3,6,2,16,256]{5,4,3,2,1,0:T(8,128)(2,1)S(1)}, u32[]{:S(2)}, u32[]{:S(2)}) collective-permute-start(bf16[1,3,6,2,16,256]{5,4,3,2,1,0:T(8,128)(2,1)S(1)} %get-tuple-element.125.refs_0_), channel_id=1, source_target_pairs={{0,8},{4,12},{8,0},{12,4},{1,9},{5,13},{9,1},{13,5},{2,10},{6,14},... | collective-permute-start | bytes 884744 | tf_op jit(solution)/shard_map/ppermute | solution.py:19
  64.6 1.5 %collective-permute-start.8 = (bf16[6,2,16,256]{3,2,1,0:T(8,128)(2,1)S(1)}, bf16[6,2,16,256]{3,2,1,0:T(8,128)(2,1)S(1)}, u32[]{:S(2)}, u32[]{:S(2)}) collective-permute-start(bf16[6,2,16,256]{3,2,1,0:T(8,128)(2,1)S(1)} %get-tuple-element.117), channel_id=1, source_target_pairs={{0,16},{16,0},{1,17},{17,1},{2,18},{18,2},{3,19},{19,3},{4,20},{20... | collective-permute-start | bytes 294920 | tf_op jit(solution)/shard_map/ppermute | solution.py:19
  66.1 3.1 %collective-permute-done.8.refs_3_ = bf16[6,2,16,256]{3,2,1,0:T(8,128)(2,1)S(1)} collective-permute-done((bf16[6,2,16,256]{3,2,1,0:T(8,128)(2,1)S(1)}, bf16[6,2,16,256]{3,2,1,0:T(8,128)(2,1)S(1)}, u32[]{:S(2)}, u32[]{:S(2)}) %collective-permute-start.8) | collective-permute-done | bytes 98336 | tf_op jit(solution)/shard_map/ppermute | solution.py:19
  69.2 1.0 gate_1.1
  70.3 0.1 collective-permute-start.12
  70.3 1.5 %collective-permute-done.9.refs_1_ = bf16[1,3,6,2,16,256]{5,4,3,2,1,0:T(8,128)(2,1)S(1)} collective-permute-done((bf16[1,3,6,2,16,256]{5,4,3,2,1,0:T(8,128)(2,1)S(1)}, bf16[1,3,6,2,16,256]{5,4,3,2,1,0:T(8,128)(2,1)S(1)}, u32[]{:S(2)}, u32[]{:S(2)}) %collective-permute-start.9) | collective-permute-done | bytes 294944 | tf_op jit(solution)/shard_map/ppermute | solution.py:19
  71.8 4.4 %backward_3.1 = (f32[3,6,64,512]{3,2,1,0:T(8,128)}, f32[512,256]{1,0:T(8,128)S(1)}, f32[9,512]{1,0:T(8,128)S(1)}, f32[8,128]{1,0:T(8,128)S(1)}) custom-call(s32[3]{0:T(128)S(1)} %pad_add_fusion.place_ref, f32[8,128]{1,0:T(8,128)S(1)} %get-tuple-element.118.after_ref, bf16[1,3,6,2,16,256]{5,4,3,2,1,0:T(8,128)(2,1)S(1)} %get-tuple-element.119.refs_0_, ...), custom_call_target="tpu_custom_call" | custom-call | flops 1 | bytes 1 | tf_op jit(solution)/shard_map/backward_3/pallas_call | solution.py:79
  76.2 1.9 %collective-permute-done.10.refs_1_ = bf16[1,3,6,2,16,256]{5,4,3,2,1,0:T(8,128)(2,1)S(1)} collective-permute-done((bf16[1,3,6,2,16,256]{5,4,3,2,1,0:T(8,128)(2,1)S(1)}, bf16[1,3,6,2,16,256]{5,4,3,2,1,0:T(8,128)(2,1)S(1)}, u32[]{:S(2)}, u32[]{:S(2)}) %collective-permute-start.10) | collective-permute-done | bytes 294944 | tf_op jit(solution)/shard_map/ppermute | solution.py:19
  78.2 1.7 %join.1 = (bf16[3,6,64,256]{3,2,1,0:T(8,128)(2,1)S(1)}, f32[512,256]{1,0:T(8,128)S(1)}, bf16[512,256]{1,0:T(8,128)(2,1)S(1)}, f32[8,128]{1,0:T(8,128)S(1)}) custom-call(s32[3]{0:T(128)S(1)} %pad_add_fusion.place_ref, f32[8,128]{1,0:T(8,128)S(1)} %get-tuple-element.121.after_ref, bf16[1,3,6,2,16,256]{5,4,3,2,1,0:T(8,128)(2,1)S(1)} %get-tuple-element.122.refs_0_, ...), custom_call_target="tpu_custom_call" | custom-call | flops 1 | bytes 1 | tf_op jit(solution)/shard_map/join/pallas_call | solution.py:79
  80.0 1.1 gate_2.1
  81.1 0.6 collective-permute-start.13
  81.7 0.1 collective-permute-start.14
  81.8 0.3 collective-permute-done.12.refs_1_
  82.1 6.3 %backward_1.1 = (f32[3,6,64,512]{3,2,1,0:T(8,128)}, f32[9,512]{1,0:T(8,128)S(1)}, f32[256,256]{1,0:T(8,128)S(1)}, bf16[256,256]{1,0:T(8,128)(2,1)S(1)}, f32[8,128]{1,0:T(8,128)S(1)}) custom-call(s32[3]{0:T(128)S(1)} %pad_add_fusion.place_ref, f32[8,128]{1,0:T(8,128)S(1)} %get-tuple-element.128.after_ref, ...), custom_call_target="tpu_custom_call" | custom-call | flops 1 | bytes 1 | tf_op jit(solution)/shard_map/backward_1/pallas_call | solution.py:79
  88.4 0.6 proj.1
  89.0 1.6 %collective-permute-start.17 = (bf16[512,256]{1,0:T(8,128)(2,1)S(1)}, bf16[512,256]{1,0:T(8,128)(2,1)S(1)}, u32[]{:S(2)}, u32[]{:S(2)}) collective-permute-start(bf16[512,256]{1,0:T(8,128)(2,1)S(1)} %get-tuple-element.147.refs_0_), channel_id=1, source_target_pairs={{0,4},{4,0},{8,12},{12,8},{1,5},{5,1},{9,13},{13,9},{2,6},{6,2},{1... | collective-permute-start | bytes 786440 | tf_op jit(solution)/shard_map/ppermute | solution.py:19
  90.6 0.6 early_1.1
  91.2 1.4 %collective-permute-start.18 = (bf16[512,256]{1,0:T(8,128)(2,1)S(1)}, bf16[512,256]{1,0:T(8,128)(2,1)S(1)}, u32[]{:S(2)}, u32[]{:S(2)}) collective-permute-start(bf16[512,256]{1,0:T(8,128)(2,1)S(1)} %get-tuple-element.149.refs_0_), channel_id=1, source_target_pairs={{0,16},{16,0},{1,17},{17,1},{2,18},{18,2},{3,19},{19,3},{4,20},{20... | collective-permute-start | bytes 786440 | tf_op jit(solution)/shard_map/ppermute | solution.py:19
  92.7 6.0 %backward_2.1 = (bf16[6,80,512]{2,1,0:T(8,128)(2,1)S(1)}, f32[2,6,64,512]{3,2,1,0:T(8,128)}, f32[288,256]{1,0:T(8,128)S(1)}, bf16[288,256]{1,0:T(8,128)(2,1)S(1)}, f32[8,128]{1,0:T(8,128)S(1)}) custom-call(s32[3]{0:T(128)S(1)} %pad_add_fusion.place_ref, f32[8,128]{1,0:T(8,128)S(1)} %get-tuple-element.139.after_ref, ...), custom_call_target="tpu_custom_call" | custom-call | flops 1 | bytes 1 | tf_op jit(solution)/shard_map/backward_2/pallas_call | solution.py:79
  98.6 0.5 collective-permute-start.20
  99.2 0.6 proj_1.1
  99.8 0.6 early_2.1
  100.4 0.6 late_1.1
  101.0 1.6 %collective-permute-start.22 = (bf16[544,256]{1,0:T(8,128)(2,1)S(1)}, bf16[544,256]{1,0:T(8,128)(2,1)S(1)}, u32[]{:S(2)}, u32[]{:S(2)}) collective-permute-start(bf16[544,256]{1,0:T(8,128)(2,1)S(1)} %get-tuple-element.158.refs_0_), channel_id=1, source_target_pairs={{0,2},{1,3},{2,0},{3,1},{4,6},{5,7},{6,4},{7,5},{8,10},{9,11},{10,... | collective-permute-start | bytes 835592 | tf_op jit(solution)/shard_map/ppermute | solution.py:19
  102.6 0.5 collective-permute-start.21
  103.1 1.0 collective-permute-start.23
  104.1 1.0 collective-permute-start.24
  105.1 10.2 %collective-permute-done.21.refs_1_ = bf16[512,256]{1,0:T(8,128)(2,1)S(1)} collective-permute-done((bf16[512,256]{1,0:T(8,128)(2,1)S(1)}, bf16[512,256]{1,0:T(8,128)(2,1)S(1)}, u32[]{:S(2)}, u32[]{:S(2)}) %collective-permute-start.21) | collective-permute-done | bytes 262176 | tf_op jit(solution)/shard_map/ppermute | solution.py:19
  115.4 0.6 early.1
  116.0 0.6 late_2.1
  116.6 0.7 collective-permute-start.26
  117.3 0.6 proj_2.1
  117.9 1.4 %collective-permute-start.25 = (bf16[512,256]{1,0:T(8,128)(2,1)S(1)}, bf16[512,256]{1,0:T(8,128)(2,1)S(1)}, u32[]{:S(2)}, u32[]{:S(2)}) collective-permute-start(bf16[512,256]{1,0:T(8,128)(2,1)S(1)} %get-tuple-element.171.refs_0_), channel_id=1, source_target_pairs={{0,2},{1,3},{2,0},{3,1},{4,6},{5,7},{6,4},{7,5},{8,10},{9,11},{10,... | collective-permute-start | bytes 786440 | tf_op jit(solution)/shard_map/ppermute | solution.py:19
  119.3 3.5 %collective-permute-done.24.refs_4_ = bf16[6,80,512]{2,1,0:T(8,128)(2,1)S(1)} collective-permute-done((bf16[6,80,512]{2,1,0:T(8,128)(2,1)S(1)}, bf16[6,80,512]{2,1,0:T(8,128)(2,1)S(1)}, u32[]{:S(2)}, u32[]{:S(2)}) %collective-permute-start.24) | collective-permute-done | bytes 491552 | tf_op jit(solution)/shard_map/ppermute | solution.py:19
  122.9 3.9 %last.1 = (bf16[3,6,64,512]{3,2,1,0:T(8,128)(2,1)}, bf16[3,6,16,256]{3,2,1,0:T(8,128)(2,1)}, f32[8,128]{1,0:T(8,128)S(1)}) custom-call(s32[3]{0:T(128)S(1)} %pad_add_fusion.place_ref, f32[8,128]{1,0:T(8,128)S(1)} %get-tuple-element.161.after_ref, bf16[3,6,64,256]{3,2,1,0:T(8,128)(2,1)S(1)} %get-tuple-element.162.refs_0_, bf16[4,512,256]{2,1,0:T(8,128)(2,1)S(1)} %copy-done.1, ...), custom_call_target="tpu_custom_call" | custom-call | flops 1 | bytes 1 | tf_op jit(solution)/shard_map/last/pallas_call | solution.py:79
  126.8 0.6 proj_sum.1
  127.4 0.6 late.1
  128.1 0.5 collective-permute-start.27
  128.6 0.1 collective-permute-start.28
  128.7 2.1 %collective-permute-done.27.refs_1_ = f32[512,256]{1,0:T(8,128)S(1)} collective-permute-done((f32[512,256]{1,0:T(8,128)S(1)}, f32[512,256]{1,0:T(8,128)S(1)}, u32[]{:S(2)}, u32[]{:S(2)}) %collective-permute-start.27) | collective-permute-done | bytes 524320 | tf_op jit(solution)/shard_map/ppermute | solution.py:19
  130.8 0.7 collective-permute-done.28.refs_3_
  131.6 2.5 %finish.1 = (f32[4,256,256]{2,1,0:T(8,128)}, f32[3,3,3,512]{3,2,1,0:T(4,128)}, f32[4,512,256]{2,1,0:T(8,128)}, f32[8,128]{1,0:T(8,128)}) custom-call(s32[3]{0:T(128)S(1)} %pad_add_fusion.place_ref, f32[8,128]{1,0:T(8,128)S(1)} %get-tuple-element.174.after_ref, f32[512,256]{1,0:T(8,128)S(1)} %get-tuple-element.175.refs_0_, ...), custom_call_target="tpu_custom_call" | custom-call | flops 1 | bytes 1 | tf_op jit(solution)/shard_map/finish/pallas_call | solution.py:79
  (42 shorter events, 0.5 us)
Async XLA Ops:
  0.7 6.9 %copy-start = (bf16[1,18,64,512]{3,2,1,0:T(8,128)(2,1)S(1)}, bf16[1,18,64,512]{3,2,1,0:T(8,128)(2,1)}, u32[]{:S(2)}) copy-start(bf16[1,18,64,512]{3,2,1,0:T(8,128)(2,1)} %param.5) | copy-start | bytes 3538948
  4.6 10.9 %collective-permute-start = (bf16[1,3,6,2,16,256]{5,4,3,2,1,0:T(8,128)(2,1)S(1)}, bf16[1,3,6,2,16,256]{5,4,3,2,1,0:T(8,128)(2,1)S(1)}, u32[]{:S(2)}, u32[]{:S(2)}) collective-permute-start(bf16[1,3,6,2,16,256]{5,4,3,2,1,0:T(8,128)(2,1)S(1)} %get-tuple-element.96), channel_id=1, source_target_pairs={{0,4},{4,0},{8,12},{12,8},{1,5},{5,1},{9,13},{13,9},{2,6},{6,2},{1... | collective-permute-start | bytes 884744 | tf_op jit(solution)/shard_map/ppermute | solution.py:19
  7.6 7.8 %copy-start.7 = (bf16[1,18,16,256]{3,2,1,0:T(8,128)(2,1)S(1)}, bf16[1,18,16,256]{3,2,1,0:T(8,128)(2,1)}, u32[]{:S(2)}) copy-start(bf16[1,18,16,256]{3,2,1,0:T(8,128)(2,1)} %param.9) | copy-start | bytes 442372
  7.6 13.0 %copy-start.3 = (bf16[3,3,3,512]{3,2,1,0:T(4,128)(2,1)S(1)}, bf16[3,3,3,512]{3,2,1,0:T(4,128)(2,1)}, u32[]{:S(2)}) copy-start(bf16[3,3,3,512]{3,2,1,0:T(4,128)(2,1)} %refs_5_.5) | copy-start | bytes 82948
  10.0 10.7 %copy-start.1 = (bf16[4,512,256]{2,1,0:T(8,128)(2,1)S(1)}, bf16[4,512,256]{2,1,0:T(8,128)(2,1)}, u32[]{:S(2)}) copy-start(bf16[4,512,256]{2,1,0:T(8,128)(2,1)} %refs_1_.1) | copy-start | bytes 3145732
  10.0 10.6 %collective-permute-start.1 = (bf16[6,64,512]{2,1,0:T(8,128)(2,1)S(1)}, bf16[6,64,512]{2,1,0:T(8,128)(2,1)S(1)}, u32[]{:S(2)}, u32[]{:S(2)}) collective-permute-start(bf16[6,64,512]{2,1,0:T(8,128)(2,1)S(1)} %get-tuple-element.98), channel_id=1, source_target_pairs={{0,16},{16,0},{1,17},{17,1},{2,18},{18,2},{3,19},{19,3},{4,20},{20... | collective-permute-start | bytes 1179656 | tf_op jit(solution)/shard_map/ppermute | solution.py:19
  11.6 14.7 %collective-permute-start.2 = (bf16[1,3,6,2,16,256]{5,4,3,2,1,0:T(8,128)(2,1)S(1)}, bf16[1,3,6,2,16,256]{5,4,3,2,1,0:T(8,128)(2,1)S(1)}, u32[]{:S(2)}, u32[]{:S(2)}) collective-permute-start(bf16[1,3,6,2,16,256]{5,4,3,2,1,0:T(8,128)(2,1)S(1)} %get-tuple-element.101), channel_id=1, source_target_pairs={{0,4},{4,0},{8,12},{12,8},{1,5},{5,1},{9,13},{13,9},{2,6},{6,2},{1... | collective-permute-start | bytes 884744 | tf_op jit(solution)/shard_map/ppermute | solution.py:19
  16.1 29.7 %collective-permute-start.3 = (bf16[1,3,6,3,16,256]{5,4,3,2,1,0:T(8,128)(2,1)S(1)}, bf16[1,3,6,3,16,256]{5,4,3,2,1,0:T(8,128)(2,1)S(1)}, u32[]{:S(2)}, u32[]{:S(2)}) collective-permute-start(bf16[1,3,6,3,16,256]{5,4,3,2,1,0:T(8,128)(2,1)S(1)} %get-tuple-element.103.refs_0_), channel_id=1, source_target_pairs={{0,8},{4,12},{8,0},{12,4},{1,9},{5,13},{9,1},{13,5},{2,10},{6,14},... | collective-permute-start | bytes 1327112 | tf_op jit(solution)/shard_map/ppermute | solution.py:19
  25.9 19.9 %copy-start.2 = (bf16[4,256,256]{2,1,0:T(8,128)(2,1)S(1)}, bf16[4,256,256]{2,1,0:T(8,128)(2,1)}, u32[]{:S(2)}) copy-start(bf16[4,256,256]{2,1,0:T(8,128)(2,1)} %refs_4_.5) | copy-start | bytes 1572868
  25.9 21.0 %collective-permute-start.4 = (bf16[1,3,6,2,16,256]{5,4,3,2,1,0:T(8,128)(2,1)S(1)}, bf16[1,3,6,2,16,256]{5,4,3,2,1,0:T(8,128)(2,1)S(1)}, u32[]{:S(2)}, u32[]{:S(2)}) collective-permute-start(bf16[1,3,6,2,16,256]{5,4,3,2,1,0:T(8,128)(2,1)S(1)} %get-tuple-element.106), channel_id=1, source_target_pairs={{0,4},{4,0},{8,12},{12,8},{1,5},{5,1},{9,13},{13,9},{2,6},{6,2},{1... | collective-permute-start | bytes 884744 | tf_op jit(solution)/shard_map/ppermute | solution.py:19
  26.8 31.6 %collective-permute-start.5 = (bf16[1,3,6,2,16,256]{5,4,3,2,1,0:T(8,128)(2,1)S(1)}, bf16[1,3,6,2,16,256]{5,4,3,2,1,0:T(8,128)(2,1)S(1)}, u32[]{:S(2)}, u32[]{:S(2)}) collective-permute-start(bf16[1,3,6,2,16,256]{5,4,3,2,1,0:T(8,128)(2,1)S(1)} %get-tuple-element.108.refs_0_), channel_id=1, source_target_pairs={{0,8},{4,12},{8,0},{12,4},{1,9},{5,13},{9,1},{13,5},{2,10},{6,14},... | collective-permute-start | bytes 884744 | tf_op jit(solution)/shard_map/ppermute | solution.py:19
  29.6 30.8 %collective-permute-start.6 = (bf16[1,3,6,2,16,256]{5,4,3,2,1,0:T(8,128)(2,1)S(1)}, bf16[1,3,6,2,16,256]{5,4,3,2,1,0:T(8,128)(2,1)S(1)}, u32[]{:S(2)}, u32[]{:S(2)}) collective-permute-start(bf16[1,3,6,2,16,256]{5,4,3,2,1,0:T(8,128)(2,1)S(1)} %get-tuple-element.114), channel_id=1, source_target_pairs={{0,4},{4,0},{8,12},{12,8},{1,5},{5,1},{9,13},{13,9},{2,6},{6,2},{1... | collective-permute-start | bytes 884744 | tf_op jit(solution)/shard_map/ppermute | solution.py:19
  47.5 21.7 %collective-permute-start.7 = (bf16[1,3,6,2,16,256]{5,4,3,2,1,0:T(8,128)(2,1)S(1)}, bf16[1,3,6,2,16,256]{5,4,3,2,1,0:T(8,128)(2,1)S(1)}, u32[]{:S(2)}, u32[]{:S(2)}) collective-permute-start(bf16[1,3,6,2,16,256]{5,4,3,2,1,0:T(8,128)(2,1)S(1)} %get-tuple-element.116.refs_0_), channel_id=1, source_target_pairs={{0,8},{4,12},{8,0},{12,4},{1,9},{5,13},{9,1},{13,5},{2,10},{6,14},... | collective-permute-start | bytes 884744 | tf_op jit(solution)/shard_map/ppermute | solution.py:19
  47.6 24.2 %collective-permute-start.9 = (bf16[1,3,6,2,16,256]{5,4,3,2,1,0:T(8,128)(2,1)S(1)}, bf16[1,3,6,2,16,256]{5,4,3,2,1,0:T(8,128)(2,1)S(1)}, u32[]{:S(2)}, u32[]{:S(2)}) collective-permute-start(bf16[1,3,6,2,16,256]{5,4,3,2,1,0:T(8,128)(2,1)S(1)} %get-tuple-element.119.refs_0_), channel_id=1, source_target_pairs={{0,4},{4,0},{8,12},{12,8},{1,5},{5,1},{9,13},{13,9},{2,6},{6,2},{1... | collective-permute-start | bytes 884744 | tf_op jit(solution)/shard_map/ppermute | solution.py:19
  59.5 18.7 %collective-permute-start.10 = (bf16[1,3,6,2,16,256]{5,4,3,2,1,0:T(8,128)(2,1)S(1)}, bf16[1,3,6,2,16,256]{5,4,3,2,1,0:T(8,128)(2,1)S(1)}, u32[]{:S(2)}, u32[]{:S(2)}) collective-permute-start(bf16[1,3,6,2,16,256]{5,4,3,2,1,0:T(8,128)(2,1)S(1)} %get-tuple-element.122.refs_0_), channel_id=1, source_target_pairs={{0,4},{4,0},{8,12},{12,8},{1,5},{5,1},{9,13},{13,9},{2,6},{6,2},{1... | collective-permute-start | bytes 884744 | tf_op jit(solution)/shard_map/ppermute | solution.py:19
  60.5 11.4 %copy-start.4 = (bf16[3,6,64,512]{3,2,1,0:T(8,128)(2,1)S(1)}, bf16[3,6,64,512]{3,2,1,0:T(8,128)(2,1)}, u32[]{:S(2)}) copy-start(bf16[3,6,64,512]{3,2,1,0:T(8,128)(2,1)} %get-tuple-element.120.refs_4_) | copy-start | bytes 3538948
  61.1 18.9 %collective-permute-start.11 = (bf16[1,3,6,2,16,256]{5,4,3,2,1,0:T(8,128)(2,1)S(1)}, bf16[1,3,6,2,16,256]{5,4,3,2,1,0:T(8,128)(2,1)S(1)}, u32[]{:S(2)}, u32[]{:S(2)}) collective-permute-start(bf16[1,3,6,2,16,256]{5,4,3,2,1,0:T(8,128)(2,1)S(1)} %get-tuple-element.125.refs_0_), channel_id=1, source_target_pairs={{0,8},{4,12},{8,0},{12,4},{1,9},{5,13},{9,1},{13,5},{2,10},{6,14},... | collective-permute-start | bytes 884744 | tf_op jit(solution)/shard_map/ppermute | solution.py:19
  64.6 4.6 %collective-permute-start.8 = (bf16[6,2,16,256]{3,2,1,0:T(8,128)(2,1)S(1)}, bf16[6,2,16,256]{3,2,1,0:T(8,128)(2,1)S(1)}, u32[]{:S(2)}, u32[]{:S(2)}) collective-permute-start(bf16[6,2,16,256]{3,2,1,0:T(8,128)(2,1)S(1)} %get-tuple-element.117), channel_id=1, source_target_pairs={{0,16},{16,0},{1,17},{17,1},{2,18},{18,2},{3,19},{19,3},{4,20},{20... | collective-permute-start | bytes 294920 | tf_op jit(solution)/shard_map/ppermute | solution.py:19
  70.3 11.8 %collective-permute-start.12 = (bf16[1,3,6,2,16,256]{5,4,3,2,1,0:T(8,128)(2,1)S(1)}, bf16[1,3,6,2,16,256]{5,4,3,2,1,0:T(8,128)(2,1)S(1)}, u32[]{:S(2)}, u32[]{:S(2)}) collective-permute-start(bf16[1,3,6,2,16,256]{5,4,3,2,1,0:T(8,128)(2,1)S(1)} %get-tuple-element.129.refs_0_), channel_id=1, source_target_pairs={{0,4},{4,0},{8,12},{12,8},{1,5},{5,1},{9,13},{13,9},{2,6},{6,2},{1... | collective-permute-start | bytes 884744 | tf_op jit(solution)/shard_map/ppermute | solution.py:19
  79.9 2.2 %copy-start.6 = (bf16[3,6,64,512]{3,2,1,0:T(8,128)(2,1)S(1)}, bf16[3,6,64,512]{3,2,1,0:T(8,128)(2,1)}, u32[]{:S(2)}) copy-start(bf16[3,6,64,512]{3,2,1,0:T(8,128)(2,1)} %get-tuple-element.130.refs_4_) | copy-start | bytes 3538948
  79.9 10.7 %collective-permute-start.15 = (bf16[512,256]{1,0:T(8,128)(2,1)S(1)}, bf16[512,256]{1,0:T(8,128)(2,1)S(1)}, u32[]{:S(2)}, u32[]{:S(2)}) collective-permute-start(bf16[512,256]{1,0:T(8,128)(2,1)S(1)} %get-tuple-element.138), channel_id=1, source_target_pairs={{0,1},{1,0},{2,3},{3,2},{4,5},{5,4},{6,7},{7,6},{8,9},{9,8},{10,11... | collective-permute-start | bytes 786440 | tf_op jit(solution)/shard_map/ppermute | solution.py:19
  81.1 11.6 %collective-permute-start.16 = (bf16[1,3,6,2,16,256]{5,4,3,2,1,0:T(8,128)(2,1)S(1)}, bf16[1,3,6,2,16,256]{5,4,3,2,1,0:T(8,128)(2,1)S(1)}, u32[]{:S(2)}, u32[]{:S(2)}) collective-permute-start(bf16[1,3,6,2,16,256]{5,4,3,2,1,0:T(8,128)(2,1)S(1)} %get-tuple-element.140.refs_0_), channel_id=1, source_target_pairs={{0,4},{4,0},{8,12},{12,8},{1,5},{5,1},{9,13},{13,9},{2,6},{6,2},{1... | collective-permute-start | bytes 884744 | tf_op jit(solution)/shard_map/ppermute | solution.py:19
  81.1 7.2 %collective-permute-start.13 = (bf16[256,256]{1,0:T(8,128)(2,1)S(1)}, bf16[256,256]{1,0:T(8,128)(2,1)S(1)}, u32[]{:S(2)}, u32[]{:S(2)}) collective-permute-start(bf16[256,256]{1,0:T(8,128)(2,1)S(1)} %get-tuple-element.133), channel_id=1, source_target_pairs={{0,1},{1,0},{2,3},{3,2},{4,5},{5,4},{6,7},{7,6},{8,9},{9,8},{10,11... | collective-permute-start | bytes 393224 | tf_op jit(solution)/shard_map/ppermute | solution.py:19
  81.7 6.7 %collective-permute-start.14 = (bf16[256,256]{1,0:T(8,128)(2,1)S(1)}, bf16[256,256]{1,0:T(8,128)(2,1)S(1)}, u32[]{:S(2)}, u32[]{:S(2)}) collective-permute-start(bf16[256,256]{1,0:T(8,128)(2,1)S(1)} %get-tuple-element.135), channel_id=1, source_target_pairs={{0,1},{1,0},{2,3},{3,2},{4,5},{5,4},{6,7},{7,6},{8,9},{9,8},{10,11... | collective-permute-start | bytes 393224 | tf_op jit(solution)/shard_map/ppermute | solution.py:19
  88.4 4.3 %copy-start.5 = (bf16[3,6,64,512]{3,2,1,0:T(8,128)(2,1)S(1)}, bf16[3,6,64,512]{3,2,1,0:T(8,128)(2,1)}, u32[]{:S(2)}) copy-start(bf16[3,6,64,512]{3,2,1,0:T(8,128)(2,1)} %get-tuple-element.141.refs_4_) | copy-start | bytes 3538948
  89.0 10.2 %collective-permute-start.17 = (bf16[512,256]{1,0:T(8,128)(2,1)S(1)}, bf16[512,256]{1,0:T(8,128)(2,1)S(1)}, u32[]{:S(2)}, u32[]{:S(2)}) collective-permute-start(bf16[512,256]{1,0:T(8,128)(2,1)S(1)} %get-tuple-element.147.refs_0_), channel_id=1, source_target_pairs={{0,4},{4,0},{8,12},{12,8},{1,5},{5,1},{9,13},{13,9},{2,6},{6,2},{1... | collective-permute-start | bytes 786440 | tf_op jit(solution)/shard_map/ppermute | solution.py:19
  91.2 8.5 %collective-permute-start.18 = (bf16[512,256]{1,0:T(8,128)(2,1)S(1)}, bf16[512,256]{1,0:T(8,128)(2,1)S(1)}, u32[]{:S(2)}, u32[]{:S(2)}) collective-permute-start(bf16[512,256]{1,0:T(8,128)(2,1)S(1)} %get-tuple-element.149.refs_0_), channel_id=1, source_target_pairs={{0,16},{16,0},{1,17},{17,1},{2,18},{18,2},{3,19},{19,3},{4,20},{20... | collective-permute-start | bytes 786440 | tf_op jit(solution)/shard_map/ppermute | solution.py:19
  98.6 1.8 %collective-permute-start.19 = (bf16[288,256]{1,0:T(8,128)(2,1)S(1)}, bf16[288,256]{1,0:T(8,128)(2,1)S(1)}, u32[]{:S(2)}, u32[]{:S(2)}) collective-permute-start(bf16[288,256]{1,0:T(8,128)(2,1)S(1)} %get-tuple-element.152), channel_id=1, source_target_pairs={{0,1},{1,0},{2,3},{3,2},{4,5},{5,4},{6,7},{7,6},{8,9},{9,8},{10,11... | collective-permute-start | bytes 442376 | tf_op jit(solution)/shard_map/ppermute | solution.py:19
  98.6 1.7 %collective-permute-start.20 = (bf16[256,256]{1,0:T(8,128)(2,1)S(1)}, bf16[256,256]{1,0:T(8,128)(2,1)S(1)}, u32[]{:S(2)}, u32[]{:S(2)}) collective-permute-start(bf16[256,256]{1,0:T(8,128)(2,1)S(1)} %get-tuple-element.154), channel_id=1, source_target_pairs={{0,1},{1,0},{2,3},{3,2},{4,5},{5,4},{6,7},{7,6},{8,9},{9,8},{10,11... | collective-permute-start | bytes 393224 | tf_op jit(solution)/shard_map/ppermute | solution.py:19
  101.0 15.0 %collective-permute-start.22 = (bf16[544,256]{1,0:T(8,128)(2,1)S(1)}, bf16[544,256]{1,0:T(8,128)(2,1)S(1)}, u32[]{:S(2)}, u32[]{:S(2)}) collective-permute-start(bf16[544,256]{1,0:T(8,128)(2,1)S(1)} %get-tuple-element.158.refs_0_), channel_id=1, source_target_pairs={{0,2},{1,3},{2,0},{3,1},{4,6},{5,7},{6,4},{7,5},{8,10},{9,11},{10,... | collective-permute-start | bytes 835592 | tf_op jit(solution)/shard_map/ppermute | solution.py:19
  102.6 12.8 %collective-permute-start.21 = (bf16[512,256]{1,0:T(8,128)(2,1)S(1)}, bf16[512,256]{1,0:T(8,128)(2,1)S(1)}, u32[]{:S(2)}, u32[]{:S(2)}) collective-permute-start(bf16[512,256]{1,0:T(8,128)(2,1)S(1)} %get-tuple-element.156.refs_0_), channel_id=1, source_target_pairs={{0,2},{1,3},{2,0},{3,1},{4,6},{5,7},{6,4},{7,5},{8,10},{9,11},{10,... | collective-permute-start | bytes 786440 | tf_op jit(solution)/shard_map/ppermute | solution.py:19
  103.1 14.2 %collective-permute-start.23 = (bf16[512,256]{1,0:T(8,128)(2,1)S(1)}, bf16[512,256]{1,0:T(8,128)(2,1)S(1)}, u32[]{:S(2)}, u32[]{:S(2)}) collective-permute-start(bf16[512,256]{1,0:T(8,128)(2,1)S(1)} %get-tuple-element.160.refs_0_), channel_id=1, source_target_pairs={{0,16},{16,0},{1,17},{17,1},{2,18},{18,2},{3,19},{19,3},{4,20},{20... | collective-permute-start | bytes 786440 | tf_op jit(solution)/shard_map/ppermute | solution.py:19
  104.1 18.8 %collective-permute-start.24 = (bf16[6,80,512]{2,1,0:T(8,128)(2,1)S(1)}, bf16[6,80,512]{2,1,0:T(8,128)(2,1)S(1)}, u32[]{:S(2)}, u32[]{:S(2)}) collective-permute-start(bf16[6,80,512]{2,1,0:T(8,128)(2,1)S(1)} %get-tuple-element.165), channel_id=1, source_target_pairs={{0,16},{16,0},{1,17},{17,1},{2,18},{18,2},{3,19},{19,3},{4,20},{20... | collective-permute-start | bytes 1474568 | tf_op jit(solution)/shard_map/ppermute | solution.py:19
  116.6 10.8 %collective-permute-start.26 = (bf16[544,256]{1,0:T(8,128)(2,1)S(1)}, bf16[544,256]{1,0:T(8,128)(2,1)S(1)}, u32[]{:S(2)}, u32[]{:S(2)}) collective-permute-start(bf16[544,256]{1,0:T(8,128)(2,1)S(1)} %get-tuple-element.173.refs_0_), channel_id=1, source_target_pairs={{0,16},{16,0},{1,17},{17,1},{2,18},{18,2},{3,19},{19,3},{4,20},{20... | collective-permute-start | bytes 835592 | tf_op jit(solution)/shard_map/ppermute | solution.py:19
  117.9 8.8 %collective-permute-start.25 = (bf16[512,256]{1,0:T(8,128)(2,1)S(1)}, bf16[512,256]{1,0:T(8,128)(2,1)S(1)}, u32[]{:S(2)}, u32[]{:S(2)}) collective-permute-start(bf16[512,256]{1,0:T(8,128)(2,1)S(1)} %get-tuple-element.171.refs_0_), channel_id=1, source_target_pairs={{0,2},{1,3},{2,0},{3,1},{4,6},{5,7},{6,4},{7,5},{8,10},{9,11},{10,... | collective-permute-start | bytes 786440 | tf_op jit(solution)/shard_map/ppermute | solution.py:19
  128.0 3.5 %collective-permute-start.29 = (f32[544,256]{1,0:T(8,128)S(1)}, f32[544,256]{1,0:T(8,128)S(1)}, u32[]{:S(2)}, u32[]{:S(2)}) collective-permute-start(f32[544,256]{1,0:T(8,128)S(1)} %get-tuple-element.177.refs_4_), channel_id=1, source_target_pairs={{0,1},{1,0},{2,3},{3,2},{4,5},{5,4},{6,7},{7,6},{8,9},{9,8},{10,11... | collective-permute-start | bytes 1671176 | tf_op jit(solution)/shard_map/ppermute | solution.py:19
  128.1 2.7 %collective-permute-start.27 = (f32[512,256]{1,0:T(8,128)S(1)}, f32[512,256]{1,0:T(8,128)S(1)}, u32[]{:S(2)}, u32[]{:S(2)}) collective-permute-start(f32[512,256]{1,0:T(8,128)S(1)} %get-tuple-element.175.refs_0_), channel_id=1, source_target_pairs={{0,1},{1,0},{2,3},{3,2},{4,5},{5,4},{6,7},{7,6},{8,9},{9,8},{10,11... | collective-permute-start | bytes 1572872 | tf_op jit(solution)/shard_map/ppermute | solution.py:19
  128.6 2.9 %collective-permute-start.28 = (f32[512,256]{1,0:T(8,128)S(1)}, f32[512,256]{1,0:T(8,128)S(1)}, u32[]{:S(2)}, u32[]{:S(2)}) collective-permute-start(f32[512,256]{1,0:T(8,128)S(1)} %get-tuple-element.176.refs_2_), channel_id=1, source_target_pairs={{0,1},{1,0},{2,3},{3,2},{4,5},{5,4},{6,7},{7,6},{8,9},{9,8},{10,11... | collective-permute-start | bytes 1572872 | tf_op jit(solution)/shard_map/ppermute | solution.py:19

commit v5 on v4

--- a/solution.py
+++ b/solution.py
@@ -11,7 +11,7 @@
 BASE_DILATION = 12
 F32 = jnp.float32
 BF16 = jnp.bfloat16
-VMEM_BYTES = 16 * 2**20
+VMEM_BYTES = 28 * 2**20
 
 
 def swap(value, axis, flip):
@@ -20,13 +20,33 @@
 
 
 def moved(value, steps):
+    count, width = value.shape
     if steps == 0:
-        return value
-    count = value.shape[0]
-    rolled = pltpu.roll(value, (-steps) % count, 0)
-    place = lax.broadcasted_iota(jnp.int32, value.shape, 0)
-    inside = place < count - steps if steps > 0 else place >= -steps
-    return jnp.where(inside, rolled, 0.0)
+        return 0, value
+    far = abs(steps)
+    whole, rest = far // 8 * 8, far % 8
+    size = count - whole
+    if rest == 0:
+        return (0, value[whole:]) if steps > 0 else (whole, value[:size])
+    blank = jnp.zeros((8, width), value.dtype)
+    if steps > 0:
+        longer = jnp.concatenate([value[whole:], blank])
+        return 0, pltpu.roll(longer, size + 8 - rest, 0)[:size]
+    longer = jnp.concatenate([blank, value[:size]])
+    return whole, pltpu.roll(longer, rest, 0)[8:]
+
+
+def add_moved(total, value, steps):
+    if steps == 0:
+        return value if total is None else total + value
+    first, part = moved(value, steps)
+    after = first + part.shape[0]
+    pieces = [total[first:after] + part]
+    if first > 0:
+        pieces = [total[:first]] + pieces
+    if after < total.shape[0]:
+        pieces = pieces + [total[after:]]
+    return jnp.concatenate(pieces)
 
 
 def row_pairs(branch, classes):
@@ -59,7 +79,7 @@
 
 
 TOKEN = (8, 128)
-STEPS = 2
+STEPS = 1
 
 
 def call(body, place, grid, after, ins, outs, name, scratch=()):
@@ -108,15 +128,14 @@
         for branch, spread_ref in spreads.items():
             for q in range(classes):
                 total = None
-                for j in range(3):
+                for j in (1, 0, 2):
                     part = None
                     for out, i, source in row_pairs(branch, classes):
                         if out == q:
                             tap = taps_ref[branch - 1, i, j].astype(F32)
                             term = rows[source] * tap[None, :]
                             part = term if part is None else part + term
-                    part = moved(part, (j - 1) * branch * BASE_DILATION)
-                    total = part if total is None else total + part
+                    total = add_moved(total, part, (j - 1) * branch * BASE_DILATION)
                 spread_ref[q, r] = total.astype(BF16)
         return carry
 
@@ -142,7 +161,7 @@
     part_shape = (1, classes, residues, 2, cols // 4, filters)
     outs = [(shape_of(part_shape, F32), part, 2) for _ in branches]
     outs += [(shape_of(part_shape, BF16), part, 2) for _ in branches]
-    outs += [(pltpu.HBM(x.shape, BF16), cell, 1) for b in branches if b]
+    outs += [(shape_of(x.shape, BF16), cell, 1) for b in branches if b]
     if not branches[0]:
         outs += [(shape_of(x.shape[1:], BF16), (group, cols, channels), 0)]
     return call(
@@ -306,26 +325,28 @@
             rows = class_rows(upper, rows[0], rows[2], arrived_ref[r].astype(F32))
         grads = [grads_ref[q, r].astype(F32) for q in range(classes)]
         for j in range(3):
-            near = [moved(row, (j - 1) * branch * BASE_DILATION) for row in rows]
+            shifts = [moved(row, (j - 1) * branch * BASE_DILATION) for row in rows]
+            first, near = shifts[0][0], [part for _, part in shifts]
+            size = near[0].shape[0]
             for i in range(3):
                 part = None
                 for q, tap, source in pairs:
                     if tap == i:
-                        term = (near[source] * grads[q]).reshape(cols // 8, 8, channels).sum(axis=0)
+                        term = near[source] * grads[q][first : first + size]
+                        term = term.reshape(size // 8, 8, channels).sum(axis=0)
                         part = term if part is None else part + term
                 if part is not None:
                     depth_ref[i * 3 + j] += part
         totals = []
         for target in range(classes):
             total = before_ref[target, r] if chained else None
-            for j in range(3):
+            for j in (1, 0, 2):
                 part = None
                 for q, i, source in pairs:
                     if source == target:
                         term = grads[q] * taps_ref[branch - 1, i, j].astype(F32)[None, :]
                         part = term if part is None else part + term
-                part = moved(part, -(j - 1) * branch * BASE_DILATION)
-                total = part if total is None else total + part
+                total = add_moved(total, part, -(j - 1) * branch * BASE_DILATION)
             totals.append(total)
         if chained:
             leaving_ref, stay_ref = outs[:2]
@@ -377,10 +398,10 @@
     if chained:
         outs = [
             (shape_of((residues, cols + cols // 4, channels), BF16), (group, cols + cols // 4, channels), 0),
-            (pltpu.HBM((2,) + x.shape[1:], F32), (2,) + thin, 1),
+            (shape_of((2,) + x.shape[1:], F32), (2,) + thin, 1),
         ]
     else:
-        outs = [(pltpu.HBM(x.shape, F32), cell, 1)]
+        outs = [(shape_of(x.shape, F32), cell, 1)]
     halves = (channels // 2 + (32 if chained else 0), filters)
     shapes = [(channels, filters), (9, channels)]
     if final:
@@ -603,14 +624,14 @@
     band, point3, depth3, token = backward(
         3, False, False, place, token, grad3, other3, x, x, spread3, *weights
     )
-    pre0, point_keep, point_send, token = join(place, token, grad0, other0, x, point3)
-    point30 = (point_keep, swap(point_send, "dp", 1))
     grad2, class_mixed, proj_keep, proj_send, mixed_leaving, token = gate(
         2, True, place, token, near2, far2, cots, cots_arrived, proj_weights, class_mixed, proj1,
         leaves=True,
     )
     other2 = swap(grad2, "chan", 1)
     proj12 = (proj_keep, swap(proj_send, "dp", 1))
+    pre0, point_keep, point_send, token = join(place, token, grad0, other0, x, point3)
+    point30 = (point_keep, swap(point_send, "dp", 1))
     total1, depth1, point_keep, point_send, token = backward(
         1, True, True, place, token, grad1, other1, x, arrived, spread1, *weights
     )
@@ -620,32 +641,32 @@
     early, token = add("early_1", place, token, [point30], BF16)
     early = (early, swap(early, "row", 1))
     leaving, stay, late_keep, late_send, token = backward(
-        2, True, True, place, token, grad2, other2, x, arrived, spread2, *weights, before=in_hbm(total1),
+        2, True, True, place, token, grad2, other2, x, arrived, spread2, *weights, before=total1,
         depths=(depth1, depth3), mixed=mixed_leaving,
     )
     input_arrived = swap(leaving, "row", 1)
     late = (late_keep, swap(late_send, "dp", 1))
-    proj, token = add("proj_1", place, token, [proj], BF16)
+    proj, token = add("proj_1", place, token, [proj], BF16, arrived=[early[1]])
     proj = (proj, swap(proj, "row", 1))
+    late, token = add("late_1", place, token, [late, point1], BF16)
+    late = (late, swap(late, "dp", 2))
+    late, token = add("late_2", place, token, [late], BF16)
+    late = (late, swap(late, "row", 1))
     early, token = add("early_2", place, token, [early], BF16)
     early = (early, swap(early, "dp", 2))
-    late, token = add("late_1", place, token, [late, point1], BF16)
-    late = (late, swap(late, "dp", 2))
+    proj, token = add("proj_2", place, token, [proj], BF16)
+    proj = (proj, swap(proj, "dp", 2))
     early, token = add("early", place, token, [early], F32, scale)
     early = (early, swap(early, "dp", 1))
-    late, token = add("late_2", place, token, [late], BF16)
-    late = (late, swap(late, "row", 1))
-    proj, token = add("proj_2", place, token, [proj], BF16)
-    proj = (proj, swap(proj, "dp", 2))
+    proj, token = add("proj_sum", place, token, [proj], F32, scale)
+    proj = (proj, swap(proj, "dp", 1))
+    late, token = add("late", place, token, [late], F32, scale, arrived=[input_arrived])
+    late = (late, swap(late, "dp", 1))
     bands = band_mixed.reshape((classes, n) + band_mixed.shape[1:])
     folds = class_mixed.reshape(bands.shape)
     grad_input, output, token = last(
-        place, token, pre0, point_weights, in_hbm(band), in_hbm(stay), input_arrived, bands, folds
-    )
-    proj, token = add("proj_sum", place, token, [proj], F32, scale)
-    proj = (proj, swap(proj, "dp", 1))
-    late, token = add("late", place, token, [late], F32, scale)
-    late = (late, swap(late, "dp", 1))
+        place, token, pre0, point_weights, band, stay, input_arrived, bands, folds
+    )
     grad_proj, grad_depth, grad_point, token = finish(
         place, token, early, proj, late, channels, filters
     )

time: 134 us -> 128 us (0.955)
  Pallas kernels: 48.9 us -> 37 us
  waiting for transfers between devices: 49.5 us -> 54.4 us
    pallas_call x27, Pallas kernels: 48.9 us -> 37 us  [call(): pl.pallas_call(kernel, grid_spec=pltpu.PrefetchScalarGridSpec(num_scalar_...]
    ppermute x30, waiting for transfers between devices: 49.5 us -> 54.4 us  [swap(): return lax.ppermute(value, axis, [(i, i ^ flip) for i in range(count)])]
  transfers between devices with their start and end apart: 30 -> 30, of which waited for: 12 -> 16; matrix products, arithmetic and copies ran while one was open for 0% -> 0% of each run, Pallas kernels for 31% -> 24%
where the time goes in v5:
time: 128 us
  waiting for transfers between devices  54.4 us (42%)
  Pallas kernels  37 us (29%)
  starting transfers between devices  35.2 us (28%)
    ppermute x30, waiting for transfers between devices, swap(): return lax.ppermute(value, axis, [(i, i ^ flip) for i in range(count)])  54.4 us
    pallas_call x27, Pallas kernels, call(): pl.pallas_call(kernel, grid_spec=pltpu.PrefetchScalarGridSpec(num_scalar_...  37 us
    ppermute x30, starting transfers between devices, swap(): return lax.ppermute(value, axis, [(i, i ^ flip) for i in range(count)])  35.2 us
  transfers between devices with their start and end apart: 30, of which 16 were waited for; matrix products, arithmetic and copies ran while one was open for 0% of the time, Pallas kernels for 24%

profile of v5, /device:TPU:0, one launch (start us, length us, event | category | flops | bytes accessed | tf_op | source)
XLA Modules:
  0.0 127.6 jit_solution(15202124070233106952)
XLA Ops:
  0.7 3.0 %forward_3.1 = (f32[1,3,6,2,16,256]{5,4,3,2,1,0:T(8,128)S(1)}, bf16[1,3,6,2,16,256]{5,4,3,2,1,0:T(8,128)(2,1)S(1)}, bf16[3,6,64,512]{3,2,1,0:T(8,128)(2,1)S(1)}, f32[8,128]{1,0:T(8,128)S(1)}) custom-call(s32[3]{0:T(128)S(1)} %pad_add_fusion.place_ref, f32[8,128]{1,0:T(8,128)S(1)} %broadcast_in_dim.6.after_ref, bf16[3,6,64,512]{3,2,1,0:T(8,128)(2,1)} %bitcast.9, ...), custom_call_target="tpu_custom_call" | custom-call | flops 1 | bytes 1 | tf_op jit(solution)/shard_map/forward_3/pallas_call | solution.py:99
  3.7 3.1 %collective-permute-start = (bf16[1,3,6,2,16,256]{5,4,3,2,1,0:T(8,128)(2,1)S(1)}, bf16[1,3,6,2,16,256]{5,4,3,2,1,0:T(8,128)(2,1)S(1)}, u32[]{:S(2)}, u32[]{:S(2)}) collective-permute-start(bf16[1,3,6,2,16,256]{5,4,3,2,1,0:T(8,128)(2,1)S(1)} %get-tuple-element.96), channel_id=1, source_target_pairs={{0,4},{4,0},{8,12},{12,8},{1,5},{5,1},{9,13},{13,9},{2,6},{6,2},{1... | collective-permute-start | bytes 884744 | tf_op jit(solution)/shard_map/ppermute | solution.py:19
  6.8 2.0 %forward_0.1 = (f32[1,3,6,2,16,256]{5,4,3,2,1,0:T(8,128)S(1)}, bf16[1,3,6,2,16,256]{5,4,3,2,1,0:T(8,128)(2,1)S(1)}, bf16[6,64,512]{2,1,0:T(8,128)(2,1)S(1)}, f32[8,128]{1,0:T(8,128)S(1)}) custom-call(s32[3]{0:T(128)S(1)} %pad_add_fusion.place_ref, f32[8,128]{1,0:T(8,128)S(1)} %get-tuple-element.93.after_ref, bf16[3,6,64,512]{3,2,1,0:T(8,128)(2,1)S(1)} %bitcast.11, ...), custom_call_target="tpu_custom_call" | custom-call | flops 1 | bytes 1 | tf_op jit(solution)/shard_map/forward_0/pallas_call | solution.py:99
  8.8 1.6 %collective-permute-start.1 = (bf16[6,64,512]{2,1,0:T(8,128)(2,1)S(1)}, bf16[6,64,512]{2,1,0:T(8,128)(2,1)S(1)}, u32[]{:S(2)}, u32[]{:S(2)}) collective-permute-start(bf16[6,64,512]{2,1,0:T(8,128)(2,1)S(1)} %get-tuple-element.98), channel_id=1, source_target_pairs={{0,16},{16,0},{1,17},{17,1},{2,18},{18,2},{3,19},{19,3},{4,20},{20... | collective-permute-start | bytes 1179656 | tf_op jit(solution)/shard_map/ppermute | solution.py:19
  10.4 0.4 collective-permute-start.2
  10.8 3.8 %collective-permute-done.refs_1_ = bf16[1,3,6,2,16,256]{5,4,3,2,1,0:T(8,128)(2,1)S(1)} collective-permute-done((bf16[1,3,6,2,16,256]{5,4,3,2,1,0:T(8,128)(2,1)S(1)}, bf16[1,3,6,2,16,256]{5,4,3,2,1,0:T(8,128)(2,1)S(1)}, u32[]{:S(2)}, u32[]{:S(2)}) %collective-permute-start) | collective-permute-done | bytes 294944 | tf_op jit(solution)/shard_map/ppermute | solution.py:19
  14.6 0.6 near_3.1
  15.2 3.1 %collective-permute-start.3 = (bf16[1,3,6,3,16,256]{5,4,3,2,1,0:T(8,128)(2,1)S(1)}, bf16[1,3,6,3,16,256]{5,4,3,2,1,0:T(8,128)(2,1)S(1)}, u32[]{:S(2)}, u32[]{:S(2)}) collective-permute-start(bf16[1,3,6,3,16,256]{5,4,3,2,1,0:T(8,128)(2,1)S(1)} %get-tuple-element.103.refs_0_), channel_id=1, source_target_pairs={{0,8},{4,12},{8,0},{12,4},{1,9},{5,13},{9,1},{13,5},{2,10},{6,14},... | collective-permute-start | bytes 1327112 | tf_op jit(solution)/shard_map/ppermute | solution.py:19
  18.4 1.1 collective-permute-done.1.refs_1_.refs_3_
  19.4 3.6 %forward_1_2.1 = (f32[1,3,6,2,16,256]{5,4,3,2,1,0:T(8,128)S(1)}, f32[1,3,6,2,16,256]{5,4,3,2,1,0:T(8,128)S(1)}, bf16[1,3,6,2,16,256]{5,4,3,2,1,0:T(8,128)(2,1)S(...) custom-call(s32[3]{0:T(128)S(1)} %pad_add_fusion.place_ref, ...), custom_call_target="tpu_custom_call" | custom-call | flops 1 | bytes 1 | tf_op jit(solution)/shard_map/forward_1_2/pallas_call | solution.py:99
  23.1 0.6 collective-permute-start.4
  23.7 2.3 %collective-permute-done.2.refs_1_ = bf16[1,3,6,2,16,256]{5,4,3,2,1,0:T(8,128)(2,1)S(1)} collective-permute-done((bf16[1,3,6,2,16,256]{5,4,3,2,1,0:T(8,128)(2,1)S(1)}, bf16[1,3,6,2,16,256]{5,4,3,2,1,0:T(8,128)(2,1)S(1)}, u32[]{:S(2)}, u32[]{:S(2)}) %collective-permute-start.2) | collective-permute-done | bytes 294944 | tf_op jit(solution)/shard_map/ppermute | solution.py:19
  25.9 0.6 near_0.1
  26.6 0.3 collective-permute-start.5
  26.9 1.6 %collective-permute-start.6 = (bf16[1,3,6,2,16,256]{5,4,3,2,1,0:T(8,128)(2,1)S(1)}, bf16[1,3,6,2,16,256]{5,4,3,2,1,0:T(8,128)(2,1)S(1)}, u32[]{:S(2)}, u32[]{:S(2)}) collective-permute-start(bf16[1,3,6,2,16,256]{5,4,3,2,1,0:T(8,128)(2,1)S(1)} %get-tuple-element.114), channel_id=1, source_target_pairs={{0,4},{4,0},{8,12},{12,8},{1,5},{5,1},{9,13},{13,9},{2,6},{6,2},{1... | collective-permute-start | bytes 884744 | tf_op jit(solution)/shard_map/ppermute | solution.py:19
  28.4 16.5 %collective-permute-done.3.refs_1_ = bf16[1,3,6,3,16,256]{5,4,3,2,1,0:T(8,128)(2,1)S(1)} collective-permute-done((bf16[1,3,6,3,16,256]{5,4,3,2,1,0:T(8,128)(2,1)S(1)}, bf16[1,3,6,3,16,256]{5,4,3,2,1,0:T(8,128)(2,1)S(1)}, u32[]{:S(2)}, u32[]{:S(2)}) %collective-permute-start.3) | collective-permute-done | bytes 442400 | tf_op jit(solution)/shard_map/ppermute | solution.py:19
  45.0 1.0 gate_3.1
  46.0 0.6 near_1.1
  46.7 4.3 %collective-permute-start.9 = (bf16[1,3,6,2,16,256]{5,4,3,2,1,0:T(8,128)(2,1)S(1)}, bf16[1,3,6,2,16,256]{5,4,3,2,1,0:T(8,128)(2,1)S(1)}, u32[]{:S(2)}, u32[]{:S(2)}) collective-permute-start(bf16[1,3,6,2,16,256]{5,4,3,2,1,0:T(8,128)(2,1)S(1)} %get-tuple-element.119.refs_0_), channel_id=1, source_target_pairs={{0,4},{4,0},{8,12},{12,8},{1,5},{5,1},{9,13},{13,9},{2,6},{6,2},{1... | collective-permute-start | bytes 884744 | tf_op jit(solution)/shard_map/ppermute | solution.py:19
  51.0 6.6 %collective-permute-done.5.refs_1_ = bf16[1,3,6,2,16,256]{5,4,3,2,1,0:T(8,128)(2,1)S(1)} collective-permute-done((bf16[1,3,6,2,16,256]{5,4,3,2,1,0:T(8,128)(2,1)S(1)}, bf16[1,3,6,2,16,256]{5,4,3,2,1,0:T(8,128)(2,1)S(1)}, u32[]{:S(2)}, u32[]{:S(2)}) %collective-permute-start.5) | collective-permute-done | bytes 294944 | tf_op jit(solution)/shard_map/ppermute | solution.py:19
  57.5 1.0 gate_0.1
  58.6 0.6 near_2.1
  59.3 4.3 %collective-permute-start.11 = (bf16[1,3,6,2,16,256]{5,4,3,2,1,0:T(8,128)(2,1)S(1)}, bf16[1,3,6,2,16,256]{5,4,3,2,1,0:T(8,128)(2,1)S(1)}, u32[]{:S(2)}, u32[]{:S(2)}) collective-permute-start(bf16[1,3,6,2,16,256]{5,4,3,2,1,0:T(8,128)(2,1)S(1)} %get-tuple-element.126.refs_0_), channel_id=1, source_target_pairs={{0,4},{4,0},{8,12},{12,8},{1,5},{5,1},{9,13},{13,9},{2,6},{6,2},{1... | collective-permute-start | bytes 884744 | tf_op jit(solution)/shard_map/ppermute | solution.py:19
  63.6 1.5 %collective-permute-start.8 = (bf16[6,2,16,256]{3,2,1,0:T(8,128)(2,1)S(1)}, bf16[6,2,16,256]{3,2,1,0:T(8,128)(2,1)S(1)}, u32[]{:S(2)}, u32[]{:S(2)}) collective-permute-start(bf16[6,2,16,256]{3,2,1,0:T(8,128)(2,1)S(1)} %get-tuple-element.117), channel_id=1, source_target_pairs={{0,16},{16,0},{1,17},{17,1},{2,18},{18,2},{3,19},{19,3},{4,20},{20... | collective-permute-start | bytes 294920 | tf_op jit(solution)/shard_map/ppermute | solution.py:19
  65.1 3.1 %collective-permute-done.8.refs_3_ = bf16[6,2,16,256]{3,2,1,0:T(8,128)(2,1)S(1)} collective-permute-done((bf16[6,2,16,256]{3,2,1,0:T(8,128)(2,1)S(1)}, bf16[6,2,16,256]{3,2,1,0:T(8,128)(2,1)S(1)}, u32[]{:S(2)}, u32[]{:S(2)}) %collective-permute-start.8) | collective-permute-done | bytes 98336 | tf_op jit(solution)/shard_map/ppermute | solution.py:19
  68.2 2.0 %collective-permute-done.7.refs_1_ = bf16[1,3,6,2,16,256]{5,4,3,2,1,0:T(8,128)(2,1)S(1)} collective-permute-done((bf16[1,3,6,2,16,256]{5,4,3,2,1,0:T(8,128)(2,1)S(1)}, bf16[1,3,6,2,16,256]{5,4,3,2,1,0:T(8,128)(2,1)S(1)}, u32[]{:S(2)}, u32[]{:S(2)}) %collective-permute-start.7) | collective-permute-done | bytes 294944 | tf_op jit(solution)/shard_map/ppermute | solution.py:19
  70.2 1.0 gate_1.1
  71.3 1.0 collective-permute-start.12
  72.3 2.5 %backward_3.1 = (f32[3,6,64,512]{3,2,1,0:T(8,128)S(1)}, f32[512,256]{1,0:T(8,128)S(1)}, f32[9,512]{1,0:T(8,128)S(1)}, f32[8,128]{1,0:T(8,128)S(1)}) custom-call(s32[3]{0:T(128)S(1)} %pad_add_fusion.place_ref, f32[8,128]{1,0:T(8,128)S(1)} %get-tuple-element.118.after_ref, bf16[1,3,6,2,16,256]{5,4,3,2,1,0:T(8,128)(2,1)S(1)} %get-tuple-element.119.refs_0_, ...), custom_call_target="tpu_custom_call" | custom-call | flops 1 | bytes 1 | tf_op jit(solution)/shard_map/backward_3/pallas_call | solution.py:99
  74.8 1.1 gate_2.1
  75.9 1.1 join.1
  77.1 1.1 collective-permute-start.16
  78.4 0.3 collective-permute-start.14
  78.7 1.6 %collective-permute-done.12.refs_1_ = bf16[1,3,6,2,16,256]{5,4,3,2,1,0:T(8,128)(2,1)S(1)} collective-permute-done((bf16[1,3,6,2,16,256]{5,4,3,2,1,0:T(8,128)(2,1)S(1)}, bf16[1,3,6,2,16,256]{5,4,3,2,1,0:T(8,128)(2,1)S(1)}, u32[]{:S(2)}, u32[]{:S(2)}) %collective-permute-start.12) | collective-permute-done | bytes 294944 | tf_op jit(solution)/shard_map/ppermute | solution.py:19
  80.3 4.3 %backward_1.1 = (f32[3,6,64,512]{3,2,1,0:T(8,128)S(1)}, f32[9,512]{1,0:T(8,128)S(1)}, f32[256,256]{1,0:T(8,128)S(1)}, bf16[256,256]{1,0:T(8,128)(2,1)S(1)}, f32[8,128]{1,0:T(8,128)S(1)}) custom-call(s32[3]{0:T(128)S(1)} %pad_add_fusion.place_ref, f32[8,128]{1,0:T(8,128)S(1)} %get-tuple-element.128.after_ref, ...), custom_call_target="tpu_custom_call" | custom-call | flops 1 | bytes 1 | tf_op jit(solution)/shard_map/backward_1/pallas_call | solution.py:99
  84.7 0.6 proj.1
  85.3 0.6 early_1.1
  85.9 1.7 %collective-permute-start.18 = (bf16[512,256]{1,0:T(8,128)(2,1)S(1)}, bf16[512,256]{1,0:T(8,128)(2,1)S(1)}, u32[]{:S(2)}, u32[]{:S(2)}) collective-permute-start(bf16[512,256]{1,0:T(8,128)(2,1)S(1)} %get-tuple-element.148.refs_0_), channel_id=1, source_target_pairs={{0,16},{16,0},{1,17},{17,1},{2,18},{18,2},{3,19},{19,3},{4,20},{20... | collective-permute-start | bytes 786440 | tf_op jit(solution)/shard_map/ppermute | solution.py:19
  87.6 1.8 %collective-permute-start.17 = (bf16[512,256]{1,0:T(8,128)(2,1)S(1)}, bf16[512,256]{1,0:T(8,128)(2,1)S(1)}, u32[]{:S(2)}, u32[]{:S(2)}) collective-permute-start(bf16[512,256]{1,0:T(8,128)(2,1)S(1)} %get-tuple-element.147.refs_0_), channel_id=1, source_target_pairs={{0,4},{4,0},{8,12},{12,8},{1,5},{5,1},{9,13},{13,9},{2,6},{6,2},{1... | collective-permute-start | bytes 786440 | tf_op jit(solution)/shard_map/ppermute | solution.py:19
  89.3 3.2 %backward_2.1 = (bf16[6,80,512]{2,1,0:T(8,128)(2,1)S(1)}, f32[2,6,64,512]{3,2,1,0:T(8,128)S(1)}, f32[288,256]{1,0:T(8,128)S(1)}, bf16[288,256]{1,0:T(8,128)(2,1)S(1)}, f32[8,128]{1,0:T(8,128)S(1)}) custom-call(s32[3]{0:T(128)S(1)} %pad_add_fusion.place_ref, f32[8,128]{1,0:T(8,128)S(1)} %get-tuple-element.139.after_ref, ...), custom_call_target="tpu_custom_call" | custom-call | flops 1 | bytes 1 | tf_op jit(solution)/shard_map/backward_2/pallas_call | solution.py:99
  92.6 0.5 collective-permute-start.20
  93.2 1.5 %collective-permute-done.17.refs_1_ = bf16[512,256]{1,0:T(8,128)(2,1)S(1)} collective-permute-done((bf16[512,256]{1,0:T(8,128)(2,1)S(1)}, bf16[512,256]{1,0:T(8,128)(2,1)S(1)}, u32[]{:S(2)}, u32[]{:S(2)}) %collective-permute-start.17) | collective-permute-done | bytes 262176 | tf_op jit(solution)/shard_map/ppermute | solution.py:19
  94.6 0.6 proj_1.1
  95.2 0.6 late_1.1
  95.8 1.6 %collective-permute-start.21 = (bf16[544,256]{1,0:T(8,128)(2,1)S(1)}, bf16[544,256]{1,0:T(8,128)(2,1)S(1)}, u32[]{:S(2)}, u32[]{:S(2)}) collective-permute-start(bf16[544,256]{1,0:T(8,128)(2,1)S(1)} %get-tuple-element.155.refs_0_), channel_id=1, source_target_pairs={{0,2},{1,3},{2,0},{3,1},{4,6},{5,7},{6,4},{7,5},{8,10},{9,11},{10,... | collective-permute-start | bytes 835592 | tf_op jit(solution)/shard_map/ppermute | solution.py:19
  97.4 0.6 collective-permute-start.22
  98.0 1.5 %collective-permute-start.26 = (bf16[6,80,512]{2,1,0:T(8,128)(2,1)S(1)}, bf16[6,80,512]{2,1,0:T(8,128)(2,1)S(1)}, u32[]{:S(2)}, u32[]{:S(2)}) collective-permute-start(bf16[6,80,512]{2,1,0:T(8,128)(2,1)S(1)} %get-tuple-element.165), channel_id=1, source_target_pairs={{0,16},{16,0},{1,17},{17,1},{2,18},{18,2},{3,19},{19,3},{4,20},{20... | collective-permute-start | bytes 1474568 | tf_op jit(solution)/shard_map/ppermute | solution.py:19
  99.4 4.2 %collective-permute-done.21.refs_1_ = bf16[544,256]{1,0:T(8,128)(2,1)S(1)} collective-permute-done((bf16[544,256]{1,0:T(8,128)(2,1)S(1)}, bf16[544,256]{1,0:T(8,128)(2,1)S(1)}, u32[]{:S(2)}, u32[]{:S(2)}) %collective-permute-start.21) | collective-permute-done | bytes 278560 | tf_op jit(solution)/shard_map/ppermute | solution.py:19
  103.7 0.6 late_2.1
  104.3 1.2 collective-permute-start.25
  105.5 0.6 early_2.1
  106.1 0.9 collective-permute-start.23
  107.0 0.6 proj_2.1
  107.6 1.3 %collective-permute-start.24 = (bf16[512,256]{1,0:T(8,128)(2,1)S(1)}, bf16[512,256]{1,0:T(8,128)(2,1)S(1)}, u32[]{:S(2)}, u32[]{:S(2)}) collective-permute-start(bf16[512,256]{1,0:T(8,128)(2,1)S(1)} %get-tuple-element.162.refs_0_), channel_id=1, source_target_pairs={{0,2},{1,3},{2,0},{3,1},{4,6},{5,7},{6,4},{7,5},{8,10},{9,11},{10,... | collective-permute-start | bytes 786440 | tf_op jit(solution)/shard_map/ppermute | solution.py:19
  108.9 6.5 %collective-permute-done.23.refs_1_ = bf16[512,256]{1,0:T(8,128)(2,1)S(1)} collective-permute-done((bf16[512,256]{1,0:T(8,128)(2,1)S(1)}, bf16[512,256]{1,0:T(8,128)(2,1)S(1)}, u32[]{:S(2)}, u32[]{:S(2)}) %collective-permute-start.23) | collective-permute-done | bytes 262176 | tf_op jit(solution)/shard_map/ppermute | solution.py:19
  115.4 0.6 early.1
  116.0 2.8 %collective-permute-done.24.refs_1_ = bf16[512,256]{1,0:T(8,128)(2,1)S(1)} collective-permute-done((bf16[512,256]{1,0:T(8,128)(2,1)S(1)}, bf16[512,256]{1,0:T(8,128)(2,1)S(1)}, u32[]{:S(2)}, u32[]{:S(2)}) %collective-permute-start.24) | collective-permute-done | bytes 262176 | tf_op jit(solution)/shard_map/ppermute | solution.py:19
  118.8 0.6 proj_sum.1
  119.5 1.6 %collective-permute-done.25.refs_1_ = bf16[544,256]{1,0:T(8,128)(2,1)S(1)} collective-permute-done((bf16[544,256]{1,0:T(8,128)(2,1)S(1)}, bf16[544,256]{1,0:T(8,128)(2,1)S(1)}, u32[]{:S(2)}, u32[]{:S(2)}) %collective-permute-start.25) | collective-permute-done | bytes 278560 | tf_op jit(solution)/shard_map/ppermute | solution.py:19
  121.0 0.6 late.1
  121.7 0.5 collective-permute-start.28
  122.3 2.2 %last.1 = (bf16[3,6,64,512]{3,2,1,0:T(8,128)(2,1)}, bf16[3,6,16,256]{3,2,1,0:T(8,128)(2,1)}, f32[8,128]{1,0:T(8,128)S(1)}) custom-call(s32[3]{0:T(128)S(1)} %pad_add_fusion.place_ref, f32[8,128]{1,0:T(8,128)S(1)} %get-tuple-element.166.after_ref, bf16[3,6,64,256]{3,2,1,0:T(8,128)(2,1)S(1)} %get-tuple-element.167.refs_0_, bf16[4,512,256]{2,1,0:T(8,128)(2,1)S(1)} %copy-done.1, ...), custom_call_target="tpu_custom_call" | custom-call | flops 1 | bytes 1 | tf_op jit(solution)/shard_map/last/pallas_call | solution.py:99
  124.5 0.7 collective-permute-done.27.refs_1_
  125.2 2.5 %finish.1 = (f32[4,256,256]{2,1,0:T(8,128)}, f32[3,3,3,512]{3,2,1,0:T(4,128)}, f32[4,512,256]{2,1,0:T(8,128)}, f32[8,128]{1,0:T(8,128)}) custom-call(s32[3]{0:T(128)S(1)} %pad_add_fusion.place_ref, f32[8,128]{1,0:T(8,128)S(1)} %get-tuple-element.174.after_ref, f32[512,256]{1,0:T(8,128)S(1)} %get-tuple-element.175.refs_0_, ...), custom_call_target="tpu_custom_call" | custom-call | flops 1 | bytes 1 | tf_op jit(solution)/shard_map/finish/pallas_call | solution.py:99
  (36 shorter events, 0.9 us)
Async XLA Ops:
  0.7 6.0 %copy-start = (bf16[1,18,64,512]{3,2,1,0:T(8,128)(2,1)S(1)}, bf16[1,18,64,512]{3,2,1,0:T(8,128)(2,1)}, u32[]{:S(2)}) copy-start(bf16[1,18,64,512]{3,2,1,0:T(8,128)(2,1)} %param.5) | copy-start | bytes 3538948
  3.7 10.9 %collective-permute-start = (bf16[1,3,6,2,16,256]{5,4,3,2,1,0:T(8,128)(2,1)S(1)}, bf16[1,3,6,2,16,256]{5,4,3,2,1,0:T(8,128)(2,1)S(1)}, u32[]{:S(2)}, u32[]{:S(2)}) collective-permute-start(bf16[1,3,6,2,16,256]{5,4,3,2,1,0:T(8,128)(2,1)S(1)} %get-tuple-element.96), channel_id=1, source_target_pairs={{0,4},{4,0},{8,12},{12,8},{1,5},{5,1},{9,13},{13,9},{2,6},{6,2},{1... | collective-permute-start | bytes 884744 | tf_op jit(solution)/shard_map/ppermute | solution.py:19
  6.8 7.8 %copy-start.4 = (bf16[1,18,16,256]{3,2,1,0:T(8,128)(2,1)S(1)}, bf16[1,18,16,256]{3,2,1,0:T(8,128)(2,1)}, u32[]{:S(2)}) copy-start(bf16[1,18,16,256]{3,2,1,0:T(8,128)(2,1)} %param.9) | copy-start | bytes 442372
  6.8 12.7 %copy-start.3 = (bf16[3,3,3,512]{3,2,1,0:T(4,128)(2,1)S(1)}, bf16[3,3,3,512]{3,2,1,0:T(4,128)(2,1)}, u32[]{:S(2)}) copy-start(bf16[3,3,3,512]{3,2,1,0:T(4,128)(2,1)} %refs_5_.5) | copy-start | bytes 82948
  8.8 10.7 %copy-start.1 = (bf16[4,512,256]{2,1,0:T(8,128)(2,1)S(1)}, bf16[4,512,256]{2,1,0:T(8,128)(2,1)}, u32[]{:S(2)}) copy-start(bf16[4,512,256]{2,1,0:T(8,128)(2,1)} %refs_1_.1) | copy-start | bytes 3145732
  8.8 10.6 %collective-permute-start.1 = (bf16[6,64,512]{2,1,0:T(8,128)(2,1)S(1)}, bf16[6,64,512]{2,1,0:T(8,128)(2,1)S(1)}, u32[]{:S(2)}, u32[]{:S(2)}) collective-permute-start(bf16[6,64,512]{2,1,0:T(8,128)(2,1)S(1)} %get-tuple-element.98), channel_id=1, source_target_pairs={{0,16},{16,0},{1,17},{17,1},{2,18},{18,2},{3,19},{19,3},{4,20},{20... | collective-permute-start | bytes 1179656 | tf_op jit(solution)/shard_map/ppermute | solution.py:19
  10.4 15.6 %collective-permute-start.2 = (bf16[1,3,6,2,16,256]{5,4,3,2,1,0:T(8,128)(2,1)S(1)}, bf16[1,3,6,2,16,256]{5,4,3,2,1,0:T(8,128)(2,1)S(1)}, u32[]{:S(2)}, u32[]{:S(2)}) collective-permute-start(bf16[1,3,6,2,16,256]{5,4,3,2,1,0:T(8,128)(2,1)S(1)} %get-tuple-element.101), channel_id=1, source_target_pairs={{0,4},{4,0},{8,12},{12,8},{1,5},{5,1},{9,13},{13,9},{2,6},{6,2},{1... | collective-permute-start | bytes 884744 | tf_op jit(solution)/shard_map/ppermute | solution.py:19
  15.2 29.7 %collective-permute-start.3 = (bf16[1,3,6,3,16,256]{5,4,3,2,1,0:T(8,128)(2,1)S(1)}, bf16[1,3,6,3,16,256]{5,4,3,2,1,0:T(8,128)(2,1)S(1)}, u32[]{:S(2)}, u32[]{:S(2)}) collective-permute-start(bf16[1,3,6,3,16,256]{5,4,3,2,1,0:T(8,128)(2,1)S(1)} %get-tuple-element.103.refs_0_), channel_id=1, source_target_pairs={{0,8},{4,12},{8,0},{12,4},{1,9},{5,13},{9,1},{13,5},{2,10},{6,14},... | collective-permute-start | bytes 1327112 | tf_op jit(solution)/shard_map/ppermute | solution.py:19
  23.1 21.9 %copy-start.2 = (bf16[4,256,256]{2,1,0:T(8,128)(2,1)S(1)}, bf16[4,256,256]{2,1,0:T(8,128)(2,1)}, u32[]{:S(2)}) copy-start(bf16[4,256,256]{2,1,0:T(8,128)(2,1)} %refs_4_.5) | copy-start | bytes 1572868
  23.1 22.9 %collective-permute-start.4 = (bf16[1,3,6,2,16,256]{5,4,3,2,1,0:T(8,128)(2,1)S(1)}, bf16[1,3,6,2,16,256]{5,4,3,2,1,0:T(8,128)(2,1)S(1)}, u32[]{:S(2)}, u32[]{:S(2)}) collective-permute-start(bf16[1,3,6,2,16,256]{5,4,3,2,1,0:T(8,128)(2,1)S(1)} %get-tuple-element.106), channel_id=1, source_target_pairs={{0,4},{4,0},{8,12},{12,8},{1,5},{5,1},{9,13},{13,9},{2,6},{6,2},{1... | collective-permute-start | bytes 884744 | tf_op jit(solution)/shard_map/ppermute | solution.py:19
  26.6 31.0 %collective-permute-start.5 = (bf16[1,3,6,2,16,256]{5,4,3,2,1,0:T(8,128)(2,1)S(1)}, bf16[1,3,6,2,16,256]{5,4,3,2,1,0:T(8,128)(2,1)S(1)}, u32[]{:S(2)}, u32[]{:S(2)}) collective-permute-start(bf16[1,3,6,2,16,256]{5,4,3,2,1,0:T(8,128)(2,1)S(1)} %get-tuple-element.108.refs_0_), channel_id=1, source_target_pairs={{0,8},{4,12},{8,0},{12,4},{1,9},{5,13},{9,1},{13,5},{2,10},{6,14},... | collective-permute-start | bytes 884744 | tf_op jit(solution)/shard_map/ppermute | solution.py:19
  26.9 31.7 %collective-permute-start.6 = (bf16[1,3,6,2,16,256]{5,4,3,2,1,0:T(8,128)(2,1)S(1)}, bf16[1,3,6,2,16,256]{5,4,3,2,1,0:T(8,128)(2,1)S(1)}, u32[]{:S(2)}, u32[]{:S(2)}) collective-permute-start(bf16[1,3,6,2,16,256]{5,4,3,2,1,0:T(8,128)(2,1)S(1)} %get-tuple-element.114), channel_id=1, source_target_pairs={{0,4},{4,0},{8,12},{12,8},{1,5},{5,1},{9,13},{13,9},{2,6},{6,2},{1... | collective-permute-start | bytes 884744 | tf_op jit(solution)/shard_map/ppermute | solution.py:19
  46.6 23.6 %collective-permute-start.7 = (bf16[1,3,6,2,16,256]{5,4,3,2,1,0:T(8,128)(2,1)S(1)}, bf16[1,3,6,2,16,256]{5,4,3,2,1,0:T(8,128)(2,1)S(1)}, u32[]{:S(2)}, u32[]{:S(2)}) collective-permute-start(bf16[1,3,6,2,16,256]{5,4,3,2,1,0:T(8,128)(2,1)S(1)} %get-tuple-element.116.refs_0_), channel_id=1, source_target_pairs={{0,8},{4,12},{8,0},{12,4},{1,9},{5,13},{9,1},{13,5},{2,10},{6,14},... | collective-permute-start | bytes 884744 | tf_op jit(solution)/shard_map/ppermute | solution.py:19
  46.7 25.5 %collective-permute-start.9 = (bf16[1,3,6,2,16,256]{5,4,3,2,1,0:T(8,128)(2,1)S(1)}, bf16[1,3,6,2,16,256]{5,4,3,2,1,0:T(8,128)(2,1)S(1)}, u32[]{:S(2)}, u32[]{:S(2)}) collective-permute-start(bf16[1,3,6,2,16,256]{5,4,3,2,1,0:T(8,128)(2,1)S(1)} %get-tuple-element.119.refs_0_), channel_id=1, source_target_pairs={{0,4},{4,0},{8,12},{12,8},{1,5},{5,1},{9,13},{13,9},{2,6},{6,2},{1... | collective-permute-start | bytes 884744 | tf_op jit(solution)/shard_map/ppermute | solution.py:19
  59.2 15.5 %collective-permute-start.10 = (bf16[1,3,6,2,16,256]{5,4,3,2,1,0:T(8,128)(2,1)S(1)}, bf16[1,3,6,2,16,256]{5,4,3,2,1,0:T(8,128)(2,1)S(1)}, u32[]{:S(2)}, u32[]{:S(2)}) collective-permute-start(bf16[1,3,6,2,16,256]{5,4,3,2,1,0:T(8,128)(2,1)S(1)} %get-tuple-element.122.refs_0_), channel_id=1, source_target_pairs={{0,8},{4,12},{8,0},{12,4},{1,9},{5,13},{9,1},{13,5},{2,10},{6,14},... | collective-permute-start | bytes 884744 | tf_op jit(solution)/shard_map/ppermute | solution.py:19
  59.3 16.6 %collective-permute-start.11 = (bf16[1,3,6,2,16,256]{5,4,3,2,1,0:T(8,128)(2,1)S(1)}, bf16[1,3,6,2,16,256]{5,4,3,2,1,0:T(8,128)(2,1)S(1)}, u32[]{:S(2)}, u32[]{:S(2)}) collective-permute-start(bf16[1,3,6,2,16,256]{5,4,3,2,1,0:T(8,128)(2,1)S(1)} %get-tuple-element.126.refs_0_), channel_id=1, source_target_pairs={{0,4},{4,0},{8,12},{12,8},{1,5},{5,1},{9,13},{13,9},{2,6},{6,2},{1... | collective-permute-start | bytes 884744 | tf_op jit(solution)/shard_map/ppermute | solution.py:19
  63.6 4.6 %collective-permute-start.8 = (bf16[6,2,16,256]{3,2,1,0:T(8,128)(2,1)S(1)}, bf16[6,2,16,256]{3,2,1,0:T(8,128)(2,1)S(1)}, u32[]{:S(2)}, u32[]{:S(2)}) collective-permute-start(bf16[6,2,16,256]{3,2,1,0:T(8,128)(2,1)S(1)} %get-tuple-element.117), channel_id=1, source_target_pairs={{0,16},{16,0},{1,17},{17,1},{2,18},{18,2},{3,19},{19,3},{4,20},{20... | collective-permute-start | bytes 294920 | tf_op jit(solution)/shard_map/ppermute | solution.py:19
  71.3 9.0 %collective-permute-start.12 = (bf16[1,3,6,2,16,256]{5,4,3,2,1,0:T(8,128)(2,1)S(1)}, bf16[1,3,6,2,16,256]{5,4,3,2,1,0:T(8,128)(2,1)S(1)}, u32[]{:S(2)}, u32[]{:S(2)}) collective-permute-start(bf16[1,3,6,2,16,256]{5,4,3,2,1,0:T(8,128)(2,1)S(1)} %get-tuple-element.129.refs_0_), channel_id=1, source_target_pairs={{0,4},{4,0},{8,12},{12,8},{1,5},{5,1},{9,13},{13,9},{2,6},{6,2},{1... | collective-permute-start | bytes 884744 | tf_op jit(solution)/shard_map/ppermute | solution.py:19
  77.0 8.3 %collective-permute-start.15 = (bf16[512,256]{1,0:T(8,128)(2,1)S(1)}, bf16[512,256]{1,0:T(8,128)(2,1)S(1)}, u32[]{:S(2)}, u32[]{:S(2)}) collective-permute-start(bf16[512,256]{1,0:T(8,128)(2,1)S(1)} %get-tuple-element.138), channel_id=1, source_target_pairs={{0,1},{1,0},{2,3},{3,2},{4,5},{5,4},{6,7},{7,6},{8,9},{9,8},{10,11... | collective-permute-start | bytes 786440 | tf_op jit(solution)/shard_map/ppermute | solution.py:19
  77.1 12.2 %collective-permute-start.16 = (bf16[1,3,6,2,16,256]{5,4,3,2,1,0:T(8,128)(2,1)S(1)}, bf16[1,3,6,2,16,256]{5,4,3,2,1,0:T(8,128)(2,1)S(1)}, u32[]{:S(2)}, u32[]{:S(2)}) collective-permute-start(bf16[1,3,6,2,16,256]{5,4,3,2,1,0:T(8,128)(2,1)S(1)} %get-tuple-element.140.refs_0_), channel_id=1, source_target_pairs={{0,4},{4,0},{8,12},{12,8},{1,5},{5,1},{9,13},{13,9},{2,6},{6,2},{1... | collective-permute-start | bytes 884744 | tf_op jit(solution)/shard_map/ppermute | solution.py:19
  78.2 6.5 %collective-permute-start.13 = (bf16[256,256]{1,0:T(8,128)(2,1)S(1)}, bf16[256,256]{1,0:T(8,128)(2,1)S(1)}, u32[]{:S(2)}, u32[]{:S(2)}) collective-permute-start(bf16[256,256]{1,0:T(8,128)(2,1)S(1)} %get-tuple-element.133), channel_id=1, source_target_pairs={{0,1},{1,0},{2,3},{3,2},{4,5},{5,4},{6,7},{7,6},{8,9},{9,8},{10,11... | collective-permute-start | bytes 393224 | tf_op jit(solution)/shard_map/ppermute | solution.py:19
  78.4 6.3 %collective-permute-start.14 = (bf16[256,256]{1,0:T(8,128)(2,1)S(1)}, bf16[256,256]{1,0:T(8,128)(2,1)S(1)}, u32[]{:S(2)}, u32[]{:S(2)}) collective-permute-start(bf16[256,256]{1,0:T(8,128)(2,1)S(1)} %get-tuple-element.135), channel_id=1, source_target_pairs={{0,1},{1,0},{2,3},{3,2},{4,5},{5,4},{6,7},{7,6},{8,9},{9,8},{10,11... | collective-permute-start | bytes 393224 | tf_op jit(solution)/shard_map/ppermute | solution.py:19
  85.9 7.2 %collective-permute-start.18 = (bf16[512,256]{1,0:T(8,128)(2,1)S(1)}, bf16[512,256]{1,0:T(8,128)(2,1)S(1)}, u32[]{:S(2)}, u32[]{:S(2)}) collective-permute-start(bf16[512,256]{1,0:T(8,128)(2,1)S(1)} %get-tuple-element.148.refs_0_), channel_id=1, source_target_pairs={{0,16},{16,0},{1,17},{17,1},{2,18},{18,2},{3,19},{19,3},{4,20},{20... | collective-permute-start | bytes 786440 | tf_op jit(solution)/shard_map/ppermute | solution.py:19
  87.6 7.0 %collective-permute-start.17 = (bf16[512,256]{1,0:T(8,128)(2,1)S(1)}, bf16[512,256]{1,0:T(8,128)(2,1)S(1)}, u32[]{:S(2)}, u32[]{:S(2)}) collective-permute-start(bf16[512,256]{1,0:T(8,128)(2,1)S(1)} %get-tuple-element.147.refs_0_), channel_id=1, source_target_pairs={{0,4},{4,0},{8,12},{12,8},{1,5},{5,1},{9,13},{13,9},{2,6},{6,2},{1... | collective-permute-start | bytes 786440 | tf_op jit(solution)/shard_map/ppermute | solution.py:19
  92.5 2.7 %collective-permute-start.19 = (bf16[288,256]{1,0:T(8,128)(2,1)S(1)}, bf16[288,256]{1,0:T(8,128)(2,1)S(1)}, u32[]{:S(2)}, u32[]{:S(2)}) collective-permute-start(bf16[288,256]{1,0:T(8,128)(2,1)S(1)} %get-tuple-element.151), channel_id=1, source_target_pairs={{0,1},{1,0},{2,3},{3,2},{4,5},{5,4},{6,7},{7,6},{8,9},{9,8},{10,11... | collective-permute-start | bytes 442376 | tf_op jit(solution)/shard_map/ppermute | solution.py:19
  92.6 2.6 %collective-permute-start.20 = (bf16[256,256]{1,0:T(8,128)(2,1)S(1)}, bf16[256,256]{1,0:T(8,128)(2,1)S(1)}, u32[]{:S(2)}, u32[]{:S(2)}) collective-permute-start(bf16[256,256]{1,0:T(8,128)(2,1)S(1)} %get-tuple-element.153), channel_id=1, source_target_pairs={{0,1},{1,0},{2,3},{3,2},{4,5},{5,4},{6,7},{7,6},{8,9},{9,8},{10,11... | collective-permute-start | bytes 393224 | tf_op jit(solution)/shard_map/ppermute | solution.py:19
  95.8 7.8 %collective-permute-start.21 = (bf16[544,256]{1,0:T(8,128)(2,1)S(1)}, bf16[544,256]{1,0:T(8,128)(2,1)S(1)}, u32[]{:S(2)}, u32[]{:S(2)}) collective-permute-start(bf16[544,256]{1,0:T(8,128)(2,1)S(1)} %get-tuple-element.155.refs_0_), channel_id=1, source_target_pairs={{0,2},{1,3},{2,0},{3,1},{4,6},{5,7},{6,4},{7,5},{8,10},{9,11},{10,... | collective-permute-start | bytes 835592 | tf_op jit(solution)/shard_map/ppermute | solution.py:19
  97.4 9.5 %collective-permute-start.22 = (bf16[512,256]{1,0:T(8,128)(2,1)S(1)}, bf16[512,256]{1,0:T(8,128)(2,1)S(1)}, u32[]{:S(2)}, u32[]{:S(2)}) collective-permute-start(bf16[512,256]{1,0:T(8,128)(2,1)S(1)} %get-tuple-element.158.refs_0_), channel_id=1, source_target_pairs={{0,16},{16,0},{1,17},{17,1},{2,18},{18,2},{3,19},{19,3},{4,20},{20... | collective-permute-start | bytes 786440 | tf_op jit(solution)/shard_map/ppermute | solution.py:19
  98.0 21.5 %collective-permute-start.26 = (bf16[6,80,512]{2,1,0:T(8,128)(2,1)S(1)}, bf16[6,80,512]{2,1,0:T(8,128)(2,1)S(1)}, u32[]{:S(2)}, u32[]{:S(2)}) collective-permute-start(bf16[6,80,512]{2,1,0:T(8,128)(2,1)S(1)} %get-tuple-element.165), channel_id=1, source_target_pairs={{0,16},{16,0},{1,17},{17,1},{2,18},{18,2},{3,19},{19,3},{4,20},{20... | collective-permute-start | bytes 1474568 | tf_op jit(solution)/shard_map/ppermute | solution.py:19
  104.3 16.7 %collective-permute-start.25 = (bf16[544,256]{1,0:T(8,128)(2,1)S(1)}, bf16[544,256]{1,0:T(8,128)(2,1)S(1)}, u32[]{:S(2)}, u32[]{:S(2)}) collective-permute-start(bf16[544,256]{1,0:T(8,128)(2,1)S(1)} %get-tuple-element.164.refs_0_), channel_id=1, source_target_pairs={{0,16},{16,0},{1,17},{17,1},{2,18},{18,2},{3,19},{19,3},{4,20},{20... | collective-permute-start | bytes 835592 | tf_op jit(solution)/shard_map/ppermute | solution.py:19
  106.1 9.3 %collective-permute-start.23 = (bf16[512,256]{1,0:T(8,128)(2,1)S(1)}, bf16[512,256]{1,0:T(8,128)(2,1)S(1)}, u32[]{:S(2)}, u32[]{:S(2)}) collective-permute-start(bf16[512,256]{1,0:T(8,128)(2,1)S(1)} %get-tuple-element.160.refs_0_), channel_id=1, source_target_pairs={{0,2},{1,3},{2,0},{3,1},{4,6},{5,7},{6,4},{7,5},{8,10},{9,11},{10,... | collective-permute-start | bytes 786440 | tf_op jit(solution)/shard_map/ppermute | solution.py:19
  107.6 11.3 %collective-permute-start.24 = (bf16[512,256]{1,0:T(8,128)(2,1)S(1)}, bf16[512,256]{1,0:T(8,128)(2,1)S(1)}, u32[]{:S(2)}, u32[]{:S(2)}) collective-permute-start(bf16[512,256]{1,0:T(8,128)(2,1)S(1)} %get-tuple-element.162.refs_0_), channel_id=1, source_target_pairs={{0,2},{1,3},{2,0},{3,1},{4,6},{5,7},{6,4},{7,5},{8,10},{9,11},{10,... | collective-permute-start | bytes 786440 | tf_op jit(solution)/shard_map/ppermute | solution.py:19
  121.6 3.5 %collective-permute-start.29 = (f32[544,256]{1,0:T(8,128)S(1)}, f32[544,256]{1,0:T(8,128)S(1)}, u32[]{:S(2)}, u32[]{:S(2)}) collective-permute-start(f32[544,256]{1,0:T(8,128)S(1)} %get-tuple-element.177.refs_4_), channel_id=1, source_target_pairs={{0,1},{1,0},{2,3},{3,2},{4,5},{5,4},{6,7},{7,6},{8,9},{9,8},{10,11... | collective-permute-start | bytes 1671176 | tf_op jit(solution)/shard_map/ppermute | solution.py:19
  121.7 2.8 %collective-permute-start.28 = (f32[512,256]{1,0:T(8,128)S(1)}, f32[512,256]{1,0:T(8,128)S(1)}, u32[]{:S(2)}, u32[]{:S(2)}) collective-permute-start(f32[512,256]{1,0:T(8,128)S(1)} %get-tuple-element.176.refs_2_), channel_id=1, source_target_pairs={{0,1},{1,0},{2,3},{3,2},{4,5},{5,4},{6,7},{7,6},{8,9},{9,8},{10,11... | collective-permute-start | bytes 1572872 | tf_op jit(solution)/shard_map/ppermute | solution.py:19
  122.2 2.9 %collective-permute-start.27 = (f32[512,256]{1,0:T(8,128)S(1)}, f32[512,256]{1,0:T(8,128)S(1)}, u32[]{:S(2)}, u32[]{:S(2)}) collective-permute-start(f32[512,256]{1,0:T(8,128)S(1)} %get-tuple-element.175.refs_0_), channel_id=1, source_target_pairs={{0,1},{1,0},{2,3},{3,2},{4,5},{5,4},{6,7},{7,6},{8,9},{9,8},{10,11... | collective-permute-start | bytes 1572872 | tf_op jit(solution)/shard_map/ppermute | solution.py:19

commit v6 on v5

--- a/solution.py
+++ b/solution.py
@@ -350,8 +350,8 @@
             totals.append(total)
         if chained:
             leaving_ref, stay_ref = outs[:2]
-            leaving_ref[r, :cols] = jnp.where(upper, totals[2], totals[0]).astype(BF16)
-            leaving_ref[r, cols:, : mixed_ref.shape[2]] = mixed_ref[r]
+            at = pl.multiple_of(r * cols, cols)
+            leaving_ref[pl.ds(at, cols)] = jnp.where(upper, totals[2], totals[0]).astype(BF16)
             stay_ref[0, r] = jnp.where(upper, totals[0], totals[1])
             stay_ref[1, r] = jnp.where(upper, totals[1], totals[2])
         else:
@@ -360,6 +360,12 @@
         return carry
 
     lax.fori_loop(0, group, residue, 0)
+    if chained:
+        width, filters = mixed_ref.shape[1:]
+        for r in range(group // 2):
+            at = group * cols + r * width
+            outs[0][at : at + width, :filters] = mixed_ref[r]
+            outs[0][at : at + width, filters:] = mixed_ref[r + group // 2]
 
     @pl.when(pl.program_id(0) == STEPS - 1)
     def _():
@@ -395,9 +401,10 @@
     cell = (classes, group, cols, channels)
     thin = (group, cols, channels)
     chained = before is not None
+    flat = (residues * cols + residues // 2 * (cols // 4), channels)
     if chained:
         outs = [
-            (shape_of((residues, cols + cols // 4, channels), BF16), (group, cols + cols // 4, channels), 0),
+            (shape_of(flat, BF16), flat, None),
             (shape_of((2,) + x.shape[1:], F32), (2,) + thin, 1),
         ]
     else:
@@ -481,13 +488,17 @@
     pre = pre_ref[...].reshape(classes * group * cols, -1)
     grads = lax.dot_general(pre, point_ref[0], (((1,), (1,)), ((), ())), preferred_element_type=F32)
     grads = grads.astype(BF16).astype(F32).reshape(band_ref.shape)
-    others = (stay_ref[0], arrived_ref[:, :cols].astype(F32), stay_ref[1])
+    cells = group * cols
+    arrived = arrived_ref[:cells].reshape(group, cols, channels).astype(F32)
+    others = (stay_ref[0], arrived, stay_ref[1])
     for q in range(classes):
         input_ref[q] = (grads[q] + band_ref[q] + others[q]).astype(BF16)
     upper = place[1] == 0
+    width, filters = mixed_ref.shape[2:]
+    rest = arrived_ref[cells:].reshape(group // 2, width, channels)
     mixed = (
         jnp.where(upper, folded_ref[0], folded_ref[1]),
-        arrived_ref[:, cols:, : mixed_ref.shape[-1]].astype(F32),
+        jnp.concatenate([rest[..., :filters], rest[..., filters:]]).astype(F32),
         jnp.where(upper, folded_ref[1], folded_ref[2]),
     )
     for q in range(classes):
@@ -507,7 +518,7 @@
             (point, (1, channels, filters), (0, 0, 0)),
             (band, cell, 1),
             (stay, (2, group, cols, channels), 1),
-            (arrived, (group,) + arrived.shape[1:], 0),
+            (arrived, arrived.shape, None),
             (mixed, thin, 1),
             (folded, thin, 1),
         ],
@@ -797,7 +808,7 @@
     return (output, grad_in.astype(jnp.bfloat16), grad_depth, grad_point, grad_proj)
 
 
-def folds(mesh, features_in):
+def folds(mesh, features_in, point_weights):
     sizes = mesh.shape
     samples, rows, cols, channels = features_in.shape
     return (
@@ -808,6 +819,7 @@
         and samples == sizes["dp"]
         and cols % 64 == 0
         and channels % (128 * sizes["chan"]) == 0
+        and channels == 2 * sizes["chan"] * point_weights.shape[2]
     )
 
 
@@ -828,7 +840,7 @@
     )
 
     def run(*args):
-        body = by_classes if folds(mesh, args[0]) else on_device
+        body = by_classes if folds(mesh, args[0], args[2]) else on_device
         return jax.shard_map(
             body, mesh=mesh, in_specs=in_specs, out_specs=out_specs, check_vma=False
         )(*args)

time: 128 us -> 127 us (level)
  no operation moved by 1% of the time
where the time goes in v6:
time: 127 us
  waiting for transfers between devices  53.3 us (42%)
  Pallas kernels  37 us (29%)
  starting transfers between devices  35.2 us (28%)
    ppermute x30, waiting for transfers between devices, swap(): return lax.ppermute(value, axis, [(i, i ^ flip) for i in range(count)])  53.3 us
    pallas_call x27, Pallas kernels, call(): pl.pallas_call(kernel, grid_spec=pltpu.PrefetchScalarGridSpec(num_scalar_...  37 us
    ppermute x30, starting transfers between devices, swap(): return lax.ppermute(value, axis, [(i, i ^ flip) for i in range(count)])  35.2 us
  transfers between devices with their start and end apart: 30, of which 16 were waited for; matrix products, arithmetic and copies ran while one was open for 0% of the time, Pallas kernels for 24%

profile of v6, /device:TPU:0, one launch (start us, length us, event | category | flops | bytes accessed | tf_op | source)
XLA Modules:
  0.0 126.6 jit_solution(14958652540506827915)
XLA Ops:
  0.7 3.0 %forward_3.1 = (f32[1,3,6,2,16,256]{5,4,3,2,1,0:T(8,128)S(1)}, bf16[1,3,6,2,16,256]{5,4,3,2,1,0:T(8,128)(2,1)S(1)}, bf16[3,6,64,512]{3,2,1,0:T(8,128)(2,1)S(1)}, f32[8,128]{1,0:T(8,128)S(1)}) custom-call(s32[3]{0:T(128)S(1)} %pad_add_fusion.place_ref, f32[8,128]{1,0:T(8,128)S(1)} %broadcast_in_dim.6.after_ref, bf16[3,6,64,512]{3,2,1,0:T(8,128)(2,1)} %bitcast.9, ...), custom_call_target="tpu_custom_call" | custom-call | flops 1 | bytes 1 | tf_op jit(solution)/shard_map/forward_3/pallas_call | solution.py:99
  3.7 3.1 %collective-permute-start = (bf16[1,3,6,2,16,256]{5,4,3,2,1,0:T(8,128)(2,1)S(1)}, bf16[1,3,6,2,16,256]{5,4,3,2,1,0:T(8,128)(2,1)S(1)}, u32[]{:S(2)}, u32[]{:S(2)}) collective-permute-start(bf16[1,3,6,2,16,256]{5,4,3,2,1,0:T(8,128)(2,1)S(1)} %get-tuple-element.96), channel_id=1, source_target_pairs={{0,4},{4,0},{8,12},{12,8},{1,5},{5,1},{9,13},{13,9},{2,6},{6,2},{1... | collective-permute-start | bytes 884744 | tf_op jit(solution)/shard_map/ppermute | solution.py:19
  6.8 2.0 %forward_0.1 = (f32[1,3,6,2,16,256]{5,4,3,2,1,0:T(8,128)S(1)}, bf16[1,3,6,2,16,256]{5,4,3,2,1,0:T(8,128)(2,1)S(1)}, bf16[6,64,512]{2,1,0:T(8,128)(2,1)S(1)}, f32[8,128]{1,0:T(8,128)S(1)}) custom-call(s32[3]{0:T(128)S(1)} %pad_add_fusion.place_ref, f32[8,128]{1,0:T(8,128)S(1)} %get-tuple-element.93.after_ref, bf16[3,6,64,512]{3,2,1,0:T(8,128)(2,1)S(1)} %bitcast.11, ...), custom_call_target="tpu_custom_call" | custom-call | flops 1 | bytes 1 | tf_op jit(solution)/shard_map/forward_0/pallas_call | solution.py:99
  8.8 1.6 %collective-permute-start.1 = (bf16[6,64,512]{2,1,0:T(8,128)(2,1)S(1)}, bf16[6,64,512]{2,1,0:T(8,128)(2,1)S(1)}, u32[]{:S(2)}, u32[]{:S(2)}) collective-permute-start(bf16[6,64,512]{2,1,0:T(8,128)(2,1)S(1)} %get-tuple-element.98), channel_id=1, source_target_pairs={{0,16},{16,0},{1,17},{17,1},{2,18},{18,2},{3,19},{19,3},{4,20},{20... | collective-permute-start | bytes 1179656 | tf_op jit(solution)/shard_map/ppermute | solution.py:19
  10.4 0.4 collective-permute-start.2
  10.8 3.8 %collective-permute-done.refs_1_ = bf16[1,3,6,2,16,256]{5,4,3,2,1,0:T(8,128)(2,1)S(1)} collective-permute-done((bf16[1,3,6,2,16,256]{5,4,3,2,1,0:T(8,128)(2,1)S(1)}, bf16[1,3,6,2,16,256]{5,4,3,2,1,0:T(8,128)(2,1)S(1)}, u32[]{:S(2)}, u32[]{:S(2)}) %collective-permute-start) | collective-permute-done | bytes 294944 | tf_op jit(solution)/shard_map/ppermute | solution.py:19
  14.6 0.6 near_3.1
  15.2 3.1 %collective-permute-start.3 = (bf16[1,3,6,3,16,256]{5,4,3,2,1,0:T(8,128)(2,1)S(1)}, bf16[1,3,6,3,16,256]{5,4,3,2,1,0:T(8,128)(2,1)S(1)}, u32[]{:S(2)}, u32[]{:S(2)}) collective-permute-start(bf16[1,3,6,3,16,256]{5,4,3,2,1,0:T(8,128)(2,1)S(1)} %get-tuple-element.103.refs_0_), channel_id=1, source_target_pairs={{0,8},{4,12},{8,0},{12,4},{1,9},{5,13},{9,1},{13,5},{2,10},{6,14},... | collective-permute-start | bytes 1327112 | tf_op jit(solution)/shard_map/ppermute | solution.py:19
  18.4 1.1 collective-permute-done.1.refs_1_.refs_3_
  19.4 3.6 %forward_1_2.1 = (f32[1,3,6,2,16,256]{5,4,3,2,1,0:T(8,128)S(1)}, f32[1,3,6,2,16,256]{5,4,3,2,1,0:T(8,128)S(1)}, bf16[1,3,6,2,16,256]{5,4,3,2,1,0:T(8,128)(2,1)S(...) custom-call(s32[3]{0:T(128)S(1)} %pad_add_fusion.place_ref, ...), custom_call_target="tpu_custom_call" | custom-call | flops 1 | bytes 1 | tf_op jit(solution)/shard_map/forward_1_2/pallas_call | solution.py:99
  23.1 0.6 collective-permute-start.4
  23.7 2.3 %collective-permute-done.2.refs_1_ = bf16[1,3,6,2,16,256]{5,4,3,2,1,0:T(8,128)(2,1)S(1)} collective-permute-done((bf16[1,3,6,2,16,256]{5,4,3,2,1,0:T(8,128)(2,1)S(1)}, bf16[1,3,6,2,16,256]{5,4,3,2,1,0:T(8,128)(2,1)S(1)}, u32[]{:S(2)}, u32[]{:S(2)}) %collective-permute-start.2) | collective-permute-done | bytes 294944 | tf_op jit(solution)/shard_map/ppermute | solution.py:19
  25.9 0.6 near_0.1
  26.6 0.3 collective-permute-start.5
  26.9 1.6 %collective-permute-start.6 = (bf16[1,3,6,2,16,256]{5,4,3,2,1,0:T(8,128)(2,1)S(1)}, bf16[1,3,6,2,16,256]{5,4,3,2,1,0:T(8,128)(2,1)S(1)}, u32[]{:S(2)}, u32[]{:S(2)}) collective-permute-start(bf16[1,3,6,2,16,256]{5,4,3,2,1,0:T(8,128)(2,1)S(1)} %get-tuple-element.114), channel_id=1, source_target_pairs={{0,4},{4,0},{8,12},{12,8},{1,5},{5,1},{9,13},{13,9},{2,6},{6,2},{1... | collective-permute-start | bytes 884744 | tf_op jit(solution)/shard_map/ppermute | solution.py:19
  28.4 16.5 %collective-permute-done.3.refs_1_ = bf16[1,3,6,3,16,256]{5,4,3,2,1,0:T(8,128)(2,1)S(1)} collective-permute-done((bf16[1,3,6,3,16,256]{5,4,3,2,1,0:T(8,128)(2,1)S(1)}, bf16[1,3,6,3,16,256]{5,4,3,2,1,0:T(8,128)(2,1)S(1)}, u32[]{:S(2)}, u32[]{:S(2)}) %collective-permute-start.3) | collective-permute-done | bytes 442400 | tf_op jit(solution)/shard_map/ppermute | solution.py:19
  45.0 1.0 gate_3.1
  46.0 0.6 near_1.1
  46.7 4.3 %collective-permute-start.9 = (bf16[1,3,6,2,16,256]{5,4,3,2,1,0:T(8,128)(2,1)S(1)}, bf16[1,3,6,2,16,256]{5,4,3,2,1,0:T(8,128)(2,1)S(1)}, u32[]{:S(2)}, u32[]{:S(2)}) collective-permute-start(bf16[1,3,6,2,16,256]{5,4,3,2,1,0:T(8,128)(2,1)S(1)} %get-tuple-element.119.refs_0_), channel_id=1, source_target_pairs={{0,4},{4,0},{8,12},{12,8},{1,5},{5,1},{9,13},{13,9},{2,6},{6,2},{1... | collective-permute-start | bytes 884744 | tf_op jit(solution)/shard_map/ppermute | solution.py:19
  51.0 6.6 %collective-permute-done.5.refs_1_ = bf16[1,3,6,2,16,256]{5,4,3,2,1,0:T(8,128)(2,1)S(1)} collective-permute-done((bf16[1,3,6,2,16,256]{5,4,3,2,1,0:T(8,128)(2,1)S(1)}, bf16[1,3,6,2,16,256]{5,4,3,2,1,0:T(8,128)(2,1)S(1)}, u32[]{:S(2)}, u32[]{:S(2)}) %collective-permute-start.5) | collective-permute-done | bytes 294944 | tf_op jit(solution)/shard_map/ppermute | solution.py:19
  57.5 1.0 gate_0.1
  58.6 0.6 near_2.1
  59.3 4.3 %collective-permute-start.11 = (bf16[1,3,6,2,16,256]{5,4,3,2,1,0:T(8,128)(2,1)S(1)}, bf16[1,3,6,2,16,256]{5,4,3,2,1,0:T(8,128)(2,1)S(1)}, u32[]{:S(2)}, u32[]{:S(2)}) collective-permute-start(bf16[1,3,6,2,16,256]{5,4,3,2,1,0:T(8,128)(2,1)S(1)} %get-tuple-element.126.refs_0_), channel_id=1, source_target_pairs={{0,4},{4,0},{8,12},{12,8},{1,5},{5,1},{9,13},{13,9},{2,6},{6,2},{1... | collective-permute-start | bytes 884744 | tf_op jit(solution)/shard_map/ppermute | solution.py:19
  63.6 1.5 %collective-permute-start.8 = (bf16[6,2,16,256]{3,2,1,0:T(8,128)(2,1)S(1)}, bf16[6,2,16,256]{3,2,1,0:T(8,128)(2,1)S(1)}, u32[]{:S(2)}, u32[]{:S(2)}) collective-permute-start(bf16[6,2,16,256]{3,2,1,0:T(8,128)(2,1)S(1)} %get-tuple-element.117), channel_id=1, source_target_pairs={{0,16},{16,0},{1,17},{17,1},{2,18},{18,2},{3,19},{19,3},{4,20},{20... | collective-permute-start | bytes 294920 | tf_op jit(solution)/shard_map/ppermute | solution.py:19
  65.1 3.1 %collective-permute-done.8.refs_3_ = bf16[6,2,16,256]{3,2,1,0:T(8,128)(2,1)S(1)} collective-permute-done((bf16[6,2,16,256]{3,2,1,0:T(8,128)(2,1)S(1)}, bf16[6,2,16,256]{3,2,1,0:T(8,128)(2,1)S(1)}, u32[]{:S(2)}, u32[]{:S(2)}) %collective-permute-start.8) | collective-permute-done | bytes 98336 | tf_op jit(solution)/shard_map/ppermute | solution.py:19
  68.2 2.0 %collective-permute-done.7.refs_1_ = bf16[1,3,6,2,16,256]{5,4,3,2,1,0:T(8,128)(2,1)S(1)} collective-permute-done((bf16[1,3,6,2,16,256]{5,4,3,2,1,0:T(8,128)(2,1)S(1)}, bf16[1,3,6,2,16,256]{5,4,3,2,1,0:T(8,128)(2,1)S(1)}, u32[]{:S(2)}, u32[]{:S(2)}) %collective-permute-start.7) | collective-permute-done | bytes 294944 | tf_op jit(solution)/shard_map/ppermute | solution.py:19
  70.2 1.0 gate_1.1
  71.3 1.0 collective-permute-start.12
  72.3 2.5 %backward_3.1 = (f32[3,6,64,512]{3,2,1,0:T(8,128)S(1)}, f32[512,256]{1,0:T(8,128)S(1)}, f32[9,512]{1,0:T(8,128)S(1)}, f32[8,128]{1,0:T(8,128)S(1)}) custom-call(s32[3]{0:T(128)S(1)} %pad_add_fusion.place_ref, f32[8,128]{1,0:T(8,128)S(1)} %get-tuple-element.118.after_ref, bf16[1,3,6,2,16,256]{5,4,3,2,1,0:T(8,128)(2,1)S(1)} %get-tuple-element.119.refs_0_, ...), custom_call_target="tpu_custom_call" | custom-call | flops 1 | bytes 1 | tf_op jit(solution)/shard_map/backward_3/pallas_call | solution.py:99
  74.8 1.1 gate_2.1
  75.9 1.1 join.1
  77.1 1.1 collective-permute-start.16
  78.4 0.3 collective-permute-start.14
  78.7 1.6 %collective-permute-done.12.refs_1_ = bf16[1,3,6,2,16,256]{5,4,3,2,1,0:T(8,128)(2,1)S(1)} collective-permute-done((bf16[1,3,6,2,16,256]{5,4,3,2,1,0:T(8,128)(2,1)S(1)}, bf16[1,3,6,2,16,256]{5,4,3,2,1,0:T(8,128)(2,1)S(1)}, u32[]{:S(2)}, u32[]{:S(2)}) %collective-permute-start.12) | collective-permute-done | bytes 294944 | tf_op jit(solution)/shard_map/ppermute | solution.py:19
  80.3 4.3 %backward_1.1 = (f32[3,6,64,512]{3,2,1,0:T(8,128)S(1)}, f32[9,512]{1,0:T(8,128)S(1)}, f32[256,256]{1,0:T(8,128)S(1)}, bf16[256,256]{1,0:T(8,128)(2,1)S(1)}, f32[8,128]{1,0:T(8,128)S(1)}) custom-call(s32[3]{0:T(128)S(1)} %pad_add_fusion.place_ref, f32[8,128]{1,0:T(8,128)S(1)} %get-tuple-element.128.after_ref, ...), custom_call_target="tpu_custom_call" | custom-call | flops 1 | bytes 1 | tf_op jit(solution)/shard_map/backward_1/pallas_call | solution.py:99
  84.7 0.6 proj.1
  85.3 0.6 early_1.1
  85.9 1.7 %collective-permute-start.18 = (bf16[512,256]{1,0:T(8,128)(2,1)S(1)}, bf16[512,256]{1,0:T(8,128)(2,1)S(1)}, u32[]{:S(2)}, u32[]{:S(2)}) collective-permute-start(bf16[512,256]{1,0:T(8,128)(2,1)S(1)} %get-tuple-element.148.refs_0_), channel_id=1, source_target_pairs={{0,16},{16,0},{1,17},{17,1},{2,18},{18,2},{3,19},{19,3},{4,20},{20... | collective-permute-start | bytes 786440 | tf_op jit(solution)/shard_map/ppermute | solution.py:19
  87.6 1.8 %collective-permute-start.17 = (bf16[512,256]{1,0:T(8,128)(2,1)S(1)}, bf16[512,256]{1,0:T(8,128)(2,1)S(1)}, u32[]{:S(2)}, u32[]{:S(2)}) collective-permute-start(bf16[512,256]{1,0:T(8,128)(2,1)S(1)} %get-tuple-element.147.refs_0_), channel_id=1, source_target_pairs={{0,4},{4,0},{8,12},{12,8},{1,5},{5,1},{9,13},{13,9},{2,6},{6,2},{1... | collective-permute-start | bytes 786440 | tf_op jit(solution)/shard_map/ppermute | solution.py:19
  89.3 3.2 %backward_2.1 = (bf16[432,512]{1,0:T(8,128)(2,1)S(1)}, f32[2,6,64,512]{3,2,1,0:T(8,128)S(1)}, f32[288,256]{1,0:T(8,128)S(1)}, bf16[288,256]{1,0:T(8,128)(2,1)S(1)}, f32[8,128]{1,0:T(8,128)S(1)}) custom-call(s32[3]{0:T(128)S(1)} %pad_add_fusion.place_ref, f32[8,128]{1,0:T(8,128)S(1)} %get-tuple-element.139.after_ref, ...), custom_call_target="tpu_custom_call" | custom-call | flops 1 | bytes 1 | tf_op jit(solution)/shard_map/backward_2/pallas_call | solution.py:99
  92.6 0.5 collective-permute-start.20
  93.2 1.5 %collective-permute-done.17.refs_1_ = bf16[512,256]{1,0:T(8,128)(2,1)S(1)} collective-permute-done((bf16[512,256]{1,0:T(8,128)(2,1)S(1)}, bf16[512,256]{1,0:T(8,128)(2,1)S(1)}, u32[]{:S(2)}, u32[]{:S(2)}) %collective-permute-start.17) | collective-permute-done | bytes 262176 | tf_op jit(solution)/shard_map/ppermute | solution.py:19
  94.6 0.6 proj_1.1
  95.2 0.6 late_1.1
  95.8 1.6 %collective-permute-start.21 = (bf16[544,256]{1,0:T(8,128)(2,1)S(1)}, bf16[544,256]{1,0:T(8,128)(2,1)S(1)}, u32[]{:S(2)}, u32[]{:S(2)}) collective-permute-start(bf16[544,256]{1,0:T(8,128)(2,1)S(1)} %get-tuple-element.155.refs_0_), channel_id=1, source_target_pairs={{0,2},{1,3},{2,0},{3,1},{4,6},{5,7},{6,4},{7,5},{8,10},{9,11},{10,... | collective-permute-start | bytes 835592 | tf_op jit(solution)/shard_map/ppermute | solution.py:19
  97.4 0.6 collective-permute-start.22
  98.0 1.5 %collective-permute-start.26 = (bf16[432,512]{1,0:T(8,128)(2,1)S(1)}, bf16[432,512]{1,0:T(8,128)(2,1)S(1)}, u32[]{:S(2)}, u32[]{:S(2)}) collective-permute-start(bf16[432,512]{1,0:T(8,128)(2,1)S(1)} %get-tuple-element.165), channel_id=1, source_target_pairs={{0,16},{16,0},{1,17},{17,1},{2,18},{18,2},{3,19},{19,3},{4,20},{20... | collective-permute-start | bytes 1327112 | tf_op jit(solution)/shard_map/ppermute | solution.py:19
  99.4 4.2 %collective-permute-done.21.refs_1_ = bf16[544,256]{1,0:T(8,128)(2,1)S(1)} collective-permute-done((bf16[544,256]{1,0:T(8,128)(2,1)S(1)}, bf16[544,256]{1,0:T(8,128)(2,1)S(1)}, u32[]{:S(2)}, u32[]{:S(2)}) %collective-permute-start.21) | collective-permute-done | bytes 278560 | tf_op jit(solution)/shard_map/ppermute | solution.py:19
  103.7 0.6 late_2.1
  104.3 1.2 collective-permute-start.25
  105.5 0.6 early_2.1
  106.1 0.9 collective-permute-start.23
  107.0 0.6 proj_2.1
  107.6 1.3 %collective-permute-start.24 = (bf16[512,256]{1,0:T(8,128)(2,1)S(1)}, bf16[512,256]{1,0:T(8,128)(2,1)S(1)}, u32[]{:S(2)}, u32[]{:S(2)}) collective-permute-start(bf16[512,256]{1,0:T(8,128)(2,1)S(1)} %get-tuple-element.162.refs_0_), channel_id=1, source_target_pairs={{0,2},{1,3},{2,0},{3,1},{4,6},{5,7},{6,4},{7,5},{8,10},{9,11},{10,... | collective-permute-start | bytes 786440 | tf_op jit(solution)/shard_map/ppermute | solution.py:19
  108.9 6.5 %collective-permute-done.23.refs_1_ = bf16[512,256]{1,0:T(8,128)(2,1)S(1)} collective-permute-done((bf16[512,256]{1,0:T(8,128)(2,1)S(1)}, bf16[512,256]{1,0:T(8,128)(2,1)S(1)}, u32[]{:S(2)}, u32[]{:S(2)}) %collective-permute-start.23) | collective-permute-done | bytes 262176 | tf_op jit(solution)/shard_map/ppermute | solution.py:19
  115.4 0.6 early.1
  116.0 2.8 %collective-permute-done.24.refs_1_ = bf16[512,256]{1,0:T(8,128)(2,1)S(1)} collective-permute-done((bf16[512,256]{1,0:T(8,128)(2,1)S(1)}, bf16[512,256]{1,0:T(8,128)(2,1)S(1)}, u32[]{:S(2)}, u32[]{:S(2)}) %collective-permute-start.24) | collective-permute-done | bytes 262176 | tf_op jit(solution)/shard_map/ppermute | solution.py:19
  118.8 0.6 proj_sum.1
  119.5 0.5 collective-permute-done.25.refs_1_
  120.0 0.6 late.1
  120.7 0.5 collective-permute-start.28
  121.3 2.2 %last.1 = (bf16[3,6,64,512]{3,2,1,0:T(8,128)(2,1)}, bf16[3,6,16,256]{3,2,1,0:T(8,128)(2,1)}, f32[8,128]{1,0:T(8,128)S(1)}) custom-call(s32[3]{0:T(128)S(1)} %pad_add_fusion.place_ref, f32[8,128]{1,0:T(8,128)S(1)} %get-tuple-element.166.after_ref, bf16[3,6,64,256]{3,2,1,0:T(8,128)(2,1)S(1)} %get-tuple-element.167.refs_0_, bf16[4,512,256]{2,1,0:T(8,128)(2,1)S(1)} %copy-done.1, ...), custom_call_target="tpu_custom_call" | custom-call | flops 1 | bytes 1 | tf_op jit(solution)/shard_map/last/pallas_call | solution.py:99
  123.5 0.6 collective-permute-done.27.refs_1_
  124.1 2.5 %finish.1 = (f32[4,256,256]{2,1,0:T(8,128)}, f32[3,3,3,512]{3,2,1,0:T(4,128)}, f32[4,512,256]{2,1,0:T(8,128)}, f32[8,128]{1,0:T(8,128)}) custom-call(s32[3]{0:T(128)S(1)} %pad_add_fusion.place_ref, f32[8,128]{1,0:T(8,128)S(1)} %get-tuple-element.174.after_ref, f32[512,256]{1,0:T(8,128)S(1)} %get-tuple-element.175.refs_0_, ...), custom_call_target="tpu_custom_call" | custom-call | flops 1 | bytes 1 | tf_op jit(solution)/shard_map/finish/pallas_call | solution.py:99
  (36 shorter events, 0.9 us)
Async XLA Ops:
  0.7 6.0 %copy-start = (bf16[1,18,64,512]{3,2,1,0:T(8,128)(2,1)S(1)}, bf16[1,18,64,512]{3,2,1,0:T(8,128)(2,1)}, u32[]{:S(2)}) copy-start(bf16[1,18,64,512]{3,2,1,0:T(8,128)(2,1)} %param.5) | copy-start | bytes 3538948
  3.7 10.9 %collective-permute-start = (bf16[1,3,6,2,16,256]{5,4,3,2,1,0:T(8,128)(2,1)S(1)}, bf16[1,3,6,2,16,256]{5,4,3,2,1,0:T(8,128)(2,1)S(1)}, u32[]{:S(2)}, u32[]{:S(2)}) collective-permute-start(bf16[1,3,6,2,16,256]{5,4,3,2,1,0:T(8,128)(2,1)S(1)} %get-tuple-element.96), channel_id=1, source_target_pairs={{0,4},{4,0},{8,12},{12,8},{1,5},{5,1},{9,13},{13,9},{2,6},{6,2},{1... | collective-permute-start | bytes 884744 | tf_op jit(solution)/shard_map/ppermute | solution.py:19
  6.8 7.8 %copy-start.4 = (bf16[1,18,16,256]{3,2,1,0:T(8,128)(2,1)S(1)}, bf16[1,18,16,256]{3,2,1,0:T(8,128)(2,1)}, u32[]{:S(2)}) copy-start(bf16[1,18,16,256]{3,2,1,0:T(8,128)(2,1)} %param.9) | copy-start | bytes 442372
  6.8 12.7 %copy-start.3 = (bf16[3,3,3,512]{3,2,1,0:T(4,128)(2,1)S(1)}, bf16[3,3,3,512]{3,2,1,0:T(4,128)(2,1)}, u32[]{:S(2)}) copy-start(bf16[3,3,3,512]{3,2,1,0:T(4,128)(2,1)} %refs_5_.5) | copy-start | bytes 82948
  8.8 10.7 %copy-start.1 = (bf16[4,512,256]{2,1,0:T(8,128)(2,1)S(1)}, bf16[4,512,256]{2,1,0:T(8,128)(2,1)}, u32[]{:S(2)}) copy-start(bf16[4,512,256]{2,1,0:T(8,128)(2,1)} %refs_1_.1) | copy-start | bytes 3145732
  8.8 10.6 %collective-permute-start.1 = (bf16[6,64,512]{2,1,0:T(8,128)(2,1)S(1)}, bf16[6,64,512]{2,1,0:T(8,128)(2,1)S(1)}, u32[]{:S(2)}, u32[]{:S(2)}) collective-permute-start(bf16[6,64,512]{2,1,0:T(8,128)(2,1)S(1)} %get-tuple-element.98), channel_id=1, source_target_pairs={{0,16},{16,0},{1,17},{17,1},{2,18},{18,2},{3,19},{19,3},{4,20},{20... | collective-permute-start | bytes 1179656 | tf_op jit(solution)/shard_map/ppermute | solution.py:19
  10.4 15.6 %collective-permute-start.2 = (bf16[1,3,6,2,16,256]{5,4,3,2,1,0:T(8,128)(2,1)S(1)}, bf16[1,3,6,2,16,256]{5,4,3,2,1,0:T(8,128)(2,1)S(1)}, u32[]{:S(2)}, u32[]{:S(2)}) collective-permute-start(bf16[1,3,6,2,16,256]{5,4,3,2,1,0:T(8,128)(2,1)S(1)} %get-tuple-element.101), channel_id=1, source_target_pairs={{0,4},{4,0},{8,12},{12,8},{1,5},{5,1},{9,13},{13,9},{2,6},{6,2},{1... | collective-permute-start | bytes 884744 | tf_op jit(solution)/shard_map/ppermute | solution.py:19
  15.2 29.7 %collective-permute-start.3 = (bf16[1,3,6,3,16,256]{5,4,3,2,1,0:T(8,128)(2,1)S(1)}, bf16[1,3,6,3,16,256]{5,4,3,2,1,0:T(8,128)(2,1)S(1)}, u32[]{:S(2)}, u32[]{:S(2)}) collective-permute-start(bf16[1,3,6,3,16,256]{5,4,3,2,1,0:T(8,128)(2,1)S(1)} %get-tuple-element.103.refs_0_), channel_id=1, source_target_pairs={{0,8},{4,12},{8,0},{12,4},{1,9},{5,13},{9,1},{13,5},{2,10},{6,14},... | collective-permute-start | bytes 1327112 | tf_op jit(solution)/shard_map/ppermute | solution.py:19
  23.1 21.9 %copy-start.2 = (bf16[4,256,256]{2,1,0:T(8,128)(2,1)S(1)}, bf16[4,256,256]{2,1,0:T(8,128)(2,1)}, u32[]{:S(2)}) copy-start(bf16[4,256,256]{2,1,0:T(8,128)(2,1)} %refs_4_.5) | copy-start | bytes 1572868
  23.1 22.9 %collective-permute-start.4 = (bf16[1,3,6,2,16,256]{5,4,3,2,1,0:T(8,128)(2,1)S(1)}, bf16[1,3,6,2,16,256]{5,4,3,2,1,0:T(8,128)(2,1)S(1)}, u32[]{:S(2)}, u32[]{:S(2)}) collective-permute-start(bf16[1,3,6,2,16,256]{5,4,3,2,1,0:T(8,128)(2,1)S(1)} %get-tuple-element.106), channel_id=1, source_target_pairs={{0,4},{4,0},{8,12},{12,8},{1,5},{5,1},{9,13},{13,9},{2,6},{6,2},{1... | collective-permute-start | bytes 884744 | tf_op jit(solution)/shard_map/ppermute | solution.py:19
  26.6 31.0 %collective-permute-start.5 = (bf16[1,3,6,2,16,256]{5,4,3,2,1,0:T(8,128)(2,1)S(1)}, bf16[1,3,6,2,16,256]{5,4,3,2,1,0:T(8,128)(2,1)S(1)}, u32[]{:S(2)}, u32[]{:S(2)}) collective-permute-start(bf16[1,3,6,2,16,256]{5,4,3,2,1,0:T(8,128)(2,1)S(1)} %get-tuple-element.108.refs_0_), channel_id=1, source_target_pairs={{0,8},{4,12},{8,0},{12,4},{1,9},{5,13},{9,1},{13,5},{2,10},{6,14},... | collective-permute-start | bytes 884744 | tf_op jit(solution)/shard_map/ppermute | solution.py:19
  26.9 31.7 %collective-permute-start.6 = (bf16[1,3,6,2,16,256]{5,4,3,2,1,0:T(8,128)(2,1)S(1)}, bf16[1,3,6,2,16,256]{5,4,3,2,1,0:T(8,128)(2,1)S(1)}, u32[]{:S(2)}, u32[]{:S(2)}) collective-permute-start(bf16[1,3,6,2,16,256]{5,4,3,2,1,0:T(8,128)(2,1)S(1)} %get-tuple-element.114), channel_id=1, source_target_pairs={{0,4},{4,0},{8,12},{12,8},{1,5},{5,1},{9,13},{13,9},{2,6},{6,2},{1... | collective-permute-start | bytes 884744 | tf_op jit(solution)/shard_map/ppermute | solution.py:19
  46.6 23.6 %collective-permute-start.7 = (bf16[1,3,6,2,16,256]{5,4,3,2,1,0:T(8,128)(2,1)S(1)}, bf16[1,3,6,2,16,256]{5,4,3,2,1,0:T(8,128)(2,1)S(1)}, u32[]{:S(2)}, u32[]{:S(2)}) collective-permute-start(bf16[1,3,6,2,16,256]{5,4,3,2,1,0:T(8,128)(2,1)S(1)} %get-tuple-element.116.refs_0_), channel_id=1, source_target_pairs={{0,8},{4,12},{8,0},{12,4},{1,9},{5,13},{9,1},{13,5},{2,10},{6,14},... | collective-permute-start | bytes 884744 | tf_op jit(solution)/shard_map/ppermute | solution.py:19
  46.7 25.5 %collective-permute-start.9 = (bf16[1,3,6,2,16,256]{5,4,3,2,1,0:T(8,128)(2,1)S(1)}, bf16[1,3,6,2,16,256]{5,4,3,2,1,0:T(8,128)(2,1)S(1)}, u32[]{:S(2)}, u32[]{:S(2)}) collective-permute-start(bf16[1,3,6,2,16,256]{5,4,3,2,1,0:T(8,128)(2,1)S(1)} %get-tuple-element.119.refs_0_), channel_id=1, source_target_pairs={{0,4},{4,0},{8,12},{12,8},{1,5},{5,1},{9,13},{13,9},{2,6},{6,2},{1... | collective-permute-start | bytes 884744 | tf_op jit(solution)/shard_map/ppermute | solution.py:19
  59.2 15.5 %collective-permute-start.10 = (bf16[1,3,6,2,16,256]{5,4,3,2,1,0:T(8,128)(2,1)S(1)}, bf16[1,3,6,2,16,256]{5,4,3,2,1,0:T(8,128)(2,1)S(1)}, u32[]{:S(2)}, u32[]{:S(2)}) collective-permute-start(bf16[1,3,6,2,16,256]{5,4,3,2,1,0:T(8,128)(2,1)S(1)} %get-tuple-element.122.refs_0_), channel_id=1, source_target_pairs={{0,8},{4,12},{8,0},{12,4},{1,9},{5,13},{9,1},{13,5},{2,10},{6,14},... | collective-permute-start | bytes 884744 | tf_op jit(solution)/shard_map/ppermute | solution.py:19
  59.3 16.6 %collective-permute-start.11 = (bf16[1,3,6,2,16,256]{5,4,3,2,1,0:T(8,128)(2,1)S(1)}, bf16[1,3,6,2,16,256]{5,4,3,2,1,0:T(8,128)(2,1)S(1)}, u32[]{:S(2)}, u32[]{:S(2)}) collective-permute-start(bf16[1,3,6,2,16,256]{5,4,3,2,1,0:T(8,128)(2,1)S(1)} %get-tuple-element.126.refs_0_), channel_id=1, source_target_pairs={{0,4},{4,0},{8,12},{12,8},{1,5},{5,1},{9,13},{13,9},{2,6},{6,2},{1... | collective-permute-start | bytes 884744 | tf_op jit(solution)/shard_map/ppermute | solution.py:19
  63.6 4.6 %collective-permute-start.8 = (bf16[6,2,16,256]{3,2,1,0:T(8,128)(2,1)S(1)}, bf16[6,2,16,256]{3,2,1,0:T(8,128)(2,1)S(1)}, u32[]{:S(2)}, u32[]{:S(2)}) collective-permute-start(bf16[6,2,16,256]{3,2,1,0:T(8,128)(2,1)S(1)} %get-tuple-element.117), channel_id=1, source_target_pairs={{0,16},{16,0},{1,17},{17,1},{2,18},{18,2},{3,19},{19,3},{4,20},{20... | collective-permute-start | bytes 294920 | tf_op jit(solution)/shard_map/ppermute | solution.py:19
  71.3 9.0 %collective-permute-start.12 = (bf16[1,3,6,2,16,256]{5,4,3,2,1,0:T(8,128)(2,1)S(1)}, bf16[1,3,6,2,16,256]{5,4,3,2,1,0:T(8,128)(2,1)S(1)}, u32[]{:S(2)}, u32[]{:S(2)}) collective-permute-start(bf16[1,3,6,2,16,256]{5,4,3,2,1,0:T(8,128)(2,1)S(1)} %get-tuple-element.129.refs_0_), channel_id=1, source_target_pairs={{0,4},{4,0},{8,12},{12,8},{1,5},{5,1},{9,13},{13,9},{2,6},{6,2},{1... | collective-permute-start | bytes 884744 | tf_op jit(solution)/shard_map/ppermute | solution.py:19
  77.0 8.3 %collective-permute-start.15 = (bf16[512,256]{1,0:T(8,128)(2,1)S(1)}, bf16[512,256]{1,0:T(8,128)(2,1)S(1)}, u32[]{:S(2)}, u32[]{:S(2)}) collective-permute-start(bf16[512,256]{1,0:T(8,128)(2,1)S(1)} %get-tuple-element.138), channel_id=1, source_target_pairs={{0,1},{1,0},{2,3},{3,2},{4,5},{5,4},{6,7},{7,6},{8,9},{9,8},{10,11... | collective-permute-start | bytes 786440 | tf_op jit(solution)/shard_map/ppermute | solution.py:19
  77.1 12.2 %collective-permute-start.16 = (bf16[1,3,6,2,16,256]{5,4,3,2,1,0:T(8,128)(2,1)S(1)}, bf16[1,3,6,2,16,256]{5,4,3,2,1,0:T(8,128)(2,1)S(1)}, u32[]{:S(2)}, u32[]{:S(2)}) collective-permute-start(bf16[1,3,6,2,16,256]{5,4,3,2,1,0:T(8,128)(2,1)S(1)} %get-tuple-element.140.refs_0_), channel_id=1, source_target_pairs={{0,4},{4,0},{8,12},{12,8},{1,5},{5,1},{9,13},{13,9},{2,6},{6,2},{1... | collective-permute-start | bytes 884744 | tf_op jit(solution)/shard_map/ppermute | solution.py:19
  78.2 6.5 %collective-permute-start.13 = (bf16[256,256]{1,0:T(8,128)(2,1)S(1)}, bf16[256,256]{1,0:T(8,128)(2,1)S(1)}, u32[]{:S(2)}, u32[]{:S(2)}) collective-permute-start(bf16[256,256]{1,0:T(8,128)(2,1)S(1)} %get-tuple-element.133), channel_id=1, source_target_pairs={{0,1},{1,0},{2,3},{3,2},{4,5},{5,4},{6,7},{7,6},{8,9},{9,8},{10,11... | collective-permute-start | bytes 393224 | tf_op jit(solution)/shard_map/ppermute | solution.py:19
  78.4 6.3 %collective-permute-start.14 = (bf16[256,256]{1,0:T(8,128)(2,1)S(1)}, bf16[256,256]{1,0:T(8,128)(2,1)S(1)}, u32[]{:S(2)}, u32[]{:S(2)}) collective-permute-start(bf16[256,256]{1,0:T(8,128)(2,1)S(1)} %get-tuple-element.135), channel_id=1, source_target_pairs={{0,1},{1,0},{2,3},{3,2},{4,5},{5,4},{6,7},{7,6},{8,9},{9,8},{10,11... | collective-permute-start | bytes 393224 | tf_op jit(solution)/shard_map/ppermute | solution.py:19
  85.9 7.2 %collective-permute-start.18 = (bf16[512,256]{1,0:T(8,128)(2,1)S(1)}, bf16[512,256]{1,0:T(8,128)(2,1)S(1)}, u32[]{:S(2)}, u32[]{:S(2)}) collective-permute-start(bf16[512,256]{1,0:T(8,128)(2,1)S(1)} %get-tuple-element.148.refs_0_), channel_id=1, source_target_pairs={{0,16},{16,0},{1,17},{17,1},{2,18},{18,2},{3,19},{19,3},{4,20},{20... | collective-permute-start | bytes 786440 | tf_op jit(solution)/shard_map/ppermute | solution.py:19
  87.6 7.0 %collective-permute-start.17 = (bf16[512,256]{1,0:T(8,128)(2,1)S(1)}, bf16[512,256]{1,0:T(8,128)(2,1)S(1)}, u32[]{:S(2)}, u32[]{:S(2)}) collective-permute-start(bf16[512,256]{1,0:T(8,128)(2,1)S(1)} %get-tuple-element.147.refs_0_), channel_id=1, source_target_pairs={{0,4},{4,0},{8,12},{12,8},{1,5},{5,1},{9,13},{13,9},{2,6},{6,2},{1... | collective-permute-start | bytes 786440 | tf_op jit(solution)/shard_map/ppermute | solution.py:19
  92.5 2.7 %collective-permute-start.19 = (bf16[288,256]{1,0:T(8,128)(2,1)S(1)}, bf16[288,256]{1,0:T(8,128)(2,1)S(1)}, u32[]{:S(2)}, u32[]{:S(2)}) collective-permute-start(bf16[288,256]{1,0:T(8,128)(2,1)S(1)} %get-tuple-element.151), channel_id=1, source_target_pairs={{0,1},{1,0},{2,3},{3,2},{4,5},{5,4},{6,7},{7,6},{8,9},{9,8},{10,11... | collective-permute-start | bytes 442376 | tf_op jit(solution)/shard_map/ppermute | solution.py:19
  92.6 2.6 %collective-permute-start.20 = (bf16[256,256]{1,0:T(8,128)(2,1)S(1)}, bf16[256,256]{1,0:T(8,128)(2,1)S(1)}, u32[]{:S(2)}, u32[]{:S(2)}) collective-permute-start(bf16[256,256]{1,0:T(8,128)(2,1)S(1)} %get-tuple-element.153), channel_id=1, source_target_pairs={{0,1},{1,0},{2,3},{3,2},{4,5},{5,4},{6,7},{7,6},{8,9},{9,8},{10,11... | collective-permute-start | bytes 393224 | tf_op jit(solution)/shard_map/ppermute | solution.py:19
  95.8 7.8 %collective-permute-start.21 = (bf16[544,256]{1,0:T(8,128)(2,1)S(1)}, bf16[544,256]{1,0:T(8,128)(2,1)S(1)}, u32[]{:S(2)}, u32[]{:S(2)}) collective-permute-start(bf16[544,256]{1,0:T(8,128)(2,1)S(1)} %get-tuple-element.155.refs_0_), channel_id=1, source_target_pairs={{0,2},{1,3},{2,0},{3,1},{4,6},{5,7},{6,4},{7,5},{8,10},{9,11},{10,... | collective-permute-start | bytes 835592 | tf_op jit(solution)/shard_map/ppermute | solution.py:19
  97.4 9.5 %collective-permute-start.22 = (bf16[512,256]{1,0:T(8,128)(2,1)S(1)}, bf16[512,256]{1,0:T(8,128)(2,1)S(1)}, u32[]{:S(2)}, u32[]{:S(2)}) collective-permute-start(bf16[512,256]{1,0:T(8,128)(2,1)S(1)} %get-tuple-element.158.refs_0_), channel_id=1, source_target_pairs={{0,16},{16,0},{1,17},{17,1},{2,18},{18,2},{3,19},{19,3},{4,20},{20... | collective-permute-start | bytes 786440 | tf_op jit(solution)/shard_map/ppermute | solution.py:19
  98.0 21.5 %collective-permute-start.26 = (bf16[432,512]{1,0:T(8,128)(2,1)S(1)}, bf16[432,512]{1,0:T(8,128)(2,1)S(1)}, u32[]{:S(2)}, u32[]{:S(2)}) collective-permute-start(bf16[432,512]{1,0:T(8,128)(2,1)S(1)} %get-tuple-element.165), channel_id=1, source_target_pairs={{0,16},{16,0},{1,17},{17,1},{2,18},{18,2},{3,19},{19,3},{4,20},{20... | collective-permute-start | bytes 1327112 | tf_op jit(solution)/shard_map/ppermute | solution.py:19
  104.3 15.7 %collective-permute-start.25 = (bf16[544,256]{1,0:T(8,128)(2,1)S(1)}, bf16[544,256]{1,0:T(8,128)(2,1)S(1)}, u32[]{:S(2)}, u32[]{:S(2)}) collective-permute-start(bf16[544,256]{1,0:T(8,128)(2,1)S(1)} %get-tuple-element.164.refs_0_), channel_id=1, source_target_pairs={{0,16},{16,0},{1,17},{17,1},{2,18},{18,2},{3,19},{19,3},{4,20},{20... | collective-permute-start | bytes 835592 | tf_op jit(solution)/shard_map/ppermute | solution.py:19
  106.1 9.3 %collective-permute-start.23 = (bf16[512,256]{1,0:T(8,128)(2,1)S(1)}, bf16[512,256]{1,0:T(8,128)(2,1)S(1)}, u32[]{:S(2)}, u32[]{:S(2)}) collective-permute-start(bf16[512,256]{1,0:T(8,128)(2,1)S(1)} %get-tuple-element.160.refs_0_), channel_id=1, source_target_pairs={{0,2},{1,3},{2,0},{3,1},{4,6},{5,7},{6,4},{7,5},{8,10},{9,11},{10,... | collective-permute-start | bytes 786440 | tf_op jit(solution)/shard_map/ppermute | solution.py:19
  107.6 11.3 %collective-permute-start.24 = (bf16[512,256]{1,0:T(8,128)(2,1)S(1)}, bf16[512,256]{1,0:T(8,128)(2,1)S(1)}, u32[]{:S(2)}, u32[]{:S(2)}) collective-permute-start(bf16[512,256]{1,0:T(8,128)(2,1)S(1)} %get-tuple-element.162.refs_0_), channel_id=1, source_target_pairs={{0,2},{1,3},{2,0},{3,1},{4,6},{5,7},{6,4},{7,5},{8,10},{9,11},{10,... | collective-permute-start | bytes 786440 | tf_op jit(solution)/shard_map/ppermute | solution.py:19
  120.6 3.5 %collective-permute-start.29 = (f32[544,256]{1,0:T(8,128)S(1)}, f32[544,256]{1,0:T(8,128)S(1)}, u32[]{:S(2)}, u32[]{:S(2)}) collective-permute-start(f32[544,256]{1,0:T(8,128)S(1)} %get-tuple-element.177.refs_4_), channel_id=1, source_target_pairs={{0,1},{1,0},{2,3},{3,2},{4,5},{5,4},{6,7},{7,6},{8,9},{9,8},{10,11... | collective-permute-start | bytes 1671176 | tf_op jit(solution)/shard_map/ppermute | solution.py:19
  120.7 2.8 %collective-permute-start.28 = (f32[512,256]{1,0:T(8,128)S(1)}, f32[512,256]{1,0:T(8,128)S(1)}, u32[]{:S(2)}, u32[]{:S(2)}) collective-permute-start(f32[512,256]{1,0:T(8,128)S(1)} %get-tuple-element.176.refs_2_), channel_id=1, source_target_pairs={{0,1},{1,0},{2,3},{3,2},{4,5},{5,4},{6,7},{7,6},{8,9},{9,8},{10,11... | collective-permute-start | bytes 1572872 | tf_op jit(solution)/shard_map/ppermute | solution.py:19
  121.2 2.9 %collective-permute-start.27 = (f32[512,256]{1,0:T(8,128)S(1)}, f32[512,256]{1,0:T(8,128)S(1)}, u32[]{:S(2)}, u32[]{:S(2)}) collective-permute-start(f32[512,256]{1,0:T(8,128)S(1)} %get-tuple-element.175.refs_0_), channel_id=1, source_target_pairs={{0,1},{1,0},{2,3},{3,2},{4,5},{5,4},{6,7},{7,6},{8,9},{9,8},{10,11... | collective-permute-start | bytes 1572872 | tf_op jit(solution)/shard_map/ppermute | solution.py:19

commit v7 on v6

--- a/solution.py
+++ b/solution.py
@@ -551,36 +551,58 @@
     )
 
 
-def finish_kernel(place, own30, far30, own_proj, far_proj, own21, far21, proj_ref, depth_ref, point_ref):
-    core = place[2] == 0
-
-    def halves(own, far, first, count):
-        own, far = own[first : first + count], far[first : first + count]
-        return jnp.where(core, own, far), jnp.where(core, far, own)
-
-    channels = point_ref.shape[1]
-    filters = proj_ref.shape[1]
+def finish_kernel(
+    place, own30, far30, own_proj, far_proj, own21, far21, low21, high21, proj_ref, depth_ref, point_ref, sems
+):
+    core = place[2]
+    channels, filters = point_ref.shape[1:]
     half = channels // 2
-    point_ref[3], point_ref[0] = halves(own30, far30, 0, channels)
-    proj_ref[3], proj_ref[0] = halves(own_proj, far_proj, 0, filters)
-    proj_ref[1], proj_ref[2] = halves(own_proj, far_proj, filters, filters)
-    point_ref[2, :half], point_ref[2, half:] = halves(own21, far21, 0, half)
-    low, high = halves(own21, far21, half, 27)
+    first = own21.shape[0] - half
+    copies = []
+
+    def copy(source, target):
+        moving = pltpu.make_async_copy(source, target, sems.at[len(copies)])
+        moving.start()
+        copies.append(moving)
+
+    for mine, pair in ((core, (own30, own_proj, own21)), (1 - core, (far30, far_proj, far21))):
+        points, projs, mixed = pair
+        copy(points, point_ref.at[3 - 3 * mine])
+        copy(projs.at[pl.ds(0, filters)], proj_ref.at[3 - 3 * mine])
+        copy(projs.at[pl.ds(filters, filters)], proj_ref.at[1 + mine])
+        rows = pl.ds(pl.multiple_of(mine * half, half), half)
+        copy(mixed.at[pl.ds(0, half)], point_ref.at[2, rows])
+        copy(mixed.at[pl.ds(first, half)], point_ref.at[1, rows])
+    low = jnp.where(core == 0, low21[...], high21[...])
+    high = jnp.where(core == 0, high21[...], low21[...])
     for k in range(9):
         rows = slice(3 * k, 3 * k + 3)
         depth_ref[k // 3, k % 3, :, :filters] = low[rows]
         depth_ref[k // 3, k % 3, :, filters:] = high[rows]
-    first = own21.shape[0] - half
-    point_ref[1, :half], point_ref[1, half:] = halves(own21, far21, first, half)
+    for moving in copies:
+        moving.wait()
 
 
 def finish(place, after, early, proj, late, channels, filters):
     arrays = [*early, *proj, *late]
+    half = channels // 2
+    depth_spec = pl.BlockSpec((32, filters), lambda r, p: (half // 32, 0))
+    anywhere = pl.BlockSpec(memory_space=pl.ANY)
     shapes = [(4, filters, filters), (3, 3, 3, channels), (4, channels, filters)]
-    return call(
-        finish_kernel, place, 1, after, [(a, a.shape, None) for a in arrays],
-        [(result_of(s, F32), s, None) for s in shapes], "finish",
-    )
+    out = pl.pallas_call(
+        finish_kernel,
+        grid_spec=pltpu.PrefetchScalarGridSpec(
+            num_scalar_prefetch=1,
+            grid=(1,),
+            in_specs=[anywhere] * 6 + [depth_spec] * 2,
+            out_specs=[anywhere, pl.BlockSpec(shapes[1], lambda r, p: (0, 0, 0, 0)), anywhere],
+            scratch_shapes=[pltpu.SemaphoreType.DMA((10,))],
+        ),
+        out_shape=[result_of(s, F32) for s in shapes],
+        compiler_params=pltpu.CompilerParams(vmem_limit_bytes=VMEM_BYTES),
+        name="finish",
+    )(place, *arrays, *late)
+    return (*out, after)
 
 
 def by_classes(features_in, depth_weights, point_weights, proj_weights, cotangent):

time: 127 us -> 127 us (level)
    pallas_call x0 -> x1, Pallas kernels: none -> 2.91 us  [finish(): pl.pallas_call(finish_kernel, grid_spec=pltpu.PrefetchScalarGridSpec(num_...]
    pallas_call x27 -> x26, Pallas kernels: 37 us -> 34.5 us  [call(): pl.pallas_call(kernel, grid_spec=pltpu.PrefetchScalarGridSpec(num_scalar_...]
  transfers between devices with their start and end apart: 30 -> 30, of which waited for: 16 -> 15; matrix products, arithmetic and copies ran while one was open for 0% -> 0% of each run, Pallas kernels for 24% -> 24%
where the time goes in v7:
time: 127 us
  waiting for transfers between devices  53.5 us (42%)
  Pallas kernels  37.4 us (29%)
  starting transfers between devices  35 us (28%)
    ppermute x30, waiting for transfers between devices, swap(): return lax.ppermute(value, axis, [(i, i ^ flip) for i in range(count)])  53.5 us
    ppermute x30, starting transfers between devices, swap(): return lax.ppermute(value, axis, [(i, i ^ flip) for i in range(count)])  35 us
    pallas_call x26, Pallas kernels, call(): pl.pallas_call(kernel, grid_spec=pltpu.PrefetchScalarGridSpec(num_scalar_...  34.5 us
    pallas_call x1, Pallas kernels, finish(): pl.pallas_call(finish_kernel, grid_spec=pltpu.PrefetchScalarGridSpec(num_...  2.91 us
  transfers between devices with their start and end apart: 30, of which 15 were waited for; matrix products, arithmetic and copies ran while one was open for 0% of the time, Pallas kernels for 24%

profile of v7, /device:TPU:0, one launch (start us, length us, event | category | flops | bytes accessed | tf_op | source)
XLA Modules:
  0.0 127.1 jit_solution(17160035624079226130)
XLA Ops:
  0.7 3.0 %forward_3.1 = (f32[1,3,6,2,16,256]{5,4,3,2,1,0:T(8,128)S(1)}, bf16[1,3,6,2,16,256]{5,4,3,2,1,0:T(8,128)(2,1)S(1)}, bf16[3,6,64,512]{3,2,1,0:T(8,128)(2,1)S(1)}, f32[8,128]{1,0:T(8,128)S(1)}) custom-call(s32[3]{0:T(128)S(1)} %pad_add_fusion.place_ref.place, f32[8,128]{1,0:T(8,128)S(1)} %broadcast_in_dim.6.after_ref, bf16[3,6,64,512]{3,2,1,0:T(8,128)(2,1)} %bitcast.9, ...), custom_call_target="tpu_custom_call" | custom-call | flops 1 | bytes 1 | tf_op jit(solution)/shard_map/forward_3/pallas_call | solution.py:99
  3.7 3.1 %collective-permute-start = (bf16[1,3,6,2,16,256]{5,4,3,2,1,0:T(8,128)(2,1)S(1)}, bf16[1,3,6,2,16,256]{5,4,3,2,1,0:T(8,128)(2,1)S(1)}, u32[]{:S(2)}, u32[]{:S(2)}) collective-permute-start(bf16[1,3,6,2,16,256]{5,4,3,2,1,0:T(8,128)(2,1)S(1)} %get-tuple-element.95), channel_id=1, source_target_pairs={{0,4},{4,0},{8,12},{12,8},{1,5},{5,1},{9,13},{13,9},{2,6},{6,2},{1... | collective-permute-start | bytes 884744 | tf_op jit(solution)/shard_map/ppermute | solution.py:19
  6.8 2.0 %forward_0.1 = (f32[1,3,6,2,16,256]{5,4,3,2,1,0:T(8,128)S(1)}, bf16[1,3,6,2,16,256]{5,4,3,2,1,0:T(8,128)(2,1)S(1)}, bf16[6,64,512]{2,1,0:T(8,128)(2,1)S(1)}, f32[8,128]{1,0:T(8,128)S(1)}) custom-call(s32[3]{0:T(128)S(1)} %pad_add_fusion.place_ref.place, f32[8,128]{1,0:T(8,128)S(1)} %get-tuple-element.92.after_ref, bf16[3,6,64,512]{3,2,1,0:T(8,128)(2,1)S(1)} %bitcast.11, ...), custom_call_target="tpu_custom_call" | custom-call | flops 1 | bytes 1 | tf_op jit(solution)/shard_map/forward_0/pallas_call | solution.py:99
  8.8 1.6 %collective-permute-start.1 = (bf16[6,64,512]{2,1,0:T(8,128)(2,1)S(1)}, bf16[6,64,512]{2,1,0:T(8,128)(2,1)S(1)}, u32[]{:S(2)}, u32[]{:S(2)}) collective-permute-start(bf16[6,64,512]{2,1,0:T(8,128)(2,1)S(1)} %get-tuple-element.97), channel_id=1, source_target_pairs={{0,16},{16,0},{1,17},{17,1},{2,18},{18,2},{3,19},{19,3},{4,20},{20... | collective-permute-start | bytes 1179656 | tf_op jit(solution)/shard_map/ppermute | solution.py:19
  10.4 0.5 collective-permute-start.2
  10.8 3.8 %collective-permute-done.refs_1_ = bf16[1,3,6,2,16,256]{5,4,3,2,1,0:T(8,128)(2,1)S(1)} collective-permute-done((bf16[1,3,6,2,16,256]{5,4,3,2,1,0:T(8,128)(2,1)S(1)}, bf16[1,3,6,2,16,256]{5,4,3,2,1,0:T(8,128)(2,1)S(1)}, u32[]{:S(2)}, u32[]{:S(2)}) %collective-permute-start) | collective-permute-done | bytes 294944 | tf_op jit(solution)/shard_map/ppermute | solution.py:19
  14.6 0.6 near_3.1
  15.2 3.1 %collective-permute-start.3 = (bf16[1,3,6,3,16,256]{5,4,3,2,1,0:T(8,128)(2,1)S(1)}, bf16[1,3,6,3,16,256]{5,4,3,2,1,0:T(8,128)(2,1)S(1)}, u32[]{:S(2)}, u32[]{:S(2)}) collective-permute-start(bf16[1,3,6,3,16,256]{5,4,3,2,1,0:T(8,128)(2,1)S(1)} %get-tuple-element.102.refs_0_), channel_id=1, source_target_pairs={{0,8},{4,12},{8,0},{12,4},{1,9},{5,13},{9,1},{13,5},{2,10},{6,14},... | collective-permute-start | bytes 1327112 | tf_op jit(solution)/shard_map/ppermute | solution.py:19
  18.4 1.1 collective-permute-done.1.refs_1_.refs_3_
  19.4 3.6 %forward_1_2.1 = (f32[1,3,6,2,16,256]{5,4,3,2,1,0:T(8,128)S(1)}, f32[1,3,6,2,16,256]{5,4,3,2,1,0:T(8,128)S(1)}, bf16[1,3,6,2,16,256]{5,4,3,2,1,0:T(8,128)(2,1)S(...) custom-call(s32[3]{0:T(128)S(1)} %pad_add_fusion.place_ref.place, ...), custom_call_target="tpu_custom_call" | custom-call | flops 1 | bytes 1 | tf_op jit(solution)/shard_map/forward_1_2/pallas_call | solution.py:99
  23.1 0.6 collective-permute-start.4
  23.7 2.3 %collective-permute-done.2.refs_1_ = bf16[1,3,6,2,16,256]{5,4,3,2,1,0:T(8,128)(2,1)S(1)} collective-permute-done((bf16[1,3,6,2,16,256]{5,4,3,2,1,0:T(8,128)(2,1)S(1)}, bf16[1,3,6,2,16,256]{5,4,3,2,1,0:T(8,128)(2,1)S(1)}, u32[]{:S(2)}, u32[]{:S(2)}) %collective-permute-start.2) | collective-permute-done | bytes 294944 | tf_op jit(solution)/shard_map/ppermute | solution.py:19
  26.0 0.6 near_0.1
  26.6 0.3 collective-permute-start.5
  26.9 1.6 %collective-permute-start.6 = (bf16[1,3,6,2,16,256]{5,4,3,2,1,0:T(8,128)(2,1)S(1)}, bf16[1,3,6,2,16,256]{5,4,3,2,1,0:T(8,128)(2,1)S(1)}, u32[]{:S(2)}, u32[]{:S(2)}) collective-permute-start(bf16[1,3,6,2,16,256]{5,4,3,2,1,0:T(8,128)(2,1)S(1)} %get-tuple-element.113), channel_id=1, source_target_pairs={{0,4},{4,0},{8,12},{12,8},{1,5},{5,1},{9,13},{13,9},{2,6},{6,2},{1... | collective-permute-start | bytes 884744 | tf_op jit(solution)/shard_map/ppermute | solution.py:19
  28.4 16.5 %collective-permute-done.3.refs_1_ = bf16[1,3,6,3,16,256]{5,4,3,2,1,0:T(8,128)(2,1)S(1)} collective-permute-done((bf16[1,3,6,3,16,256]{5,4,3,2,1,0:T(8,128)(2,1)S(1)}, bf16[1,3,6,3,16,256]{5,4,3,2,1,0:T(8,128)(2,1)S(1)}, u32[]{:S(2)}, u32[]{:S(2)}) %collective-permute-start.3) | collective-permute-done | bytes 442400 | tf_op jit(solution)/shard_map/ppermute | solution.py:19
  45.0 1.0 gate_3.1
  46.0 0.6 near_1.1
  46.7 4.3 %collective-permute-start.9 = (bf16[1,3,6,2,16,256]{5,4,3,2,1,0:T(8,128)(2,1)S(1)}, bf16[1,3,6,2,16,256]{5,4,3,2,1,0:T(8,128)(2,1)S(1)}, u32[]{:S(2)}, u32[]{:S(2)}) collective-permute-start(bf16[1,3,6,2,16,256]{5,4,3,2,1,0:T(8,128)(2,1)S(1)} %get-tuple-element.118.refs_0_), channel_id=1, source_target_pairs={{0,4},{4,0},{8,12},{12,8},{1,5},{5,1},{9,13},{13,9},{2,6},{6,2},{1... | collective-permute-start | bytes 884744 | tf_op jit(solution)/shard_map/ppermute | solution.py:19
  51.0 6.6 %collective-permute-done.5.refs_1_ = bf16[1,3,6,2,16,256]{5,4,3,2,1,0:T(8,128)(2,1)S(1)} collective-permute-done((bf16[1,3,6,2,16,256]{5,4,3,2,1,0:T(8,128)(2,1)S(1)}, bf16[1,3,6,2,16,256]{5,4,3,2,1,0:T(8,128)(2,1)S(1)}, u32[]{:S(2)}, u32[]{:S(2)}) %collective-permute-start.5) | collective-permute-done | bytes 294944 | tf_op jit(solution)/shard_map/ppermute | solution.py:19
  57.6 1.0 gate_0.1
  58.7 0.6 near_2.1
  59.3 4.3 %collective-permute-start.11 = (bf16[1,3,6,2,16,256]{5,4,3,2,1,0:T(8,128)(2,1)S(1)}, bf16[1,3,6,2,16,256]{5,4,3,2,1,0:T(8,128)(2,1)S(1)}, u32[]{:S(2)}, u32[]{:S(2)}) collective-permute-start(bf16[1,3,6,2,16,256]{5,4,3,2,1,0:T(8,128)(2,1)S(1)} %get-tuple-element.125.refs_0_), channel_id=1, source_target_pairs={{0,4},{4,0},{8,12},{12,8},{1,5},{5,1},{9,13},{13,9},{2,6},{6,2},{1... | collective-permute-start | bytes 884744 | tf_op jit(solution)/shard_map/ppermute | solution.py:19
  63.6 1.5 %collective-permute-start.8 = (bf16[6,2,16,256]{3,2,1,0:T(8,128)(2,1)S(1)}, bf16[6,2,16,256]{3,2,1,0:T(8,128)(2,1)S(1)}, u32[]{:S(2)}, u32[]{:S(2)}) collective-permute-start(bf16[6,2,16,256]{3,2,1,0:T(8,128)(2,1)S(1)} %get-tuple-element.116), channel_id=1, source_target_pairs={{0,16},{16,0},{1,17},{17,1},{2,18},{18,2},{3,19},{19,3},{4,20},{20... | collective-permute-start | bytes 294920 | tf_op jit(solution)/shard_map/ppermute | solution.py:19
  65.1 3.1 %collective-permute-done.8.refs_3_ = bf16[6,2,16,256]{3,2,1,0:T(8,128)(2,1)S(1)} collective-permute-done((bf16[6,2,16,256]{3,2,1,0:T(8,128)(2,1)S(1)}, bf16[6,2,16,256]{3,2,1,0:T(8,128)(2,1)S(1)}, u32[]{:S(2)}, u32[]{:S(2)}) %collective-permute-start.8) | collective-permute-done | bytes 98336 | tf_op jit(solution)/shard_map/ppermute | solution.py:19
  68.2 2.1 %collective-permute-done.7.refs_1_ = bf16[1,3,6,2,16,256]{5,4,3,2,1,0:T(8,128)(2,1)S(1)} collective-permute-done((bf16[1,3,6,2,16,256]{5,4,3,2,1,0:T(8,128)(2,1)S(1)}, bf16[1,3,6,2,16,256]{5,4,3,2,1,0:T(8,128)(2,1)S(1)}, u32[]{:S(2)}, u32[]{:S(2)}) %collective-permute-start.7) | collective-permute-done | bytes 294944 | tf_op jit(solution)/shard_map/ppermute | solution.py:19
  70.3 1.0 gate_1.1
  71.3 0.9 collective-permute-start.12
  72.3 2.5 %backward_3.1 = (f32[3,6,64,512]{3,2,1,0:T(8,128)S(1)}, f32[512,256]{1,0:T(8,128)S(1)}, f32[9,512]{1,0:T(8,128)S(1)}, f32[8,128]{1,0:T(8,128)S(1)}) custom-call(s32[3]{0:T(128)S(1)} %pad_add_fusion.place_ref.place, f32[8,128]{1,0:T(8,128)S(1)} %get-tuple-element.117.after_ref, bf16[1,3,6,2,16,256]{5,4,3,2,1,0:T(8,128)(2,1)S(1)} %get-tuple-element.118.refs_0_, ...), custom_call_target="tpu_custom_call" | custom-call | flops 1 | bytes 1 | tf_op jit(solution)/shard_map/backward_3/pallas_call | solution.py:99
  74.7 1.1 gate_2.1
  75.9 1.1 join.1
  77.1 1.2 collective-permute-start.16
  78.4 0.3 collective-permute-start.14
  78.8 1.5 %collective-permute-done.12.refs_1_ = bf16[1,3,6,2,16,256]{5,4,3,2,1,0:T(8,128)(2,1)S(1)} collective-permute-done((bf16[1,3,6,2,16,256]{5,4,3,2,1,0:T(8,128)(2,1)S(1)}, bf16[1,3,6,2,16,256]{5,4,3,2,1,0:T(8,128)(2,1)S(1)}, u32[]{:S(2)}, u32[]{:S(2)}) %collective-permute-start.12) | collective-permute-done | bytes 294944 | tf_op jit(solution)/shard_map/ppermute | solution.py:19
  80.3 4.3 %backward_1.1 = (f32[3,6,64,512]{3,2,1,0:T(8,128)S(1)}, f32[9,512]{1,0:T(8,128)S(1)}, f32[256,256]{1,0:T(8,128)S(1)}, bf16[256,256]{1,0:T(8,128)(2,1)S(1)}, f32[8,128]{1,0:T(8,128)S(1)}) custom-call(s32[3]{0:T(128)S(1)} %pad_add_fusion.place_ref.place, f32[8,128]{1,0:T(8,128)S(1)} %get-tuple-element.127.after_ref, ...), custom_call_target="tpu_custom_call" | custom-call | flops 1 | bytes 1 | tf_op jit(solution)/shard_map/backward_1/pallas_call | solution.py:99
  84.6 0.6 proj.1
  85.2 2.5 %collective-permute-start.17 = (bf16[512,256]{1,0:T(8,128)(2,1)S(1)}, bf16[512,256]{1,0:T(8,128)(2,1)S(1)}, u32[]{:S(2)}, u32[]{:S(2)}) collective-permute-start(bf16[512,256]{1,0:T(8,128)(2,1)S(1)} %get-tuple-element.146.refs_0_), channel_id=1, source_target_pairs={{0,4},{4,0},{8,12},{12,8},{1,5},{5,1},{9,13},{13,9},{2,6},{6,2},{1... | collective-permute-start | bytes 786440 | tf_op jit(solution)/shard_map/ppermute | solution.py:19
  87.8 0.6 early_1.1
  88.4 1.0 collective-permute-start.18
  89.3 3.2 %backward_2.1 = (bf16[432,512]{1,0:T(8,128)(2,1)S(1)}, f32[2,6,64,512]{3,2,1,0:T(8,128)S(1)}, f32[288,256]{1,0:T(8,128)S(1)}, bf16[288,256]{1,0:T(8,128)(2,1)S(1)}, f32[8,128]{1,0:T(8,128)S(1)}) custom-call(s32[3]{0:T(128)S(1)} %pad_add_fusion.place_ref.place, f32[8,128]{1,0:T(8,128)S(1)} %get-tuple-element.138.after_ref, ...), custom_call_target="tpu_custom_call" | custom-call | flops 1 | bytes 1 | tf_op jit(solution)/shard_map/backward_2/pallas_call | solution.py:99
  92.6 0.5 collective-permute-start.20
  93.1 1.7 %collective-permute-done.18.refs_2_.refs_1_ = bf16[512,256]{1,0:T(8,128)(2,1)S(1)} collective-permute-done((bf16[512,256]{1,0:T(8,128)(2,1)S(1)}, bf16[512,256]{1,0:T(8,128)(2,1)S(1)}, u32[]{:S(2)}, u32[]{:S(2)}) %collective-permute-start.18) | collective-permute-done | bytes 262176 | tf_op jit(solution)/shard_map/ppermute | solution.py:19
  94.8 0.6 proj_1.1
  95.4 0.6 late_1.1
  96.0 1.4 %collective-permute-start.21 = (bf16[544,256]{1,0:T(8,128)(2,1)S(1)}, bf16[544,256]{1,0:T(8,128)(2,1)S(1)}, u32[]{:S(2)}, u32[]{:S(2)}) collective-permute-start(bf16[544,256]{1,0:T(8,128)(2,1)S(1)} %get-tuple-element.154.refs_0_), channel_id=1, source_target_pairs={{0,2},{1,3},{2,0},{3,1},{4,6},{5,7},{6,4},{7,5},{8,10},{9,11},{10,... | collective-permute-start | bytes 835592 | tf_op jit(solution)/shard_map/ppermute | solution.py:19
  97.4 1.5 %collective-permute-start.22 = (bf16[512,256]{1,0:T(8,128)(2,1)S(1)}, bf16[512,256]{1,0:T(8,128)(2,1)S(1)}, u32[]{:S(2)}, u32[]{:S(2)}) collective-permute-start(bf16[512,256]{1,0:T(8,128)(2,1)S(1)} %get-tuple-element.157.refs_0_), channel_id=1, source_target_pairs={{0,16},{16,0},{1,17},{17,1},{2,18},{18,2},{3,19},{19,3},{4,20},{20... | collective-permute-start | bytes 786440 | tf_op jit(solution)/shard_map/ppermute | solution.py:19
  99.0 0.5 collective-permute-start.26
  99.5 4.2 %collective-permute-done.21.refs_1_ = bf16[544,256]{1,0:T(8,128)(2,1)S(1)} collective-permute-done((bf16[544,256]{1,0:T(8,128)(2,1)S(1)}, bf16[544,256]{1,0:T(8,128)(2,1)S(1)}, u32[]{:S(2)}, u32[]{:S(2)}) %collective-permute-start.21) | collective-permute-done | bytes 278560 | tf_op jit(solution)/shard_map/ppermute | solution.py:19
  103.7 0.6 late_2.1
  104.3 1.2 collective-permute-start.25
  105.5 0.6 early_2.1
  106.1 0.9 collective-permute-start.23
  107.0 0.6 proj_2.1
  107.6 1.2 collective-permute-start.24
  108.9 5.9 %collective-permute-done.23.refs_1_ = bf16[512,256]{1,0:T(8,128)(2,1)S(1)} collective-permute-done((bf16[512,256]{1,0:T(8,128)(2,1)S(1)}, bf16[512,256]{1,0:T(8,128)(2,1)S(1)}, u32[]{:S(2)}, u32[]{:S(2)}) %collective-permute-start.23) | collective-permute-done | bytes 262176 | tf_op jit(solution)/shard_map/ppermute | solution.py:19
  114.8 0.6 early.1
  115.4 2.2 %collective-permute-done.24.refs_1_ = bf16[512,256]{1,0:T(8,128)(2,1)S(1)} collective-permute-done((bf16[512,256]{1,0:T(8,128)(2,1)S(1)}, bf16[512,256]{1,0:T(8,128)(2,1)S(1)}, u32[]{:S(2)}, u32[]{:S(2)}) %collective-permute-start.24) | collective-permute-done | bytes 262176 | tf_op jit(solution)/shard_map/ppermute | solution.py:19
  117.6 0.6 proj_sum.1
  118.2 1.8 %collective-permute-done.25.refs_1_ = bf16[544,256]{1,0:T(8,128)(2,1)S(1)} collective-permute-done((bf16[544,256]{1,0:T(8,128)(2,1)S(1)}, bf16[544,256]{1,0:T(8,128)(2,1)S(1)}, u32[]{:S(2)}, u32[]{:S(2)}) %collective-permute-start.25) | collective-permute-done | bytes 278560 | tf_op jit(solution)/shard_map/ppermute | solution.py:19
  120.0 0.6 late.1
  120.7 0.5 collective-permute-start.27
  121.3 2.2 %last.1 = (bf16[3,6,64,512]{3,2,1,0:T(8,128)(2,1)}, bf16[3,6,16,256]{3,2,1,0:T(8,128)(2,1)}, f32[8,128]{1,0:T(8,128)}) custom-call(s32[3]{0:T(128)S(1)} %pad_add_fusion.place_ref.place, f32[8,128]{1,0:T(8,128)S(1)} %get-tuple-element.165.after_ref, bf16[3,6,64,256]{3,2,1,0:T(8,128)(2,1)S(1)} %get-tuple-element.166.refs_0_, ...), custom_call_target="tpu_custom_call" | custom-call | flops 1 | bytes 1 | tf_op jit(solution)/shard_map/last/pallas_call | solution.py:99
  123.5 0.6 collective-permute-done.28.far_proj
  124.1 2.9 %finish.1 = (f32[4,256,256]{2,1,0:T(8,128)}, f32[3,3,3,512]{3,2,1,0:T(4,128)}, f32[4,512,256]{2,1,0:T(8,128)}) custom-call(s32[3]{0:T(128)S(1)} %pad_add_fusion.place_ref.place, f32[512,256]{1,0:T(8,128)S(1)} %get-tuple-element.173.own30, f32[512,256]{1,0:T(8,128)S(1)} %collective-permute-done.27.far30, f32[512,256]{1,0:T(8,128)S(1)} %get-tuple-element.174.own_proj, ...), custom_call_target="tpu_custom_call" | custom-call | tf_op jit(solution)/shard_map/finish/pallas_call | solution.py:592
  (36 shorter events, 0.9 us)
Async XLA Ops:
  0.7 6.1 %copy-start = (bf16[1,18,64,512]{3,2,1,0:T(8,128)(2,1)S(1)}, bf16[1,18,64,512]{3,2,1,0:T(8,128)(2,1)}, u32[]{:S(2)}) copy-start(bf16[1,18,64,512]{3,2,1,0:T(8,128)(2,1)} %param.5) | copy-start | bytes 3538948
  3.7 10.9 %collective-permute-start = (bf16[1,3,6,2,16,256]{5,4,3,2,1,0:T(8,128)(2,1)S(1)}, bf16[1,3,6,2,16,256]{5,4,3,2,1,0:T(8,128)(2,1)S(1)}, u32[]{:S(2)}, u32[]{:S(2)}) collective-permute-start(bf16[1,3,6,2,16,256]{5,4,3,2,1,0:T(8,128)(2,1)S(1)} %get-tuple-element.95), channel_id=1, source_target_pairs={{0,4},{4,0},{8,12},{12,8},{1,5},{5,1},{9,13},{13,9},{2,6},{6,2},{1... | collective-permute-start | bytes 884744 | tf_op jit(solution)/shard_map/ppermute | solution.py:19
  6.8 7.8 %copy-start.4 = (bf16[1,18,16,256]{3,2,1,0:T(8,128)(2,1)S(1)}, bf16[1,18,16,256]{3,2,1,0:T(8,128)(2,1)}, u32[]{:S(2)}) copy-start(bf16[1,18,16,256]{3,2,1,0:T(8,128)(2,1)} %param.9) | copy-start | bytes 442372
  6.8 12.7 %copy-start.3 = (bf16[3,3,3,512]{3,2,1,0:T(4,128)(2,1)S(1)}, bf16[3,3,3,512]{3,2,1,0:T(4,128)(2,1)}, u32[]{:S(2)}) copy-start(bf16[3,3,3,512]{3,2,1,0:T(4,128)(2,1)} %refs_5_.5) | copy-start | bytes 82948
  8.8 10.7 %copy-start.1 = (bf16[4,512,256]{2,1,0:T(8,128)(2,1)S(1)}, bf16[4,512,256]{2,1,0:T(8,128)(2,1)}, u32[]{:S(2)}) copy-start(bf16[4,512,256]{2,1,0:T(8,128)(2,1)} %refs_1_.1) | copy-start | bytes 3145732
  8.8 10.6 %collective-permute-start.1 = (bf16[6,64,512]{2,1,0:T(8,128)(2,1)S(1)}, bf16[6,64,512]{2,1,0:T(8,128)(2,1)S(1)}, u32[]{:S(2)}, u32[]{:S(2)}) collective-permute-start(bf16[6,64,512]{2,1,0:T(8,128)(2,1)S(1)} %get-tuple-element.97), channel_id=1, source_target_pairs={{0,16},{16,0},{1,17},{17,1},{2,18},{18,2},{3,19},{19,3},{4,20},{20... | collective-permute-start | bytes 1179656 | tf_op jit(solution)/shard_map/ppermute | solution.py:19
  10.4 15.6 %collective-permute-start.2 = (bf16[1,3,6,2,16,256]{5,4,3,2,1,0:T(8,128)(2,1)S(1)}, bf16[1,3,6,2,16,256]{5,4,3,2,1,0:T(8,128)(2,1)S(1)}, u32[]{:S(2)}, u32[]{:S(2)}) collective-permute-start(bf16[1,3,6,2,16,256]{5,4,3,2,1,0:T(8,128)(2,1)S(1)} %get-tuple-element.100), channel_id=1, source_target_pairs={{0,4},{4,0},{8,12},{12,8},{1,5},{5,1},{9,13},{13,9},{2,6},{6,2},{1... | collective-permute-start | bytes 884744 | tf_op jit(solution)/shard_map/ppermute | solution.py:19
  15.2 29.7 %collective-permute-start.3 = (bf16[1,3,6,3,16,256]{5,4,3,2,1,0:T(8,128)(2,1)S(1)}, bf16[1,3,6,3,16,256]{5,4,3,2,1,0:T(8,128)(2,1)S(1)}, u32[]{:S(2)}, u32[]{:S(2)}) collective-permute-start(bf16[1,3,6,3,16,256]{5,4,3,2,1,0:T(8,128)(2,1)S(1)} %get-tuple-element.102.refs_0_), channel_id=1, source_target_pairs={{0,8},{4,12},{8,0},{12,4},{1,9},{5,13},{9,1},{13,5},{2,10},{6,14},... | collective-permute-start | bytes 1327112 | tf_op jit(solution)/shard_map/ppermute | solution.py:19
  23.1 21.9 %copy-start.2 = (bf16[4,256,256]{2,1,0:T(8,128)(2,1)S(1)}, bf16[4,256,256]{2,1,0:T(8,128)(2,1)}, u32[]{:S(2)}) copy-start(bf16[4,256,256]{2,1,0:T(8,128)(2,1)} %refs_4_.5) | copy-start | bytes 1572868
  23.1 22.9 %collective-permute-start.4 = (bf16[1,3,6,2,16,256]{5,4,3,2,1,0:T(8,128)(2,1)S(1)}, bf16[1,3,6,2,16,256]{5,4,3,2,1,0:T(8,128)(2,1)S(1)}, u32[]{:S(2)}, u32[]{:S(2)}) collective-permute-start(bf16[1,3,6,2,16,256]{5,4,3,2,1,0:T(8,128)(2,1)S(1)} %get-tuple-element.105), channel_id=1, source_target_pairs={{0,4},{4,0},{8,12},{12,8},{1,5},{5,1},{9,13},{13,9},{2,6},{6,2},{1... | collective-permute-start | bytes 884744 | tf_op jit(solution)/shard_map/ppermute | solution.py:19
  26.6 31.0 %collective-permute-start.5 = (bf16[1,3,6,2,16,256]{5,4,3,2,1,0:T(8,128)(2,1)S(1)}, bf16[1,3,6,2,16,256]{5,4,3,2,1,0:T(8,128)(2,1)S(1)}, u32[]{:S(2)}, u32[]{:S(2)}) collective-permute-start(bf16[1,3,6,2,16,256]{5,4,3,2,1,0:T(8,128)(2,1)S(1)} %get-tuple-element.107.refs_0_), channel_id=1, source_target_pairs={{0,8},{4,12},{8,0},{12,4},{1,9},{5,13},{9,1},{13,5},{2,10},{6,14},... | collective-permute-start | bytes 884744 | tf_op jit(solution)/shard_map/ppermute | solution.py:19
  26.9 31.8 %collective-permute-start.6 = (bf16[1,3,6,2,16,256]{5,4,3,2,1,0:T(8,128)(2,1)S(1)}, bf16[1,3,6,2,16,256]{5,4,3,2,1,0:T(8,128)(2,1)S(1)}, u32[]{:S(2)}, u32[]{:S(2)}) collective-permute-start(bf16[1,3,6,2,16,256]{5,4,3,2,1,0:T(8,128)(2,1)S(1)} %get-tuple-element.113), channel_id=1, source_target_pairs={{0,4},{4,0},{8,12},{12,8},{1,5},{5,1},{9,13},{13,9},{2,6},{6,2},{1... | collective-permute-start | bytes 884744 | tf_op jit(solution)/shard_map/ppermute | solution.py:19
  46.6 23.7 %collective-permute-start.7 = (bf16[1,3,6,2,16,256]{5,4,3,2,1,0:T(8,128)(2,1)S(1)}, bf16[1,3,6,2,16,256]{5,4,3,2,1,0:T(8,128)(2,1)S(1)}, u32[]{:S(2)}, u32[]{:S(2)}) collective-permute-start(bf16[1,3,6,2,16,256]{5,4,3,2,1,0:T(8,128)(2,1)S(1)} %get-tuple-element.115.refs_0_), channel_id=1, source_target_pairs={{0,8},{4,12},{8,0},{12,4},{1,9},{5,13},{9,1},{13,5},{2,10},{6,14},... | collective-permute-start | bytes 884744 | tf_op jit(solution)/shard_map/ppermute | solution.py:19
  46.7 25.5 %collective-permute-start.9 = (bf16[1,3,6,2,16,256]{5,4,3,2,1,0:T(8,128)(2,1)S(1)}, bf16[1,3,6,2,16,256]{5,4,3,2,1,0:T(8,128)(2,1)S(1)}, u32[]{:S(2)}, u32[]{:S(2)}) collective-permute-start(bf16[1,3,6,2,16,256]{5,4,3,2,1,0:T(8,128)(2,1)S(1)} %get-tuple-element.118.refs_0_), channel_id=1, source_target_pairs={{0,4},{4,0},{8,12},{12,8},{1,5},{5,1},{9,13},{13,9},{2,6},{6,2},{1... | collective-permute-start | bytes 884744 | tf_op jit(solution)/shard_map/ppermute | solution.py:19
  59.3 15.5 %collective-permute-start.10 = (bf16[1,3,6,2,16,256]{5,4,3,2,1,0:T(8,128)(2,1)S(1)}, bf16[1,3,6,2,16,256]{5,4,3,2,1,0:T(8,128)(2,1)S(1)}, u32[]{:S(2)}, u32[]{:S(2)}) collective-permute-start(bf16[1,3,6,2,16,256]{5,4,3,2,1,0:T(8,128)(2,1)S(1)} %get-tuple-element.121.refs_0_), channel_id=1, source_target_pairs={{0,8},{4,12},{8,0},{12,4},{1,9},{5,13},{9,1},{13,5},{2,10},{6,14},... | collective-permute-start | bytes 884744 | tf_op jit(solution)/shard_map/ppermute | solution.py:19
  59.3 16.6 %collective-permute-start.11 = (bf16[1,3,6,2,16,256]{5,4,3,2,1,0:T(8,128)(2,1)S(1)}, bf16[1,3,6,2,16,256]{5,4,3,2,1,0:T(8,128)(2,1)S(1)}, u32[]{:S(2)}, u32[]{:S(2)}) collective-permute-start(bf16[1,3,6,2,16,256]{5,4,3,2,1,0:T(8,128)(2,1)S(1)} %get-tuple-element.125.refs_0_), channel_id=1, source_target_pairs={{0,4},{4,0},{8,12},{12,8},{1,5},{5,1},{9,13},{13,9},{2,6},{6,2},{1... | collective-permute-start | bytes 884744 | tf_op jit(solution)/shard_map/ppermute | solution.py:19
  63.6 4.6 %collective-permute-start.8 = (bf16[6,2,16,256]{3,2,1,0:T(8,128)(2,1)S(1)}, bf16[6,2,16,256]{3,2,1,0:T(8,128)(2,1)S(1)}, u32[]{:S(2)}, u32[]{:S(2)}) collective-permute-start(bf16[6,2,16,256]{3,2,1,0:T(8,128)(2,1)S(1)} %get-tuple-element.116), channel_id=1, source_target_pairs={{0,16},{16,0},{1,17},{17,1},{2,18},{18,2},{3,19},{19,3},{4,20},{20... | collective-permute-start | bytes 294920 | tf_op jit(solution)/shard_map/ppermute | solution.py:19
  71.3 8.9 %collective-permute-start.12 = (bf16[1,3,6,2,16,256]{5,4,3,2,1,0:T(8,128)(2,1)S(1)}, bf16[1,3,6,2,16,256]{5,4,3,2,1,0:T(8,128)(2,1)S(1)}, u32[]{:S(2)}, u32[]{:S(2)}) collective-permute-start(bf16[1,3,6,2,16,256]{5,4,3,2,1,0:T(8,128)(2,1)S(1)} %get-tuple-element.128.refs_0_), channel_id=1, source_target_pairs={{0,4},{4,0},{8,12},{12,8},{1,5},{5,1},{9,13},{13,9},{2,6},{6,2},{1... | collective-permute-start | bytes 884744 | tf_op jit(solution)/shard_map/ppermute | solution.py:19
  77.0 10.8 %collective-permute-start.15 = (bf16[512,256]{1,0:T(8,128)(2,1)S(1)}, bf16[512,256]{1,0:T(8,128)(2,1)S(1)}, u32[]{:S(2)}, u32[]{:S(2)}) collective-permute-start(bf16[512,256]{1,0:T(8,128)(2,1)S(1)} %get-tuple-element.137), channel_id=1, source_target_pairs={{0,1},{1,0},{2,3},{3,2},{4,5},{5,4},{6,7},{7,6},{8,9},{9,8},{10,11... | collective-permute-start | bytes 786440 | tf_op jit(solution)/shard_map/ppermute | solution.py:19
  77.1 12.3 %collective-permute-start.16 = (bf16[1,3,6,2,16,256]{5,4,3,2,1,0:T(8,128)(2,1)S(1)}, bf16[1,3,6,2,16,256]{5,4,3,2,1,0:T(8,128)(2,1)S(1)}, u32[]{:S(2)}, u32[]{:S(2)}) collective-permute-start(bf16[1,3,6,2,16,256]{5,4,3,2,1,0:T(8,128)(2,1)S(1)} %get-tuple-element.139.refs_0_), channel_id=1, source_target_pairs={{0,4},{4,0},{8,12},{12,8},{1,5},{5,1},{9,13},{13,9},{2,6},{6,2},{1... | collective-permute-start | bytes 884744 | tf_op jit(solution)/shard_map/ppermute | solution.py:19
  78.2 6.3 %collective-permute-start.13 = (bf16[256,256]{1,0:T(8,128)(2,1)S(1)}, bf16[256,256]{1,0:T(8,128)(2,1)S(1)}, u32[]{:S(2)}, u32[]{:S(2)}) collective-permute-start(bf16[256,256]{1,0:T(8,128)(2,1)S(1)} %get-tuple-element.132), channel_id=1, source_target_pairs={{0,1},{1,0},{2,3},{3,2},{4,5},{5,4},{6,7},{7,6},{8,9},{9,8},{10,11... | collective-permute-start | bytes 393224 | tf_op jit(solution)/shard_map/ppermute | solution.py:19
  78.4 6.2 %collective-permute-start.14 = (bf16[256,256]{1,0:T(8,128)(2,1)S(1)}, bf16[256,256]{1,0:T(8,128)(2,1)S(1)}, u32[]{:S(2)}, u32[]{:S(2)}) collective-permute-start(bf16[256,256]{1,0:T(8,128)(2,1)S(1)} %get-tuple-element.134), channel_id=1, source_target_pairs={{0,1},{1,0},{2,3},{3,2},{4,5},{5,4},{6,7},{7,6},{8,9},{9,8},{10,11... | collective-permute-start | bytes 393224 | tf_op jit(solution)/shard_map/ppermute | solution.py:19
  85.2 7.9 %collective-permute-start.17 = (bf16[512,256]{1,0:T(8,128)(2,1)S(1)}, bf16[512,256]{1,0:T(8,128)(2,1)S(1)}, u32[]{:S(2)}, u32[]{:S(2)}) collective-permute-start(bf16[512,256]{1,0:T(8,128)(2,1)S(1)} %get-tuple-element.146.refs_0_), channel_id=1, source_target_pairs={{0,4},{4,0},{8,12},{12,8},{1,5},{5,1},{9,13},{13,9},{2,6},{6,2},{1... | collective-permute-start | bytes 786440 | tf_op jit(solution)/shard_map/ppermute | solution.py:19
  88.4 6.4 %collective-permute-start.18 = (bf16[512,256]{1,0:T(8,128)(2,1)S(1)}, bf16[512,256]{1,0:T(8,128)(2,1)S(1)}, u32[]{:S(2)}, u32[]{:S(2)}) collective-permute-start(bf16[512,256]{1,0:T(8,128)(2,1)S(1)} %get-tuple-element.147.refs_0_), channel_id=1, source_target_pairs={{0,16},{16,0},{1,17},{17,1},{2,18},{18,2},{3,19},{19,3},{4,20},{20... | collective-permute-start | bytes 786440 | tf_op jit(solution)/shard_map/ppermute | solution.py:19
  92.5 2.9 %collective-permute-start.19 = (bf16[288,256]{1,0:T(8,128)(2,1)S(1)}, bf16[288,256]{1,0:T(8,128)(2,1)S(1)}, u32[]{:S(2)}, u32[]{:S(2)}) collective-permute-start(bf16[288,256]{1,0:T(8,128)(2,1)S(1)} %get-tuple-element.150), channel_id=1, source_target_pairs={{0,1},{1,0},{2,3},{3,2},{4,5},{5,4},{6,7},{7,6},{8,9},{9,8},{10,11... | collective-permute-start | bytes 442376 | tf_op jit(solution)/shard_map/ppermute | solution.py:19
  92.6 2.8 %collective-permute-start.20 = (bf16[256,256]{1,0:T(8,128)(2,1)S(1)}, bf16[256,256]{1,0:T(8,128)(2,1)S(1)}, u32[]{:S(2)}, u32[]{:S(2)}) collective-permute-start(bf16[256,256]{1,0:T(8,128)(2,1)S(1)} %get-tuple-element.152), channel_id=1, source_target_pairs={{0,1},{1,0},{2,3},{3,2},{4,5},{5,4},{6,7},{7,6},{8,9},{9,8},{10,11... | collective-permute-start | bytes 393224 | tf_op jit(solution)/shard_map/ppermute | solution.py:19
  96.0 7.6 %collective-permute-start.21 = (bf16[544,256]{1,0:T(8,128)(2,1)S(1)}, bf16[544,256]{1,0:T(8,128)(2,1)S(1)}, u32[]{:S(2)}, u32[]{:S(2)}) collective-permute-start(bf16[544,256]{1,0:T(8,128)(2,1)S(1)} %get-tuple-element.154.refs_0_), channel_id=1, source_target_pairs={{0,2},{1,3},{2,0},{3,1},{4,6},{5,7},{6,4},{7,5},{8,10},{9,11},{10,... | collective-permute-start | bytes 835592 | tf_op jit(solution)/shard_map/ppermute | solution.py:19
  97.4 9.6 %collective-permute-start.22 = (bf16[512,256]{1,0:T(8,128)(2,1)S(1)}, bf16[512,256]{1,0:T(8,128)(2,1)S(1)}, u32[]{:S(2)}, u32[]{:S(2)}) collective-permute-start(bf16[512,256]{1,0:T(8,128)(2,1)S(1)} %get-tuple-element.157.refs_0_), channel_id=1, source_target_pairs={{0,16},{16,0},{1,17},{17,1},{2,18},{18,2},{3,19},{19,3},{4,20},{20... | collective-permute-start | bytes 786440 | tf_op jit(solution)/shard_map/ppermute | solution.py:19
  99.0 19.2 %collective-permute-start.26 = (bf16[432,512]{1,0:T(8,128)(2,1)S(1)}, bf16[432,512]{1,0:T(8,128)(2,1)S(1)}, u32[]{:S(2)}, u32[]{:S(2)}) collective-permute-start(bf16[432,512]{1,0:T(8,128)(2,1)S(1)} %get-tuple-element.164), channel_id=1, source_target_pairs={{0,16},{16,0},{1,17},{17,1},{2,18},{18,2},{3,19},{19,3},{4,20},{20... | collective-permute-start | bytes 1327112 | tf_op jit(solution)/shard_map/ppermute | solution.py:19
  104.3 15.7 %collective-permute-start.25 = (bf16[544,256]{1,0:T(8,128)(2,1)S(1)}, bf16[544,256]{1,0:T(8,128)(2,1)S(1)}, u32[]{:S(2)}, u32[]{:S(2)}) collective-permute-start(bf16[544,256]{1,0:T(8,128)(2,1)S(1)} %get-tuple-element.163.refs_0_), channel_id=1, source_target_pairs={{0,16},{16,0},{1,17},{17,1},{2,18},{18,2},{3,19},{19,3},{4,20},{20... | collective-permute-start | bytes 835592 | tf_op jit(solution)/shard_map/ppermute | solution.py:19
  106.1 8.7 %collective-permute-start.23 = (bf16[512,256]{1,0:T(8,128)(2,1)S(1)}, bf16[512,256]{1,0:T(8,128)(2,1)S(1)}, u32[]{:S(2)}, u32[]{:S(2)}) collective-permute-start(bf16[512,256]{1,0:T(8,128)(2,1)S(1)} %get-tuple-element.159.refs_0_), channel_id=1, source_target_pairs={{0,2},{1,3},{2,0},{3,1},{4,6},{5,7},{6,4},{7,5},{8,10},{9,11},{10,... | collective-permute-start | bytes 786440 | tf_op jit(solution)/shard_map/ppermute | solution.py:19
  107.6 9.9 %collective-permute-start.24 = (bf16[512,256]{1,0:T(8,128)(2,1)S(1)}, bf16[512,256]{1,0:T(8,128)(2,1)S(1)}, u32[]{:S(2)}, u32[]{:S(2)}) collective-permute-start(bf16[512,256]{1,0:T(8,128)(2,1)S(1)} %get-tuple-element.161.refs_0_), channel_id=1, source_target_pairs={{0,2},{1,3},{2,0},{3,1},{4,6},{5,7},{6,4},{7,5},{8,10},{9,11},{10,... | collective-permute-start | bytes 786440 | tf_op jit(solution)/shard_map/ppermute | solution.py:19
  120.6 3.5 %collective-permute-start.29 = (f32[544,256]{1,0:T(8,128)S(1)}, f32[544,256]{1,0:T(8,128)S(1)}, u32[]{:S(2)}, u32[]{:S(2)}) collective-permute-start(f32[544,256]{1,0:T(8,128)S(1)} %get-tuple-element.175.own21.low21), channel_id=1, source_target_pairs={{0,1},{1,0},{2,3},{3,2},{4,5},{5,4},{6,7},{7,6},{8,9},{9,8},{10,11... | collective-permute-start | bytes 1671176 | tf_op jit(solution)/shard_map/ppermute | solution.py:19
  120.7 2.8 %collective-permute-start.27 = (f32[512,256]{1,0:T(8,128)S(1)}, f32[512,256]{1,0:T(8,128)S(1)}, u32[]{:S(2)}, u32[]{:S(2)}) collective-permute-start(f32[512,256]{1,0:T(8,128)S(1)} %get-tuple-element.173.own30), channel_id=1, source_target_pairs={{0,1},{1,0},{2,3},{3,2},{4,5},{5,4},{6,7},{7,6},{8,9},{9,8},{10,11... | collective-permute-start | bytes 1572872 | tf_op jit(solution)/shard_map/ppermute | solution.py:19
  121.2 2.9 %collective-permute-start.28 = (f32[512,256]{1,0:T(8,128)S(1)}, f32[512,256]{1,0:T(8,128)S(1)}, u32[]{:S(2)}, u32[]{:S(2)}) collective-permute-start(f32[512,256]{1,0:T(8,128)S(1)} %get-tuple-element.174.own_proj), channel_id=1, source_target_pairs={{0,1},{1,0},{2,3},{3,2},{4,5},{5,4},{6,7},{7,6},{8,9},{9,8},{10,11... | collective-permute-start | bytes 1572872 | tf_op jit(solution)/shard_map/ppermute | solution.py:19
